TPU v7x, 32 devices: a whole 2x2x4 slice. The times are simulated.
32 devices in a mesh: section: 2 (over y), dp: 16 (over z, x, core).
Axes of the slice: x: 2, y: 2, z: 4, core: 2. Of those that a mesh axis runs over, the one named last changes fastest.
Arguments:
- features: bfloat16 [2, 16, 512, 1024], P(None, 'dp'), may hold values from -18 to 18
- cotangent: bfloat16 [2, 16, 512, 1024], P(None, 'dp'), may hold values from -6 to 6
- lengths: int32 [2, 16], P(None, 'dp'), may hold values from 32 to 512, as said below
- codebook_index: int32 [2, 16], P(None, 'dp'), may hold values from 0 to 6
- attention_in: bfloat16 [2, 1024, 3072], P('section'), may hold values from -0.1875 to 0.1875
- attention_out: bfloat16 [2, 1024, 1024], P('section'), may hold values from -0.75 to 0.75
- feed_up: bfloat16 [2, 1024, 4096], P('section'), may hold values from -1 to 1
- feed_down: bfloat16 [2, 4096, 1024], P('section'), may hold values from -0.09375 to 0.09375
- vectors: float32 [2, 12288], P('section'), may hold values from -1.5 to 1.5
- adaptive_weight: bfloat16 [1024, 4096], replicated, may hold values from -0.046875 to 0.046875
- codebook_table: bfloat16 [7, 1024], replicated, may hold values from -6 to 6
Outputs:
- layer_outputs: bfloat16 [2, 2, 16, 512, 1024], P('section', None, 'dp')
- input_grads: bfloat16 [2, 2, 16, 512, 1024], P('section', None, 'dp')
- grad_attention_in: float32 [2, 1024, 3072], P('section', 'dp')
- grad_attention_out: float32 [2, 1024, 1024], P('section', 'dp')
- grad_feed_up: float32 [2, 1024, 4096], P('section', 'dp')
- grad_feed_down: float32 [2, 4096, 1024], P('section', 'dp')
- grad_vectors: float32 [2, 12288], P('section', 'dp')
- grad_adaptive: float32 [1024, 4096], P(None, ('section', 'dp'))
- residual_rms: float32 [2, 4], P('section')
Inputs may be any that keep to these rules, and one draw needn't show every extreme that they name: `lengths`: in every draw some utterance has all 512 frames valid.
All inputs are finite; a program needn't handle non-finite values.
Results may differ from a plain program's by a relative error of at most 0.017.
Values may be sent and summed in bfloat16 or wider, within the bound.
No kernel may reach another device: no remote copies, remote signals or barrier semaphores. Data moves between devices by JAX's collectives and lax.ppermute only.
A program may use at most 384 MiB of HBM per device.

v0:
```python
import jax
import jax.numpy as jnp
from jax import lax
from jax.sharding import PartitionSpec as P

HEAD = 64


norm_eps = 1e-05
root_half = 0.7071067811865476
slope_scale = 0.3989422804014327
score_scale = 0.125
big_negative = -1e30
highest = lax.Precision.HIGHEST


def from_behind(value, axis, by):
    length = lax.axis_size(axis)
    pairs = [(i, i + by) for i in range(length) if 0 <= i + by < length]
    return lax.ppermute(value, axis, pairs)


def transposed_product(former, latter):
    return lax.dot_general(
        former, latter, (((0,), (0,)), ((), ())), preferred_element_type=jnp.float32
    )


def product_back(former, latter):
    return lax.dot_general(
        former, latter, (((1,), (1,)), ((), ())), preferred_element_type=jnp.float32
    )


def norm_forward(residual, scaling, offset):
    average = jnp.mean(residual, axis=-1, keepdims=True)
    centered = residual - average
    inverse = lax.rsqrt(jnp.mean(centered * centered, axis=-1, keepdims=True) + norm_eps)
    normed = centered * inverse
    return (normed * scaling + offset, normed, inverse)


def norm_backward(grad_out, normed, inverse, scaling):
    grad_normed = grad_out * scaling
    inner_mean = jnp.mean(grad_normed, axis=-1, keepdims=True)
    cross_mean = jnp.mean(grad_normed * normed, axis=-1, keepdims=True)
    grad_rows = inverse * (grad_normed - inner_mean - normed * cross_mean)
    return (grad_rows, jnp.sum(grad_out * normed, axis=0), jnp.sum(grad_out, axis=0))


def smooth_gate(values):
    return 0.5 * values * (1.0 + lax.erf(values * root_half))


def gate_slope(values):
    return 0.5 * (1.0 + lax.erf(values * root_half)) + values * slope_scale * jnp.exp(
        -0.5 * values * values
    )


def key_mask(frames, length, adaptive_flag):
    places = jnp.arange(frames, dtype=jnp.int32)
    allowed = places[None, :] < length
    return allowed & ((places[None, :] <= places[:, None]) | adaptive_flag)


def split_vectors(vector, condition, model_width):
    gain_rows = vector[: 4 * model_width] + condition
    return (
        gain_rows[:model_width],
        gain_rows[model_width : 2 * model_width],
        gain_rows[2 * model_width : 3 * model_width],
        gain_rows[3 * model_width :],
        vector[4 * model_width : 5 * model_width],
        vector[5 * model_width : 6 * model_width],
        vector[6 * model_width : 7 * model_width],
        vector[7 * model_width : 8 * model_width],
        vector[8 * model_width :],
    )


def attention_scores(projected, length, adaptive_flag):
    frames = projected.shape[0]
    model_width = projected.shape[1] // 3
    head_count = model_width // HEAD
    queries = projected[:, :model_width].reshape(frames, head_count, HEAD)
    key_rows = projected[:, model_width : 2 * model_width].reshape(frames, head_count, HEAD)
    scores = (
        jnp.einsum("qhd,khd->hqk", queries, key_rows, preferred_element_type=jnp.float32)
        * score_scale
    )
    return jnp.where(key_mask(frames, length, adaptive_flag)[None], scores, big_negative)


def layer_forward(residual, length, adaptive_flag, vector_parts, matrices):
    (
        gain_one,
        bias_one,
        gain_two,
        bias_two,
        query_bias,
        value_bias,
        mixer_bias,
        down_bias,
        up_bias,
    ) = vector_parts
    weight_in, weight_out, weight_up, weight_down = matrices
    frames, model_width = residual.shape
    head_count = model_width // HEAD
    mixer_full, mixer_normed, mixer_inverse = norm_forward(residual, gain_one, bias_one)
    mixer_input = mixer_full.astype(jnp.bfloat16)
    projected = jnp.dot(mixer_input, weight_in, preferred_element_type=jnp.float32)
    projected = (
        projected + jnp.concatenate([query_bias, jnp.zeros_like(query_bias), value_bias])
    ).astype(jnp.bfloat16)
    scores = attention_scores(projected, length, adaptive_flag)
    row_max = jnp.max(scores, axis=-1, keepdims=True)
    exponent = jnp.exp(scores - row_max)
    row_total = jnp.sum(exponent, axis=-1, keepdims=True)
    attn_weights = (exponent / row_total).astype(jnp.bfloat16)
    log_total = row_max + jnp.log(row_total)
    value_rows = projected[:, 2 * model_width :].reshape(frames, head_count, HEAD)
    context = jnp.einsum(
        "hqk,khd->qhd", attn_weights, value_rows, preferred_element_type=jnp.float32
    )
    context = context.reshape(frames, model_width).astype(jnp.bfloat16)
    attn_branch = jnp.dot(context, weight_out, preferred_element_type=jnp.float32) + mixer_bias
    middle = residual + attn_branch
    feed_full, feed_normed, feed_inverse = norm_forward(middle, gain_two, bias_two)
    feed_input = feed_full.astype(jnp.bfloat16)
    hidden_pre = jnp.dot(feed_input, weight_up, preferred_element_type=jnp.float32) + up_bias
    hidden_act = smooth_gate(hidden_pre).astype(jnp.bfloat16)
    feed_branch = jnp.dot(hidden_act, weight_down, preferred_element_type=jnp.float32) + down_bias
    output = middle + feed_branch
    valid_rows = (jnp.arange(frames, dtype=jnp.int32) < length).astype(jnp.float32)[:, None]
    squares = jnp.stack(
        [
            jnp.sum(valid_rows * middle * middle),
            jnp.sum(valid_rows * output * output),
            jnp.sum(valid_rows * attn_branch * attn_branch),
            jnp.sum(valid_rows * feed_branch * feed_branch),
        ]
    )
    stored = (
        mixer_input,
        mixer_normed,
        mixer_inverse,
        projected,
        log_total,
        context,
        feed_input,
        feed_normed,
        feed_inverse,
        hidden_pre,
        hidden_act,
    )
    return (output, stored, squares)


def layer_backward(grad_out, stored, length, adaptive_flag, vector_parts, matrices):
    gain_one = vector_parts[0]
    gain_two = vector_parts[2]
    weight_in, weight_out, weight_up, weight_down = matrices
    (
        mixer_input,
        mixer_normed,
        mixer_inverse,
        projected,
        log_total,
        context,
        feed_input,
        feed_normed,
        feed_inverse,
        hidden_pre,
        hidden_act,
    ) = stored
    frames, model_width = grad_out.shape
    head_count = model_width // HEAD
    grad_feed = grad_out.astype(jnp.bfloat16)
    grad_down = transposed_product(hidden_act, grad_feed)
    bias_down = jnp.sum(grad_feed, axis=0, dtype=jnp.float32)
    grad_pre = (product_back(grad_feed, weight_down) * gate_slope(hidden_pre)).astype(jnp.bfloat16)
    grad_up = transposed_product(feed_input, grad_pre)
    bias_up = jnp.sum(grad_pre, axis=0, dtype=jnp.float32)
    grad_feed_input = product_back(grad_pre, weight_up)
    grad_middle, gain_two_grad, bias_two_grad = norm_backward(
        grad_feed_input, feed_normed, feed_inverse, gain_two
    )
    grad_middle = grad_middle + grad_out
    grad_attn = grad_middle.astype(jnp.bfloat16)
    grad_out_weight = transposed_product(context, grad_attn)
    bias_mixer = jnp.sum(grad_attn, axis=0, dtype=jnp.float32)
    grad_context = (
        product_back(grad_attn, weight_out).astype(jnp.bfloat16).reshape(frames, head_count, HEAD)
    )
    scores = attention_scores(projected, length, adaptive_flag)
    attn_weights = jnp.exp(scores - log_total)
    queries = projected[:, :model_width].reshape(frames, head_count, HEAD)
    key_rows = projected[:, model_width : 2 * model_width].reshape(frames, head_count, HEAD)
    value_rows = projected[:, 2 * model_width :].reshape(frames, head_count, HEAD)
    grad_weights = jnp.einsum(
        "qhd,khd->hqk", grad_context, value_rows, preferred_element_type=jnp.float32
    )
    grad_values = jnp.einsum(
        "hqk,qhd->khd",
        attn_weights.astype(jnp.bfloat16),
        grad_context,
        preferred_element_type=jnp.float32,
    )
    row_inner = jnp.sum(grad_weights * attn_weights, axis=-1, keepdims=True)
    grad_scores = (attn_weights * (grad_weights - row_inner)).astype(jnp.bfloat16)
    grad_queries = (
        jnp.einsum("hqk,khd->qhd", grad_scores, key_rows, preferred_element_type=jnp.float32)
        * score_scale
    )
    grad_keys = (
        jnp.einsum("hqk,qhd->khd", grad_scores, queries, preferred_element_type=jnp.float32)
        * score_scale
    )
    grad_projected = jnp.concatenate(
        [
            grad_queries.reshape(frames, model_width),
            grad_keys.reshape(frames, model_width),
            grad_values.reshape(frames, model_width),
        ],
        axis=1,
    ).astype(jnp.bfloat16)
    grad_in_weight = transposed_product(mixer_input, grad_projected)
    column_sums = jnp.sum(grad_projected, axis=0, dtype=jnp.float32)
    grad_mixer_input = product_back(grad_projected, weight_in)
    grad_rows, gain_one_grad, bias_one_grad = norm_backward(
        grad_mixer_input, mixer_normed, mixer_inverse, gain_one
    )
    grad_input = grad_middle + grad_rows
    vector_grad = jnp.concatenate(
        [
            gain_one_grad,
            bias_one_grad,
            gain_two_grad,
            bias_two_grad,
            column_sums[:model_width],
            column_sums[2 * model_width :],
            bias_mixer,
            bias_down,
            bias_up,
        ]
    )
    return (grad_input, (grad_in_weight, grad_out_weight, grad_up, grad_down, vector_grad))


def guarded(active, function, operands):

    def skipped(*inputs):
        return jax.tree.map(jnp.zeros_like, function(*inputs))

    return lax.cond(active, function, skipped, *operands)


def shards(
    features,
    cotangent,
    lengths,
    codebook_index,
    attention_in,
    attention_out,
    feed_up,
    feed_down,
    vectors,
    adaptive_weight,
    codebook_table,
):
    section_index = lax.axis_index("section")
    is_first = section_index == 0
    adaptive_flag = section_index == 1
    micro_count = features.shape[0]
    frames = features.shape[2]
    model_width = features.shape[3]
    matrices = (attention_in[0], attention_out[0], feed_up[0], feed_down[0])
    vector = vectors[0]
    condition_table = jnp.dot(codebook_table, adaptive_weight, preferred_element_type=jnp.float32)
    one_hot = (
        codebook_index[:, 0][:, None]
        == jnp.arange(condition_table.shape[0], dtype=jnp.int32)[None, :]
    ).astype(jnp.float32)
    condition_rows = jnp.dot(one_hot, condition_table, precision=highest) * adaptive_flag.astype(
        jnp.float32
    )
    valid_lengths = lengths[:, 0]
    places = jnp.arange(frames, dtype=jnp.int32)

    def forward_step(residual, length, vector_parts):
        return layer_forward(residual, length, adaptive_flag, vector_parts, matrices)

    def backward_again(upstream, residual, length, vector_parts):
        output, stored, squares = layer_forward(
            residual.astype(jnp.float32), length, adaptive_flag, vector_parts, matrices
        )
        return layer_backward(upstream, stored, length, adaptive_flag, vector_parts, matrices)

    received = jnp.zeros((frames, model_width), jnp.bfloat16)
    tick_outputs = []
    tick_inputs = []
    square_sums = jnp.zeros((4,), jnp.float32)
    for step_index in range(micro_count + 1):
        own_slot = min(step_index, micro_count - 1)
        prior_slot = max(step_index - 1, 0)
        slot_index = jnp.where(is_first, own_slot, prior_slot)
        active = jnp.where(is_first, step_index < micro_count, step_index >= 1)
        residual_in = jnp.where(is_first, features[own_slot, 0], received)
        vector_parts = split_vectors(vector, condition_rows[slot_index], model_width)
        output, stored, squares = guarded(
            active,
            forward_step,
            (residual_in.astype(jnp.float32), valid_lengths[slot_index], vector_parts),
        )
        square_sums = square_sums + squares
        outgoing = output.astype(jnp.bfloat16)
        tick_outputs.append(outgoing)
        tick_inputs.append(residual_in)
        if step_index < micro_count:
            received = from_behind(outgoing, "section", 1)
    grad_received = jnp.zeros((frames, model_width), jnp.bfloat16)
    tick_grads = []
    weight_totals = (
        jnp.zeros(matrices[0].shape, jnp.float32),
        jnp.zeros(matrices[1].shape, jnp.float32),
        jnp.zeros(matrices[2].shape, jnp.float32),
        jnp.zeros(matrices[3].shape, jnp.float32),
        jnp.zeros(vector.shape, jnp.float32),
    )
    table_grad = jnp.zeros(condition_table.shape, jnp.float32)
    for step_index in range(micro_count + 1):
        late_slot = max(micro_count - 1 - step_index, 0)
        early_slot = min(micro_count - step_index, micro_count - 1)
        slot_index = jnp.where(is_first, early_slot, late_slot)
        active = jnp.where(is_first, step_index >= 1, step_index < micro_count)
        masked = (
            cotangent[late_slot, 0].astype(jnp.float32)
            * (places < valid_lengths[late_slot]).astype(jnp.float32)[:, None]
        )
        upstream = jnp.where(is_first, grad_received.astype(jnp.float32), masked)
        length = valid_lengths[slot_index]
        vector_parts = split_vectors(vector, condition_rows[slot_index], model_width)
        residual_in = jnp.where(is_first, tick_inputs[early_slot], tick_inputs[late_slot + 1])
        grad_input, gradients = guarded(
            active, backward_again, (upstream, residual_in, length, vector_parts)
        )
        outgoing = grad_input.astype(jnp.bfloat16)
        tick_grads.append(outgoing)
        if step_index < micro_count:
            grad_received = from_behind(outgoing, "section", -1)
        table_grad = table_grad + one_hot[slot_index][:, None] * gradients[4][
            None, : 4 * model_width
        ] * adaptive_flag.astype(jnp.float32)
        weight_totals = jax.tree.map(jnp.add, weight_totals, gradients)
    reduced = (
        lax.psum_scatter(weight_totals[0][None], "dp", scatter_dimension=1, tiled=True),
        lax.psum_scatter(weight_totals[1][None], "dp", scatter_dimension=1, tiled=True),
        lax.psum_scatter(weight_totals[2][None], "dp", scatter_dimension=1, tiled=True),
        lax.psum_scatter(weight_totals[3][None], "dp", scatter_dimension=1, tiled=True),
        lax.psum_scatter(weight_totals[4][None], "dp", scatter_dimension=1, tiled=True),
    )
    table_share = lax.psum_scatter(table_grad, ("section", "dp"), scatter_dimension=1, tiled=True)
    grad_adaptive = lax.dot_general(
        codebook_table.astype(jnp.float32),
        table_share,
        (((0,), (0,)), ((), ())),
        precision=highest,
        preferred_element_type=jnp.float32,
    )
    token_count = jnp.sum(valid_lengths).astype(jnp.float32)
    totals, counted = lax.psum((square_sums, token_count), "dp")
    residual_rms = jnp.sqrt(totals / (counted * model_width))[None]
    layer_outputs = jnp.stack(
        [
            jnp.where(is_first, tick_outputs[micro_slot], tick_outputs[micro_slot + 1])
            for micro_slot in range(micro_count)
        ]
    )[None, :, None]
    input_grads = jnp.stack(
        [
            jnp.where(
                is_first,
                tick_grads[micro_count - micro_slot],
                tick_grads[micro_count - 1 - micro_slot],
            )
            for micro_slot in range(micro_count)
        ]
    )[None, :, None]
    return (
        layer_outputs,
        input_grads,
        reduced[0],
        reduced[1],
        reduced[2],
        reduced[3],
        reduced[4],
        grad_adaptive,
        residual_rms,
    )


def solution(mesh):
    placed = (
        P(None, "dp", None, None),
        P(None, "dp", None, None),
        P(None, "dp"),
        P(None, "dp"),
        P("section", None, None),
        P("section", None, None),
        P("section", None, None),
        P("section", None, None),
        P("section", None),
        P(),
        P(),
    )
    return jax.shard_map(
        shards,
        mesh=mesh,
        in_specs=placed,
        out_specs=(
            P("section", None, "dp", None, None),
            P("section", None, "dp", None, None),
            P("section", "dp", None),
            P("section", "dp", None),
            P("section", "dp", None),
            P("section", "dp", None),
            P("section", "dp"),
            P(None, ("section", "dp")),
            P("section", None),
        ),
        check_vma=False,
    )
```

profile of v0, /device:TPU:0, one launch (start us, length us, event | category | flops | bytes accessed | tf_op | source)
XLA Modules:
  0.0 1475.3 jit_solution(13460258338540388367)
XLA Ops:
  16.7 59.3 %conditional.4 = (f32[4]{0:T(128)S(1)}, bf16[512,1024]{1,0:T(8,128)(2,1)}) conditional(s32[]{:T(128)} %convert_element_type.415, () %tuple.60, (s32[]{:T(128)}, bf16[512,1024]{1,0:T(8,128)(2,1)S(1)}, f32[1024]{0:T(1024)}, f32[1024]{0:T(1024)}, bf16[1024,3072]{1,0:T(8,128)(2,1)S(1)}, /*index=5*/f32[1024]{0:T(1024)S(1)}, f32[1024]{0:T(1024)S(1)}, ...), branch_computations={%region_0.1_spmd, %region_1.12_spmd} | conditional | flops 14021828608 | bytes 104526952 | solution.py:256
  31.5 10.9 fusion.231
  54.4 18.7 %fusion.13 = (f32[]{:T(128)}, f32[]{:T(128)}, f32[]{:T(128)}, f32[]{:T(128)}, bf16[512,1024]{1,0:T(8,128)(2,1)}) fusion(f32[512]{0:T(512)S(1)} %get-tuple-element.518, f32[512,1024]{1,0:T(8,128)} %copy-done.72, f32[1024]{0:T(1024)S(1)} %get-tuple-element.317, f32[512,1024]{1,0:T(8,128)} %get-tuple-element.516, f32[1024]{0:T(1024)S(1)} %get-tuple-element.311, ...), kind=kOutput, calls=%fused_computation.25 | convolution fusion | flops 8613527552 | bytes 22059024 | tf_op jit(solution)/shard_map/cond/branch_1_fun/dot_general | solution.py:133
  78.9 22.1 %collective-permute-done = bf16[512,1024]{1,0:T(8,128)(2,1)S(1)} collective-permute-done((bf16[512,1024]{1,0:T(8,128)(2,1)}, bf16[512,1024]{1,0:T(8,128)(2,1)S(1)}, u32[]{:S(2)}, u32[]{:S(2)}) %collective-permute-start) | collective-permute-done | bytes 1048608 | tf_op jit(solution)/shard_map/ppermute | solution.py:20
  141.7 11.0 multiply_convert_fusion.13
  165.5 21.1 %collective-permute-done.1 = bf16[512,1024]{1,0:T(8,128)(2,1)} collective-permute-done((bf16[512,1024]{1,0:T(8,128)(2,1)}, bf16[512,1024]{1,0:T(8,128)(2,1)}, u32[]{:S(2)}, u32[]{:S(2)}) %collective-permute-start.1) | collective-permute-done | bytes 1048608 | tf_op jit(solution)/shard_map/ppermute | solution.py:20
  188.2 34.4 %conditional.6 = (f32[1024,3072]{1,0:T(8,128)}, f32[1024,1024]{1,0:T(8,128)}, f32[1024,4096]{1,0:T(8,128)}, f32[4096,1024]{1,0:T(8,128)}, f32[12288]{0:T(1024)}, /*index=5*/bf16[512,1024]{1,0:T(8,128)(2,1)}) conditional(s32[]{:T(128)} %convert_element_type.428, () %tuple.65, (pred[]{:T(512)}, bf16[512,1024]{1,0:T(8,128)(2,1)S(1)}, ...), branch_computations={%region_30.31_spmd, %region_31.51_spmd} | conditional | flops 37777809408 | bytes 622088000 | solution.py:256
  226.5 154.6 %collective-permute-done.2 = bf16[512,1024]{1,0:T(8,128)(2,1)S(1)} collective-permute-done((bf16[512,1024]{1,0:T(8,128)(2,1)}, bf16[512,1024]{1,0:T(8,128)(2,1)S(1)}, u32[]{:S(2)}, u32[]{:S(2)}) %collective-permute-start.2) | collective-permute-done | bytes 1048608 | tf_op jit(solution)/shard_map/ppermute | solution.py:20
  384.2 12.6 convert_reduce_fusion.11
  396.8 10.5 fusion.184
  422.2 13.5 multiply_reduce_fusion.15
  435.8 10.4 multiply_convert_fusion.12
  469.2 19.9 %collective-permute-done.3 = bf16[512,1024]{1,0:T(8,128)(2,1)S(1)} collective-permute-done((bf16[512,1024]{1,0:T(8,128)(2,1)S(1)}, bf16[512,1024]{1,0:T(8,128)(2,1)S(1)}, u32[]{:S(2)}, u32[]{:S(2)}) %collective-permute-start.3) | collective-permute-done | bytes 1048608 | tf_op jit(solution)/shard_map/ppermute | solution.py:20
  489.4 175.2 %conditional.7 = (f32[1024,3072]{1,0:T(8,128)}, f32[1024,1024]{1,0:T(8,128)}, f32[1024,4096]{1,0:T(8,128)}, f32[4096,1024]{1,0:T(8,128)}, f32[12288]{0:T(1024)}, /*index=5*/bf16[512,1024]{1,0:T(8,128)(2,1)}) conditional(s32[]{:T(128)} %convert_element_type.415, () %tuple.64, (pred[]{:T(512)}, bf16[512,1024]{1,0:T(8,128)(2,1)S(1)}, ...), branch_computations={%region_56.57_spmd, %region_57.77_spmd} | conditional | flops 37772566528 | bytes 655636288 | solution.py:256
  507.5 9.9 fusion.238
  535.2 11.0 fusion.156
  546.2 12.2 convert_reduce_fusion.6
  570.7 9.8 fusion.141
  580.5 13.9 multiply_reduce_fusion.9
  597.5 10.4 multiply_convert_fusion.7
  616.0 10.4 fusion.151
  630.6 9.7 fusion.155
  640.3 10.5 fusion.122
  687.8 15.5 %add_bitcast_fusion.2 = f32[1,1024,3072]{2,1,0:T(8,128)} fusion(f32[1024,3072]{1,0:T(8,128)} %get-tuple-element.402, f32[1024,3072]{1,0:T(8,128)} %get-tuple-element.401, f32[1024,3072]{1,0:T(8,128)S(1)} %fusion.217), kind=kLoop, calls=%fused_computation.301 | loop fusion | flops 6291456 | bytes 50331648 | tf_op jit(solution)/shard_map/broadcast_in_dim | solution.py:357
  711.8 17.9 %add_bitcast_fusion.1 = f32[1,1024,4096]{2,1,0:T(8,128)} fusion(f32[1024,4096]{1,0:T(8,128)} %get-tuple-element.406, f32[1024,4096]{1,0:T(8,128)} %get-tuple-element.405, f32[1024,4096]{1,0:T(8,128)S(1)} %fusion.220), kind=kLoop, calls=%fused_computation.292 | loop fusion | flops 8388608 | bytes 67108864 | tf_op jit(solution)/shard_map/broadcast_in_dim | solution.py:359
  737.4 17.6 %add_bitcast_fusion = f32[1,4096,1024]{2,1,0:T(8,128)} fusion(f32[4096,1024]{1,0:T(8,128)} %get-tuple-element.408, f32[4096,1024]{1,0:T(8,128)} %get-tuple-element.407, f32[4096,1024]{1,0:T(8,128)S(1)} %fusion.248), kind=kLoop, calls=%fused_computation.291 | loop fusion | flops 8388608 | bytes 67108864 | tf_op jit(solution)/shard_map/broadcast_in_dim | solution.py:360
  762.8 30.6 %all-reduce = (f32[4]{0:T(128)S(1)}, f32[]{:T(128)}) all-reduce(f32[4]{0:T(128)S(1)} %fusion.198, f32[]{:T(128)S(6)} %convert_element_type.449), channel_id=1, replica_groups=mesh['section'=2,'dp'=16] {'dp'}, use_global_device_ids=true, to_apply=%region_95.96 | all-reduce | flops 5 | bytes 40 | tf_op jit(solution)/shard_map/psum | solution.py:372
  799.2 91.3 %reduce-scatter.17.cloned.1.call-done = f32[7,128]{1,0:T(8,128)} async-done(((f32[7,4096]{1,0:T(8,128)}), f32[7,128]{1,0:T(8,128)}) %reduce-scatter.17.cloned.1.call-update) | async-done | bytes 3600 | tf_op jit(solution)/shard_map/reduce_scatter | solution.py:363
  892.6 71.0 %reduce-scatter.11.cloned.1.call-done = f32[1,64,1024]{2,1,0:T(8,128)} async-done(((f32[1,1024,1024]{2,1,0:T(8,128)}), f32[1,64,1024]{2,1,0:T(8,128)}) %reduce-scatter.11.cloned.1.call-update) | async-done | bytes 262160 | tf_op jit(solution)/shard_map/reduce_scatter | solution.py:358
  963.6 139.0 %reduce-scatter.9.cloned.1.call-done = f32[1,64,3072]{2,1,0:T(8,128)} async-done(((f32[1,1024,3072]{2,1,0:T(8,128)}), f32[1,64,3072]{2,1,0:T(8,128)}) %reduce-scatter.9.cloned.1.call-update) | async-done | bytes 786448 | tf_op jit(solution)/shard_map/reduce_scatter | solution.py:357
  1102.6 182.9 %reduce-scatter.13.cloned.1.call-done = f32[1,64,4096]{2,1,0:T(8,128)} async-done(((f32[1,1024,4096]{2,1,0:T(8,128)}), f32[1,64,4096]{2,1,0:T(8,128)}) %reduce-scatter.13.cloned.1.call-update) | async-done | bytes 1048592 | tf_op jit(solution)/shard_map/reduce_scatter | solution.py:359
  1285.4 182.7 %reduce-scatter.15.cloned.1.call-done = f32[1,256,1024]{2,1,0:T(8,128)} async-done(((f32[1,4096,1024]{2,1,0:T(8,128)}), f32[1,256,1024]{2,1,0:T(8,128)}) %reduce-scatter.15.cloned.1.call-update) | async-done | bytes 1048592 | tf_op jit(solution)/shard_map/reduce_scatter | solution.py:360
  (435 shorter events, 297.5 us)
Async XLA Ops:
  7.2 790.3 %reduce-scatter.19.cloned.1.call-start = ((), (), s32[]{:S(2)}) async-start(), calls=%async_computation.11 | async-start | bytes 6684672
  9.5 147.8 %copy-start.94 = (f32[1,1024]{1,0:T(1,128)}, f32[1,1024]{1,0:T(1,128)S(1)}, u32[]{:S(2)}) copy-start(f32[1,1024]{1,0:T(1,128)S(1)} %get-tuple-element.567) | copy-start | bytes 12292
  76.1 24.9 %collective-permute-start = (bf16[512,1024]{1,0:T(8,128)(2,1)}, bf16[512,1024]{1,0:T(8,128)(2,1)S(1)}, u32[]{:S(2)}, u32[]{:S(2)}) collective-permute-start(bf16[512,1024]{1,0:T(8,128)(2,1)} %get-tuple-element.397), channel_id=1, source_target_pairs={{0,16},{1,17},{2,18},{3,19},{4,20},{5,21},{6,22},{7,23},{8,24},{9,... | collective-permute-start | bytes 3145736 | tf_op jit(solution)/shard_map/ppermute | solution.py:20
  78.7 24.4 %copy-start.102 = (f32[1,1024]{1,0:T(1,128)}, f32[1,1024]{1,0:T(1,128)S(1)}, u32[]{:S(2)}) copy-start(f32[1,1024]{1,0:T(1,128)S(1)} %get-tuple-element.600) | copy-start | bytes 12292
  78.7 24.4 %copy-start.120 = (f32[1,1024]{1,0:T(1,128)}, f32[1,1024]{1,0:T(1,128)S(1)}, u32[]{:S(2)}) copy-start(f32[1,1024]{1,0:T(1,128)S(1)} %get-tuple-element.601) | copy-start | bytes 12292
  78.7 62.9 %copy-start.99 = (f32[1,1024]{1,0:T(1,128)}, f32[1,1024]{1,0:T(1,128)S(1)}, u32[]{:S(2)}) copy-start(f32[1,1024]{1,0:T(1,128)S(1)} %get-tuple-element.603) | copy-start | bytes 12292
  78.7 62.9 %copy-start.118 = (f32[1,1024]{1,0:T(1,128)}, f32[1,1024]{1,0:T(1,128)S(1)}, u32[]{:S(2)}) copy-start(f32[1,1024]{1,0:T(1,128)S(1)} %get-tuple-element.602) | copy-start | bytes 12292
  78.7 109.4 %copy-start.97 = (f32[1,1024]{1,0:T(1,128)}, f32[1,1024]{1,0:T(1,128)S(1)}, u32[]{:S(2)}) copy-start(f32[1,1024]{1,0:T(1,128)S(1)} %get-tuple-element.572) | copy-start | bytes 12292
  78.8 109.4 %copy-start.105 = (f32[1,1024]{1,0:T(1,128)}, f32[1,1024]{1,0:T(1,128)S(1)}, u32[]{:S(2)}) copy-start(f32[1,1024]{1,0:T(1,128)S(1)} %get-tuple-element.574) | copy-start | bytes 12292
  78.8 109.4 %copy-start.114 = (f32[1,1024]{1,0:T(1,128)}, f32[1,1024]{1,0:T(1,128)S(1)}, u32[]{:S(2)}) copy-start(f32[1,1024]{1,0:T(1,128)S(1)} %get-tuple-element.571) | copy-start | bytes 12292
  78.8 109.4 %copy-start.116 = (f32[1,1024]{1,0:T(1,128)}, f32[1,1024]{1,0:T(1,128)S(1)}, u32[]{:S(2)}) copy-start(f32[1,1024]{1,0:T(1,128)S(1)} %get-tuple-element.573) | copy-start | bytes 12292
  102.6 85.6 %copy-start.4 = (bf16[512,1024]{1,0:T(8,128)(2,1)}, bf16[512,1024]{1,0:T(8,128)(2,1)S(1)}, u32[]{:S(2)}) copy-start(bf16[512,1024]{1,0:T(8,128)(2,1)S(1)} %get-tuple-element.509) | copy-start | bytes 3145732
  157.3 29.3 %copy-start.52 = (bf16[2,1,512,1024]{3,2,1,0:T(8,128)(2,1)S(1)}, bf16[2,1,512,1024]{3,2,1,0:T(8,128)(2,1)}, u32[]{:S(2)}) copy-start(bf16[2,1,512,1024]{3,2,1,0:T(8,128)(2,1)} %param.19) | copy-start | bytes 6291460
  161.4 25.2 %collective-permute-start.1 = (bf16[512,1024]{1,0:T(8,128)(2,1)}, bf16[512,1024]{1,0:T(8,128)(2,1)}, u32[]{:S(2)}, u32[]{:S(2)}) collective-permute-start(bf16[512,1024]{1,0:T(8,128)(2,1)} %get-tuple-element.503), channel_id=1, source_target_pairs={{0,16},{1,17},{2,18},{3,19},{4,20},{5,21},{6,22},{7,23},{8,24},{9,... | collective-permute-start | bytes 3145736 | tf_op jit(solution)/shard_map/ppermute | solution.py:20
  188.1 36.3 %copy-start.127 = (s32[2,1]{0,1:T(1,128)S(1)}, s32[2,1]{0,1:T(1,128)}, u32[]{:S(2)}) copy-start(s32[2,1]{0,1:T(1,128)} %param.22) | copy-start | bytes 28
  188.1 37.0 %copy-start.80 = (f32[16,512]{1,0:T(8,128)S(1)}, f32[16,512]{1,0:T(8,128)}, u32[]{:S(2)}) copy-start(f32[16,512]{1,0:T(8,128)} %copy-done.79) | copy-start | bytes 98308
  188.1 37.0 %copy-start.82 = (f32[16,512]{1,0:T(8,128)S(1)}, f32[16,512]{1,0:T(8,128)}, u32[]{:S(2)}) copy-start(f32[16,512]{1,0:T(8,128)} %copy-done.81) | copy-start | bytes 98308
  222.6 158.5 %collective-permute-start.2 = (bf16[512,1024]{1,0:T(8,128)(2,1)}, bf16[512,1024]{1,0:T(8,128)(2,1)S(1)}, u32[]{:S(2)}, u32[]{:S(2)}) collective-permute-start(bf16[512,1024]{1,0:T(8,128)(2,1)} %get-tuple-element.399), channel_id=1, source_target_pairs={{16,0},{17,1},{18,2},{19,3},{20,4},{21,5},{22,6},{23,7},{24,8},{25... | collective-permute-start | bytes 3145736 | tf_op jit(solution)/shard_map/ppermute | solution.py:20
  412.6 23.1 %slice-start = ((s8[16777216]{0:T(1024)(128)(4,1)}), s8[4194304]{0:T(1024)(128)(4,1)S(1)}, s32[]{:S(2)}) async-start(s8[16777216]{0:T(1024)(128)(4,1)} %bitcast.285), calls=%async_computation.12 | async-start | bytes 8388608
  412.6 23.1 %slice-start.1 = ((s8[16777216]{0:T(1024)(128)(4,1)}), s8[4194304]{0:T(1024)(128)(4,1)S(1)}, s32[]{:S(2)}) async-start(s8[16777216]{0:T(1024)(128)(4,1)} %bitcast.285), calls=%async_computation.13 | async-start | bytes 8388608
  463.8 25.3 %collective-permute-start.3 = (bf16[512,1024]{1,0:T(8,128)(2,1)S(1)}, bf16[512,1024]{1,0:T(8,128)(2,1)S(1)}, u32[]{:S(2)}, u32[]{:S(2)}) collective-permute-start(bf16[512,1024]{1,0:T(8,128)(2,1)S(1)} %get-tuple-element.501), channel_id=1, source_target_pairs={{16,0},{17,1},{18,2},{19,3},{20,4},{21,5},{22,6},{23,7},{24,8},{25... | collective-permute-start | bytes 3145736 | tf_op jit(solution)/shard_map/ppermute | solution.py:20
  489.4 176.0 %copy-start.86 = (f32[12288]{0:T(1024)S(1)}, f32[12288]{0:T(1024)}, u32[]{:S(2)}) copy-start(f32[12288]{0:T(1024)} %copy-done.85) | copy-start | bytes 147460
  491.8 41.7 %copy-start.28 = (bf16[512,1024]{1,0:T(8,128)(2,1)}, bf16[512,1024]{1,0:T(8,128)(2,1)S(1)}, u32[]{:S(2)}) copy-start(bf16[512,1024]{1,0:T(8,128)(2,1)S(1)} %get-tuple-element.495) | copy-start | bytes 3145732 | tf_op jit(solution)/shard_map/cond
  534.8 30.8 %copy-start.22 = (f32[512,1024]{1,0:T(8,128)}, f32[512,1024]{1,0:T(8,128)S(1)}, u32[]{:S(2)}) copy-start(f32[512,1024]{1,0:T(8,128)S(1)} %get-tuple-element.550) | copy-start | bytes 6291460 | tf_op jit(solution)/shard_map/cond
  535.2 23.2 %slice-start.14 = ((s8[8388608]{0:T(1024)(128)(4,1)}), s8[4194304]{0:T(1024)(128)(4,1)S(1)}, s32[]{:S(2)}) async-start(s8[8388608]{0:T(1024)(128)(4,1)} %bitcast.418), calls=%async_computation.26 | async-start | bytes 8388608 | tf_op jit(solution)/shard_map/cond
  670.3 220.3 %reduce-scatter.17.cloned.1.call-start = ((), (), s32[]{:S(2)}) async-start(), calls=%async_computation.10 | async-start | bytes 135168 | tf_op jit(solution)/shard_map/reduce_scatter | solution.py:363
  671.7 291.9 %reduce-scatter.11.cloned.1.call-start = ((), (), s32[]{:S(2)}) async-start(), calls=%async_computation.7 | async-start | bytes 4456448 | tf_op jit(solution)/shard_map/reduce_scatter | solution.py:358
  680.7 421.9 %reduce-scatter.9.cloned.1.call-start = ((), (), s32[]{:S(2)}) async-start(), calls=%async_computation.6 | async-start | bytes 13369344 | tf_op jit(solution)/shard_map/reduce_scatter | solution.py:357
  703.4 582.1 %reduce-scatter.13.cloned.1.call-start = ((), (), s32[]{:S(2)}) async-start(), calls=%async_computation.8 | async-start | bytes 17825792 | tf_op jit(solution)/shard_map/reduce_scatter | solution.py:359
  729.7 738.4 %reduce-scatter.15.cloned.1.call-start = ((), (), s32[]{:S(2)}) async-start(), calls=%async_computation.9 | async-start | bytes 17825792 | tf_op jit(solution)/shard_map/reduce_scatter | solution.py:360
  757.2 37.4 %copy-start.57 = (bf16[512,1024]{1,0:T(8,128)(2,1)S(1)}, bf16[512,1024]{1,0:T(8,128)(2,1)}, u32[]{:S(2)}) copy-start(bf16[512,1024]{1,0:T(8,128)(2,1)} %copy-done.56) | copy-start | bytes 3145732
  761.3 34.7 %copy-start.67 = (bf16[1,512,1024]{2,1,0:T(8,128)(2,1)S(1)}, bf16[1,512,1024]{2,1,0:T(8,128)(2,1)}, u32[]{:S(2)}) copy-start(bf16[1,512,1024]{2,1,0:T(8,128)(2,1)} %get-tuple-element.500) | copy-start | bytes 3145732
  (108 other events, 680.2 us)
Sparse Core Ops, SparseCore 0:
  670.4 84.4 reduce-scatter.18
  757.8 132.6 reduce-scatter.16
  895.0 68.6 reduce-scatter.10
  968.6 133.9 reduce-scatter.8
  1107.7 177.7 reduce-scatter.12
  1290.5 177.5 reduce-scatter.14
where the time goes:
time: 1480 us
  waiting for transfers between devices  885 us (60%)
  matrix products  298 us (20%)
  other arithmetic  142 us (10%)
  local copies, waits for them, and re-layouts  85.8 us (6%)
  blocking collectives  30.6 us (2%)
  between operations  17.1 us (1%)
    ppermute x4, waiting for transfers between devices, from_behind(): return lax.ppermute(value, axis, pairs)  218 us
    reduce_scatter x1, waiting for transfers between devices, shards(): lax.psum_scatter(weight_totals[2][None], 'dp', scatter_dimension=1, tiled...  183 us
    reduce_scatter x1, waiting for transfers between devices, shards(): lax.psum_scatter(weight_totals[3][None], 'dp', scatter_dimension=1, tiled...  183 us
    reduce_scatter x1, waiting for transfers between devices, shards(): lax.psum_scatter(weight_totals[0][None], 'dp', scatter_dimension=1, tiled...  139 us
    reduce_scatter x1, waiting for transfers between devices, shards(): lax.psum_scatter(table_grad, ('section', 'dp'), scatter_dimension=1, tile...  91.3 us
    reduce_scatter x1, waiting for transfers between devices, shards(): lax.psum_scatter(weight_totals[1][None], 'dp', scatter_dimension=1, tiled...  71 us
    dot_general x8, matrix products, transposed_product(): lax.dot_general(former, latter, (((0,), (0,)), ((), ())), preferred_eleme...  55.5 us
    dot_general x8, matrix products, product_back(): lax.dot_general(former, latter, (((1,), (1,)), ((), ())), preferred_eleme...  54.1 us
  transfers between devices with their start and end apart: 10, of which 9 were waited for; matrix products, arithmetic and copies ran while one was open for 7% of the time, Pallas kernels for 0%

commit v1 on v0

v1 whole, which is shorter than its diff:
```python
import functools

import jax
import jax.numpy as jnp
from jax import lax
from jax.experimental import pallas as pl
from jax.experimental.pallas import tpu as pltpu
from jax.sharding import PartitionSpec as P

HEAD = 64
norm_eps = 1e-05
root_half = 0.7071067811865476
slope_scale = 0.3989422804014327
score_scale = 0.125
big_negative = -1e30
f32 = jnp.float32
bf16 = jnp.bfloat16
GROUP = 4 * HEAD
TILE = 512
WIDE = 1024
STASH = 10


def nn(a, b):
    return lax.dot_general(a, b, (((1,), (0,)), ((), ())), preferred_element_type=f32)


def nt(a, b):
    return lax.dot_general(a, b, (((1,), (1,)), ((), ())), preferred_element_type=f32)


def row_stats(rows):
    average = jnp.mean(rows, axis=-1, keepdims=True)
    centered = rows - average
    inverse = lax.rsqrt(jnp.mean(centered * centered, axis=-1, keepdims=True) + norm_eps)
    return centered * inverse, inverse


def gate(values):
    bell = jnp.exp(-0.5 * values * values)
    upper = 0.5 * (1.0 + lax.erf(values * root_half))
    return values * upper, upper + values * bell * slope_scale


def loop(count, body, unroll=1):
    def run(i, carry):
        body(i)
        return carry

    lax.fori_loop(0, count, run, 0, unroll=unroll)


def part(i, size):
    return pl.ds(pl.multiple_of(i * size, size), size)


def copies(pairs, sem):
    return [pltpu.make_async_copy(a, b, sem.at[i]) for i, (a, b) in enumerate(pairs)]


def forward_kernel(slot, *refs):
    flags, norms, biases, feat, recv, w_in, w_out, w_up, w_down = refs[:9]
    z_out, squares_out = refs[19:21]
    s_x, s_a, s_qkv, s_c, s_l, s_h, s_b, s_g, s_d, s_p = refs[21:31]
    (v_in, v_out, v_up, v_down, v_x, v_a, v_qkv, v_c, v_l, v_h, v_b, v_g, v_d, v_p, v_bias, v_acc, v_z,
     sem_w, sem_x, sem_o, sem_p, sem_g, sem_d) = refs[31:]
    rows, width = v_x.shape
    hidden = v_up.shape[1]
    here = pl.ds(slot * rows, rows)

    @pl.when(flags[0] == 1)
    def _():
        length = flags[1]
        causal = flags[2] == 1
        from_feat = flags[3] == 1
        picked = flags[4]

        @pl.when(from_feat)
        def _():
            pltpu.make_async_copy(feat.at[picked], v_x, sem_x.at[0]).start()

        @pl.when(jnp.logical_not(from_feat))
        def _():
            pltpu.make_async_copy(recv, v_x, sem_x.at[0]).start()

        def column(source, target, index):
            def at(i):
                return pltpu.make_async_copy(
                    source.at[:, part(i, WIDE)], target.at[:, part(i, WIDE)], sem_w.at[index + i]
                )

            return at

        def down_copy(i):
            return pltpu.make_async_copy(
                w_down.at[part(i, WIDE)], v_down.at[part(i, WIDE)], sem_w.at[3 + 1 + hidden // WIDE + i]
            )

        in_copy, out_copy, up_copy = column(w_in, v_in, 0), column(w_out, v_out, 3), column(w_up, v_up, 4)
        for i in range(3):
            in_copy(i).start()
        out_copy(0).start()
        for i in range(hidden // WIDE):
            up_copy(i).start()
            down_copy(i).start()

        def bias_rows(i):
            at = part(i, 128)
            query = lax.broadcasted_iota(jnp.int32, (128, rows), 0) + i * 128
            key = lax.broadcasted_iota(jnp.int32, (128, rows), 1)
            open_ = (key < length) & ((key <= query) | jnp.logical_not(causal))
            v_bias[at, :] = jnp.where(open_, 0.0, big_negative)

        loop(rows // 128, bias_rows)
        pltpu.make_async_copy(recv, v_x, sem_x.at[0]).wait()

        def first_norm(i):
            at = part(i, 64)
            normed, _ = row_stats(v_x[at, :].astype(f32))
            v_a[at, :] = (normed * norms[0:1, :] + norms[1:2, :]).astype(bf16)

        loop(rows // 64, first_norm)
        outs = []

        def send(source, target, index):
            copy = pltpu.make_async_copy(source, target, sem_o.at[index])
            copy.start()
            outs.append(copy)

        send(v_x, s_x.at[here], 0)
        send(v_a, s_a.at[here], 1)
        def project(i):
            in_copy(i).wait()
            at = part(i, WIDE)
            tile = nn(v_a[...], v_in[:, at]) + biases[0:1, at]
            v_qkv[:, at] = tile.astype(bf16)

        loop(3 * width // WIDE, project)
        send(v_qkv, s_qkv.at[here], 2)
        lane = lax.broadcasted_iota(jnp.int32, (1, GROUP), 1) // HEAD
        groups = width // GROUP

        def p_copy(i):
            return pltpu.make_async_copy(
                v_p.at[i % 2], s_p.at[slot, pl.ds(i * 4, 4)], sem_p.at[i % 2]
            )

        def attend(i):
            at = part(i, GROUP)
            query = v_qkv[:, at]
            key = v_qkv[:, pl.ds(pl.multiple_of(width + i * GROUP, GROUP), GROUP)]
            value = v_qkv[:, pl.ds(pl.multiple_of(2 * width + i * GROUP, GROUP), GROUP)]

            @pl.when(i >= 2)
            def _():
                p_copy(i - 2).wait()

            half = rows // 2
            for r in range(2):
                picked_rows = slice(r * half, (r + 1) * half)
                scaled = query[picked_rows] * score_scale
                total = jnp.zeros((half, GROUP), f32)
                sums = jnp.ones((half, GROUP), f32)
                for h in range(4):
                    masked = jnp.where(lane == h, scaled, 0).astype(bf16)
                    scores = nt(masked, key) + v_bias[picked_rows, :]
                    top = jnp.max(scores, axis=-1, keepdims=True)
                    raised = jnp.exp(scores - top).astype(bf16)
                    v_p[i % 2, h, picked_rows, :] = raised
                    product = nn(raised, jnp.where(lane == h, value, 1).astype(bf16))
                    total = jnp.where(lane == h, product, total)
                    sums = jnp.where(lane == (h ^ 1), product, sums)
                inverse = 1.0 / jnp.concatenate(
                    [pltpu.roll(sums[:, k : k + 128], HEAD, 1) for k in (0, 128)], axis=1
                )
                v_l[picked_rows, at] = inverse
                v_c[picked_rows, at] = (total * inverse).astype(bf16)
            p_copy(i).start()

        loop(groups, attend)
        send(v_c, s_c.at[here], 8)
        send(v_l, s_l.at[here], 9)
        out_copy(0).wait()
        def mix(i):
            at = part(i, WIDE)
            v_acc[:, at] = nn(v_c[...], v_out[:, at]) + biases[3:4, at]

        loop(width // WIDE, mix)

        valid = lambda i, n: (lax.broadcasted_iota(jnp.int32, (n, 1), 0) + i * n < length).astype(f32)

        def square(values, mask):
            return jnp.sum((values * values * mask).reshape(-1, 8, width), axis=0)

        def second_norm(i, carry):
            at = part(i, 64)
            branch = v_acc[at, :]
            middle = v_x[at, :].astype(f32) + branch
            v_h[at, :] = middle
            normed, _ = row_stats(middle)
            v_b[at, :] = (normed * norms[2:3, :] + norms[3:4, :]).astype(bf16)
            v_acc[at, :] = jnp.broadcast_to(biases[4:5, :width], (64, width))
            mask = valid(i, 64)
            return (carry[0] + square(middle, mask), carry[1] + square(branch, mask))

        nothing = jnp.zeros((8, width), f32)
        sums_one = (nothing, nothing)
        sums_one = lax.fori_loop(0, rows // 64, second_norm, sums_one)
        send(v_h, s_h.at[here], 3)
        send(v_b, s_b.at[here], 4)

        def feed(i):
            up_copy(i).wait()
            down_copy(i).wait()
            at = part(i, WIDE)
            half = rows // 2
            for r in range(2):
                rr = slice(r * half, (r + 1) * half)
                pre = nn(v_b[rr, :], v_up[:, at]) + biases[5:6, at]
                act, slope = gate(pre)
                act = act.astype(bf16)
                v_g[rr, at] = act
                v_d[rr, at] = slope.astype(bf16)
                v_acc[rr, :] += nn(act, v_down[at, :])
            g_copy(i).start()
            d_copy(i).start()

        def g_copy(i):
            at = part(i, WIDE)
            return pltpu.make_async_copy(v_g.at[:, at], s_g.at[here, at], sem_g.at[i])

        def d_copy(i):
            at = part(i, WIDE)
            return pltpu.make_async_copy(v_d.at[:, at], s_d.at[here, at], sem_d.at[i])

        loop(hidden // WIDE, feed)

        def finish(i, carry):
            at = part(i, 64)
            branch = v_acc[at, :]
            output = v_h[at, :] + branch
            v_z[at, :] = output.astype(bf16)
            mask = valid(i, 64)
            return (carry[0] + square(output, mask), carry[1] + square(branch, mask))

        sums_two = (nothing, nothing)
        sums_two = lax.fori_loop(0, rows // 64, finish, sums_two)
        send(v_z, z_out, 7)
        for k, value in enumerate((sums_one[0], sums_two[0], sums_one[1], sums_two[1])):
            squares_out[k] = value
        for copy in outs:
            copy.wait()
        for i in range(hidden // WIDE):
            g_copy(i).wait()
            d_copy(i).wait()
        p_copy(groups - 2).wait()
        p_copy(groups - 1).wait()

    @pl.when(flags[0] != 1)
    def _():
        squares_out[...] = jnp.zeros_like(squares_out)


def stash_shapes(rows, width, hidden):
    heads = width // HEAD
    return [
        jax.ShapeDtypeStruct((2 * rows, width), bf16),
        jax.ShapeDtypeStruct((2 * rows, width), bf16),
        jax.ShapeDtypeStruct((2 * rows, 3 * width), bf16),
        jax.ShapeDtypeStruct((2 * rows, width), bf16),
        jax.ShapeDtypeStruct((2 * rows, width), f32),
        jax.ShapeDtypeStruct((2 * rows, width), f32),
        jax.ShapeDtypeStruct((2 * rows, width), bf16),
        jax.ShapeDtypeStruct((2 * rows, hidden), bf16),
        jax.ShapeDtypeStruct((2 * rows, hidden), bf16),
        jax.ShapeDtypeStruct((2, heads, rows, rows), bf16),
    ]


def forward_call(slot, flags, norms, biases, feat, recv, weights, stash):
    rows, width = recv.shape
    hidden = weights[2].shape[1]
    any_ = pl.BlockSpec(memory_space=pl.ANY)
    vm = pl.BlockSpec(memory_space=pltpu.VMEM)
    first = stash is None
    shapes = stash_shapes(rows, width, hidden)
    if first:
        stash = [jnp.zeros((8, 128), f32)] * STASH
    results = pl.pallas_call(
        functools.partial(forward_kernel, slot),
        in_specs=[pl.BlockSpec(memory_space=pltpu.SMEM), vm, vm] + [any_] * 6 + [any_] * STASH,
        out_specs=[any_, vm] + [any_] * STASH,
        out_shape=[jax.ShapeDtypeStruct((rows, width), bf16), jax.ShapeDtypeStruct((4, 8, width), f32)] + shapes,
        input_output_aliases={} if first else {9 + k: 2 + k for k in range(STASH)},
        scratch_shapes=[
            pltpu.VMEM(w.shape, bf16) for w in weights
        ] + [
            pltpu.VMEM((rows, width), bf16),
            pltpu.VMEM((rows, width), bf16),
            pltpu.VMEM((rows, 3 * width), bf16),
            pltpu.VMEM((rows, width), bf16),
            pltpu.VMEM((rows, width), f32),
            pltpu.VMEM((rows, width), f32),
            pltpu.VMEM((rows, width), bf16),
            pltpu.VMEM((rows, hidden), bf16),
            pltpu.VMEM((rows, hidden), bf16),
            pltpu.VMEM((2, 4, rows, rows), bf16),
            pltpu.VMEM((rows, rows), f32),
            pltpu.VMEM((rows, width), f32),
            pltpu.VMEM((rows, width), bf16),
            pltpu.SemaphoreType.DMA((4 + 2 * hidden // WIDE,)),
            pltpu.SemaphoreType.DMA((1,)),
            pltpu.SemaphoreType.DMA((10,)),
            pltpu.SemaphoreType.DMA((2,)),
            pltpu.SemaphoreType.DMA((hidden // WIDE,)),
            pltpu.SemaphoreType.DMA((hidden // WIDE,)),
        ],
        compiler_params=pltpu.CompilerParams(vmem_limit_bytes=62 * 2**20),
        cost_estimate=pl.CostEstimate(flops=14 * 10**9, bytes_accessed=50 * 10**6, transcendentals=6 * 10**6),
        name="layer_forward",
    )(flags, norms, biases, feat, recv, *weights, *stash)
    return results[0], results[1], results[2:]


def backward_kernel(slot, *refs):
    flags, norms, cot, recv, w_in, w_out, w_up, w_down = refs[:8]
    s_x, s_qkv, s_c, s_l, s_h, s_d, s_p = refs[8:15]
    dx_out, smalls = refs[18:20]
    g_up, g_mid, g_qkv = refs[20:23]
    (v_in, v_out, v_up, v_down, v_x, v_dy, v_qkv, v_c, v_l, v_h, v_d, v_p, v_du, v_do, v_dc, v_dqkv, v_acc,
     v_s, v_k, v_dx, sem_w, sem_x, sem_d, sem_p, sem_o) = refs[23:]
    rows, width = v_x.shape
    hidden = v_up.shape[1]
    here = pl.ds(slot * rows, rows)
    tiles = hidden // WIDE

    @pl.when(flags[0] == 1)
    def _():
        length = flags[1]
        from_cot = flags[3] == 0
        picked = flags[4]

        @pl.when(from_cot)
        def _():
            pltpu.make_async_copy(cot.at[picked], v_dy, sem_x.at[0]).start()

        @pl.when(jnp.logical_not(from_cot))
        def _():
            pltpu.make_async_copy(recv, v_dy, sem_x.at[0]).start()

        def down_copy(i):
            return pltpu.make_async_copy(
                w_down.at[part(i, WIDE)], v_down.at[part(i, WIDE)], sem_w.at[i]
            )

        def up_copy(i):
            at = part(i, WIDE)
            return pltpu.make_async_copy(w_up.at[:, at], v_up.at[:, at], sem_w.at[tiles + i])

        def d_copy(i):
            return pltpu.make_async_copy(
                s_d.at[here, part(i, WIDE)], v_d.at[i % 2], sem_d.at[i % 2]
            )

        def p_copy(i):
            return pltpu.make_async_copy(
                s_p.at[slot, pl.ds(i * 4, 4)], v_p.at[i % 2], sem_p.at[i % 2]
            )

        loads = copies(
            [
                (s_x.at[here], v_x),
                (s_qkv.at[here], v_qkv),
                (s_c.at[here], v_c),
                (s_l.at[here], v_l),
                (s_h.at[here], v_h),
                (w_out, v_out),
                (w_in, v_in),
            ],
            sem_x.at[pl.ds(1, 7)],
        )
        d_copy(0).start()
        for i in range(tiles):
            down_copy(i).start()
            up_copy(i).start()
            if i == 0:
                d_copy(1).start()
        for k in (4, 5, 1, 2, 3):
            loads[k].start()
        p_copy(0).start()
        p_copy(1).start()
        loads[6].start()
        loads[0].start()
        pltpu.make_async_copy(recv, v_dy, sem_x.at[0]).wait()
        nothing = jnp.zeros((8, width), f32)

        def fold(values):
            return jnp.sum(values.reshape(-1, 8, width), axis=0)

        def enter(i, total):
            at = part(i, 64)
            place = lax.broadcasted_iota(jnp.int32, (64, 1), 0) + i * 64
            masked = jnp.where(place < length, v_dy[at, :].astype(f32), 0.0)
            v_dy[at, :] = masked.astype(bf16)
            v_acc[at, :] = jnp.zeros((64, width), f32)
            return total + fold(masked)

        total = lax.fori_loop(0, rows // 64, enter, nothing)
        smalls[7:8, :] = jnp.sum(total, axis=0, keepdims=True)

        def feed(i):
            down_copy(i).wait()
            up_copy(i).wait()
            d_copy(i).wait()
            at = part(i, WIDE)
            half = rows // 2
            for r in range(2):
                rr = slice(r * half, (r + 1) * half)
                pre = nt(v_dy[rr, :], v_down[at, :]) * v_d[i % 2, rr, :].astype(f32)
                pre = pre.astype(bf16)
                v_du[rr, at] = pre
                v_acc[rr, :] += nt(pre, v_up[:, at])
            smalls[pl.ds(8 + i, 1), :] = jnp.sum(v_du[:, at].astype(f32), axis=0, keepdims=True)
            pltpu.make_async_copy(v_du.at[:, at], g_up.at[here, at], sem_o.at[3]).start()

            @pl.when(i + 2 < tiles)
            def _():
                d_copy(i + 2).start()

        loop(tiles, feed)
        loads[4].wait()
        loads[5].wait()

        def norm_back(source, grad, gain):
            normed, inverse = row_stats(source)
            scaled = grad * gain
            mean_one = jnp.mean(scaled, axis=-1, keepdims=True)
            mean_two = jnp.mean(scaled * normed, axis=-1, keepdims=True)
            return inverse * (scaled - mean_one - normed * mean_two), fold(grad * normed), fold(grad)

        def second_norm(i, carry):
            at = part(i, 64)
            rows_back, one, two = norm_back(v_h[at, :], v_acc[at, :], norms[2:3, :])
            middle = rows_back + v_dy[at, :].astype(f32)
            v_acc[at, :] = middle
            low = middle.astype(bf16)
            v_do[at, :] = low
            return carry[0] + one, carry[1] + two, carry[2] + fold(low.astype(f32))

        sums = lax.fori_loop(0, rows // 64, second_norm, (nothing,) * 3)
        for k, value in zip((2, 3, 6), sums):
            smalls[k : k + 1, :] = jnp.sum(value, axis=0, keepdims=True)
        do_copy = pltpu.make_async_copy(v_do, g_mid.at[here], sem_o.at[0])
        do_copy.start()
        v_dc[...] = nt(v_do[...], v_out[...]).astype(bf16)
        for k in (1, 2, 3):
            loads[k].wait()
        lane = lax.broadcasted_iota(jnp.int32, (1, GROUP), 1) // HEAD

        def attend(i):
            p_copy(i).wait()
            at = part(i, GROUP)
            key_at = pl.ds(pl.multiple_of(width + i * GROUP, GROUP), GROUP)
            value_at = pl.ds(pl.multiple_of(2 * width + i * GROUP, GROUP), GROUP)
            key = v_qkv[:, key_at]
            value = v_qkv[:, value_at]
            query = v_qkv[:, at]
            wide = v_dc[:, at].astype(f32) * v_l[:, at]
            low = wide.astype(bf16)
            dots = wide * v_c[:, at].astype(f32)
            for h in range(4):
                hs = slice(h * rows, (h + 1) * rows)
                v_k[hs, :] = jnp.where(lane == h, key, 0).astype(bf16)
                masked = jnp.where(lane == h, low, 0).astype(bf16)
                delta = jnp.sum(jnp.where(lane == h, dots, 0.0), axis=-1, keepdims=True)
                inner = nt(masked, value) - delta
                v_s[:, hs] = (v_p[i % 2, h].astype(f32) * inner).astype(bf16)
            grad_query = (nn(v_s[...], v_k[...]) * score_scale).astype(bf16)
            query_t = query.T
            low_t = low.T
            keys, values = [], []
            for h in range(4):
                hs = slice(h * HEAD, (h + 1) * HEAD)
                keys.append(nn(query_t[hs], v_s[:, h * rows : (h + 1) * rows]))
                values.append(nn(low_t[hs], v_p[i % 2, h]))
            grad_key = (jnp.concatenate(keys, axis=0) * score_scale).astype(bf16).T
            grad_value = jnp.concatenate(values, axis=0).astype(bf16).T
            v_dqkv[:, at] = grad_query
            v_dqkv[:, key_at] = grad_key
            v_dqkv[:, value_at] = grad_value
            smalls[4:5, at] = jnp.sum(grad_query.astype(f32), axis=0, keepdims=True)
            smalls[5:6, at] = jnp.sum(grad_value.astype(f32), axis=0, keepdims=True)

            @pl.when(i + 2 < width // GROUP)
            def _():
                p_copy(i + 2).start()

        loop(width // GROUP, attend)
        qkv_copy = pltpu.make_async_copy(v_dqkv, g_qkv.at[here], sem_o.at[1])
        qkv_copy.start()
        loads[6].wait()
        loads[0].wait()
        def enter_grad(i):
            at = part(i, TILE)
            v_h[:, at] = nt(v_dqkv[...], v_in[at, :])

        loop(width // TILE, enter_grad)

        def first_norm(i, carry):
            at = part(i, 64)
            rows_back, one, two = norm_back(v_x[at, :].astype(f32), v_h[at, :], norms[0:1, :])
            v_dx[at, :] = (rows_back + v_acc[at, :]).astype(bf16)
            return carry[0] + one, carry[1] + two

        sums = lax.fori_loop(0, rows // 64, first_norm, (nothing,) * 2)
        for k, value in enumerate(sums):
            smalls[k : k + 1, :] = jnp.sum(value, axis=0, keepdims=True)
        dx_copy = pltpu.make_async_copy(v_dx, dx_out, sem_o.at[2])
        dx_copy.start()
        for copy in (do_copy, qkv_copy, dx_copy):
            copy.wait()
        pltpu.make_async_copy(v_du, g_up.at[here], sem_o.at[3]).wait()

    @pl.when(flags[0] != 1)
    def _():
        smalls[...] = jnp.zeros_like(smalls)


def backward_call(slot, flags, norms, cot, recv, weights, stash, grads):
    rows, width = recv.shape
    hidden = weights[2].shape[1]
    any_ = pl.BlockSpec(memory_space=pl.ANY)
    vm = pl.BlockSpec(memory_space=pltpu.VMEM)
    first = grads is None
    shapes = [jax.ShapeDtypeStruct((2 * rows, n), bf16) for n in (hidden, width, 3 * width)]
    if first:
        grads = [jnp.zeros((8, 128), f32)] * 3
    s_x, s_a, s_qkv, s_c, s_l, s_h, s_b, s_g, s_d, s_p = stash
    results = pl.pallas_call(
        functools.partial(backward_kernel, slot),
        in_specs=[pl.BlockSpec(memory_space=pltpu.SMEM), vm] + [any_] * 16,
        out_specs=[any_, vm] + [any_] * 3,
        out_shape=[
            jax.ShapeDtypeStruct((rows, width), bf16),
            jax.ShapeDtypeStruct((8 + hidden // WIDE, width), f32),
        ] + shapes,
        input_output_aliases={} if first else {15 + k: 2 + k for k in range(3)},
        scratch_shapes=[pltpu.VMEM(w.shape, bf16) for w in weights] + [
            pltpu.VMEM((rows, width), bf16),
            pltpu.VMEM((rows, width), bf16),
            pltpu.VMEM((rows, 3 * width), bf16),
            pltpu.VMEM((rows, width), bf16),
            pltpu.VMEM((rows, width), f32),
            pltpu.VMEM((rows, width), f32),
            pltpu.VMEM((2, rows, WIDE), bf16),
            pltpu.VMEM((2, 4, rows, rows), bf16),
            pltpu.VMEM((rows, hidden), bf16),
            pltpu.VMEM((rows, width), bf16),
            pltpu.VMEM((rows, width), bf16),
            pltpu.VMEM((rows, 3 * width), bf16),
            pltpu.VMEM((rows, width), f32),
            pltpu.VMEM((rows, 4 * rows), bf16),
            pltpu.VMEM((4 * rows, GROUP), bf16),
            pltpu.VMEM((rows, width), bf16),
            pltpu.SemaphoreType.DMA((2 * hidden // WIDE,)),
            pltpu.SemaphoreType.DMA((8,)),
            pltpu.SemaphoreType.DMA((2,)),
            pltpu.SemaphoreType.DMA((2,)),
            pltpu.SemaphoreType.DMA((4,)),
        ],
        compiler_params=pltpu.CompilerParams(vmem_limit_bytes=62 * 2**20),
        cost_estimate=pl.CostEstimate(flops=18 * 10**9, bytes_accessed=60 * 10**6, transcendentals=0),
        name="layer_backward",
    )(flags, norms, cot, recv, *weights, s_x, s_qkv, s_c, s_l, s_h, s_d, s_p, *grads)
    return results[0], results[1], results[2:]


highest = lax.Precision.HIGHEST


def transposed_product(former, latter):
    return lax.dot_general(
        former, latter, (((0,), (0,)), ((), ())), preferred_element_type=jnp.float32
    )


def added(terms):
    total = terms[0].astype(f32)
    for term in terms[1:]:
        total = total + term.astype(f32)
    return total


def pick(array, axis, index):
    return lax.dynamic_index_in_dim(array, index, axis, keepdims=False)


class Exchange:
    def __init__(self, terms, bits, order):
        self.terms = terms
        self.left = list(range(bits - 1, -1, -1))
        self.order = list(order)
        self.kind = terms[0].dtype

    def step(self, theirs=None):
        bit = self.order.pop(0)
        axis = self.left.index(bit)
        self.left.pop(axis)
        mine = (lax.axis_index("dp") >> bit) & 1
        if theirs is None:
            theirs = added([pick(term, axis, 1 - mine) for term in self.terms]).astype(self.kind)
            self.terms = [pick(term, axis, mine) for term in self.terms]
        size = lax.axis_size("dp")
        pairs = [(i, i ^ (1 << bit)) for i in range(size)]
        self.terms = self.terms + [lax.ppermute(theirs, "dp", pairs)]

    def finish(self):
        while self.order:
            self.step()
        return added(self.terms)


def weight_sum(former, latter, bits, orders):
    rows = former.shape[0]
    size = 1 << bits
    blocks = former.reshape((rows, size // 2, 2, former.shape[1] // size))
    core = lax.axis_index("dp") & 1
    halves = []
    for which in (1 - core, core):
        columns = pick(blocks, 2, which).reshape(rows, former.shape[1] // 2)
        halves.append(transposed_product(columns, latter).astype(bf16))
    theirs, mine = halves
    size_of = [2] * (bits - 1) + [former.shape[1] // size]
    pairs = [(i, i ^ 1) for i in range(size)]
    received = lax.ppermute(theirs, "dp", pairs)
    start = 0
    parts = []
    for columns, order in orders:
        cut = slice(start, start + columns)
        start += columns
        exchange = Shifted(
            [half[:, cut].reshape(size_of + [columns]) for half in (mine, received)], bits - 1, order
        )
        parts.append(exchange)
    return parts


class Shifted(Exchange):
    def __init__(self, terms, bits, order):
        super().__init__(terms, bits, order)
        self.left = list(range(bits, 0, -1))


def shards(
    features,
    cotangent,
    lengths,
    codebook_index,
    attention_in,
    attention_out,
    feed_up,
    feed_down,
    vectors,
    adaptive_weight,
    codebook_table,
):
    is_first = lax.axis_index("section") == 0
    first = is_first.astype(jnp.int32)
    last = 1 - first
    rows, width = features.shape[2:]
    hidden = feed_up.shape[2]
    size = lax.axis_size("dp")
    bits = size.bit_length() - 1
    feats = features[:, 0]
    cots = cotangent[:, 0]
    spans = lengths[:, 0]
    weights = (attention_in[0], attention_out[0], feed_up[0], feed_down[0])
    vector = vectors[0]
    raw_norms = vector[: 4 * width].reshape(4, width)
    pad = jnp.zeros((hidden - width,), f32)
    query_bias, value_bias, out_bias, down_bias = [
        vector[k * width : (k + 1) * width] for k in range(4, 8)
    ]
    zero = jnp.zeros((width,), f32)
    empty = jnp.zeros((hidden,), f32)
    biases = jnp.stack(
        [
            jnp.concatenate([query_bias, zero, value_bias, empty[: hidden - 3 * width]]),
            empty,
            empty,
            jnp.concatenate([out_bias, pad]),
            jnp.concatenate([down_bias, pad]),
            vector[8 * width :],
            empty,
            empty,
        ]
    )

    def flags(*values):
        return jnp.stack([jnp.asarray(value, jnp.int32) for value in values])

    def chosen(a, b):
        return jnp.where(is_first, a, b)

    def send(value, to):
        return lax.ppermute(value, "section", [(1 - to, to)])

    z_one, squares_one, stash = forward_call(
        0, flags(first, spans[0], 1, 1, 0), raw_norms, biases, feats, feats[0], weights, None
    )
    received_one = send(z_one, 1)
    table, z_one = lax.optimization_barrier((codebook_table, z_one))
    condition_table = jnp.dot(table, adaptive_weight, preferred_element_type=f32)
    one_hot = (
        codebook_index[:, 0][:, None]
        == jnp.arange(codebook_table.shape[0], dtype=jnp.int32)[None, :]
    ).astype(f32)
    condition = (jnp.dot(one_hot, condition_table, precision=highest) * last.astype(f32)).reshape(
        -1, 4, width
    )
    norms = [raw_norms + condition[k] for k in range(2)]
    z_two, squares_two, stash = forward_call(
        1,
        flags(1, chosen(spans[1], spans[0]), first, first, 1),
        norms[0],
        biases,
        feats,
        received_one,
        weights,
        stash,
    )
    received_two = send(z_two, 1)
    dx_one, smalls_one, grads = backward_call(
        1, flags(last, spans[0], 0, 0, 0), norms[0], cots, cots[0], weights, stash, None
    )
    back_one = send(dx_one, 0)
    z_three, squares_three, stash = forward_call(
        0,
        flags(last, spans[1], 0, 0, 0),
        norms[1],
        biases,
        feats,
        received_two,
        weights,
        stash,
    )
    dx_two, smalls_two, grads = backward_call(
        0,
        flags(1, chosen(spans[0], spans[1]), 0, first, 1),
        norms[1],
        cots,
        back_one,
        weights,
        stash,
        grads,
    )
    back_two = send(dx_two, 0)
    places = jnp.arange(rows, dtype=jnp.int32)[None, :, None]
    masked = jnp.where(places < spans[:, None, None], cots, 0)
    grad_feed = chosen(
        jnp.stack([back_one, back_two]), jnp.stack([masked[1], masked[0]])
    ).reshape(2 * rows, width)
    s_x, s_a, s_qkv, s_c, s_l, s_h, s_b, s_g, s_d, s_p = stash
    lower = list(range(1, bits))
    side_first = lower
    line_first = lower[1:] + lower[:1]
    half = width // 2
    down_parts = weight_sum(
        s_g, grad_feed, bits, [(half, line_first), (half, side_first)]
    )
    for part_ in down_parts:
        part_.step()
    dx_three, smalls_three, (g_up, g_mid, g_qkv) = backward_call(
        1, flags(first, spans[1], 0, 1, 0), raw_norms, cots, back_two, weights, stash, grads
    )
    up_parts = weight_sum(s_b, g_up, bits, [(hidden // 2, side_first)] * 2)
    out_parts = weight_sum(s_c, g_mid, bits, [(width, side_first)])
    in_parts = weight_sum(s_a, g_qkv, bits, [(width, side_first)] * 3)

    smalls = smalls_one + smalls_two + smalls_three
    picks = [one_hot[0], one_hot[1]]
    table_grad = (
        picks[0][:, None] * smalls_one[:4].reshape(1, -1)
        + picks[1][:, None] * (smalls_two[:4].reshape(1, -1) * last.astype(f32))
    )
    codes = table_grad.shape[0]
    share = table_grad.shape[1] // (2 * size)
    table_blocks = table_grad.reshape(codes, 2, size, share).transpose(2, 1, 0, 3)
    squares = jnp.sum(squares_one + squares_two + squares_three, axis=(1, 2))
    counted = jnp.sum(spans).astype(f32)
    totals = jnp.concatenate([squares, counted[None], jnp.zeros((123,), f32)])
    packed = jnp.concatenate(
        [
            smalls.reshape(size, -1),
            table_blocks.reshape(size, -1),
            jnp.broadcast_to(totals[None], (size, 128)),
        ],
        axis=1,
    )
    length = packed.shape[1]
    small_sum = Exchange(
        [packed.reshape([2] * bits + [length])], bits, list(range(bits))
    ).finish()
    vector_share = small_sum[: smalls.size // size]
    table_share = small_sum[smalls.size // size : -128].reshape(2, codes, share)
    totals = small_sum[-128:]
    table_own = chosen(send(table_share[0], 0), table_share[1])
    grad_adaptive = lax.dot_general(
        codebook_table.astype(f32),
        table_own,
        (((0,), (0,)), ((), ())),
        precision=highest,
        preferred_element_type=f32,
    )
    residual_rms = jnp.sqrt(totals[:4] / (totals[4] * width))[None]

    def joined(parts):
        return jnp.concatenate([part_.finish() for part_ in parts], axis=-1)[None]

    layer_outputs = jnp.stack([chosen(z_one, z_two), chosen(z_two, z_three)])[None, :, None]
    input_grads = jnp.stack([chosen(dx_two, dx_one), chosen(dx_three, dx_two)])[None, :, None]
    down_sum = joined(down_parts)
    up_sum = joined(up_parts)
    out_sum = joined(out_parts)
    in_sum = joined(in_parts)
    return (
        layer_outputs,
        input_grads,
        in_sum,
        out_sum,
        up_sum,
        down_sum,
        vector_share[None],
        grad_adaptive,
        residual_rms,
    )


def solution(mesh):
    placed = (
        P(None, "dp", None, None),
        P(None, "dp", None, None),
        P(None, "dp"),
        P(None, "dp"),
        P("section", None, None),
        P("section", None, None),
        P("section", None, None),
        P("section", None, None),
        P("section", None),
        P(),
        P(),
    )
    return jax.shard_map(
        shards,
        mesh=mesh,
        in_specs=placed,
        out_specs=(
            P("section", None, "dp", None, None),
            P("section", None, "dp", None, None),
            P("section", "dp", None),
            P("section", "dp", None),
            P("section", "dp", None),
            P("section", "dp", None),
            P("section", "dp"),
            P(None, ("section", "dp")),
            P("section", None),
        ),
        check_vma=False,
    )
```

time: 1480 us -> 631 us (0.43)
  waiting for transfers between devices: 885 us -> 194 us
  matrix products: 298 us -> 44 us
  Pallas kernels: 0 us -> 166 us
  other arithmetic: 142 us -> 41.6 us
  local copies, waits for them, and re-layouts: 85.8 us -> 127 us
  starting transfers between devices: 8.08 us -> 42.9 us
  blocking collectives: 30.6 us -> 0 us
    reduce_scatter x5 -> x0, waiting for transfers between devices: 667 us -> none  [the longest x1 183 us: shards(): lax.psum_scatter(weight_totals[2][None], 'dp', scatter_dimension=1, tiled...]
    dot_general x34 -> x3, matrix products: 231 us -> 6.22 us  [the longest x1 4.73 us: shards(): jnp.dot(table, adaptive_weight, preferred_element_type=f32)]
    pallas_call x0 -> x6, Pallas kernels: none -> 166 us  [the longest x3 84.8 us: backward_call(): pl.pallas_call(functools.partial(backward_kernel, slot), in_specs=[pl.Blo...]
    broadcast_in_dim x5, other arithmetic: 60.4 us -> 5.38 us  [the longest x4 4.86 us: joined(): return jnp.concatenate([part_.finish() for part_ in parts], axis=-1)[None]]
    ppermute x4 -> x37, starting transfers between devices: 7.62 us -> 42.9 us  [the longest x28 31.3 us: step(): self.terms = self.terms + [lax.ppermute(theirs, 'dp', pairs)]]
    unnamed x213 -> x98, local copies, waits for them, and re-layouts: 17.7 us -> 48.9 us
    reduce_sum x17 -> x2, other arithmetic: 31.5 us -> 0.83 us  [the longest x1 0.7 us: shards(): counted = jnp.sum(spans).astype(f32)]
    psum x1 -> x0, blocking collectives: 30.6 us -> none  [shards(): totals, counted = lax.psum((square_sums, token_count), 'dp')]
  transfers between devices with their start and end apart: 10 -> 37, of which waited for: 9 -> 22; matrix products, arithmetic and copies ran while one was open for 7% -> 30% of each run, Pallas kernels for 0% -> 1%
where the time goes in v1:
time: 631 us; the launch traced here: 622 us
  waiting for transfers between devices  194 us (31%)
  Pallas kernels  166 us (26%)
  local copies, waits for them, and re-layouts  127 us (20%)
  matrix products  44 us (7%)
  starting transfers between devices  42.9 us (7%)
  other arithmetic  41.6 us (7%)
    ppermute x28, waiting for transfers between devices, step(): self.terms = self.terms + [lax.ppermute(theirs, 'dp', pairs)]  130 us
    pallas_call x3, Pallas kernels, backward_call(): pl.pallas_call(functools.partial(backward_kernel, slot), in_specs=[pl.Blo...  84.8 us
    pallas_call x3, Pallas kernels, forward_call(): pl.pallas_call(functools.partial(forward_kernel, slot), in_specs=[pl.Bloc...  81.1 us
    ppermute x5, waiting for transfers between devices, send(): return lax.ppermute(value, 'section', [(1 - to, to)])  64.2 us
    unnamed x98, local copies, waits for them, and re-layouts  48.9 us
    dot_general x8, matrix products, transposed_product(): lax.dot_general(former, latter, (((0,), (0,)), ((), ())), preferred_eleme...  37.8 us
    ppermute x28, starting transfers between devices, step(): self.terms = self.terms + [lax.ppermute(theirs, 'dp', pairs)]  31.3 us
    dynamic_slice x13, local copies, waits for them, and re-layouts, pick(): return lax.dynamic_index_in_dim(array, index, axis, keepdims=False)  26.2 us
  transfers between devices with their start and end apart: 37, of which 22 were waited for; matrix products, arithmetic and copies ran while one was open for 30% of the time, Pallas kernels for 1%

profile of v1, /device:TPU:0, one launch (start us, length us, event | category | flops | bytes accessed | tf_op | source)
XLA Modules:
  0.0 621.7 jit_solution(11142487702095864257)
XLA Ops:
  9.1 39.4 %layer_forward.3 = (bf16[512,1024]{1,0:T(8,128)(2,1)}, f32[4,8,1024]{2,1,0:T(8,128)}, bf16[1024,1024]{1,0:T(8,128)(2,1)}, bf16[1024,1024]{1,0:T(8,128)(2,1)}, bf...) custom-call(s32[5]{0:T(128)} %pad_add_fusion.4.refs_0_, ...), custom_call_target="tpu_custom_call" | custom-call | flops 14000000000 | bytes 50000000 | tf_op jit(solution)/shard_map/layer_forward/pallas_call | solution.py:289
  49.9 4.7 fusion.59
  67.2 6.2 collective-permute-done.refs_4_
  74.4 39.6 %layer_forward.4 = (bf16[512,1024]{1,0:T(8,128)(2,1)}, f32[4,8,1024]{2,1,0:T(8,128)}, bf16[1024,1024]{1,0:T(8,128)(2,1)}, bf16[1024,1024]{1,0:T(8,128)(2,1)}, bf...) custom-call(s32[5]{0:T(128)} %stack.85.refs_0_, ...), custom_call_target="tpu_custom_call", output_to_operand_aliasing={{2}: (9, {}), {3}: (10, {}), {4}: (11, {}), {5}: (12, {}), ... | custom-call | flops 14000000000 | bytes 50000000 | tf_op jit(solution)/shard_map/layer_forward/pallas_call | solution.py:289
  114.0 5.3 collective-permute-start.1
  123.3 17.7 %collective-permute-done.1.refs_4_ = bf16[512,1024]{1,0:T(8,128)(2,1)} collective-permute-done((bf16[512,1024]{1,0:T(8,128)(2,1)}, bf16[512,1024]{1,0:T(8,128)(2,1)}, u32[]{:S(2)}, u32[]{:S(2)}) %collective-permute-start.1) | collective-permute-done | bytes 1048608 | tf_op jit(solution)/shard_map/ppermute | solution.py:706
  143.2 40.3 %collective-permute-done.2.refs_3_ = bf16[512,1024]{1,0:T(8,128)(2,1)S(1)} collective-permute-done((bf16[512,1024]{1,0:T(8,128)(2,1)}, bf16[512,1024]{1,0:T(8,128)(2,1)S(1)}, u32[]{:S(2)}, u32[]{:S(2)}) %collective-permute-start.2) | collective-permute-done | bytes 1048608 | tf_op jit(solution)/shard_map/ppermute | solution.py:706
  184.4 41.8 %layer_backward.4 = (bf16[512,1024]{1,0:T(8,128)(2,1)}, f32[12,1024]{1,0:T(8,128)}, bf16[1024,4096]{1,0:T(8,128)(2,1)}, bf16[1024,1024]{1,0:T(8,128)(2,1)}, bf16[1024,3072]{1,0:T(8,128)(2,1)}) custom-call(s32[5]{0:T(128)} %stack.92.refs_0_, f32[4,1024]{1,0:T(4,128)} %get-tuple-element.177.refs_1_, ...), custom_call_target="tpu_custom_call", output_to_operand_aliasing={{2}: (15, {}), {3}: (16, {}), {4}: (17, {})} | custom-call | flops 17999998976 | bytes 60000000 | tf_op jit(solution)/shard_map/layer_backward/pallas_call | solution.py:539
  230.3 14.4 %reshape.646 = bf16[1024,8,2,256]{3,2,1,0:T(2,128)(2,1)} reshape(bf16[1024,4096]{1,0:T(8,128)(2,1)} %get-tuple-element.108) | data formatting | bytes 16777216 | tf_op jit(solution)/shard_map/reshape | solution.py:626
  246.4 20.3 %constant_dynamic-slice_fusion.10 = (bf16[1024,8,1,256]{3,2,1,0:T(2,128)(2,1)}, bf16[1024,8,1,256]{3,2,1,0:T(2,128)(2,1)}) fusion(bf16[1024,8,2,256]{3,2,1,0:T(2,128)(2,1)} %reshape.646, s32[]{:T(128)S(6)} %select_n.291, s32[]{:T(128)S(6)} %select_n.298), kind=kLoop, calls=%fused_computation.120 | loop fusion | bytes 16777224 | tf_op jit(solution)/shard_map/jit(dynamic_index_in_dim)/dynamic_slice | solution.py:595
  270.1 3.9 copy.64
  274.1 20.0 %copy.88 = bf16[1024,8,1,256]{0,3,1,2:T(8,128)(2,1)} copy(bf16[1024,8,1,256]{3,2,1,0:T(2,128)(2,1)} %get-tuple-element.144) | data formatting | bytes 8388608
  294.1 20.1 %copy.87 = bf16[1024,8,1,256]{0,3,1,2:T(8,128)(2,1)} copy(bf16[1024,8,1,256]{3,2,1,0:T(2,128)(2,1)} %get-tuple-element.143) | data formatting | bytes 8388608
  314.3 3.9 constant_dynamic-slice_fusion.4
  320.8 41.2 %layer_backward.5 = (bf16[512,1024]{1,0:T(8,128)(2,1)}, f32[12,1024]{1,0:T(8,128)}, bf16[1024,4096]{1,0:T(8,128)(2,1)}, bf16[1024,1024]{1,0:T(8,128)(2,1)}, bf16[1024,3072]{1,0:T(8,128)(2,1)}) custom-call(s32[5]{0:T(128)} %stack.95.refs_0_, f32[4,1024]{1,0:T(4,128)} %reshape.624.refs_1_, ...), custom_call_target="tpu_custom_call", output_to_operand_aliasing={{2}: (15, {}), {3}: (16, {}), {4}: (17, {})} | custom-call | flops 17999998976 | bytes 60000000 | tf_op jit(solution)/shard_map/layer_backward/pallas_call | solution.py:539
  365.2 7.7 %convolution_convert_fusion.2 = bf16[512,3072]{1,0:T(8,128)(2,1)} fusion(bf16[1024,512]{0,1:T(8,128)(2,1)S(1)} %bitcast.434, bf16[1024,3072]{1,0:T(8,128)(2,1)} %get-tuple-element.104), kind=kOutput, calls=%fused_computation.2 | convolution fusion | flops 3222798336 | bytes 10485760 | tf_op jit(solution)/shard_map/dot_general | solution.py:582
  384.0 6.1 convolution_convert_fusion
  390.2 4.8 convolution_convert_fusion.1
  400.8 6.1 convolution_convert_fusion.4
  407.4 4.9 convolution_convert_fusion.5
  421.7 4.7 maximum_bitcast_fusion
  435.8 7.1 %collective-permute-done.15 = bf16[2,2,64,1024]{3,2,1,0:T(8,128)(2,1)S(1)} collective-permute-done((bf16[2,2,64,1024]{3,2,1,0:T(8,128)(2,1)S(1)}, bf16[2,2,64,1024]{3,2,1,0:T(8,128)(2,1)S(1)}, u32[]{:S(2)}, u32[]{:S(2)}) %collective-permute-start.15) | collective-permute-done | bytes 524320 | tf_op jit(solution)/shard_map/ppermute | solution.py:615
  458.3 5.1 collective-permute-done.11
  465.0 9.7 %collective-permute-done.8 = bf16[2,2,64,1024]{3,2,1,0:T(8,128)(2,1)} collective-permute-done((bf16[2,2,64,1024]{3,2,1,0:T(8,128)(2,1)}, bf16[2,2,64,1024]{3,2,1,0:T(8,128)(2,1)}, u32[]{:S(2)}, u32[]{:S(2)}) %collective-permute-start.8) | collective-permute-done | bytes 524320 | tf_op jit(solution)/shard_map/ppermute | solution.py:615
  477.4 4.8 collective-permute-done.5
  493.5 3.8 collective-permute-done.6
  515.6 16.7 %collective-permute-done.22 = bf16[2,2,64,2048]{3,2,1,0:T(8,128)(2,1)S(1)} collective-permute-done((bf16[2,2,64,2048]{3,2,1,0:T(8,128)(2,1)S(1)}, bf16[2,2,64,2048]{3,2,1,0:T(8,128)(2,1)S(1)}, u32[]{:S(2)}, u32[]{:S(2)}) %collective-permute-start.22) | collective-permute-done | bytes 1048608 | tf_op jit(solution)/shard_map/ppermute | solution.py:615
  533.8 21.0 %collective-permute-done.19 = bf16[2,2,64,2048]{3,2,1,0:T(8,128)(2,1)S(1)} collective-permute-done((bf16[2,2,64,2048]{3,2,1,0:T(8,128)(2,1)S(1)}, bf16[2,2,64,2048]{3,2,1,0:T(8,128)(2,1)S(1)}, u32[]{:S(2)}, u32[]{:S(2)}) %collective-permute-start.19) | collective-permute-done | bytes 1048608 | tf_op jit(solution)/shard_map/ppermute | solution.py:615
  557.2 9.7 %collective-permute-done.29 = bf16[2,2,256,512]{3,2,1,0:T(8,128)(2,1)S(1)} collective-permute-done((bf16[2,2,256,512]{3,2,1,0:T(8,128)(2,1)S(1)}, bf16[2,2,256,512]{3,2,1,0:T(8,128)(2,1)S(1)}, u32[]{:S(2)}, u32[]{:S(2)}) %collective-permute-start.29) | collective-permute-done | bytes 1048608 | tf_op jit(solution)/shard_map/ppermute | solution.py:615
  572.7 5.3 collective-permute-done.20
  578.2 11.1 %collective-permute-done.30 = bf16[2,256,512]{2,1,0:T(8,128)(2,1)S(1)} collective-permute-done((bf16[2,256,512]{2,1,0:T(8,128)(2,1)S(1)}, bf16[2,256,512]{2,1,0:T(8,128)(2,1)S(1)}, u32[]{:S(2)}, u32[]{:S(2)}) %collective-permute-start.30) | collective-permute-done | bytes 524320 | tf_op jit(solution)/shard_map/ppermute | solution.py:615
  589.5 21.9 %collective-permute-done.27 = bf16[2,256,512]{2,1,0:T(8,128)(2,1)S(1)} collective-permute-done((bf16[2,256,512]{2,1,0:T(8,128)(2,1)S(1)}, bf16[2,256,512]{2,1,0:T(8,128)(2,1)S(1)}, u32[]{:S(2)}, u32[]{:S(2)}) %collective-permute-start.27) | collective-permute-done | bytes 524320 | tf_op jit(solution)/shard_map/ppermute | solution.py:615
  (281 shorter events, 146.7 us)
Async XLA Ops:
  48.5 24.9 %collective-permute-start = (bf16[512,1024]{1,0:T(8,128)(2,1)}, bf16[512,1024]{1,0:T(8,128)(2,1)S(1)}, u32[]{:S(2)}, u32[]{:S(2)}) collective-permute-start(bf16[512,1024]{1,0:T(8,128)(2,1)} %get-tuple-element.63), channel_id=1, source_target_pairs={{0,16},{1,17},{2,18},{3,19},{4,20},{5,21},{6,22},{7,23},{8,24},{9,... | collective-permute-start | bytes 3145736 | tf_op jit(solution)/shard_map/ppermute | solution.py:706
  114.0 27.0 %collective-permute-start.1 = (bf16[512,1024]{1,0:T(8,128)(2,1)}, bf16[512,1024]{1,0:T(8,128)(2,1)}, u32[]{:S(2)}, u32[]{:S(2)}) collective-permute-start(bf16[512,1024]{1,0:T(8,128)(2,1)} %get-tuple-element.75), channel_id=1, source_target_pairs={{0,16},{1,17},{2,18},{3,19},{4,20},{5,21},{6,22},{7,23},{8,24},{9,... | collective-permute-start | bytes 3145736 | tf_op jit(solution)/shard_map/ppermute | solution.py:706
  121.1 62.3 %collective-permute-start.2 = (bf16[512,1024]{1,0:T(8,128)(2,1)}, bf16[512,1024]{1,0:T(8,128)(2,1)S(1)}, u32[]{:S(2)}, u32[]{:S(2)}) collective-permute-start(bf16[512,1024]{1,0:T(8,128)(2,1)} %get-tuple-element.87), channel_id=1, source_target_pairs={{16,0},{17,1},{18,2},{19,3},{20,4},{21,5},{22,6},{23,7},{24,8},{25... | collective-permute-start | bytes 3145736 | tf_op jit(solution)/shard_map/ppermute | solution.py:706
  226.2 93.6 %collective-permute-start.3 = (bf16[512,1024]{1,0:T(8,128)(2,1)}, bf16[512,1024]{1,0:T(8,128)(2,1)S(1)}, u32[]{:S(2)}, u32[]{:S(2)}) collective-permute-start(bf16[512,1024]{1,0:T(8,128)(2,1)} %get-tuple-element.98), channel_id=1, source_target_pairs={{16,0},{17,1},{18,2},{19,3},{20,4},{21,5},{22,6},{23,7},{24,8},{25... | collective-permute-start | bytes 3145736 | tf_op jit(solution)/shard_map/ppermute | solution.py:706
  373.0 71.8 %collective-permute-start.4 = (bf16[512,3072]{1,0:T(8,128)(2,1)}, bf16[512,3072]{1,0:T(8,128)(2,1)}, u32[]{:S(2)}, u32[]{:S(2)}) collective-permute-start(bf16[512,3072]{1,0:T(8,128)(2,1)} %convolution_convert_fusion.2), channel_id=1, source_target_pairs={{0,1},{1,0},{2,3},{3,2},{4,5},{5,4},{6,7},{7,6},{8,9},{9,8},{10,11... | collective-permute-start | bytes 9437192 | tf_op jit(solution)/shard_map/ppermute | solution.py:635
  381.2 48.1 %collective-permute-start.14 = (bf16[512,1024]{1,0:T(8,128)(2,1)}, bf16[512,1024]{1,0:T(8,128)(2,1)}, u32[]{:S(2)}, u32[]{:S(2)}) collective-permute-start(bf16[512,1024]{1,0:T(8,128)(2,1)} %convolution_convert_fusion.6), channel_id=1, source_target_pairs={{0,1},{1,0},{2,3},{3,2},{4,5},{5,4},{6,7},{7,6},{8,9},{9,8},{10,11... | collective-permute-start | bytes 3145736 | tf_op jit(solution)/shard_map/ppermute | solution.py:635
  390.2 112.6 %collective-permute-start.18 = (bf16[512,4096]{1,0:T(8,128)(2,1)}, bf16[512,4096]{1,0:T(8,128)(2,1)}, u32[]{:S(2)}, u32[]{:S(2)}) collective-permute-start(bf16[512,4096]{1,0:T(8,128)(2,1)} %convolution_convert_fusion), channel_id=1, source_target_pairs={{0,1},{1,0},{2,3},{3,2},{4,5},{5,4},{6,7},{7,6},{8,9},{9,8},{10,11... | collective-permute-start | bytes 12582920 | tf_op jit(solution)/shard_map/ppermute | solution.py:635
  406.9 102.4 %collective-permute-start.25 = (bf16[2048,1024]{1,0:T(8,128)(2,1)}, bf16[2048,1024]{1,0:T(8,128)(2,1)}, u32[]{:S(2)}, u32[]{:S(2)}) collective-permute-start(bf16[2048,1024]{1,0:T(8,128)(2,1)} %convolution_convert_fusion.4), channel_id=1, source_target_pairs={{0,1},{1,0},{2,3},{3,2},{4,5},{5,4},{6,7},{7,6},{8,9},{9,8},{10,11... | collective-permute-start | bytes 12582920 | tf_op jit(solution)/shard_map/ppermute | solution.py:635
  430.6 12.3 %collective-permute-start.15 = (bf16[2,2,64,1024]{3,2,1,0:T(8,128)(2,1)S(1)}, bf16[2,2,64,1024]{3,2,1,0:T(8,128)(2,1)S(1)}, u32[]{:S(2)}, u32[]{:S(2)}) collective-permute-start(bf16[2,2,64,1024]{3,2,1,0:T(8,128)(2,1)S(1)} %fusion.11), channel_id=1, source_target_pairs={{0,2},{1,3},{2,0},{3,1},{4,6},{5,7},{6,4},{7,5},{8,10},{9,11},{10,... | collective-permute-start | bytes 1572872 | tf_op jit(solution)/shard_map/ppermute | solution.py:615
  433.4 17.4 %collective-permute-start.36 = (f32[7,128]{1,0:T(8,128)S(1)}, f32[7,128]{1,0:T(8,128)S(1)}, u32[]{:S(2)}, u32[]{:S(2)}) collective-permute-start(f32[7,128]{1,0:T(8,128)S(1)} %slice_bitcast_fusion.3), channel_id=1, source_target_pairs={{16,0},{17,1},{18,2},{19,3},{20,4},{21,5},{22,6},{23,7},{24,8},{25... | collective-permute-start | bytes 10760 | tf_op jit(solution)/shard_map/ppermute | solution.py:706
  448.3 15.2 %collective-permute-start.11 = (bf16[2,2,64,1024]{3,2,1,0:T(8,128)(2,1)}, bf16[2,2,64,1024]{3,2,1,0:T(8,128)(2,1)}, u32[]{:S(2)}, u32[]{:S(2)}) collective-permute-start(bf16[2,2,64,1024]{3,2,1,0:T(8,128)(2,1)} %fusion.10), channel_id=1, source_target_pairs={{0,2},{1,3},{2,0},{3,1},{4,6},{5,7},{6,4},{7,5},{8,10},{9,11},{10,... | collective-permute-start | bytes 1572872 | tf_op jit(solution)/shard_map/ppermute | solution.py:615
  450.8 23.9 %collective-permute-start.8 = (bf16[2,2,64,1024]{3,2,1,0:T(8,128)(2,1)}, bf16[2,2,64,1024]{3,2,1,0:T(8,128)(2,1)}, u32[]{:S(2)}, u32[]{:S(2)}) collective-permute-start(bf16[2,2,64,1024]{3,2,1,0:T(8,128)(2,1)} %fusion.9), channel_id=1, source_target_pairs={{0,2},{1,3},{2,0},{3,1},{4,6},{5,7},{6,4},{7,5},{8,10},{9,11},{10,... | collective-permute-start | bytes 1572872 | tf_op jit(solution)/shard_map/ppermute | solution.py:615
  452.3 29.8 %collective-permute-start.5 = (bf16[2,2,64,1024]{3,2,1,0:T(8,128)(2,1)}, bf16[2,2,64,1024]{3,2,1,0:T(8,128)(2,1)}, u32[]{:S(2)}, u32[]{:S(2)}) collective-permute-start(bf16[2,2,64,1024]{3,2,1,0:T(8,128)(2,1)} %fusion.8), channel_id=1, source_target_pairs={{0,2},{1,3},{2,0},{3,1},{4,6},{5,7},{6,4},{7,5},{8,10},{9,11},{10,... | collective-permute-start | bytes 1572872 | tf_op jit(solution)/shard_map/ppermute | solution.py:615
  463.4 21.2 %collective-permute-start.17 = (bf16[64,1024]{1,0:T(8,128)(2,1)S(1)}, bf16[64,1024]{1,0:T(8,128)(2,1)S(1)}, u32[]{:S(2)}, u32[]{:S(2)}) collective-permute-start(bf16[64,1024]{1,0:T(8,128)(2,1)S(1)} %fusion.24), channel_id=1, source_target_pairs={{0,8},{1,9},{2,10},{3,11},{4,12},{5,13},{6,14},{7,15},{8,0},{9,1},... | collective-permute-start | bytes 393224 | tf_op jit(solution)/shard_map/ppermute | solution.py:615
  474.7 12.5 %collective-permute-start.12 = (bf16[2,64,1024]{2,1,0:T(8,128)(2,1)S(1)}, bf16[2,64,1024]{2,1,0:T(8,128)(2,1)S(1)}, u32[]{:S(2)}, u32[]{:S(2)}) collective-permute-start(bf16[2,64,1024]{2,1,0:T(8,128)(2,1)S(1)} %fusion.21), channel_id=1, source_target_pairs={{0,4},{1,5},{2,6},{3,7},{4,0},{5,1},{6,2},{7,3},{8,12},{9,13},{10,... | collective-permute-start | bytes 786440 | tf_op jit(solution)/shard_map/ppermute | solution.py:615
  482.2 10.2 %collective-permute-start.9 = (bf16[2,64,1024]{2,1,0:T(8,128)(2,1)S(1)}, bf16[2,64,1024]{2,1,0:T(8,128)(2,1)S(1)}, u32[]{:S(2)}, u32[]{:S(2)}) collective-permute-start(bf16[2,64,1024]{2,1,0:T(8,128)(2,1)S(1)} %fusion.22), channel_id=1, source_target_pairs={{0,4},{1,5},{2,6},{3,7},{4,0},{5,1},{6,2},{7,3},{8,12},{9,13},{10,... | collective-permute-start | bytes 786440 | tf_op jit(solution)/shard_map/ppermute | solution.py:615
  484.7 12.6 %collective-permute-start.6 = (bf16[2,64,1024]{2,1,0:T(8,128)(2,1)S(1)}, bf16[2,64,1024]{2,1,0:T(8,128)(2,1)S(1)}, u32[]{:S(2)}, u32[]{:S(2)}) collective-permute-start(bf16[2,64,1024]{2,1,0:T(8,128)(2,1)S(1)} %fusion.23), channel_id=1, source_target_pairs={{0,4},{1,5},{2,6},{3,7},{4,0},{5,1},{6,2},{7,3},{8,12},{9,13},{10,... | collective-permute-start | bytes 786440 | tf_op jit(solution)/shard_map/ppermute | solution.py:615
  488.3 12.0 %collective-permute-start.13 = (bf16[64,1024]{1,0:T(8,128)(2,1)S(1)}, bf16[64,1024]{1,0:T(8,128)(2,1)S(1)}, u32[]{:S(2)}, u32[]{:S(2)}) collective-permute-start(bf16[64,1024]{1,0:T(8,128)(2,1)S(1)} %fusion.27), channel_id=1, source_target_pairs={{0,8},{1,9},{2,10},{3,11},{4,12},{5,13},{6,14},{7,15},{8,0},{9,1},... | collective-permute-start | bytes 393224 | tf_op jit(solution)/shard_map/ppermute | solution.py:615
  493.5 8.2 %collective-permute-start.10 = (bf16[64,1024]{1,0:T(8,128)(2,1)S(1)}, bf16[64,1024]{1,0:T(8,128)(2,1)S(1)}, u32[]{:S(2)}, u32[]{:S(2)}) collective-permute-start(bf16[64,1024]{1,0:T(8,128)(2,1)S(1)} %fusion.29), channel_id=1, source_target_pairs={{0,8},{1,9},{2,10},{3,11},{4,12},{5,13},{6,14},{7,15},{8,0},{9,1},... | collective-permute-start | bytes 393224 | tf_op jit(solution)/shard_map/ppermute | solution.py:615
  498.3 16.3 %collective-permute-start.7 = (bf16[64,1024]{1,0:T(8,128)(2,1)S(1)}, bf16[64,1024]{1,0:T(8,128)(2,1)S(1)}, u32[]{:S(2)}, u32[]{:S(2)}) collective-permute-start(bf16[64,1024]{1,0:T(8,128)(2,1)S(1)} %fusion.31), channel_id=1, source_target_pairs={{0,8},{1,9},{2,10},{3,11},{4,12},{5,13},{6,14},{7,15},{8,0},{9,1},... | collective-permute-start | bytes 393224 | tf_op jit(solution)/shard_map/ppermute | solution.py:615
  506.1 26.2 %collective-permute-start.22 = (bf16[2,2,64,2048]{3,2,1,0:T(8,128)(2,1)S(1)}, bf16[2,2,64,2048]{3,2,1,0:T(8,128)(2,1)S(1)}, u32[]{:S(2)}, u32[]{:S(2)}) collective-permute-start(bf16[2,2,64,2048]{3,2,1,0:T(8,128)(2,1)S(1)} %fusion.1), channel_id=1, source_target_pairs={{0,2},{1,3},{2,0},{3,1},{4,6},{5,7},{6,4},{7,5},{8,10},{9,11},{10,... | collective-permute-start | bytes 3145736 | tf_op jit(solution)/shard_map/ppermute | solution.py:615
  508.1 46.6 %collective-permute-start.19 = (bf16[2,2,64,2048]{3,2,1,0:T(8,128)(2,1)S(1)}, bf16[2,2,64,2048]{3,2,1,0:T(8,128)(2,1)S(1)}, u32[]{:S(2)}, u32[]{:S(2)}) collective-permute-start(bf16[2,2,64,2048]{3,2,1,0:T(8,128)(2,1)S(1)} %fusion), channel_id=1, source_target_pairs={{0,2},{1,3},{2,0},{3,1},{4,6},{5,7},{6,4},{7,5},{8,10},{9,11},{10,... | collective-permute-start | bytes 3145736 | tf_op jit(solution)/shard_map/ppermute | solution.py:615
  512.1 54.7 %collective-permute-start.29 = (bf16[2,2,256,512]{3,2,1,0:T(8,128)(2,1)S(1)}, bf16[2,2,256,512]{3,2,1,0:T(8,128)(2,1)S(1)}, u32[]{:S(2)}, u32[]{:S(2)}) collective-permute-start(bf16[2,2,256,512]{3,2,1,0:T(8,128)(2,1)S(1)} %fusion.3), channel_id=1, source_target_pairs={{0,2},{1,3},{2,0},{3,1},{4,6},{5,7},{6,4},{7,5},{8,10},{9,11},{10,... | collective-permute-start | bytes 3145736 | tf_op jit(solution)/shard_map/ppermute | solution.py:615
  513.5 55.9 %collective-permute-start.26 = (bf16[2,2,256,512]{3,2,1,0:T(8,128)(2,1)S(1)}, bf16[2,2,256,512]{3,2,1,0:T(8,128)(2,1)S(1)}, u32[]{:S(2)}, u32[]{:S(2)}) collective-permute-start(bf16[2,2,256,512]{3,2,1,0:T(8,128)(2,1)S(1)} %fusion.2), channel_id=1, source_target_pairs={{0,4},{1,5},{2,6},{3,7},{4,0},{5,1},{6,2},{7,3},{8,12},{9,13},{10,... | collective-permute-start | bytes 3145736 | tf_op jit(solution)/shard_map/ppermute | solution.py:615
  532.5 39.3 %collective-permute-start.23 = (bf16[2,64,2048]{2,1,0:T(8,128)(2,1)S(1)}, bf16[2,64,2048]{2,1,0:T(8,128)(2,1)S(1)}, u32[]{:S(2)}, u32[]{:S(2)}) collective-permute-start(bf16[2,64,2048]{2,1,0:T(8,128)(2,1)S(1)} %fusion.6), channel_id=1, source_target_pairs={{0,4},{1,5},{2,6},{3,7},{4,0},{5,1},{6,2},{7,3},{8,12},{9,13},{10,... | collective-permute-start | bytes 1572872 | tf_op jit(solution)/shard_map/ppermute | solution.py:615
  555.0 23.0 %collective-permute-start.20 = (bf16[2,64,2048]{2,1,0:T(8,128)(2,1)S(1)}, bf16[2,64,2048]{2,1,0:T(8,128)(2,1)S(1)}, u32[]{:S(2)}, u32[]{:S(2)}) collective-permute-start(bf16[2,64,2048]{2,1,0:T(8,128)(2,1)S(1)} %fusion.7), channel_id=1, source_target_pairs={{0,4},{1,5},{2,6},{3,7},{4,0},{5,1},{6,2},{7,3},{8,12},{9,13},{10,... | collective-permute-start | bytes 1572872 | tf_op jit(solution)/shard_map/ppermute | solution.py:615
  567.1 22.2 %collective-permute-start.30 = (bf16[2,256,512]{2,1,0:T(8,128)(2,1)S(1)}, bf16[2,256,512]{2,1,0:T(8,128)(2,1)S(1)}, u32[]{:S(2)}, u32[]{:S(2)}) collective-permute-start(bf16[2,256,512]{2,1,0:T(8,128)(2,1)S(1)} %fusion.4), channel_id=1, source_target_pairs={{0,4},{1,5},{2,6},{3,7},{4,0},{5,1},{6,2},{7,3},{8,12},{9,13},{10,... | collective-permute-start | bytes 1572872 | tf_op jit(solution)/shard_map/ppermute | solution.py:615
  569.5 41.8 %collective-permute-start.27 = (bf16[2,256,512]{2,1,0:T(8,128)(2,1)S(1)}, bf16[2,256,512]{2,1,0:T(8,128)(2,1)S(1)}, u32[]{:S(2)}, u32[]{:S(2)}) collective-permute-start(bf16[2,256,512]{2,1,0:T(8,128)(2,1)S(1)} %fusion.5), channel_id=1, source_target_pairs={{0,8},{1,9},{2,10},{3,11},{4,12},{5,13},{6,14},{7,15},{8,0},{9,1},... | collective-permute-start | bytes 1572872 | tf_op jit(solution)/shard_map/ppermute | solution.py:615
  571.9 42.3 %collective-permute-start.24 = (bf16[64,2048]{1,0:T(8,128)(2,1)S(1)}, bf16[64,2048]{1,0:T(8,128)(2,1)S(1)}, u32[]{:S(2)}, u32[]{:S(2)}) collective-permute-start(bf16[64,2048]{1,0:T(8,128)(2,1)S(1)} %fusion.16), channel_id=1, source_target_pairs={{0,8},{1,9},{2,10},{3,11},{4,12},{5,13},{6,14},{7,15},{8,0},{9,1},... | collective-permute-start | bytes 786440 | tf_op jit(solution)/shard_map/ppermute | solution.py:615
  578.2 38.9 %collective-permute-start.21 = (bf16[64,2048]{1,0:T(8,128)(2,1)S(1)}, bf16[64,2048]{1,0:T(8,128)(2,1)S(1)}, u32[]{:S(2)}, u32[]{:S(2)}) collective-permute-start(bf16[64,2048]{1,0:T(8,128)(2,1)S(1)} %fusion.18), channel_id=1, source_target_pairs={{0,8},{1,9},{2,10},{3,11},{4,12},{5,13},{6,14},{7,15},{8,0},{9,1},... | collective-permute-start | bytes 786440 | tf_op jit(solution)/shard_map/ppermute | solution.py:615
  589.4 30.4 %collective-permute-start.31 = (bf16[256,512]{1,0:T(8,128)(2,1)S(1)}, bf16[256,512]{1,0:T(8,128)(2,1)S(1)}, u32[]{:S(2)}, u32[]{:S(2)}) collective-permute-start(bf16[256,512]{1,0:T(8,128)(2,1)S(1)} %fusion.12), channel_id=1, source_target_pairs={{0,8},{1,9},{2,10},{3,11},{4,12},{5,13},{6,14},{7,15},{8,0},{9,1},... | collective-permute-start | bytes 786440 | tf_op jit(solution)/shard_map/ppermute | solution.py:615
  611.5 8.5 %collective-permute-start.28 = (bf16[256,512]{1,0:T(8,128)(2,1)S(1)}, bf16[256,512]{1,0:T(8,128)(2,1)S(1)}, u32[]{:S(2)}, u32[]{:S(2)}) collective-permute-start(bf16[256,512]{1,0:T(8,128)(2,1)S(1)} %fusion.14), channel_id=1, source_target_pairs={{0,2},{1,3},{2,0},{3,1},{4,6},{5,7},{6,4},{7,5},{8,10},{9,11},{10,... | collective-permute-start | bytes 786440 | tf_op jit(solution)/shard_map/ppermute | solution.py:615
  (52 other events, 415.1 us)

commit v2 on v1

--- a/solution.py
+++ b/solution.py
@@ -18,7 +18,6 @@
 GROUP = 4 * HEAD
 TILE = 512
 WIDE = 1024
-STASH = 10
 
 
 def nn(a, b):
@@ -58,28 +57,41 @@
     return [pltpu.make_async_copy(a, b, sem.at[i]) for i, (a, b) in enumerate(pairs)]
 
 
-def forward_kernel(slot, *refs):
-    flags, norms, biases, feat, recv, w_in, w_out, w_up, w_down = refs[:9]
-    z_out, squares_out = refs[19:21]
-    s_x, s_a, s_qkv, s_c, s_l, s_h, s_b, s_g, s_d, s_p = refs[21:31]
+def chosen_tick(first, plan):
+    picked = jnp.where(first, plan[0] or 0, plan[1] or 0)
+    active = jnp.where(first, int(plan[0] is not None), int(plan[1] is not None)) == 1
+    return active, picked
+
+
+def forward_kernel(slot, plan, aliased, *refs):
+    spans, norms, vectors, feat, recv, w_in, w_out, w_up, w_down = refs[:9]
+    refs = refs[9 + aliased :]
+    z_out, squares_out = refs[:2]
+    s_x, s_a, s_qkv, s_c, s_l, s_h, s_b, s_g, s_d, s_p, layers = refs[2:13]
     (v_in, v_out, v_up, v_down, v_x, v_a, v_qkv, v_c, v_l, v_h, v_b, v_g, v_d, v_p, v_bias, v_acc, v_z,
-     sem_w, sem_x, sem_o, sem_p, sem_g, sem_d) = refs[31:]
+     sem_w, sem_x, sem_o, sem_p, sem_g, sem_d) = refs[13:]
     rows, width = v_x.shape
     hidden = v_up.shape[1]
     here = pl.ds(slot * rows, rows)
-
-    @pl.when(flags[0] == 1)
+    first = lax.axis_index("section") == 0
+    active, picked = chosen_tick(first, plan)
+
+    def norm(k):
+        return norms[:, k * width : (k + 1) * width]
+
+    def bias(k):
+        return vectors[:, k * width : (k + 1) * width]
+
+    @pl.when(active)
     def _():
-        length = flags[1]
-        causal = flags[2] == 1
-        from_feat = flags[3] == 1
-        picked = flags[4]
-
-        @pl.when(from_feat)
+        length = spans[picked, 0]
+        causal = first
+
+        @pl.when(first)
         def _():
-            pltpu.make_async_copy(feat.at[picked], v_x, sem_x.at[0]).start()
-
-        @pl.when(jnp.logical_not(from_feat))
+            pltpu.make_async_copy(feat.at[picked, 0], v_x, sem_x.at[0]).start()
+
+        @pl.when(jnp.logical_not(first))
         def _():
             pltpu.make_async_copy(recv, v_x, sem_x.at[0]).start()
 
@@ -117,7 +129,7 @@
         def first_norm(i):
             at = part(i, 64)
             normed, _ = row_stats(v_x[at, :].astype(f32))
-            v_a[at, :] = (normed * norms[0:1, :] + norms[1:2, :]).astype(bf16)
+            v_a[at, :] = (normed * norm(0) + norm(1)).astype(bf16)
 
         loop(rows // 64, first_norm)
         outs = []
@@ -132,7 +144,8 @@
         def project(i):
             in_copy(i).wait()
             at = part(i, WIDE)
-            tile = nn(v_a[...], v_in[:, at]) + biases[0:1, at]
+            shift = vectors[:, pl.ds(pl.multiple_of((4 + i // 2) * width, width), width)]
+            tile = nn(v_a[...], v_in[:, at]) + jnp.where(i == 1, 0.0, shift)
             v_qkv[:, at] = tile.astype(bf16)
 
         loop(3 * width // WIDE, project)
@@ -183,7 +196,7 @@
         out_copy(0).wait()
         def mix(i):
             at = part(i, WIDE)
-            v_acc[:, at] = nn(v_c[...], v_out[:, at]) + biases[3:4, at]
+            v_acc[:, at] = nn(v_c[...], v_out[:, at]) + bias(6)
 
         loop(width // WIDE, mix)
 
@@ -198,8 +211,8 @@
             middle = v_x[at, :].astype(f32) + branch
             v_h[at, :] = middle
             normed, _ = row_stats(middle)
-            v_b[at, :] = (normed * norms[2:3, :] + norms[3:4, :]).astype(bf16)
-            v_acc[at, :] = jnp.broadcast_to(biases[4:5, :width], (64, width))
+            v_b[at, :] = (normed * norm(2) + norm(3)).astype(bf16)
+            v_acc[at, :] = jnp.broadcast_to(bias(7), (64, width))
             mask = valid(i, 64)
             return (carry[0] + square(middle, mask), carry[1] + square(branch, mask))
 
@@ -216,7 +229,8 @@
             half = rows // 2
             for r in range(2):
                 rr = slice(r * half, (r + 1) * half)
-                pre = nn(v_b[rr, :], v_up[:, at]) + biases[5:6, at]
+                shift = vectors[:, pl.ds(pl.multiple_of(8 * width + i * WIDE, WIDE), WIDE)]
+                pre = nn(v_b[rr, :], v_up[:, at]) + shift
                 act, slope = gate(pre)
                 act = act.astype(bf16)
                 v_g[rr, at] = act
@@ -246,6 +260,7 @@
         sums_two = (nothing, nothing)
         sums_two = lax.fori_loop(0, rows // 64, finish, sums_two)
         send(v_z, z_out, 7)
+        send(v_z, layers.at[0, picked, 0], 5)
         for k, value in enumerate((sums_one[0], sums_two[0], sums_one[1], sums_two[1])):
             squares_out[k] = value
         for copy in outs:
@@ -256,7 +271,7 @@
         p_copy(groups - 2).wait()
         p_copy(groups - 1).wait()
 
-    @pl.when(flags[0] != 1)
+    @pl.when(jnp.logical_not(active))
     def _():
         squares_out[...] = jnp.zeros_like(squares_out)
 
@@ -274,24 +289,22 @@
         jax.ShapeDtypeStruct((2 * rows, hidden), bf16),
         jax.ShapeDtypeStruct((2 * rows, hidden), bf16),
         jax.ShapeDtypeStruct((2, heads, rows, rows), bf16),
+        jax.ShapeDtypeStruct((1, 2, 1, rows, width), bf16),
     ]
 
 
-def forward_call(slot, flags, norms, biases, feat, recv, weights, stash):
+def forward_call(slot, plan, spans, norms, vectors, feat, recv, weights, stash=()):
     rows, width = recv.shape
     hidden = weights[2].shape[1]
     any_ = pl.BlockSpec(memory_space=pl.ANY)
     vm = pl.BlockSpec(memory_space=pltpu.VMEM)
-    first = stash is None
     shapes = stash_shapes(rows, width, hidden)
-    if first:
-        stash = [jnp.zeros((8, 128), f32)] * STASH
     results = pl.pallas_call(
-        functools.partial(forward_kernel, slot),
-        in_specs=[pl.BlockSpec(memory_space=pltpu.SMEM), vm, vm] + [any_] * 6 + [any_] * STASH,
-        out_specs=[any_, vm] + [any_] * STASH,
+        functools.partial(forward_kernel, slot, plan, len(stash)),
+        in_specs=[pl.BlockSpec(memory_space=pltpu.SMEM), vm, vm] + [any_] * (6 + len(stash)),
+        out_specs=[any_, vm] + [any_] * len(shapes),
         out_shape=[jax.ShapeDtypeStruct((rows, width), bf16), jax.ShapeDtypeStruct((4, 8, width), f32)] + shapes,
-        input_output_aliases={} if first else {9 + k: 2 + k for k in range(STASH)},
+        input_output_aliases={9 + k: 2 + k for k in range(len(stash))},
         scratch_shapes=[
             pltpu.VMEM(w.shape, bf16) for w in weights
         ] + [
@@ -318,33 +331,41 @@
         compiler_params=pltpu.CompilerParams(vmem_limit_bytes=62 * 2**20),
         cost_estimate=pl.CostEstimate(flops=14 * 10**9, bytes_accessed=50 * 10**6, transcendentals=6 * 10**6),
         name="layer_forward",
-    )(flags, norms, biases, feat, recv, *weights, *stash)
+    )(spans, norms, vectors, feat, recv, *weights, *stash)
     return results[0], results[1], results[2:]
 
 
-def backward_kernel(slot, *refs):
-    flags, norms, cot, recv, w_in, w_out, w_up, w_down = refs[:8]
+def backward_kernel(slot, plan, aliased, fed, *refs):
+    spans, norms, cot, recv, w_in, w_out, w_up, w_down = refs[:8]
     s_x, s_qkv, s_c, s_l, s_h, s_d, s_p = refs[8:15]
-    dx_out, smalls = refs[18:20]
-    g_up, g_mid, g_qkv = refs[20:23]
+    refs = refs[15 + aliased :]
+    dx_out, smalls = refs[:2]
+    g_up, g_mid, g_qkv, inputs = refs[2:6]
+    if fed:
+        g_feed = refs[6]
+    refs = refs[6 + fed :]
     (v_in, v_out, v_up, v_down, v_x, v_dy, v_qkv, v_c, v_l, v_h, v_d, v_p, v_du, v_do, v_dc, v_dqkv, v_acc,
-     v_s, v_k, v_dx, sem_w, sem_x, sem_d, sem_p, sem_o) = refs[23:]
+     v_s, v_k, v_dx, sem_w, sem_x, sem_d, sem_p, sem_o) = refs
     rows, width = v_x.shape
     hidden = v_up.shape[1]
     here = pl.ds(slot * rows, rows)
     tiles = hidden // WIDE
 
-    @pl.when(flags[0] == 1)
+    first = lax.axis_index("section") == 0
+    active, picked = chosen_tick(first, plan)
+
+    def norm(k):
+        return norms[:, k * width : (k + 1) * width]
+
+    @pl.when(active)
     def _():
-        length = flags[1]
-        from_cot = flags[3] == 0
-        picked = flags[4]
-
-        @pl.when(from_cot)
+        length = spans[picked, 0]
+
+        @pl.when(jnp.logical_not(first))
         def _():
-            pltpu.make_async_copy(cot.at[picked], v_dy, sem_x.at[0]).start()
-
-        @pl.when(jnp.logical_not(from_cot))
+            pltpu.make_async_copy(cot.at[picked, 0], v_dy, sem_x.at[0]).start()
+
+        @pl.when(first)
         def _():
             pltpu.make_async_copy(recv, v_dy, sem_x.at[0]).start()
 
@@ -407,6 +428,9 @@
 
         total = lax.fori_loop(0, rows // 64, enter, nothing)
         smalls[7:8, :] = jnp.sum(total, axis=0, keepdims=True)
+        if fed:
+            feed_copy = pltpu.make_async_copy(v_dy, g_feed.at[here], sem_o.at[4])
+            feed_copy.start()
 
         def feed(i):
             down_copy(i).wait()
@@ -440,7 +464,7 @@
 
         def second_norm(i, carry):
             at = part(i, 64)
-            rows_back, one, two = norm_back(v_h[at, :], v_acc[at, :], norms[2:3, :])
+            rows_back, one, two = norm_back(v_h[at, :], v_acc[at, :], norm(2))
             middle = rows_back + v_dy[at, :].astype(f32)
             v_acc[at, :] = middle
             low = middle.astype(bf16)
@@ -508,7 +532,7 @@
 
         def first_norm(i, carry):
             at = part(i, 64)
-            rows_back, one, two = norm_back(v_x[at, :].astype(f32), v_h[at, :], norms[0:1, :])
+            rows_back, one, two = norm_back(v_x[at, :].astype(f32), v_h[at, :], norm(0))
             v_dx[at, :] = (rows_back + v_acc[at, :]).astype(bf16)
             return carry[0] + one, carry[1] + two
 
@@ -517,34 +541,39 @@
             smalls[k : k + 1, :] = jnp.sum(value, axis=0, keepdims=True)
         dx_copy = pltpu.make_async_copy(v_dx, dx_out, sem_o.at[2])
         dx_copy.start()
-        for copy in (do_copy, qkv_copy, dx_copy):
+        input_copy = pltpu.make_async_copy(v_dx, inputs.at[0, picked, 0], sem_o.at[5])
+        input_copy.start()
+        for copy in (do_copy, qkv_copy, dx_copy, input_copy):
             copy.wait()
+        if fed:
+            feed_copy.wait()
         pltpu.make_async_copy(v_du, g_up.at[here], sem_o.at[3]).wait()
 
-    @pl.when(flags[0] != 1)
+    @pl.when(jnp.logical_not(active))
     def _():
         smalls[...] = jnp.zeros_like(smalls)
 
 
-def backward_call(slot, flags, norms, cot, recv, weights, stash, grads):
+def backward_call(slot, plan, spans, norms, cot, recv, weights, stash, grads=(), fed=True):
     rows, width = recv.shape
     hidden = weights[2].shape[1]
     any_ = pl.BlockSpec(memory_space=pl.ANY)
     vm = pl.BlockSpec(memory_space=pltpu.VMEM)
-    first = grads is None
     shapes = [jax.ShapeDtypeStruct((2 * rows, n), bf16) for n in (hidden, width, 3 * width)]
-    if first:
-        grads = [jnp.zeros((8, 128), f32)] * 3
-    s_x, s_a, s_qkv, s_c, s_l, s_h, s_b, s_g, s_d, s_p = stash
+    shapes.append(jax.ShapeDtypeStruct((1, 2, 1, rows, width), bf16))
+    if fed:
+        shapes.append(jax.ShapeDtypeStruct((2 * rows, width), bf16))
+    s_x, s_a, s_qkv, s_c, s_l, s_h, s_b, s_g, s_d, s_p, _ = stash
+    grads = grads[: len(shapes)]
     results = pl.pallas_call(
-        functools.partial(backward_kernel, slot),
-        in_specs=[pl.BlockSpec(memory_space=pltpu.SMEM), vm] + [any_] * 16,
-        out_specs=[any_, vm] + [any_] * 3,
+        functools.partial(backward_kernel, slot, plan, len(grads), int(fed)),
+        in_specs=[pl.BlockSpec(memory_space=pltpu.SMEM), vm] + [any_] * (13 + len(grads)),
+        out_specs=[any_, vm] + [any_] * len(shapes),
         out_shape=[
             jax.ShapeDtypeStruct((rows, width), bf16),
             jax.ShapeDtypeStruct((8 + hidden // WIDE, width), f32),
         ] + shapes,
-        input_output_aliases={} if first else {15 + k: 2 + k for k in range(3)},
+        input_output_aliases={15 + k: 2 + k for k in range(len(grads))},
         scratch_shapes=[pltpu.VMEM(w.shape, bf16) for w in weights] + [
             pltpu.VMEM((rows, width), bf16),
             pltpu.VMEM((rows, width), bf16),
@@ -566,22 +595,82 @@
             pltpu.SemaphoreType.DMA((8,)),
             pltpu.SemaphoreType.DMA((2,)),
             pltpu.SemaphoreType.DMA((2,)),
-            pltpu.SemaphoreType.DMA((4,)),
+            pltpu.SemaphoreType.DMA((6,)),
         ],
         compiler_params=pltpu.CompilerParams(vmem_limit_bytes=62 * 2**20),
         cost_estimate=pl.CostEstimate(flops=18 * 10**9, bytes_accessed=60 * 10**6, transcendentals=0),
         name="layer_backward",
-    )(flags, norms, cot, recv, *weights, s_x, s_qkv, s_c, s_l, s_h, s_d, s_p, *grads)
+    )(spans, norms, cot, recv, *weights, s_x, s_qkv, s_c, s_l, s_h, s_d, s_p, *grads)
     return results[0], results[1], results[2:]
 
 
+def turned_blocks(source, target, block):
+    half = target.shape[0] // 2
+    flat = source[...].T
+    for core in range(2):
+
+        @pl.when(lax.axis_index("dp") % 2 == core)
+        def _(core=core):
+            for k in range(half // block):
+                other = (2 * k + 1 - core) * block
+                own = (2 * k + core) * block
+                target[k * block : (k + 1) * block, :] = flat[other : other + block]
+                target[half + k * block : half + (k + 1) * block, :] = flat[own : own + block]
+
+
+def weight_kernel(block, left, right, theirs, mine, turned):
+    half = left.shape[1] // 2
+
+    @pl.when(pl.program_id(1) == 0)
+    def _():
+        turned_blocks(left, turned, block)
+
+    theirs[...] = nn(turned[:half, :], right[...]).astype(bf16)
+    mine[...] = nn(turned[half:, :], right[...]).astype(bf16)
+
+
+def feed_weight_kernel(block, left, right, late, theirs, mine, turned):
+    half = left.shape[1] // 2
+    rows = late.shape[0]
+    turned_blocks(left, turned, block)
+    second = jnp.where(lax.axis_index("section") == 0, late[...], right[rows:, :])
+    for at, out in ((slice(0, half), theirs), (slice(half, 2 * half), mine)):
+        out[...] = (nn(turned[at, :rows], right[:rows, :]) + nn(turned[at, rows:], second)).astype(bf16)
+
+
+def weight_call(left, right, start, columns, late=None):
+    rows, height = left.shape
+    tall = min(height, WIDE)
+    wide = min(columns, WIDE)
+    block = height // lax.axis_size("dp")
+    shape = jax.ShapeDtypeStruct((height // 2, columns), bf16)
+    specs = [
+        pl.BlockSpec((rows, tall), lambda i, j: (0, i)),
+        pl.BlockSpec((rows, wide), lambda i, j: (0, start // wide + j)),
+    ]
+    operands = (left, right)
+    if late is not None:
+        assert wide == columns
+        specs.append(pl.BlockSpec((rows // 2, wide), lambda i, j: (0, start // wide + j)))
+        operands += (late,)
+    return pl.pallas_call(
+        functools.partial(weight_kernel if late is None else feed_weight_kernel, block),
+        grid=(height // tall, columns // wide),
+        in_specs=specs,
+        out_specs=[pl.BlockSpec((tall // 2, wide), lambda i, j: (i, j))] * 2,
+        out_shape=[shape] * 2,
+        scratch_shapes=[pltpu.VMEM((tall, rows), bf16)],
+        compiler_params=pltpu.CompilerParams(vmem_limit_bytes=40 * 2**20),
+        cost_estimate=pl.CostEstimate(
+            flops=2 * rows * height * columns,
+            bytes_accessed=2 * (rows * height + rows * columns + height * columns),
+            transcendentals=0,
+        ),
+        name="weight_product",
+    )(*operands)
+
+
 highest = lax.Precision.HIGHEST
-
-
-def transposed_product(former, latter):
-    return lax.dot_general(
-        former, latter, (((0,), (0,)), ((), ())), preferred_element_type=jnp.float32
-    )
 
 
 def added(terms):
@@ -595,60 +684,60 @@
     return lax.dynamic_index_in_dim(array, index, axis, keepdims=False)
 
 
+class Line:
+    def __init__(self):
+        self.last = None
+
+    def after(self, values):
+        if self.last is not None:
+            values = lax.optimization_barrier(tuple(values) + (self.last,))[:-1]
+        return list(values)
+
+    def done(self, value):
+        self.last = value
+
+
 class Exchange:
-    def __init__(self, terms, bits, order):
+    def __init__(self, line, terms, left, order):
+        self.line = line
         self.terms = terms
-        self.left = list(range(bits - 1, -1, -1))
+        self.left = sorted(left, reverse=True)
         self.order = list(order)
         self.kind = terms[0].dtype
 
-    def step(self, theirs=None):
+    def step(self):
         bit = self.order.pop(0)
         axis = self.left.index(bit)
         self.left.pop(axis)
         mine = (lax.axis_index("dp") >> bit) & 1
-        if theirs is None:
-            theirs = added([pick(term, axis, 1 - mine) for term in self.terms]).astype(self.kind)
-            self.terms = [pick(term, axis, mine) for term in self.terms]
-        size = lax.axis_size("dp")
-        pairs = [(i, i ^ (1 << bit)) for i in range(size)]
-        self.terms = self.terms + [lax.ppermute(theirs, "dp", pairs)]
+        self.terms = self.line.after(self.terms)
+        theirs = added([pick(term, axis, 1 - mine) for term in self.terms]).astype(self.kind)
+        self.line.done(theirs)
+        self.terms = [pick(term, axis, mine) for term in self.terms] + [crossed(theirs, bit)]
 
     def finish(self):
         while self.order:
             self.step()
-        return added(self.terms)
-
-
-def weight_sum(former, latter, bits, orders):
-    rows = former.shape[0]
-    size = 1 << bits
-    blocks = former.reshape((rows, size // 2, 2, former.shape[1] // size))
-    core = lax.axis_index("dp") & 1
-    halves = []
-    for which in (1 - core, core):
-        columns = pick(blocks, 2, which).reshape(rows, former.shape[1] // 2)
-        halves.append(transposed_product(columns, latter).astype(bf16))
-    theirs, mine = halves
-    size_of = [2] * (bits - 1) + [former.shape[1] // size]
-    pairs = [(i, i ^ 1) for i in range(size)]
-    received = lax.ppermute(theirs, "dp", pairs)
-    start = 0
-    parts = []
-    for columns, order in orders:
-        cut = slice(start, start + columns)
-        start += columns
-        exchange = Shifted(
-            [half[:, cut].reshape(size_of + [columns]) for half in (mine, received)], bits - 1, order
-        )
-        parts.append(exchange)
-    return parts
-
-
-class Shifted(Exchange):
-    def __init__(self, terms, bits, order):
-        super().__init__(terms, bits, order)
-        self.left = list(range(bits, 0, -1))
+        self.terms = self.line.after(self.terms)
+        total = added(self.terms)
+        self.line.done(total)
+        return total
+
+
+def crossed(value, bit):
+    return lax.ppermute(value, "dp", [(i, i ^ (1 << bit)) for i in range(lax.axis_size("dp"))])
+
+
+def weight_sum(line, left, right, start, columns, order, late=None):
+    left, right = line.after((left, right))
+    theirs, mine = weight_call(left, right, start, columns, late)
+    line.done(theirs)
+    size = lax.axis_size("dp")
+    bits = size.bit_length() - 1
+    shape = [2] * (bits - 1) + [left.shape[1] // size, columns]
+    received = crossed(theirs, 0)
+    terms = [half.reshape(shape) for half in (mine, received)]
+    return Exchange(line, terms, range(1, bits), order)
 
 
 def shards(
@@ -665,49 +754,27 @@
     codebook_table,
 ):
     is_first = lax.axis_index("section") == 0
-    first = is_first.astype(jnp.int32)
-    last = 1 - first
+    adaptive = jnp.where(is_first, 0.0, 1.0)
     rows, width = features.shape[2:]
     hidden = feed_up.shape[2]
     size = lax.axis_size("dp")
     bits = size.bit_length() - 1
-    feats = features[:, 0]
-    cots = cotangent[:, 0]
-    spans = lengths[:, 0]
     weights = (attention_in[0], attention_out[0], feed_up[0], feed_down[0])
-    vector = vectors[0]
-    raw_norms = vector[: 4 * width].reshape(4, width)
-    pad = jnp.zeros((hidden - width,), f32)
-    query_bias, value_bias, out_bias, down_bias = [
-        vector[k * width : (k + 1) * width] for k in range(4, 8)
-    ]
-    zero = jnp.zeros((width,), f32)
-    empty = jnp.zeros((hidden,), f32)
-    biases = jnp.stack(
-        [
-            jnp.concatenate([query_bias, zero, value_bias, empty[: hidden - 3 * width]]),
-            empty,
-            empty,
-            jnp.concatenate([out_bias, pad]),
-            jnp.concatenate([down_bias, pad]),
-            vector[8 * width :],
-            empty,
-            empty,
-        ]
-    )
-
-    def flags(*values):
-        return jnp.stack([jnp.asarray(value, jnp.int32) for value in values])
-
-    def chosen(a, b):
-        return jnp.where(is_first, a, b)
 
     def send(value, to):
         return lax.ppermute(value, "section", [(1 - to, to)])
 
-    z_one, squares_one, stash = forward_call(
-        0, flags(first, spans[0], 1, 1, 0), raw_norms, biases, feats, feats[0], weights, None
-    )
+    nowhere = jnp.zeros((rows, width), bf16)
+
+    def forward(slot, plan, norms, recv, stash=()):
+        return forward_call(slot, plan, lengths, norms, vectors, features, recv, weights, stash)
+
+    def backward(slot, plan, norms, recv, stash, grads=(), fed=True):
+        return backward_call(
+            slot, plan, lengths, norms, cotangent, recv, weights, stash, grads, fed
+        )
+
+    z_one, squares_one, stash = forward(0, (0, None), vectors, nowhere)
     received_one = send(z_one, 1)
     table, z_one = lax.optimization_barrier((codebook_table, z_one))
     condition_table = jnp.dot(table, adaptive_weight, preferred_element_type=f32)
@@ -715,79 +782,51 @@
         codebook_index[:, 0][:, None]
         == jnp.arange(codebook_table.shape[0], dtype=jnp.int32)[None, :]
     ).astype(f32)
-    condition = (jnp.dot(one_hot, condition_table, precision=highest) * last.astype(f32)).reshape(
-        -1, 4, width
+    norms = vectors[:, : 4 * width] + adaptive * jnp.dot(
+        one_hot, condition_table, precision=highest
     )
-    norms = [raw_norms + condition[k] for k in range(2)]
-    z_two, squares_two, stash = forward_call(
-        1,
-        flags(1, chosen(spans[1], spans[0]), first, first, 1),
-        norms[0],
-        biases,
-        feats,
-        received_one,
-        weights,
-        stash,
+    norms_one, norms_two = norms[:1], norms[1:]
+    z_two, squares_two, stash = forward(1, (1, 0), norms_one, received_one, stash)
+    received_two = send(z_two, 1)
+    dx_one, smalls_one, grads = backward(1, (None, 0), norms_one, nowhere, stash)
+    back_one = send(dx_one, 0)
+    z_three, squares_three, stash = forward(0, (None, 1), norms_two, received_two, stash)
+    dx_two, smalls_two, grads = backward(0, (0, 1), norms_two, back_one, stash, grads)
+    back_two = send(dx_two, 0)
+
+    s_x, s_a, s_qkv, s_c, s_l, s_h, s_b, s_g, s_d, s_p, layer_outputs = stash
+    side_first = list(range(1, bits))
+    line_first = side_first[1:] + side_first[:1]
+    line = Line()
+    half = width // 2
+    g_feed = grads[4]
+    down_one = weight_sum(line, s_g, g_feed, 0, half, line_first, back_two)
+    down_two = weight_sum(line, s_g, g_feed, half, half, side_first, back_two)
+    down_one.step()
+    down_two.step()
+    (back_two,) = line.after((back_two,))
+    _, smalls_three, grads = backward(
+        1, (1, None), vectors, back_two, stash, grads[:4], fed=False
     )
-    received_two = send(z_two, 1)
-    dx_one, smalls_one, grads = backward_call(
-        1, flags(last, spans[0], 0, 0, 0), norms[0], cots, cots[0], weights, stash, None
-    )
-    back_one = send(dx_one, 0)
-    z_three, squares_three, stash = forward_call(
-        0,
-        flags(last, spans[1], 0, 0, 0),
-        norms[1],
-        biases,
-        feats,
-        received_two,
-        weights,
-        stash,
-    )
-    dx_two, smalls_two, grads = backward_call(
-        0,
-        flags(1, chosen(spans[0], spans[1]), 0, first, 1),
-        norms[1],
-        cots,
-        back_one,
-        weights,
-        stash,
-        grads,
-    )
-    back_two = send(dx_two, 0)
-    places = jnp.arange(rows, dtype=jnp.int32)[None, :, None]
-    masked = jnp.where(places < spans[:, None, None], cots, 0)
-    grad_feed = chosen(
-        jnp.stack([back_one, back_two]), jnp.stack([masked[1], masked[0]])
-    ).reshape(2 * rows, width)
-    s_x, s_a, s_qkv, s_c, s_l, s_h, s_b, s_g, s_d, s_p = stash
-    lower = list(range(1, bits))
-    side_first = lower
-    line_first = lower[1:] + lower[:1]
-    half = width // 2
-    down_parts = weight_sum(
-        s_g, grad_feed, bits, [(half, line_first), (half, side_first)]
-    )
-    for part_ in down_parts:
-        part_.step()
-    dx_three, smalls_three, (g_up, g_mid, g_qkv) = backward_call(
-        1, flags(first, spans[1], 0, 1, 0), raw_norms, cots, back_two, weights, stash, grads
-    )
-    up_parts = weight_sum(s_b, g_up, bits, [(hidden // 2, side_first)] * 2)
-    out_parts = weight_sum(s_c, g_mid, bits, [(width, side_first)])
-    in_parts = weight_sum(s_a, g_qkv, bits, [(width, side_first)] * 3)
+    line.done(smalls_three)
+    g_up, g_mid, g_qkv, input_grads = grads
+    down_one.step()
+    down_two.step()
+    up_one = weight_sum(line, s_b, g_up, 0, hidden // 2, side_first)
+    up_two = weight_sum(line, s_b, g_up, hidden // 2, hidden // 2, side_first)
+    up_one.step()
+    down_two.step()
+    down_one.step()
 
     smalls = smalls_one + smalls_two + smalls_three
-    picks = [one_hot[0], one_hot[1]]
-    table_grad = (
-        picks[0][:, None] * smalls_one[:4].reshape(1, -1)
-        + picks[1][:, None] * (smalls_two[:4].reshape(1, -1) * last.astype(f32))
+    table_grad = one_hot[0][:, None] * smalls_one[:4].reshape(1, -1) + one_hot[1][:, None] * (
+        smalls_two[:4].reshape(1, -1) * adaptive
     )
     codes = table_grad.shape[0]
     share = table_grad.shape[1] // (2 * size)
     table_blocks = table_grad.reshape(codes, 2, size, share).transpose(2, 1, 0, 3)
     squares = jnp.sum(squares_one + squares_two + squares_three, axis=(1, 2))
-    counted = jnp.sum(spans).astype(f32)
+    counted = jnp.sum(lengths).astype(f32)
     totals = jnp.concatenate([squares, counted[None], jnp.zeros((123,), f32)])
     packed = jnp.concatenate(
         [
@@ -797,14 +836,41 @@
         ],
         axis=1,
     )
-    length = packed.shape[1]
-    small_sum = Exchange(
-        [packed.reshape([2] * bits + [length])], bits, list(range(bits))
-    ).finish()
+    small = Exchange(
+        line, [packed.reshape([2] * bits + [packed.shape[1]])], range(bits), range(bits)
+    )
+    small.step()
+    in_one = weight_sum(line, s_a, g_qkv, 0, 2 * width, side_first)
+    small.step()
+    up_two.step()
+    in_two = weight_sum(line, s_a, g_qkv, 2 * width, width, side_first)
+    out_one = weight_sum(line, s_c, g_mid, 0, width, side_first)
+    small.step()
+    up_one.step()
+    in_one.step()
+    down_sum = [down_one.finish(), down_two.finish()]
+    small.step()
+    up_one.step()
+    up_two.step()
+    in_two.step()
+    out_one.step()
+    small_sum = small.finish()
     vector_share = small_sum[: smalls.size // size]
     table_share = small_sum[smalls.size // size : -128].reshape(2, codes, share)
     totals = small_sum[-128:]
-    table_own = chosen(send(table_share[0], 0), table_share[1])
+    table_own = jnp.where(is_first, send(table_share[0], 0), table_share[1])
+    up_two.step()
+    in_one.step()
+    up_one_sum = up_one.finish()
+    in_one.step()
+    up_sum = [up_one_sum, up_two.finish()]
+    in_two.step()
+    in_one_sum = in_one.finish()
+    in_two.step()
+    out_one.step()
+    out_one.step()
+    in_sum = [in_one_sum, in_two.finish()]
+    out_sum = [out_one.finish()]
     grad_adaptive = lax.dot_general(
         codebook_table.astype(f32),
         table_own,
@@ -815,21 +881,15 @@
     residual_rms = jnp.sqrt(totals[:4] / (totals[4] * width))[None]
 
     def joined(parts):
-        return jnp.concatenate([part_.finish() for part_ in parts], axis=-1)[None]
-
-    layer_outputs = jnp.stack([chosen(z_one, z_two), chosen(z_two, z_three)])[None, :, None]
-    input_grads = jnp.stack([chosen(dx_two, dx_one), chosen(dx_three, dx_two)])[None, :, None]
-    down_sum = joined(down_parts)
-    up_sum = joined(up_parts)
-    out_sum = joined(out_parts)
-    in_sum = joined(in_parts)
+        return jnp.concatenate(parts, axis=-1)[None]
+
     return (
         layer_outputs,
         input_grads,
-        in_sum,
-        out_sum,
-        up_sum,
-        down_sum,
+        joined(in_sum),
+        joined(out_sum),
+        joined(up_sum),
+        joined(down_sum),
         vector_share[None],
         grad_adaptive,
         residual_rms,

time: 631 us -> 525 us (0.83)
  local copies, waits for them, and re-layouts: 127 us -> 40.8 us
  Pallas kernels: 166 us -> 222 us
  matrix products: 44 us -> 6.09 us
  waiting for transfers between devices: 194 us -> 167 us
    ppermute x32, waiting for transfers between devices: 130 us -> 50.5 us  [crossed(): lax.ppermute(value, 'dp', [(i, i ^ 1 << bit) for i in range(lax.axis_size...]
    pallas_call x6 -> x13, Pallas kernels: 166 us -> 222 us  [the longest x3 88.3 us: forward_call(): pl.pallas_call(functools.partial(forward_kernel, slot, plan, len(stash)),...]
    ppermute x5, waiting for transfers between devices: 64.2 us -> 116 us  [send(): return lax.ppermute(value, 'section', [(1 - to, to)])]
    dot_general x9 -> x1, matrix products: 38.1 us -> 0.26 us  [shards(): jnp.dot(one_hot, condition_table, precision=highest)]
    unnamed x98 -> x99, local copies, waits for them, and re-layouts: 48.9 us -> 13.5 us
    dynamic_slice x13 -> x4, local copies, waits for them, and re-layouts: 26.2 us -> 2.06 us  [pick(): return lax.dynamic_index_in_dim(array, index, axis, keepdims=False)]
    squeeze x4 -> x60, local copies, waits for them, and re-layouts: 3.33 us -> 21.9 us  [pick(): return lax.dynamic_index_in_dim(array, index, axis, keepdims=False)]
    slice x12 -> x4, local copies, waits for them, and re-layouts: 17.8 us -> 0.64 us  [the longest x1 0.63 us: shards(): norms_one, norms_two = (norms[:1], norms[1:])]
  transfers between devices with their start and end apart: 37 -> 37, of which waited for: 22 -> 12; matrix products, arithmetic and copies ran while one was open for 30% -> 13% of each run, Pallas kernels for 1% -> 16%
where the time goes in v2:
time: 525 us; the launch traced here: 518 us
  Pallas kernels  222 us (42%)
  waiting for transfers between devices  167 us (32%)
  starting transfers between devices  41.7 us (8%)
  local copies, waits for them, and re-layouts  40.8 us (8%)
  other arithmetic  37.9 us (7%)
  matrix products  6.09 us (1%)
    ppermute x5, waiting for transfers between devices, send(): return lax.ppermute(value, 'section', [(1 - to, to)])  116 us
    pallas_call x3, Pallas kernels, forward_call(): pl.pallas_call(functools.partial(forward_kernel, slot, plan, len(stash)),...  88.3 us
    pallas_call x3, Pallas kernels, backward_call(): pl.pallas_call(functools.partial(backward_kernel, slot, plan, len(grads),...  85.5 us
    ppermute x32, waiting for transfers between devices, crossed(): lax.ppermute(value, 'dp', [(i, i ^ 1 << bit) for i in range(lax.axis_size...  50.5 us
    pallas_call x7, Pallas kernels, weight_call(): pl.pallas_call(functools.partial(weight_kernel if late is None else feed_...  48 us
    ppermute x32, starting transfers between devices, crossed(): lax.ppermute(value, 'dp', [(i, i ^ 1 << bit) for i in range(lax.axis_size...  31.8 us
    convert_element_type x14, other arithmetic, step(): added([pick(term, axis, 1 - mine) for term in self.terms]).astype(self.kind)  24.2 us
    squeeze x60, local copies, waits for them, and re-layouts, pick(): return lax.dynamic_index_in_dim(array, index, axis, keepdims=False)  21.9 us
  transfers between devices with their start and end apart: 37, of which 12 were waited for; matrix products, arithmetic and copies ran while one was open for 13% of the time, Pallas kernels for 16%

profile of v2, /device:TPU:0, one launch (start us, length us, event | category | flops | bytes accessed | tf_op | source)
XLA Modules:
  0.0 518.5 jit_solution(10660858305564308418)
XLA Ops:
  3.1 40.3 %layer_forward.3 = (bf16[512,1024]{1,0:T(8,128)(2,1)}, f32[4,8,1024]{2,1,0:T(8,128)}, bf16[1024,1024]{1,0:T(8,128)(2,1)}, bf16[1024,1024]{1,0:T(8,128)(2,1)}, bf...) custom-call(s32[2,1]{1,0:T(2,128)} %copy.88.refs_0_, ...), custom_call_target="tpu_custom_call" | custom-call | flops 14000000000 | bytes 50000000 | tf_op jit(solution)/shard_map/layer_forward/pallas_call | solution.py:302
  44.9 4.6 fusion.40
  50.4 17.9 %collective-permute-done.refs_4_ = bf16[512,1024]{1,0:T(8,128)(2,1)S(1)} collective-permute-done((bf16[512,1024]{1,0:T(8,128)(2,1)}, bf16[512,1024]{1,0:T(8,128)(2,1)S(1)}, u32[]{:S(2)}, u32[]{:S(2)}) %collective-permute-start) | collective-permute-done | bytes 1048608 | tf_op jit(solution)/shard_map/ppermute | solution.py:765
  69.2 40.2 %layer_forward.4 = (bf16[512,1024]{1,0:T(8,128)(2,1)}, f32[4,8,1024]{2,1,0:T(8,128)}, bf16[1024,1024]{1,0:T(8,128)(2,1)}, bf16[1024,1024]{1,0:T(8,128)(2,1)}, bf...) custom-call(s32[2,1]{1,0:T(2,128)} %copy.88.refs_0_, ...), custom_call_target="tpu_custom_call", output_to_operand_aliasing={{2}: (9, {}), {3}: (10, {}), {4}: (11, {}), {5}: (12, {}), ... | custom-call | flops 14000000000 | bytes 50000000 | tf_op jit(solution)/shard_map/layer_forward/pallas_call | solution.py:302
  109.4 4.3 collective-permute-start.1
  116.9 19.6 %collective-permute-done.1.refs_4_ = bf16[512,1024]{1,0:T(8,128)(2,1)S(1)} collective-permute-done((bf16[512,1024]{1,0:T(8,128)(2,1)}, bf16[512,1024]{1,0:T(8,128)(2,1)S(1)}, u32[]{:S(2)}, u32[]{:S(2)}) %collective-permute-start.1) | collective-permute-done | bytes 1048608 | tf_op jit(solution)/shard_map/ppermute | solution.py:765
  137.4 7.8 %layer_forward.5 = (bf16[512,1024]{1,0:T(8,128)(2,1)}, f32[4,8,1024]{2,1,0:T(8,128)}, bf16[1024,1024]{1,0:T(8,128)(2,1)}, bf16[1024,1024]{1,0:T(8,128)(2,1)}, bf...) custom-call(s32[2,1]{1,0:T(2,128)} %copy.88.refs_0_, ...), custom_call_target="tpu_custom_call", output_to_operand_aliasing={{2}: (9, {}), {3}: (10, {}), {4}: (11, {}), {5}: (12, {}), ... | custom-call | flops 14000000000 | bytes 50000000 | tf_op jit(solution)/shard_map/layer_forward/pallas_call | solution.py:302
  145.2 34.4 %collective-permute-done.2.refs_3_ = bf16[512,1024]{1,0:T(8,128)(2,1)} collective-permute-done((bf16[512,1024]{1,0:T(8,128)(2,1)}, bf16[512,1024]{1,0:T(8,128)(2,1)}, u32[]{:S(2)}, u32[]{:S(2)}) %collective-permute-start.2) | collective-permute-done | bytes 1048608 | tf_op jit(solution)/shard_map/ppermute | solution.py:765
  179.7 42.0 %layer_backward.4 = (bf16[512,1024]{1,0:T(8,128)(2,1)}, f32[12,1024]{1,0:T(8,128)}, bf16[1024,4096]{1,0:T(8,128)(2,1)}, bf16[1024,1024]{1,0:T(8,128)(2,1)}, bf16...) custom-call(s32[2,1]{1,0:T(2,128)} %copy.88.refs_0_, ...), custom_call_target="tpu_custom_call", output_to_operand_aliasing={{2}: (15, {}), {3}: (16, {}), {4}: (17, {}), {5}: (18, {}),... | custom-call | flops 17999998976 | bytes 60000000 | tf_op jit(solution)/shard_map/layer_backward/pallas_call | solution.py:568
  223.1 42.0 %collective-permute-done.3.late.refs_3_ = bf16[512,1024]{1,0:T(8,128)(2,1)S(1)} collective-permute-done((bf16[512,1024]{1,0:T(8,128)(2,1)}, bf16[512,1024]{1,0:T(8,128)(2,1)S(1)}, u32[]{:S(2)}, u32[]{:S(2)}) %collective-permute-start.3) | collective-permute-done | bytes 1048608 | tf_op jit(solution)/shard_map/ppermute | solution.py:765
  267.1 9.8 %weight_product.7 = (bf16[2048,512]{1,0:T(8,128)(2,1)}, bf16[2048,512]{1,0:T(8,128)(2,1)S(1)}) custom-call(bf16[1024,4096]{1,0:T(8,128)(2,1)} %get-tuple-element.250.left, bf16[1024,1024]{1,0:T(8,128)(2,1)S(1)} %copy-done.10, bf16[512,1024]{1,0:T(8,128)(2,1)S(1)} %collective-permute-done.3.late.refs_3_), custom_call_target="tpu_custom_call" | custom-call | flops 4294967296 | bytes 13631488 | tf_op jit(solution)/shard_map/weight_product/pallas_call | solution.py:656
  277.1 10.7 %weight_product.8 = (bf16[2048,512]{1,0:T(8,128)(2,1)}, bf16[2048,512]{1,0:T(8,128)(2,1)S(1)}) custom-call(bf16[1024,4096]{1,0:T(8,128)(2,1)} %get-tuple-element.250.left, bf16[1024,1024]{1,0:T(8,128)(2,1)S(1)} %copy-done.10, bf16[512,1024]{1,0:T(8,128)(2,1)S(1)} %collective-permute-done.3.late.refs_3_), custom_call_target="tpu_custom_call" | custom-call | flops 4294967296 | bytes 13631488 | tf_op jit(solution)/shard_map/weight_product/pallas_call | solution.py:656
  291.2 2.6 fusion.1
  295.7 2.5 fusion.2
  299.7 41.7 %layer_backward.5 = (bf16[512,1024]{1,0:T(8,128)(2,1)}, f32[12,1024]{1,0:T(8,128)}, bf16[1024,4096]{1,0:T(8,128)(2,1)}, bf16[1024,1024]{1,0:T(8,128)(2,1)}, bf16...) custom-call(s32[2,1]{1,0:T(2,128)} %copy.88.refs_0_, ...), custom_call_target="tpu_custom_call", output_to_operand_aliasing={{2}: (15, {}), {3}: (16, {}), {4}: (17, {}), {5}: (18, {})} | custom-call | flops 17999998976 | bytes 60000000 | tf_op jit(solution)/shard_map/layer_backward/pallas_call | solution.py:568
  351.4 7.7 %weight_product.9 = (bf16[512,2048]{1,0:T(8,128)(2,1)}, bf16[512,2048]{1,0:T(8,128)(2,1)S(1)}) custom-call(bf16[1024,1024]{1,0:T(8,128)(2,1)S(1)} %copy-done.3, bf16[1024,4096]{1,0:T(8,128)(2,1)} %get-tuple-element.286.right), custom_call_target="tpu_custom_call" | custom-call | flops 4294967296 | bytes 10485760 | tf_op jit(solution)/shard_map/weight_product/pallas_call | solution.py:656
  359.9 2.6 collective-permute-start.7
  364.1 7.4 %weight_product.10 = (bf16[512,2048]{1,0:T(8,128)(2,1)S(1)}, bf16[512,2048]{1,0:T(8,128)(2,1)S(1)}) custom-call(bf16[1024,1024]{1,0:T(8,128)(2,1)S(1)} %copy-done.4, bf16[1024,4096]{1,0:T(8,128)(2,1)} %get-tuple-element.286.right), custom_call_target="tpu_custom_call" | custom-call | flops 4294967296 | bytes 10485760 | tf_op jit(solution)/shard_map/weight_product/pallas_call | solution.py:656
  374.1 2.7 fusion.3
  377.5 7.8 %collective-permute-done.9 = bf16[2,256,512]{2,1,0:T(8,128)(2,1)S(1)} collective-permute-done((bf16[2,256,512]{2,1,0:T(8,128)(2,1)}, bf16[2,256,512]{2,1,0:T(8,128)(2,1)S(1)}, u32[]{:S(2)}, u32[]{:S(2)}) %collective-permute-start.9) | collective-permute-done | bytes 524320 | tf_op jit(solution)/shard_map/ppermute | solution.py:728
  391.3 6.0 %weight_product.11 = (bf16[512,2048]{1,0:T(8,128)(2,1)S(1)}, bf16[512,2048]{1,0:T(8,128)(2,1)S(1)}) custom-call(bf16[1024,1024]{1,0:T(8,128)(2,1)S(1)} %copy-done.2, bf16[1024,3072]{1,0:T(8,128)(2,1)S(1)} %bitcast.249), custom_call_target="tpu_custom_call" | custom-call | flops 4294967296 | bytes 10485760 | tf_op jit(solution)/shard_map/weight_product/pallas_call | solution.py:656
  400.3 2.6 fusion.4
  402.9 3.3 weight_product.12
  408.7 3.1 weight_product.13
  421.6 10.1 %collective-permute-done.19 = f32[2,2688]{1,0:T(2,128)S(1)} collective-permute-done((f32[2,2688]{1,0:T(2,128)S(1)}, f32[2,2688]{1,0:T(2,128)S(1)}, u32[]{:S(2)}, u32[]{:S(2)}) %collective-permute-start.19) | collective-permute-done | bytes 21536 | tf_op jit(solution)/shard_map/ppermute | solution.py:728
  433.4 3.0 collective-permute-start.23
  470.5 12.9 %collective-permute-done.26 = bf16[2,64,2048]{2,1,0:T(8,128)(2,1)S(1)} collective-permute-done((bf16[2,64,2048]{2,1,0:T(8,128)(2,1)S(1)}, bf16[2,64,2048]{2,1,0:T(8,128)(2,1)S(1)}, u32[]{:S(2)}, u32[]{:S(2)}) %collective-permute-start.26) | collective-permute-done | bytes 524320 | tf_op jit(solution)/shard_map/ppermute | solution.py:728
  487.9 2.5 collective-permute-start.31
  490.5 5.7 %collective-permute-done.28 = bf16[64,2048]{1,0:T(8,128)(2,1)S(1)} collective-permute-done((bf16[64,2048]{1,0:T(8,128)(2,1)S(1)}, bf16[64,2048]{1,0:T(8,128)(2,1)S(1)}, u32[]{:S(2)}, u32[]{:S(2)}) %collective-permute-start.28) | collective-permute-done | bytes 262176 | tf_op jit(solution)/shard_map/ppermute | solution.py:728
  496.4 3.3 collective-permute-done.31
  504.4 5.7 %collective-permute-done.34 = bf16[2,64,1024]{2,1,0:T(8,128)(2,1)S(1)} collective-permute-done((bf16[2,64,1024]{2,1,0:T(8,128)(2,1)S(1)}, bf16[2,64,1024]{2,1,0:T(8,128)(2,1)S(1)}, u32[]{:S(2)}, u32[]{:S(2)}) %collective-permute-start.34) | collective-permute-done | bytes 262176 | tf_op jit(solution)/shard_map/ppermute | solution.py:728
  512.6 4.9 collective-permute-done.35
  (290 shorter events, 103.2 us)
Async XLA Ops:
  43.3 24.9 %collective-permute-start = (bf16[512,1024]{1,0:T(8,128)(2,1)}, bf16[512,1024]{1,0:T(8,128)(2,1)S(1)}, u32[]{:S(2)}, u32[]{:S(2)}) collective-permute-start(bf16[512,1024]{1,0:T(8,128)(2,1)} %get-tuple-element.207), channel_id=1, source_target_pairs={{0,16},{1,17},{2,18},{3,19},{4,20},{5,21},{6,22},{7,23},{8,24},{9,... | collective-permute-start | bytes 3145736 | tf_op jit(solution)/shard_map/ppermute | solution.py:765
  109.4 27.0 %collective-permute-start.1 = (bf16[512,1024]{1,0:T(8,128)(2,1)}, bf16[512,1024]{1,0:T(8,128)(2,1)S(1)}, u32[]{:S(2)}, u32[]{:S(2)}) collective-permute-start(bf16[512,1024]{1,0:T(8,128)(2,1)} %get-tuple-element.220), channel_id=1, source_target_pairs={{0,16},{1,17},{2,18},{3,19},{4,20},{5,21},{6,22},{7,23},{8,24},{9,... | collective-permute-start | bytes 3145736 | tf_op jit(solution)/shard_map/ppermute | solution.py:765
  115.6 64.1 %collective-permute-start.2 = (bf16[512,1024]{1,0:T(8,128)(2,1)}, bf16[512,1024]{1,0:T(8,128)(2,1)}, u32[]{:S(2)}, u32[]{:S(2)}) collective-permute-start(bf16[512,1024]{1,0:T(8,128)(2,1)} %get-tuple-element.233), channel_id=1, source_target_pairs={{16,0},{17,1},{18,2},{19,3},{20,4},{21,5},{22,6},{23,7},{24,8},{25... | collective-permute-start | bytes 3145736 | tf_op jit(solution)/shard_map/ppermute | solution.py:765
  221.7 43.5 %collective-permute-start.3 = (bf16[512,1024]{1,0:T(8,128)(2,1)}, bf16[512,1024]{1,0:T(8,128)(2,1)S(1)}, u32[]{:S(2)}, u32[]{:S(2)}) collective-permute-start(bf16[512,1024]{1,0:T(8,128)(2,1)} %get-tuple-element.246), channel_id=1, source_target_pairs={{16,0},{17,1},{18,2},{19,3},{20,4},{21,5},{22,6},{23,7},{24,8},{25... | collective-permute-start | bytes 3145736 | tf_op jit(solution)/shard_map/ppermute | solution.py:765
  277.0 14.2 %collective-permute-start.5 = (bf16[2048,512]{1,0:T(8,128)(2,1)}, bf16[2048,512]{1,0:T(8,128)(2,1)}, u32[]{:S(2)}, u32[]{:S(2)}) collective-permute-start(bf16[2048,512]{1,0:T(8,128)(2,1)} %get-tuple-element.249), channel_id=1, source_target_pairs={{0,1},{1,0},{2,3},{3,2},{4,5},{5,4},{6,7},{7,6},{8,9},{9,8},{10,11... | collective-permute-start | bytes 6291464 | tf_op jit(solution)/shard_map/ppermute | solution.py:728
  293.9 53.0 %collective-permute-start.6 = (bf16[2,2,256,512]{3,2,1,0:T(8,128)(2,1)}, bf16[2,2,256,512]{3,2,1,0:T(8,128)(2,1)}, u32[]{:S(2)}, u32[]{:S(2)}) collective-permute-start(bf16[2,2,256,512]{3,2,1,0:T(8,128)(2,1)} %fusion.1), channel_id=1, source_target_pairs={{0,4},{1,5},{2,6},{3,7},{4,0},{5,1},{6,2},{7,3},{8,12},{9,13},{10,... | collective-permute-start | bytes 3145736 | tf_op jit(solution)/shard_map/ppermute | solution.py:728
  298.2 51.2 %collective-permute-start.8 = (bf16[2,2,256,512]{3,2,0,1:T(8,128)(2,1)}, bf16[2,2,256,512]{3,2,0,1:T(8,128)(2,1)}, u32[]{:S(2)}, u32[]{:S(2)}) collective-permute-start(bf16[2,2,256,512]{3,2,0,1:T(8,128)(2,1)} %fusion.2), channel_id=1, source_target_pairs={{0,2},{1,3},{2,0},{3,1},{4,6},{5,7},{6,4},{7,5},{8,10},{9,11},{10,... | collective-permute-start | bytes 3145736 | tf_op jit(solution)/shard_map/ppermute | solution.py:728
  359.2 15.0 %collective-permute-start.10 = (bf16[512,2048]{1,0:T(8,128)(2,1)}, bf16[512,2048]{1,0:T(8,128)(2,1)}, u32[]{:S(2)}, u32[]{:S(2)}) collective-permute-start(bf16[512,2048]{1,0:T(8,128)(2,1)} %get-tuple-element.284), channel_id=1, source_target_pairs={{0,1},{1,0},{2,3},{3,2},{4,5},{5,4},{6,7},{7,6},{8,9},{9,8},{10,11... | collective-permute-start | bytes 6291464 | tf_op jit(solution)/shard_map/ppermute | solution.py:728
  359.4 25.8 %collective-permute-start.9 = (bf16[2,256,512]{2,1,0:T(8,128)(2,1)}, bf16[2,256,512]{2,1,0:T(8,128)(2,1)S(1)}, u32[]{:S(2)}, u32[]{:S(2)}) collective-permute-start(bf16[2,256,512]{2,1,0:T(8,128)(2,1)} %fusion.7), channel_id=1, source_target_pairs={{0,4},{1,5},{2,6},{3,7},{4,0},{5,1},{6,2},{7,3},{8,12},{9,13},{10,... | collective-permute-start | bytes 1572872 | tf_op jit(solution)/shard_map/ppermute | solution.py:728
  359.9 26.2 %collective-permute-start.7 = (bf16[2,256,512]{2,1,0:T(8,128)(2,1)}, bf16[2,256,512]{2,1,0:T(8,128)(2,1)S(1)}, u32[]{:S(2)}, u32[]{:S(2)}) collective-permute-start(bf16[2,256,512]{2,1,0:T(8,128)(2,1)} %fusion.6), channel_id=1, source_target_pairs={{0,8},{1,9},{2,10},{3,11},{4,12},{5,13},{6,14},{7,15},{8,0},{9,1},... | collective-permute-start | bytes 1572872 | tf_op jit(solution)/shard_map/ppermute | solution.py:728
  371.5 27.2 %collective-permute-start.15 = (bf16[512,2048]{1,0:T(8,128)(2,1)S(1)}, bf16[512,2048]{1,0:T(8,128)(2,1)}, u32[]{:S(2)}, u32[]{:S(2)}) collective-permute-start(bf16[512,2048]{1,0:T(8,128)(2,1)S(1)} %get-tuple-element.287), channel_id=1, source_target_pairs={{0,1},{1,0},{2,3},{3,2},{4,5},{5,4},{6,7},{7,6},{8,9},{9,8},{10,11... | collective-permute-start | bytes 6291464 | tf_op jit(solution)/shard_map/ppermute | solution.py:728
  376.9 35.8 %collective-permute-start.12 = (bf16[2,2,64,2048]{3,2,0,1:T(8,128)(2,1)}, bf16[2,2,64,2048]{3,2,0,1:T(8,128)(2,1)}, u32[]{:S(2)}, u32[]{:S(2)}) collective-permute-start(bf16[2,2,64,2048]{3,2,0,1:T(8,128)(2,1)} %fusion.3), channel_id=1, source_target_pairs={{0,2},{1,3},{2,0},{3,1},{4,6},{5,7},{6,4},{7,5},{8,10},{9,11},{10,... | collective-permute-start | bytes 3145736 | tf_op jit(solution)/shard_map/ppermute | solution.py:728
  386.1 34.0 %collective-permute-start.20 = (bf16[256,512]{1,0:T(8,128)(2,1)}, bf16[256,512]{1,0:T(8,128)(2,1)}, u32[]{:S(2)}, u32[]{:S(2)}) collective-permute-start(bf16[256,512]{1,0:T(8,128)(2,1)} %fusion.13), channel_id=1, source_target_pairs={{0,8},{1,9},{2,10},{3,11},{4,12},{5,13},{6,14},{7,15},{8,0},{9,1},... | collective-permute-start | bytes 786440 | tf_op jit(solution)/shard_map/ppermute | solution.py:728
  387.0 30.3 %collective-permute-start.21 = (bf16[256,512]{1,0:T(8,128)(2,1)}, bf16[256,512]{1,0:T(8,128)(2,1)}, u32[]{:S(2)}, u32[]{:S(2)}) collective-permute-start(bf16[256,512]{1,0:T(8,128)(2,1)} %fusion.14), channel_id=1, source_target_pairs={{0,2},{1,3},{2,0},{3,1},{4,6},{5,7},{6,4},{7,5},{8,10},{9,11},{10,... | collective-permute-start | bytes 786440 | tf_op jit(solution)/shard_map/ppermute | solution.py:728
  398.0 17.2 %collective-permute-start.11 = (bf16[512,2048]{1,0:T(8,128)(2,1)S(1)}, bf16[512,2048]{1,0:T(8,128)(2,1)S(1)}, u32[]{:S(2)}, u32[]{:S(2)}) collective-permute-start(bf16[512,2048]{1,0:T(8,128)(2,1)S(1)} %get-tuple-element.302), channel_id=1, source_target_pairs={{0,1},{1,0},{2,3},{3,2},{4,5},{5,4},{6,7},{7,6},{8,9},{9,8},{10,11... | collective-permute-start | bytes 6291464 | tf_op jit(solution)/shard_map/ppermute | solution.py:728
  398.7 13.1 %collective-permute-start.14 = (f32[2,2,2688]{2,1,0:T(2,128)S(1)}, f32[2,2,2688]{2,1,0:T(2,128)S(1)}, u32[]{:S(2)}, u32[]{:S(2)}) collective-permute-start(f32[2,2,2688]{2,1,0:T(2,128)S(1)} %bitcast.308), channel_id=1, source_target_pairs={{0,2},{1,3},{2,0},{3,1},{4,6},{5,7},{6,4},{7,5},{8,10},{9,11},{10,... | collective-permute-start | bytes 129032 | tf_op jit(solution)/shard_map/ppermute | solution.py:728
  411.9 26.8 %collective-permute-start.17 = (bf16[2,2,64,2048]{3,2,0,1:T(8,128)(2,1)S(1)}, bf16[2,2,64,2048]{3,2,0,1:T(8,128)(2,1)S(1)}, u32[]{:S(2)}, u32[]{:S(2)}) collective-permute-start(bf16[2,2,64,2048]{3,2,0,1:T(8,128)(2,1)S(1)} %copy-done.33), channel_id=1, source_target_pairs={{0,2},{1,3},{2,0},{3,1},{4,6},{5,7},{6,4},{7,5},{8,10},{9,11},{10,... | collective-permute-start | bytes 3145736 | tf_op jit(solution)/shard_map/ppermute | solution.py:728
  412.7 31.2 %collective-permute-start.25 = (bf16[512,1024]{1,0:T(8,128)(2,1)S(1)}, bf16[512,1024]{1,0:T(8,128)(2,1)S(1)}, u32[]{:S(2)}, u32[]{:S(2)}) collective-permute-start(bf16[512,1024]{1,0:T(8,128)(2,1)S(1)} %get-tuple-element.311), channel_id=1, source_target_pairs={{0,1},{1,0},{2,3},{3,2},{4,5},{5,4},{6,7},{7,6},{8,9},{9,8},{10,11... | collective-permute-start | bytes 3145736 | tf_op jit(solution)/shard_map/ppermute | solution.py:728
  415.3 33.9 %collective-permute-start.24 = (bf16[512,1024]{1,0:T(8,128)(2,1)S(1)}, bf16[512,1024]{1,0:T(8,128)(2,1)S(1)}, u32[]{:S(2)}, u32[]{:S(2)}) collective-permute-start(bf16[512,1024]{1,0:T(8,128)(2,1)S(1)} %get-tuple-element.314), channel_id=1, source_target_pairs={{0,1},{1,0},{2,3},{3,2},{4,5},{5,4},{6,7},{7,6},{8,9},{9,8},{10,11... | collective-permute-start | bytes 3145736 | tf_op jit(solution)/shard_map/ppermute | solution.py:728
  417.2 16.2 %collective-permute-start.18 = (bf16[2,64,2048]{2,1,0:T(8,128)(2,1)S(1)}, bf16[2,64,2048]{2,1,0:T(8,128)(2,1)S(1)}, u32[]{:S(2)}, u32[]{:S(2)}) collective-permute-start(bf16[2,64,2048]{2,1,0:T(8,128)(2,1)S(1)} %fusion.8), channel_id=1, source_target_pairs={{0,4},{1,5},{2,6},{3,7},{4,0},{5,1},{6,2},{7,3},{8,12},{9,13},{10,... | collective-permute-start | bytes 1572872 | tf_op jit(solution)/shard_map/ppermute | solution.py:728
  420.1 11.6 %collective-permute-start.19 = (f32[2,2688]{1,0:T(2,128)S(1)}, f32[2,2688]{1,0:T(2,128)S(1)}, u32[]{:S(2)}, u32[]{:S(2)}) collective-permute-start(f32[2,2688]{1,0:T(2,128)S(1)} %bitcast.309), channel_id=1, source_target_pairs={{0,4},{1,5},{2,6},{3,7},{4,0},{5,1},{6,2},{7,3},{8,12},{9,13},{10,... | collective-permute-start | bytes 64520 | tf_op jit(solution)/shard_map/ppermute | solution.py:728
  431.7 34.7 %collective-permute-start.16 = (bf16[2,2,64,2048]{3,2,0,1:T(8,128)(2,1)}, bf16[2,2,64,2048]{3,2,0,1:T(8,128)(2,1)}, u32[]{:S(2)}, u32[]{:S(2)}) collective-permute-start(bf16[2,2,64,2048]{3,2,0,1:T(8,128)(2,1)} %fusion.5), channel_id=1, source_target_pairs={{0,2},{1,3},{2,0},{3,1},{4,6},{5,7},{6,4},{7,5},{8,10},{9,11},{10,... | collective-permute-start | bytes 3145736 | tf_op jit(solution)/shard_map/ppermute | solution.py:728
  433.4 19.2 %collective-permute-start.23 = (f32[2688]{0:T(1024)S(1)}, f32[2688]{0:T(1024)S(1)}, u32[]{:S(2)}, u32[]{:S(2)}) collective-permute-start(f32[2688]{0:T(1024)S(1)} %get-tuple-element.424), channel_id=1, source_target_pairs={{0,8},{1,9},{2,10},{3,11},{4,12},{5,13},{6,14},{7,15},{8,0},{9,1},... | collective-permute-start | bytes 32264 | tf_op jit(solution)/shard_map/ppermute | solution.py:728
  438.7 30.7 %collective-permute-start.27 = (bf16[64,2048]{1,0:T(8,128)(2,1)}, bf16[64,2048]{1,0:T(8,128)(2,1)}, u32[]{:S(2)}, u32[]{:S(2)}) collective-permute-start(bf16[64,2048]{1,0:T(8,128)(2,1)} %fusion.15), channel_id=1, source_target_pairs={{0,8},{1,9},{2,10},{3,11},{4,12},{5,13},{6,14},{7,15},{8,0},{9,1},... | collective-permute-start | bytes 786440 | tf_op jit(solution)/shard_map/ppermute | solution.py:728
  443.9 19.4 %collective-permute-start.22 = (bf16[2,64,2048]{2,1,0:T(8,128)(2,1)}, bf16[2,64,2048]{2,1,0:T(8,128)(2,1)}, u32[]{:S(2)}, u32[]{:S(2)}) collective-permute-start(bf16[2,64,2048]{2,1,0:T(8,128)(2,1)} %fusion.9), channel_id=1, source_target_pairs={{0,4},{1,5},{2,6},{3,7},{4,0},{5,1},{6,2},{7,3},{8,12},{9,13},{10,... | collective-permute-start | bytes 1572872 | tf_op jit(solution)/shard_map/ppermute | solution.py:728
  449.2 36.5 %collective-permute-start.29 = (bf16[2,2,64,1024]{3,2,0,1:T(8,128)(2,1)}, bf16[2,2,64,1024]{3,2,0,1:T(8,128)(2,1)}, u32[]{:S(2)}, u32[]{:S(2)}) collective-permute-start(bf16[2,2,64,1024]{3,2,0,1:T(8,128)(2,1)} %fusion.10), channel_id=1, source_target_pairs={{0,2},{1,3},{2,0},{3,1},{4,6},{5,7},{6,4},{7,5},{8,10},{9,11},{10,... | collective-permute-start | bytes 1572872 | tf_op jit(solution)/shard_map/ppermute | solution.py:728
  458.7 41.2 %collective-permute-start.33 = (bf16[2,2,64,1024]{3,2,0,1:T(8,128)(2,1)}, bf16[2,2,64,1024]{3,2,0,1:T(8,128)(2,1)}, u32[]{:S(2)}, u32[]{:S(2)}) collective-permute-start(bf16[2,2,64,1024]{3,2,0,1:T(8,128)(2,1)} %fusion.11), channel_id=1, source_target_pairs={{0,2},{1,3},{2,0},{3,1},{4,6},{5,7},{6,4},{7,5},{8,10},{9,11},{10,... | collective-permute-start | bytes 1572872 | tf_op jit(solution)/shard_map/ppermute | solution.py:728
  464.5 19.9 %collective-permute-start.30 = (bf16[64,2048]{1,0:T(8,128)(2,1)S(1)}, bf16[64,2048]{1,0:T(8,128)(2,1)S(1)}, u32[]{:S(2)}, u32[]{:S(2)}) collective-permute-start(bf16[64,2048]{1,0:T(8,128)(2,1)S(1)} %fusion.16), channel_id=1, source_target_pairs={{0,8},{1,9},{2,10},{3,11},{4,12},{5,13},{6,14},{7,15},{8,0},{9,1},... | collective-permute-start | bytes 786440 | tf_op jit(solution)/shard_map/ppermute | solution.py:728
  468.9 14.5 %collective-permute-start.26 = (bf16[2,64,2048]{2,1,0:T(8,128)(2,1)S(1)}, bf16[2,64,2048]{2,1,0:T(8,128)(2,1)S(1)}, u32[]{:S(2)}, u32[]{:S(2)}) collective-permute-start(bf16[2,64,2048]{2,1,0:T(8,128)(2,1)S(1)} %fusion.12), channel_id=1, source_target_pairs={{0,4},{1,5},{2,6},{3,7},{4,0},{5,1},{6,2},{7,3},{8,12},{9,13},{10,... | collective-permute-start | bytes 1572872 | tf_op jit(solution)/shard_map/ppermute | solution.py:728
  483.6 12.6 %collective-permute-start.28 = (bf16[64,2048]{1,0:T(8,128)(2,1)S(1)}, bf16[64,2048]{1,0:T(8,128)(2,1)S(1)}, u32[]{:S(2)}, u32[]{:S(2)}) collective-permute-start(bf16[64,2048]{1,0:T(8,128)(2,1)S(1)} %fusion.17), channel_id=1, source_target_pairs={{0,8},{1,9},{2,10},{3,11},{4,12},{5,13},{6,14},{7,15},{8,0},{9,1},... | collective-permute-start | bytes 786440 | tf_op jit(solution)/shard_map/ppermute | solution.py:728
  487.9 11.8 %collective-permute-start.31 = (bf16[2,64,1024]{2,1,0:T(8,128)(2,1)S(1)}, bf16[2,64,1024]{2,1,0:T(8,128)(2,1)S(1)}, u32[]{:S(2)}, u32[]{:S(2)}) collective-permute-start(bf16[2,64,1024]{2,1,0:T(8,128)(2,1)S(1)} %fusion.18), channel_id=1, source_target_pairs={{0,4},{1,5},{2,6},{3,7},{4,0},{5,1},{6,2},{7,3},{8,12},{9,13},{10,... | collective-permute-start | bytes 786440 | tf_op jit(solution)/shard_map/ppermute | solution.py:728
  499.8 11.8 %collective-permute-start.32 = (bf16[64,1024]{1,0:T(8,128)(2,1)S(1)}, bf16[64,1024]{1,0:T(8,128)(2,1)S(1)}, u32[]{:S(2)}, u32[]{:S(2)}) collective-permute-start(bf16[64,1024]{1,0:T(8,128)(2,1)S(1)} %fusion.20), channel_id=1, source_target_pairs={{0,8},{1,9},{2,10},{3,11},{4,12},{5,13},{6,14},{7,15},{8,0},{9,1},... | collective-permute-start | bytes 393224 | tf_op jit(solution)/shard_map/ppermute | solution.py:728
  (50 other events, 342.4 us)

commit v3 on v2

--- a/solution.py
+++ b/solution.py
@@ -1,4 +1,5 @@
 import functools
+import itertools
 
 import jax
 import jax.numpy as jnp
@@ -18,6 +19,10 @@
 GROUP = 4 * HEAD
 TILE = 512
 WIDE = 1024
+VMEM = 62 * 2**20
+SMALL = 10**6
+LARGE = 10**11
+LESS = 40 * 2**20
 
 
 def nn(a, b):
@@ -328,22 +333,37 @@
             pltpu.SemaphoreType.DMA((hidden // WIDE,)),
             pltpu.SemaphoreType.DMA((hidden // WIDE,)),
         ],
-        compiler_params=pltpu.CompilerParams(vmem_limit_bytes=62 * 2**20),
-        cost_estimate=pl.CostEstimate(flops=14 * 10**9, bytes_accessed=50 * 10**6, transcendentals=6 * 10**6),
+        compiler_params=pltpu.CompilerParams(vmem_limit_bytes=VMEM),
+        cost_estimate=pl.CostEstimate(flops=LARGE, bytes_accessed=1, transcendentals=0),
         name="layer_forward",
     )(spans, norms, vectors, feat, recv, *weights, *stash)
     return results[0], results[1], results[2:]
 
 
-def backward_kernel(slot, plan, aliased, fed, *refs):
+BOTH, FIRST, SECOND = range(3)
+
+
+def backward_kernel(slot, plan, stage, aliased, given, *refs):
+    feeds, attends = stage != SECOND, stage != FIRST
     spans, norms, cot, recv, w_in, w_out, w_up, w_down = refs[:8]
     s_x, s_qkv, s_c, s_l, s_h, s_d, s_p = refs[8:15]
-    refs = refs[15 + aliased :]
-    dx_out, smalls = refs[:2]
-    g_up, g_mid, g_qkv, inputs = refs[2:6]
-    if fed:
-        g_feed = refs[6]
-    refs = refs[6 + fed :]
+    if stage == SECOND:
+        mid_in, middle_in = refs[15:17]
+    refs = refs[15 + given + aliased :]
+    smalls = refs[0]
+    refs = refs[1:]
+    if feeds:
+        g_up, g_mid = refs[:2]
+        refs = refs[2:]
+    if attends:
+        dx_out, g_qkv, inputs = refs[:3]
+        refs = refs[3:]
+    if stage == BOTH:
+        g_feed = refs[0]
+        refs = refs[1:]
+    if stage == FIRST:
+        middle_out = refs[0]
+        refs = refs[1:]
     (v_in, v_out, v_up, v_down, v_x, v_dy, v_qkv, v_c, v_l, v_h, v_d, v_p, v_du, v_do, v_dc, v_dqkv, v_acc,
      v_s, v_k, v_dx, sem_w, sem_x, sem_d, sem_p, sem_o) = refs
     rows, width = v_x.shape
@@ -360,14 +380,18 @@
     @pl.when(active)
     def _():
         length = spans[picked, 0]
-
-        @pl.when(jnp.logical_not(first))
-        def _():
-            pltpu.make_async_copy(cot.at[picked, 0], v_dy, sem_x.at[0]).start()
-
-        @pl.when(first)
-        def _():
-            pltpu.make_async_copy(recv, v_dy, sem_x.at[0]).start()
+        if stage != BOTH:
+            smalls[...] = jnp.zeros_like(smalls)
+
+        if feeds:
+
+            @pl.when(jnp.logical_not(first))
+            def _():
+                pltpu.make_async_copy(cot.at[picked, 0], v_dy, sem_x.at[0]).start()
+
+            @pl.when(first)
+            def _():
+                pltpu.make_async_copy(recv, v_dy, sem_x.at[0]).start()
 
         def down_copy(i):
             return pltpu.make_async_copy(
@@ -400,19 +424,28 @@
             ],
             sem_x.at[pl.ds(1, 7)],
         )
-        d_copy(0).start()
-        for i in range(tiles):
-            down_copy(i).start()
-            up_copy(i).start()
-            if i == 0:
-                d_copy(1).start()
-        for k in (4, 5, 1, 2, 3):
-            loads[k].start()
-        p_copy(0).start()
-        p_copy(1).start()
-        loads[6].start()
-        loads[0].start()
-        pltpu.make_async_copy(recv, v_dy, sem_x.at[0]).wait()
+        if feeds:
+            d_copy(0).start()
+            for i in range(tiles):
+                down_copy(i).start()
+                up_copy(i).start()
+                if i == 0:
+                    d_copy(1).start()
+            loads[4].start()
+        if stage == SECOND:
+            entries = [
+                pltpu.make_async_copy(mid_in.at[here], v_do, sem_o.at[0]),
+                pltpu.make_async_copy(middle_in, v_acc, sem_o.at[3]),
+            ]
+            for copy in entries:
+                copy.start()
+        if attends:
+            for k in (5, 1, 2, 3):
+                loads[k].start()
+            p_copy(0).start()
+            p_copy(1).start()
+            loads[6].start()
+            loads[0].start()
         nothing = jnp.zeros((8, width), f32)
 
         def fold(values):
@@ -426,9 +459,11 @@
             v_acc[at, :] = jnp.zeros((64, width), f32)
             return total + fold(masked)
 
-        total = lax.fori_loop(0, rows // 64, enter, nothing)
-        smalls[7:8, :] = jnp.sum(total, axis=0, keepdims=True)
-        if fed:
+        if feeds:
+            pltpu.make_async_copy(recv, v_dy, sem_x.at[0]).wait()
+            total = lax.fori_loop(0, rows // 64, enter, nothing)
+            smalls[7:8, :] = jnp.sum(total, axis=0, keepdims=True)
+        if stage == BOTH:
             feed_copy = pltpu.make_async_copy(v_dy, g_feed.at[here], sem_o.at[4])
             feed_copy.start()
 
@@ -451,9 +486,9 @@
             def _():
                 d_copy(i + 2).start()
 
-        loop(tiles, feed)
-        loads[4].wait()
-        loads[5].wait()
+        if feeds:
+            loop(tiles, feed)
+            loads[4].wait()
 
         def norm_back(source, grad, gain):
             normed, inverse = row_stats(source)
@@ -471,14 +506,23 @@
             v_do[at, :] = low
             return carry[0] + one, carry[1] + two, carry[2] + fold(low.astype(f32))
 
-        sums = lax.fori_loop(0, rows // 64, second_norm, (nothing,) * 3)
-        for k, value in zip((2, 3, 6), sums):
-            smalls[k : k + 1, :] = jnp.sum(value, axis=0, keepdims=True)
-        do_copy = pltpu.make_async_copy(v_do, g_mid.at[here], sem_o.at[0])
-        do_copy.start()
-        v_dc[...] = nt(v_do[...], v_out[...]).astype(bf16)
-        for k in (1, 2, 3):
-            loads[k].wait()
+        if feeds:
+            sums = lax.fori_loop(0, rows // 64, second_norm, (nothing,) * 3)
+            for k, value in zip((2, 3, 6), sums):
+                smalls[k : k + 1, :] = jnp.sum(value, axis=0, keepdims=True)
+            outs = [pltpu.make_async_copy(v_do, g_mid.at[here], sem_o.at[0])]
+            if stage == FIRST:
+                outs.append(pltpu.make_async_copy(v_acc, middle_out, sem_o.at[1]))
+            for copy in outs:
+                copy.start()
+        if stage == SECOND:
+            for copy in entries:
+                copy.wait()
+        if attends:
+            loads[5].wait()
+            v_dc[...] = nt(v_do[...], v_out[...]).astype(bf16)
+            for k in (1, 2, 3):
+                loads[k].wait()
         lane = lax.broadcasted_iota(jnp.int32, (1, GROUP), 1) // HEAD
 
         def attend(i):
@@ -519,16 +563,18 @@
             def _():
                 p_copy(i + 2).start()
 
-        loop(width // GROUP, attend)
-        qkv_copy = pltpu.make_async_copy(v_dqkv, g_qkv.at[here], sem_o.at[1])
-        qkv_copy.start()
-        loads[6].wait()
-        loads[0].wait()
-        def enter_grad(i):
-            at = part(i, TILE)
-            v_h[:, at] = nt(v_dqkv[...], v_in[at, :])
-
-        loop(width // TILE, enter_grad)
+        if attends:
+            loop(width // GROUP, attend)
+            qkv_copy = pltpu.make_async_copy(v_dqkv, g_qkv.at[here], sem_o.at[1])
+            qkv_copy.start()
+            loads[6].wait()
+            loads[0].wait()
+
+            def enter_grad(i):
+                at = part(i, TILE)
+                v_h[:, at] = nt(v_dqkv[...], v_in[at, :])
+
+            loop(width // TILE, enter_grad)
 
         def first_norm(i, carry):
             at = part(i, 64)
@@ -536,44 +582,55 @@
             v_dx[at, :] = (rows_back + v_acc[at, :]).astype(bf16)
             return carry[0] + one, carry[1] + two
 
-        sums = lax.fori_loop(0, rows // 64, first_norm, (nothing,) * 2)
-        for k, value in enumerate(sums):
-            smalls[k : k + 1, :] = jnp.sum(value, axis=0, keepdims=True)
-        dx_copy = pltpu.make_async_copy(v_dx, dx_out, sem_o.at[2])
-        dx_copy.start()
-        input_copy = pltpu.make_async_copy(v_dx, inputs.at[0, picked, 0], sem_o.at[5])
-        input_copy.start()
-        for copy in (do_copy, qkv_copy, dx_copy, input_copy):
-            copy.wait()
-        if fed:
+        if attends:
+            sums = lax.fori_loop(0, rows // 64, first_norm, (nothing,) * 2)
+            for k, value in enumerate(sums):
+                smalls[k : k + 1, :] = jnp.sum(value, axis=0, keepdims=True)
+            dx_copy = pltpu.make_async_copy(v_dx, dx_out, sem_o.at[2])
+            dx_copy.start()
+            input_copy = pltpu.make_async_copy(v_dx, inputs.at[0, picked, 0], sem_o.at[5])
+            input_copy.start()
+            for copy in (qkv_copy, dx_copy, input_copy):
+                copy.wait()
+        if stage == BOTH:
             feed_copy.wait()
-        pltpu.make_async_copy(v_du, g_up.at[here], sem_o.at[3]).wait()
+        if feeds:
+            for copy in outs:
+                copy.wait()
+            pltpu.make_async_copy(v_du, g_up.at[here], sem_o.at[3]).wait()
 
     @pl.when(jnp.logical_not(active))
     def _():
         smalls[...] = jnp.zeros_like(smalls)
 
 
-def backward_call(slot, plan, spans, norms, cot, recv, weights, stash, grads=(), fed=True):
+def backward_call(slot, plan, stage, spans, norms, cot, recv, weights, stash, given, grads):
     rows, width = recv.shape
     hidden = weights[2].shape[1]
     any_ = pl.BlockSpec(memory_space=pl.ANY)
     vm = pl.BlockSpec(memory_space=pltpu.VMEM)
-    shapes = [jax.ShapeDtypeStruct((2 * rows, n), bf16) for n in (hidden, width, 3 * width)]
-    shapes.append(jax.ShapeDtypeStruct((1, 2, 1, rows, width), bf16))
-    if fed:
-        shapes.append(jax.ShapeDtypeStruct((2 * rows, width), bf16))
+    shape = jax.ShapeDtypeStruct
+    outs = {"smalls": shape((8 + hidden // WIDE, width), f32)}
+    if stage != SECOND:
+        outs["up"] = shape((2 * rows, hidden), bf16)
+        outs["mid"] = shape((2 * rows, width), bf16)
+    if stage != FIRST:
+        outs["dx"] = shape((rows, width), bf16)
+        outs["qkv"] = shape((2 * rows, 3 * width), bf16)
+        outs["inputs"] = shape((1, 2, 1, rows, width), bf16)
+    if stage == BOTH:
+        outs["feed"] = shape((2 * rows, width), bf16)
+    if stage == FIRST:
+        outs["middle"] = shape((rows, width), f32)
+    names = list(outs)
+    kept = [name for name in names if name in grads and name not in ("smalls", "dx")]
     s_x, s_a, s_qkv, s_c, s_l, s_h, s_b, s_g, s_d, s_p, _ = stash
-    grads = grads[: len(shapes)]
     results = pl.pallas_call(
-        functools.partial(backward_kernel, slot, plan, len(grads), int(fed)),
-        in_specs=[pl.BlockSpec(memory_space=pltpu.SMEM), vm] + [any_] * (13 + len(grads)),
-        out_specs=[any_, vm] + [any_] * len(shapes),
-        out_shape=[
-            jax.ShapeDtypeStruct((rows, width), bf16),
-            jax.ShapeDtypeStruct((8 + hidden // WIDE, width), f32),
-        ] + shapes,
-        input_output_aliases={15 + k: 2 + k for k in range(len(grads))},
+        functools.partial(backward_kernel, slot, plan, stage, len(kept), len(given)),
+        in_specs=[pl.BlockSpec(memory_space=pltpu.SMEM), vm] + [any_] * (13 + len(given) + len(kept)),
+        out_specs=[vm] + [any_] * (len(names) - 1),
+        out_shape=list(outs.values()),
+        input_output_aliases={15 + len(given) + k: names.index(n) for k, n in enumerate(kept)},
         scratch_shapes=[pltpu.VMEM(w.shape, bf16) for w in weights] + [
             pltpu.VMEM((rows, width), bf16),
             pltpu.VMEM((rows, width), bf16),
@@ -597,76 +654,203 @@
             pltpu.SemaphoreType.DMA((2,)),
             pltpu.SemaphoreType.DMA((6,)),
         ],
-        compiler_params=pltpu.CompilerParams(vmem_limit_bytes=62 * 2**20),
-        cost_estimate=pl.CostEstimate(flops=18 * 10**9, bytes_accessed=60 * 10**6, transcendentals=0),
+        compiler_params=pltpu.CompilerParams(vmem_limit_bytes=VMEM),
+        cost_estimate=pl.CostEstimate(flops=LARGE, bytes_accessed=1, transcendentals=0),
         name="layer_backward",
-    )(spans, norms, cot, recv, *weights, s_x, s_qkv, s_c, s_l, s_h, s_d, s_p, *grads)
-    return results[0], results[1], results[2:]
-
-
-def turned_blocks(source, target, block):
-    half = target.shape[0] // 2
-    flat = source[...].T
-    for core in range(2):
-
-        @pl.when(lax.axis_index("dp") % 2 == core)
-        def _(core=core):
-            for k in range(half // block):
-                other = (2 * k + 1 - core) * block
-                own = (2 * k + core) * block
-                target[k * block : (k + 1) * block, :] = flat[other : other + block]
-                target[half + k * block : half + (k + 1) * block, :] = flat[own : own + block]
-
-
-def weight_kernel(block, left, right, theirs, mine, turned):
-    half = left.shape[1] // 2
-
-    @pl.when(pl.program_id(1) == 0)
-    def _():
-        turned_blocks(left, turned, block)
-
-    theirs[...] = nn(turned[:half, :], right[...]).astype(bf16)
-    mine[...] = nn(turned[half:, :], right[...]).astype(bf16)
-
-
-def feed_weight_kernel(block, left, right, late, theirs, mine, turned):
-    half = left.shape[1] // 2
-    rows = late.shape[0]
-    turned_blocks(left, turned, block)
-    second = jnp.where(lax.axis_index("section") == 0, late[...], right[rows:, :])
-    for at, out in ((slice(0, half), theirs), (slice(half, 2 * half), mine)):
-        out[...] = (nn(turned[at, :rows], right[:rows, :]) + nn(turned[at, rows:], second)).astype(bf16)
-
-
-def weight_call(left, right, start, columns, late=None):
-    rows, height = left.shape
-    tall = min(height, WIDE)
+    )(
+        spans, norms, cot, recv, *weights, s_x, s_qkv, s_c, s_l, s_h, s_d, s_p, *given,
+        *[grads[name] for name in kept],
+    )
+    return {**grads, **dict(zip(names, results))}
+
+
+def turn_kernel(blocks, *refs):
+    count = len(blocks)
+    for k, block in enumerate(blocks):
+        source, target = refs[k], refs[count + k]
+
+        @pl.when((pl.program_id(0) == k) if k + 1 < count else (pl.program_id(0) >= k))
+        def _(source=source, target=target, block=block):
+            flat = source[...].T
+            pairs = flat.shape[0] // (2 * block)
+            for core in range(2):
+
+                @pl.when(lax.axis_index("dp") % 2 == core)
+                def _(core=core):
+                    for j in range(pairs):
+                        at = slice(j * block, (j + 1) * block)
+                        other = (2 * j + 1 - core) * block
+                        own = (2 * j + core) * block
+                        target[0, at, :] = flat[other : other + block]
+                        target[1, at, :] = flat[own : own + block]
+
+
+def turn_call(sources):
+    rows = sources[0].shape[0]
+    count = len(sources)
+    size = lax.axis_size("dp")
+    steps = count - 1 + sources[-1].shape[1] // WIDE
+
+    def last(i):
+        return jnp.maximum(i - (count - 1), 0)
+
+    ins = [pl.BlockSpec((rows, WIDE), lambda i: (0, 0))] * (count - 1)
+    ins.append(pl.BlockSpec((rows, WIDE), lambda i: (0, last(i))))
+    outs = [pl.BlockSpec((2, WIDE // 2, rows), lambda i: (0, 0, 0))] * (count - 1)
+    outs.append(pl.BlockSpec((2, WIDE // 2, rows), lambda i: (0, last(i), 0)))
+    return pl.pallas_call(
+        functools.partial(turn_kernel, [s.shape[1] // size for s in sources]),
+        grid=(steps,),
+        in_specs=ins,
+        out_specs=outs,
+        out_shape=[jax.ShapeDtypeStruct((2, s.shape[1] // 2, rows), bf16) for s in sources],
+        compiler_params=pltpu.CompilerParams(vmem_limit_bytes=VMEM),
+        cost_estimate=pl.CostEstimate(flops=1, bytes_accessed=1, transcendentals=0),
+        name="turn",
+    )(*sources)
+
+
+def weight_kernel(widths, half, left, right, *rest):
+    late, outs = rest[: -len(widths)], rest[-len(widths) :]
+    if late:
+        rows = late[0].shape[0]
+        second = jnp.where(lax.axis_index("section") == 0, late[0][...], right[rows:, :])
+        total = nn(left[0, :, :rows], right[:rows, :]) + nn(left[0, :, rows:], second)
+    else:
+        total = nn(left[0], right[...])
+    total = total.astype(bf16)
+    at = 0
+    for width, out in zip(widths, outs):
+        step, offset = divmod(at, right.shape[1])
+        if len(widths) == 1:
+            out[...] = total
+        else:
+
+            @pl.when(pl.program_id(1) == step)
+            def _(out=out, cut=slice(offset, offset + width)):
+                out[...] = total[:, cut]
+
+        at += width
+
+
+def weight_call(left, right, start, widths, half, late=None):
+    _, height, rows = left.shape
+    columns = sum(widths)
+    tall = min(height, 512)
     wide = min(columns, WIDE)
-    block = height // lax.axis_size("dp")
-    shape = jax.ShapeDtypeStruct((height // 2, columns), bf16)
     specs = [
-        pl.BlockSpec((rows, tall), lambda i, j: (0, i)),
+        pl.BlockSpec((1, tall, rows), lambda i, j: (half, i, 0)),
         pl.BlockSpec((rows, wide), lambda i, j: (0, start // wide + j)),
     ]
     operands = (left, right)
     if late is not None:
-        assert wide == columns
-        specs.append(pl.BlockSpec((rows // 2, wide), lambda i, j: (0, start // wide + j)))
+        specs.append(pl.BlockSpec((rows // 2, wide), lambda i, j: (0, j)))
         operands += (late,)
+
+    def out(width):
+        if width > wide:
+            return pl.BlockSpec((tall, wide), lambda i, j: (i, j))
+        return pl.BlockSpec((tall, width), lambda i, j: (i, 0))
+
     return pl.pallas_call(
-        functools.partial(weight_kernel if late is None else feed_weight_kernel, block),
+        functools.partial(weight_kernel, widths, half),
         grid=(height // tall, columns // wide),
         in_specs=specs,
-        out_specs=[pl.BlockSpec((tall // 2, wide), lambda i, j: (i, j))] * 2,
-        out_shape=[shape] * 2,
-        scratch_shapes=[pltpu.VMEM((tall, rows), bf16)],
-        compiler_params=pltpu.CompilerParams(vmem_limit_bytes=40 * 2**20),
-        cost_estimate=pl.CostEstimate(
-            flops=2 * rows * height * columns,
-            bytes_accessed=2 * (rows * height + rows * columns + height * columns),
-            transcendentals=0,
-        ),
+        out_specs=[out(width) for width in widths],
+        out_shape=[jax.ShapeDtypeStruct((height, width), bf16) for width in widths],
+        compiler_params=pltpu.CompilerParams(vmem_limit_bytes=VMEM),
+        cost_estimate=pl.CostEstimate(flops=1, bytes_accessed=1, transcendentals=0),
         name="weight_product",
+    )(*operands)
+
+
+def sum_kernel(layout, lefts, fixed, free, place, *refs):
+    count = sum(len(arrays) for arrays in layout)
+    sources = iter(refs[:count])
+    terms = [[next(sources) for _ in arrays] for arrays in layout]
+    out, held, total, sem, out_sem = refs[-5:]
+    me = lax.axis_index("dp")
+    cells = list(itertools.product(range(2), repeat=len(free)))
+    loads, slot = [], 0
+    for cell in cells:
+        loads.append([])
+        for arrays, left, widths in zip(terms, lefts, layout):
+            index = []
+            for bit in left:
+                if bit in free:
+                    index.append(cell[free.index(bit)])
+                else:
+                    own = (me >> bit) & 1
+                    index.append(own if fixed[bit] else 1 - own)
+            at = 0
+            for ref, (start, width) in zip(arrays, widths):
+                copy = pltpu.make_async_copy(
+                    ref.at[(*index, slice(None), pl.ds(start, width))],
+                    held.at[slot, :, pl.ds(at, width)],
+                    sem.at[len(loads[-1]), len(loads) - 1],
+                )
+                copy.start()
+                loads[-1].append(copy)
+                at += width
+            slot += 1
+    stores = []
+    for k, cell in enumerate(cells):
+        for copy in loads[k]:
+            copy.wait()
+        value = added([held[k * len(terms) + j] for j in range(len(terms))])
+        total[k] = value.astype(total.dtype)
+        stores.append(pltpu.make_async_copy(total.at[k], place(out, cell), out_sem.at[k]))
+        stores[-1].start()
+    for copy in stores:
+        copy.wait()
+
+
+def sum_call(terms, fixed, kind, into=None, start=0):
+    rows = terms[0][0][0][0].shape[-2]
+    layout = [[(at, width) for _, at, width in arrays] for arrays, _ in terms]
+    lefts = [left for _, left in terms]
+    columns = sum(width for _, width in layout[0])
+    free = [bit for bit in lefts[0] if bit not in fixed]
+    operands = [array for arrays, _ in terms for array, _, _ in arrays]
+    cells = 2 ** len(free)
+    aliases = {}
+    wide = 0
+    if into is None:
+        shape = jax.ShapeDtypeStruct((2,) * len(free) + (rows, columns), kind)
+    else:
+        wide, into = into
+        shape = jax.ShapeDtypeStruct((1, rows, wide), kind)
+        if into is not None:
+            aliases = {len(operands): 0}
+            operands.append(into)
+
+    given = len(operands)
+
+    def place(out, cell):
+        if wide:
+            return out.at[0, :, pl.ds(start, columns)]
+        return out.at[cell] if cell else out
+
+    def kernel(*refs):
+        refs = refs[: given - len(aliases)] + refs[given:]
+        sum_kernel(layout, lefts, fixed, free, place, *refs)
+
+    any_ = pl.BlockSpec(memory_space=pl.ANY)
+    return pl.pallas_call(
+        kernel,
+        in_specs=[any_] * len(operands),
+        out_specs=any_,
+        out_shape=shape,
+        input_output_aliases=aliases,
+        scratch_shapes=[
+            pltpu.VMEM((cells * len(terms), rows, columns), terms[0][0][0][0].dtype),
+            pltpu.VMEM((cells, rows, columns), kind),
+            pltpu.SemaphoreType.DMA((max(sum(len(arrays) for arrays, _ in terms), 1), cells)),
+            pltpu.SemaphoreType.DMA((cells,)),
+        ],
+        compiler_params=pltpu.CompilerParams(vmem_limit_bytes=VMEM),
+        cost_estimate=pl.CostEstimate(flops=SMALL, bytes_accessed=1, transcendentals=0),
+        name="sum_terms",
     )(*operands)
 
 
@@ -680,10 +864,6 @@
     return total
 
 
-def pick(array, axis, index):
-    return lax.dynamic_index_in_dim(array, index, axis, keepdims=False)
-
-
 class Line:
     def __init__(self):
         self.last = None
@@ -700,44 +880,86 @@
 class Exchange:
     def __init__(self, line, terms, left, order):
         self.line = line
-        self.terms = terms
-        self.left = sorted(left, reverse=True)
+        self.terms = [(arrays, sorted(left, reverse=True)) for arrays in terms]
+        self.fixed = {}
         self.order = list(order)
-        self.kind = terms[0].dtype
+        self.kind = terms[0][0][0].dtype
+
+    def total(self, fixed, kind, **where):
+        values = iter(self.line.after([array for arrays, _ in self.terms for array, _, _ in arrays]))
+        self.terms = [
+            ([(next(values), at, width) for _, at, width in arrays], left)
+            for arrays, left in self.terms
+        ]
+        total = sum_call(self.terms, fixed, kind, **where)
+        self.line.done(total)
+        return total
 
     def step(self):
         bit = self.order.pop(0)
-        axis = self.left.index(bit)
-        self.left.pop(axis)
-        mine = (lax.axis_index("dp") >> bit) & 1
-        self.terms = self.line.after(self.terms)
-        theirs = added([pick(term, axis, 1 - mine) for term in self.terms]).astype(self.kind)
-        self.line.done(theirs)
-        self.terms = [pick(term, axis, mine) for term in self.terms] + [crossed(theirs, bit)]
-
-    def finish(self):
+        theirs = self.total({**self.fixed, bit: False}, self.kind)
+        self.fixed[bit] = True
+        left = [k for k in self.terms[0][1] if k not in self.fixed]
+        self.terms.append((whole(crossed(theirs, bit)), left))
+
+    def cut(self, widths):
+        parts = []
+        low = 0
+        for width in widths:
+            high = low + width
+            terms = []
+            for arrays, left in self.terms:
+                chosen, at = [], 0
+                for array, start, columns in arrays:
+                    a, b = max(low, at), min(high, at + columns)
+                    if a < b:
+                        chosen.append((array, start + a - at, b - a))
+                    at += columns
+                terms.append((chosen, left))
+            part_ = Exchange(self.line, [terms[0][0]], (), self.order)
+            part_.terms = terms
+            part_.fixed = dict(self.fixed)
+            parts.append(part_)
+            low = high
+        return parts
+
+    def finish(self, **where):
         while self.order:
             self.step()
-        self.terms = self.line.after(self.terms)
-        total = added(self.terms)
-        self.line.done(total)
-        return total
+        return self.total(self.fixed, f32, **where)
 
 
 def crossed(value, bit):
     return lax.ppermute(value, "dp", [(i, i ^ (1 << bit)) for i in range(lax.axis_size("dp"))])
 
 
-def weight_sum(line, left, right, start, columns, order, late=None):
-    left, right = line.after((left, right))
-    theirs, mine = weight_call(left, right, start, columns, late)
-    line.done(theirs)
-    size = lax.axis_size("dp")
-    bits = size.bit_length() - 1
-    shape = [2] * (bits - 1) + [left.shape[1] // size, columns]
-    received = crossed(theirs, 0)
-    terms = [half.reshape(shape) for half in (mine, received)]
-    return Exchange(line, terms, range(1, bits), order)
+def whole(array):
+    return [(array, 0, array.shape[-1])]
+
+
+def whole(array):
+    return [(array, 0, array.shape[-1])]
+
+
+class WeightSum(Exchange):
+    def __init__(self, line, left, right, start, widths, order, late=None):
+        size = lax.axis_size("dp")
+        bits = size.bit_length() - 1
+        shape = [2] * (bits - 1) + [2 * left.shape[1] // size, -1]
+        left, right = line.after((left, right))
+        theirs = weight_call(left, right, start, widths, 0, late)
+        line.done(theirs[-1])
+        received = [whole(crossed(array, 0).reshape(shape)) for array in theirs]
+        self.product = (left, right, start, [sum(widths)], 1, late)
+        self.shape = shape
+        super().__init__(line, (sum(received, []),), range(1, bits), order)
+
+    def own(self):
+        left, right = self.line.after(self.product[:2])
+        (mine,) = weight_call(left, right, *self.product[2:])
+        self.line.done(mine)
+        self.terms.append((whole(mine.reshape(self.shape)), self.terms[0][1]))
+        return self
 
 
 def shards(
@@ -769,9 +991,9 @@
     def forward(slot, plan, norms, recv, stash=()):
         return forward_call(slot, plan, lengths, norms, vectors, features, recv, weights, stash)
 
-    def backward(slot, plan, norms, recv, stash, grads=(), fed=True):
+    def backward(slot, plan, stage, norms, recv, stash, grads, given=()):
         return backward_call(
-            slot, plan, lengths, norms, cotangent, recv, weights, stash, grads, fed
+            slot, plan, stage, lengths, norms, cotangent, recv, weights, stash, given, grads
         )
 
     z_one, squares_one, stash = forward(0, (0, None), vectors, nowhere)
@@ -788,89 +1010,96 @@
     norms_one, norms_two = norms[:1], norms[1:]
     z_two, squares_two, stash = forward(1, (1, 0), norms_one, received_one, stash)
     received_two = send(z_two, 1)
-    dx_one, smalls_one, grads = backward(1, (None, 0), norms_one, nowhere, stash)
-    back_one = send(dx_one, 0)
+    grads = backward(1, (None, 0), BOTH, norms_one, nowhere, stash, {})
+    smalls_one = grads["smalls"]
+    back_one = send(grads["dx"], 0)
     z_three, squares_three, stash = forward(0, (None, 1), norms_two, received_two, stash)
-    dx_two, smalls_two, grads = backward(0, (0, 1), norms_two, back_one, stash, grads)
-    back_two = send(dx_two, 0)
+    grads = backward(0, (0, 1), BOTH, norms_two, back_one, stash, grads)
+    smalls_two = grads["smalls"]
+    back_two = send(grads["dx"], 0)
 
     s_x, s_a, s_qkv, s_c, s_l, s_h, s_b, s_g, s_d, s_p, layer_outputs = stash
     side_first = list(range(1, bits))
     line_first = side_first[1:] + side_first[:1]
     line = Line()
-    half = width // 2
-    g_feed = grads[4]
-    down_one = weight_sum(line, s_g, g_feed, 0, half, line_first, back_two)
-    down_two = weight_sum(line, s_g, g_feed, half, half, side_first, back_two)
-    down_one.step()
-    down_two.step()
+    line.done(smalls_two)
+    squares = jnp.sum(squares_one + squares_two + squares_three, axis=(1, 2))
+    counted = jnp.sum(lengths).astype(f32)
+    (totals,) = line.after((jnp.concatenate([squares, counted[None], jnp.zeros((123,), f32)]),))
+    for bit in range(bits):
+        totals = totals + crossed(totals, bit)
+    t_a, t_b, t_c, t_g = turn_call(line.after((s_a, s_b, s_c, s_g)))
+    line.done(t_a)
+    (totals,) = line.after((totals,))
+    line.done(totals)
+    down = WeightSum(line, t_g, grads["feed"], 0, [width], side_first, back_two).own()
+    down.step()
     (back_two,) = line.after((back_two,))
-    _, smalls_three, grads = backward(
-        1, (1, None), vectors, back_two, stash, grads[:4], fed=False
+    grads = backward(1, (1, None), FIRST, vectors, back_two, stash, grads)
+    smalls_three = grads["smalls"]
+    line.done(smalls_three)
+    up = WeightSum(line, t_b, grads["up"], 0, [WIDE] * (hidden // WIDE), side_first).own()
+    up.step()
+    down.step()
+    out = WeightSum(line, t_c, grads["mid"], 0, [width], side_first).own()
+    (middle,) = line.after((grads["middle"],))
+    grads = backward(
+        1, (1, None), SECOND, vectors, back_two, stash, grads, (grads["mid"], middle)
     )
-    line.done(smalls_three)
-    g_up, g_mid, g_qkv, input_grads = grads
-    down_one.step()
-    down_two.step()
-    up_one = weight_sum(line, s_b, g_up, 0, hidden // 2, side_first)
-    up_two = weight_sum(line, s_b, g_up, hidden // 2, hidden // 2, side_first)
-    up_one.step()
-    down_two.step()
-    down_one.step()
-
-    smalls = smalls_one + smalls_two + smalls_three
+    smalls_four = grads["smalls"]
+    line.done(smalls_four)
+    g_qkv, input_grads = grads["qkv"], grads["inputs"]
+    down.step()
+    into_one = WeightSum(line, t_a, g_qkv, 0, [width] * 3, side_first).own()
+
+    smalls = smalls_one + smalls_two + smalls_three + smalls_four
     table_grad = one_hot[0][:, None] * smalls_one[:4].reshape(1, -1) + one_hot[1][:, None] * (
         smalls_two[:4].reshape(1, -1) * adaptive
     )
     codes = table_grad.shape[0]
     share = table_grad.shape[1] // (2 * size)
     table_blocks = table_grad.reshape(codes, 2, size, share).transpose(2, 1, 0, 3)
-    squares = jnp.sum(squares_one + squares_two + squares_three, axis=(1, 2))
-    counted = jnp.sum(lengths).astype(f32)
-    totals = jnp.concatenate([squares, counted[None], jnp.zeros((123,), f32)])
-    packed = jnp.concatenate(
-        [
-            smalls.reshape(size, -1),
-            table_blocks.reshape(size, -1),
-            jnp.broadcast_to(totals[None], (size, 128)),
-        ],
-        axis=1,
-    )
-    small = Exchange(
-        line, [packed.reshape([2] * bits + [packed.shape[1]])], range(bits), range(bits)
-    )
-    small.step()
-    in_one = weight_sum(line, s_a, g_qkv, 0, 2 * width, side_first)
-    small.step()
-    up_two.step()
-    in_two = weight_sum(line, s_a, g_qkv, 2 * width, width, side_first)
-    out_one = weight_sum(line, s_c, g_mid, 0, width, side_first)
-    small.step()
-    up_one.step()
-    in_one.step()
-    down_sum = [down_one.finish(), down_two.finish()]
-    small.step()
+    packed = jnp.concatenate([smalls.reshape(size, -1), table_blocks.reshape(size, -1)], axis=1)
+    count = packed.shape[1]
+    block = width // size
+    packed = jnp.pad(packed.reshape(size, block, -1), ((0, 0), (0, 0), (0, 128 - count // block)))
+    packed = packed.astype(bf16).reshape([2] * bits + [block, 128])
+    core = lax.axis_index("dp") & 1
+    (other, own) = [
+        lax.dynamic_index_in_dim(packed, which, bits - 1, keepdims=False)
+        for which in (1 - core, core)
+    ]
+    other = crossed(other, 0)
+    into_one, into_two = into_one.cut([2 * width, width])
+    up_one, up_two = up.cut([hidden // 2] * 2)
+    into_two.terms = [
+        (arrays + whole(extra), left)
+        for (arrays, left), extra in zip(into_two.terms, (other, own))
+    ]
+    into_one.step()
     up_one.step()
     up_two.step()
-    in_two.step()
-    out_one.step()
-    small_sum = small.finish()
+    into_two.step()
+    out.step()
+    down = down.finish(into=(width, None))
+    up_one.step()
+    into_one.step()
+    up_two.step()
+    into_two.step()
+    up = up_one.finish(into=(hidden, None))
+    into_one.step()
+    out.step()
+    up = up_two.finish(into=(hidden, up), start=hidden // 2)
+    into_two.step()
+    into = into_one.finish(into=(3 * width, None))
+    out.step()
+    last = into_two.finish()
+    out = out.finish(into=(width, None))
+    into = lax.dynamic_update_slice(into, last[None, :, :width], (0, 0, 2 * width))
+    small_sum = last[:, width : width + count // block].reshape(-1)
     vector_share = small_sum[: smalls.size // size]
-    table_share = small_sum[smalls.size // size : -128].reshape(2, codes, share)
-    totals = small_sum[-128:]
+    table_share = small_sum[smalls.size // size :].reshape(2, codes, share)
     table_own = jnp.where(is_first, send(table_share[0], 0), table_share[1])
-    up_two.step()
-    in_one.step()
-    up_one_sum = up_one.finish()
-    in_one.step()
-    up_sum = [up_one_sum, up_two.finish()]
-    in_two.step()
-    in_one_sum = in_one.finish()
-    in_two.step()
-    out_one.step()
-    out_one.step()
-    in_sum = [in_one_sum, in_two.finish()]
-    out_sum = [out_one.finish()]
     grad_adaptive = lax.dot_general(
         codebook_table.astype(f32),
         table_own,
@@ -880,16 +1109,13 @@
     )
     residual_rms = jnp.sqrt(totals[:4] / (totals[4] * width))[None]
 
-    def joined(parts):
-        return jnp.concatenate(parts, axis=-1)[None]
-
     return (
         layer_outputs,
         input_grads,
-        joined(in_sum),
-        joined(out_sum),
-        joined(up_sum),
-        joined(down_sum),
+        into,
+        out,
+        up,
+        down,
         vector_share[None],
         grad_adaptive,
         residual_rms,

time: 525 us -> 507 us (0.966)
  Pallas kernels: 222 us -> 307 us
  waiting for transfers between devices: 167 us -> 126 us
  other arithmetic: 37.9 us -> 2.01 us
  local copies, waits for them, and re-layouts: 40.8 us -> 20.8 us
  starting transfers between devices: 41.7 us -> 35.9 us
    pallas_call x10 -> x36, Pallas kernels: 133 us -> 219 us  [the longest x4 90.4 us: backward_call(): pl.pallas_call(functools.partial(backward_kernel, slot, plan, stage, len(...]
    ppermute x5, waiting for transfers between devices: 116 us -> 86.1 us  [send(): return lax.ppermute(value, 'section', [(1 - to, to)])]
    convert_element_type x14 -> x0, other arithmetic: 24.2 us -> none  [step(): added([pick(term, axis, 1 - mine) for term in self.terms]).astype(self.kind)]
    squeeze x60 -> x1, local copies, waits for them, and re-layouts: 21.9 us -> 0.67 us  [shards(): lax.dynamic_index_in_dim(packed, which, bits - 1, keepdims=False)]
    ppermute x32 -> x31, waiting for transfers between devices: 50.5 us -> 39.7 us  [crossed(): lax.ppermute(value, 'dp', [(i, i ^ 1 << bit) for i in range(lax.axis_size...]
    add x16 -> x4, other arithmetic: 7.87 us -> 0.52 us  [shards(): totals = totals + crossed(totals, bit)]
    ppermute x32 -> x31, starting transfers between devices: 31.8 us -> 25.1 us  [crossed(): lax.ppermute(value, 'dp', [(i, i ^ 1 << bit) for i in range(lax.axis_size...]
    unnamed x99 -> x60, local copies, waits for them, and re-layouts: 13.5 us -> 13.8 us
  transfers between devices with their start and end apart: 37 -> 36, of which waited for: 12 -> 15; matrix products, arithmetic and copies ran while one was open for 13% -> 3% of each run, Pallas kernels for 16% -> 34%
where the time goes in v3:
time: 507 us; the launch traced here: 500 us
  Pallas kernels  307 us (61%)
  waiting for transfers between devices  126 us (25%)
  starting transfers between devices  35.9 us (7%)
  local copies, waits for them, and re-layouts  20.8 us (4%)
  matrix products  5.28 us (1%)
    pallas_call x4, Pallas kernels, backward_call(): pl.pallas_call(functools.partial(backward_kernel, slot, plan, stage, len(...  90.4 us
    pallas_call x3, Pallas kernels, forward_call(): pl.pallas_call(functools.partial(forward_kernel, slot, plan, len(stash)),...  88.3 us
    ppermute x5, waiting for transfers between devices, send(): return lax.ppermute(value, 'section', [(1 - to, to)])  86.1 us
    pallas_call x8, Pallas kernels, weight_call(): pl.pallas_call(functools.partial(weight_kernel, widths, half), grid=(heig...  59.6 us
    pallas_call x23, Pallas kernels, sum_call(): pl.pallas_call(kernel, in_specs=[any_] * len(operands), out_specs=any_, o...  54 us
    ppermute x31, waiting for transfers between devices, crossed(): lax.ppermute(value, 'dp', [(i, i ^ 1 << bit) for i in range(lax.axis_size...  39.7 us
    ppermute x31, starting transfers between devices, crossed(): lax.ppermute(value, 'dp', [(i, i ^ 1 << bit) for i in range(lax.axis_size...  25.1 us
    pallas_call x1, Pallas kernels, turn_call(): pl.pallas_call(functools.partial(turn_kernel, [s.shape[1] // size for s i...  14.7 us
  transfers between devices with their start and end apart: 36, of which 15 were waited for; matrix products, arithmetic and copies ran while one was open for 3% of the time, Pallas kernels for 34%

profile of v3, /device:TPU:0, one launch (start us, length us, event | category | flops | bytes accessed | tf_op | source)
XLA Modules:
  0.0 499.8 jit_solution(1694324385371245894)
XLA Ops:
  3.1 40.2 %layer_forward.3 = (bf16[512,1024]{1,0:T(8,128)(2,1)}, f32[4,8,1024]{2,1,0:T(8,128)}, bf16[1024,1024]{1,0:T(8,128)(2,1)}, bf16[1024,1024]{1,0:T(8,128)(2,1)}, bf...) custom-call(s32[2,1]{1,0:T(2,128)} %copy.64.refs_0_, ...), custom_call_target="tpu_custom_call" | custom-call | flops 99999997952 | bytes 1 | tf_op jit(solution)/shard_map/layer_forward/pallas_call | solution.py:307
  44.9 4.6 fusion.6
  50.4 17.9 %collective-permute-done.refs_4_ = bf16[512,1024]{1,0:T(8,128)(2,1)S(1)} collective-permute-done((bf16[512,1024]{1,0:T(8,128)(2,1)}, bf16[512,1024]{1,0:T(8,128)(2,1)S(1)}, u32[]{:S(2)}, u32[]{:S(2)}) %collective-permute-start) | collective-permute-done | bytes 1048608 | tf_op jit(solution)/shard_map/ppermute | solution.py:987
  69.2 40.2 %layer_forward.4 = (bf16[512,1024]{1,0:T(8,128)(2,1)}, f32[4,8,1024]{2,1,0:T(8,128)}, bf16[1024,1024]{1,0:T(8,128)(2,1)}, bf16[1024,1024]{1,0:T(8,128)(2,1)}, bf...) custom-call(s32[2,1]{1,0:T(2,128)} %copy.64.refs_0_, ...), custom_call_target="tpu_custom_call", output_to_operand_aliasing={{2}: (9, {}), {3}: (10, {}), {4}: (11, {}), {5}: (12, {}), ... | custom-call | flops 99999997952 | bytes 1 | tf_op jit(solution)/shard_map/layer_forward/pallas_call | solution.py:307
  109.4 5.3 %collective-permute-start.1 = (bf16[512,1024]{1,0:T(8,128)(2,1)}, bf16[512,1024]{1,0:T(8,128)(2,1)}, u32[]{:S(2)}, u32[]{:S(2)}) collective-permute-start(bf16[512,1024]{1,0:T(8,128)(2,1)} %get-tuple-element.220), channel_id=1, source_target_pairs={{0,16},{1,17},{2,18},{3,19},{4,20},{5,21},{6,22},{7,23},{8,24},{9,... | collective-permute-start | bytes 3145736 | tf_op jit(solution)/shard_map/ppermute | solution.py:987
  117.8 18.6 %collective-permute-done.1.refs_4_ = bf16[512,1024]{1,0:T(8,128)(2,1)} collective-permute-done((bf16[512,1024]{1,0:T(8,128)(2,1)}, bf16[512,1024]{1,0:T(8,128)(2,1)}, u32[]{:S(2)}, u32[]{:S(2)}) %collective-permute-start.1) | collective-permute-done | bytes 1048608 | tf_op jit(solution)/shard_map/ppermute | solution.py:987
  136.4 7.9 %layer_forward.5 = (bf16[512,1024]{1,0:T(8,128)(2,1)}, f32[4,8,1024]{2,1,0:T(8,128)}, bf16[1024,1024]{1,0:T(8,128)(2,1)}, bf16[1024,1024]{1,0:T(8,128)(2,1)}, bf...) custom-call(s32[2,1]{1,0:T(2,128)} %copy.64.refs_0_, ...), custom_call_target="tpu_custom_call", output_to_operand_aliasing={{2}: (9, {}), {3}: (10, {}), {4}: (11, {}), {5}: (12, {}), ... | custom-call | flops 99999997952 | bytes 1 | tf_op jit(solution)/shard_map/layer_forward/pallas_call | solution.py:307
  144.3 35.3 %collective-permute-done.2.refs_3_ = bf16[512,1024]{1,0:T(8,128)(2,1)S(1)} collective-permute-done((bf16[512,1024]{1,0:T(8,128)(2,1)}, bf16[512,1024]{1,0:T(8,128)(2,1)S(1)}, u32[]{:S(2)}, u32[]{:S(2)}) %collective-permute-start.2) | collective-permute-done | bytes 1048608 | tf_op jit(solution)/shard_map/ppermute | solution.py:987
  180.6 42.1 %layer_backward.5 = (f32[12,1024]{1,0:T(8,128)}, bf16[1024,4096]{1,0:T(8,128)(2,1)}, bf16[1024,1024]{1,0:T(8,128)(2,1)}, bf16[512,1024]{1,0:T(8,128)(2,1)}, bf16...) custom-call(s32[2,1]{1,0:T(2,128)} %copy.64.refs_0_, ...), custom_call_target="tpu_custom_call", output_to_operand_aliasing={{1}: (15, {}), {2}: (16, {}), {4}: (17, {}), {5}: (18, {}),... | custom-call | flops 99999997952 | bytes 1 | tf_op jit(solution)/shard_map/layer_backward/pallas_call | solution.py:628
  233.9 2.8 collective-permute-start.7
  236.7 14.7 %turn.1 = (bf16[2,512,1024]{2,1,0:T(8,128)(2,1)}, bf16[2,512,1024]{2,1,0:T(8,128)(2,1)}, bf16[2,512,1024]{2,1,0:T(8,128)(2,1)}, bf16[2,2048,1024]{2,1,0:T(8,128)(2,1)}) custom-call(bf16[1024,1024]{1,0:T(8,128)(2,1)} %get-tuple-element.251.refs_0_, bf16[1024,1024]{1,0:T(8,128)(2,1)} %get-tuple-element.252.refs_1_, ...), custom_call_target="tpu_custom_call" | custom-call | flops 1 | bytes 1 | tf_op jit(solution)/shard_map/turn/pallas_call | solution.py:701
  252.0 12.5 %collective-permute-done.3.rest_0_.refs_3_ = bf16[512,1024]{1,0:T(8,128)(2,1)S(1)} collective-permute-done((bf16[512,1024]{1,0:T(8,128)(2,1)}, bf16[512,1024]{1,0:T(8,128)(2,1)S(1)}, u32[]{:S(2)}, u32[]{:S(2)}) %collective-permute-start.3) | collective-permute-done | bytes 1048608 | tf_op jit(solution)/shard_map/ppermute | solution.py:987
  265.4 8.7 %weight_product.8 = bf16[2048,1024]{1,0:T(8,128)(2,1)} custom-call(bf16[2,2048,1024]{2,1,0:T(8,128)(2,1)} %get-tuple-element.265.left, bf16[1024,1024]{1,0:T(8,128)(2,1)} %get-tuple-element.266.right, bf16[512,1024]{1,0:T(8,128)(2,1)} %copy-done.6), custom_call_target="tpu_custom_call" | custom-call | flops 1 | bytes 1 | tf_op jit(solution)/shard_map/weight_product/pallas_call | solution.py:755
  274.2 8.7 %weight_product.9 = bf16[2048,1024]{1,0:T(8,128)(2,1)} custom-call(bf16[2,2048,1024]{2,1,0:T(8,128)(2,1)} %get-tuple-element.265.left, bf16[1024,1024]{1,0:T(8,128)(2,1)} %get-tuple-element.266.right, bf16[512,1024]{1,0:T(8,128)(2,1)} %copy-done.6), custom_call_target="tpu_custom_call" | custom-call | flops 1 | bytes 1 | tf_op jit(solution)/shard_map/weight_product/pallas_call | solution.py:755
  282.9 3.2 sum_terms.23
  287.8 21.3 %layer_backward.6 = (f32[12,1024]{1,0:T(8,128)}, bf16[1024,4096]{1,0:T(8,128)(2,1)}, bf16[1024,1024]{1,0:T(8,128)(2,1)}, f32[512,1024]{1,0:T(8,128)}) custom-call(s32[2,1]{1,0:T(2,128)} %copy.64.refs_0_, f32[1,12288]{1,0:T(1,128)} %refs_1_.5, bf16[2,1,512,1024]{3,2,1,0:T(8,128)(2,1)} %refs_2_.13, ...), custom_call_target="tpu_custom_call", output_to_operand_aliasing={{1}: (15, {}), {2}: (16, {})} | custom-call | flops 99999997952 | bytes 1 | tf_op jit(solution)/shard_map/layer_backward/pallas_call | solution.py:628
  309.2 9.7 %weight_product.10 = (bf16[512,1024]{1,0:T(8,128)(2,1)}, bf16[512,1024]{1,0:T(8,128)(2,1)}, bf16[512,1024]{1,0:T(8,128)(2,1)}, bf16[512,1024]{1,0:T(8,128)(2,1)}) custom-call(bf16[2,512,1024]{2,1,0:T(8,128)(2,1)} %get-tuple-element.284.left, bf16[1024,4096]{1,0:T(8,128)(2,1)} %get-tuple-element.285.right), custom_call_target="tpu_custom_call" | custom-call | flops 1 | bytes 1 | tf_op jit(solution)/shard_map/weight_product/pallas_call | solution.py:755
  319.9 8.8 %weight_product.11 = bf16[512,4096]{1,0:T(8,128)(2,1)} custom-call(bf16[2,512,1024]{2,1,0:T(8,128)(2,1)} %get-tuple-element.284.left, bf16[1024,4096]{1,0:T(8,128)(2,1)} %get-tuple-element.285.right), custom_call_target="tpu_custom_call" | custom-call | flops 1 | bytes 1 | tf_op jit(solution)/shard_map/weight_product/pallas_call | solution.py:755
  329.7 3.4 sum_terms.24
  334.5 2.9 sum_terms.25
  339.2 4.2 weight_product.12
  343.4 4.2 weight_product.13
  347.5 25.1 %layer_backward.7 = (f32[12,1024]{1,0:T(8,128)}, bf16[512,1024]{1,0:T(8,128)(2,1)}, bf16[1024,3072]{1,0:T(8,128)(2,1)}, bf16[1,2,1,512,1024]{4,3,2,1,0:T(8,128)(2,1)}) custom-call(s32[2,1]{1,0:T(2,128)} %copy.64.refs_0_, f32[1,12288]{1,0:T(1,128)} %refs_1_.5, bf16[2,1,512,1024]{3,2,1,0:T(8,128)(2,1)} %refs_2_.13, ...), custom_call_target="tpu_custom_call", output_to_operand_aliasing={{2}: (17, {}), {3}: (18, {})} | custom-call | flops 99999997952 | bytes 1 | tf_op jit(solution)/shard_map/layer_backward/pallas_call | solution.py:628
  373.7 2.6 sum_terms.26
  376.3 7.9 %weight_product.14 = (bf16[512,1024]{1,0:T(8,128)(2,1)}, bf16[512,1024]{1,0:T(8,128)(2,1)}, bf16[512,1024]{1,0:T(8,128)(2,1)}) custom-call(bf16[2,512,1024]{2,1,0:T(8,128)(2,1)} %get-tuple-element.313.left, bf16[1024,3072]{1,0:T(8,128)(2,1)} %get-tuple-element.314.right), custom_call_target="tpu_custom_call" | custom-call | flops 1 | bytes 1 | tf_op jit(solution)/shard_map/weight_product/pallas_call | solution.py:755
  385.8 7.4 %weight_product.15 = bf16[512,3072]{1,0:T(8,128)(2,1)} custom-call(bf16[2,512,1024]{2,1,0:T(8,128)(2,1)} %get-tuple-element.313.left, bf16[1024,3072]{1,0:T(8,128)(2,1)} %get-tuple-element.314.right), custom_call_target="tpu_custom_call" | custom-call | flops 1 | bytes 1 | tf_op jit(solution)/shard_map/weight_product/pallas_call | solution.py:755
  398.5 2.6 collective-permute-start.20
  412.8 12.5 %collective-permute-done.20.refs_4_ = bf16[256,1024]{1,0:T(8,128)(2,1)} collective-permute-done((bf16[256,1024]{1,0:T(8,128)(2,1)}, bf16[256,1024]{1,0:T(8,128)(2,1)}, u32[]{:S(2)}, u32[]{:S(2)}) %collective-permute-start.20) | collective-permute-done | bytes 524320 | tf_op jit(solution)/shard_map/ppermute | solution.py:933
  425.3 3.0 sum_terms.32
  436.5 10.0 %collective-permute-done.27.refs_4_ = bf16[2,64,2048]{2,1,0:T(8,128)(2,1)} collective-permute-done((bf16[2,64,2048]{2,1,0:T(8,128)(2,1)}, bf16[2,64,2048]{2,1,0:T(8,128)(2,1)}, u32[]{:S(2)}, u32[]{:S(2)}) %collective-permute-start.27) | collective-permute-done | bytes 524320 | tf_op jit(solution)/shard_map/ppermute | solution.py:933
  455.4 7.9 %collective-permute-done.24.refs_4_ = bf16[2,64,2048]{2,1,0:T(8,128)(2,1)S(1)} collective-permute-done((bf16[2,64,2048]{2,1,0:T(8,128)(2,1)}, bf16[2,64,2048]{2,1,0:T(8,128)(2,1)S(1)}, u32[]{:S(2)}, u32[]{:S(2)}) %collective-permute-start.24) | collective-permute-done | bytes 524320 | tf_op jit(solution)/shard_map/ppermute | solution.py:933
  476.1 3.0 collective-permute-start.32
  (186 shorter events, 97.6 us)
Async XLA Ops:
  43.3 24.9 %collective-permute-start = (bf16[512,1024]{1,0:T(8,128)(2,1)}, bf16[512,1024]{1,0:T(8,128)(2,1)S(1)}, u32[]{:S(2)}, u32[]{:S(2)}) collective-permute-start(bf16[512,1024]{1,0:T(8,128)(2,1)} %get-tuple-element.207), channel_id=1, source_target_pairs={{0,16},{1,17},{2,18},{3,19},{4,20},{5,21},{6,22},{7,23},{8,24},{9,... | collective-permute-start | bytes 3145736 | tf_op jit(solution)/shard_map/ppermute | solution.py:987
  109.4 27.0 %collective-permute-start.1 = (bf16[512,1024]{1,0:T(8,128)(2,1)}, bf16[512,1024]{1,0:T(8,128)(2,1)}, u32[]{:S(2)}, u32[]{:S(2)}) collective-permute-start(bf16[512,1024]{1,0:T(8,128)(2,1)} %get-tuple-element.220), channel_id=1, source_target_pairs={{0,16},{1,17},{2,18},{3,19},{4,20},{5,21},{6,22},{7,23},{8,24},{9,... | collective-permute-start | bytes 3145736 | tf_op jit(solution)/shard_map/ppermute | solution.py:987
  116.5 63.1 %collective-permute-start.2 = (bf16[512,1024]{1,0:T(8,128)(2,1)}, bf16[512,1024]{1,0:T(8,128)(2,1)S(1)}, u32[]{:S(2)}, u32[]{:S(2)}) collective-permute-start(bf16[512,1024]{1,0:T(8,128)(2,1)} %get-tuple-element.233), channel_id=1, source_target_pairs={{16,0},{17,1},{18,2},{19,3},{20,4},{21,5},{22,6},{23,7},{24,8},{25... | collective-permute-start | bytes 3145736 | tf_op jit(solution)/shard_map/ppermute | solution.py:987
  222.7 41.8 %collective-permute-start.3 = (bf16[512,1024]{1,0:T(8,128)(2,1)}, bf16[512,1024]{1,0:T(8,128)(2,1)S(1)}, u32[]{:S(2)}, u32[]{:S(2)}) collective-permute-start(bf16[512,1024]{1,0:T(8,128)(2,1)} %get-tuple-element.246), channel_id=1, source_target_pairs={{16,0},{17,1},{18,2},{19,3},{20,4},{21,5},{22,6},{23,7},{24,8},{25... | collective-permute-start | bytes 3145736 | tf_op jit(solution)/shard_map/ppermute | solution.py:987
  233.9 17.5 %collective-permute-start.7 = (f32[128]{0:T(128)S(1)}, f32[128]{0:T(128)S(1)}, u32[]{:S(2)}, u32[]{:S(2)}) collective-permute-start(f32[128]{0:T(128)S(1)} %add.60), channel_id=1, source_target_pairs={{0,8},{1,9},{2,10},{3,11},{4,12},{5,13},{6,14},{7,15},{8,0},{9,1},... | collective-permute-start | bytes 1544 | tf_op jit(solution)/shard_map/ppermute | solution.py:933
  274.2 8.7 %collective-permute-start.8 = (bf16[2048,1024]{1,0:T(8,128)(2,1)}, bf16[2048,1024]{1,0:T(8,128)(2,1)}, u32[]{:S(2)}, u32[]{:S(2)}) collective-permute-start(bf16[2048,1024]{1,0:T(8,128)(2,1)} %weight_product.8), channel_id=1, source_target_pairs={{0,1},{1,0},{2,3},{3,2},{4,5},{5,4},{6,7},{7,6},{8,9},{9,8},{10,11... | collective-permute-start | bytes 12582920 | tf_op jit(solution)/shard_map/ppermute | solution.py:933
  286.1 48.4 %collective-permute-start.9 = (bf16[2,2,256,1024]{3,2,1,0:T(8,128)(2,1)}, bf16[2,2,256,1024]{3,2,1,0:T(8,128)(2,1)}, u32[]{:S(2)}, u32[]{:S(2)}) collective-permute-start(bf16[2,2,256,1024]{3,2,1,0:T(8,128)(2,1)} %sum_terms.23), channel_id=1, source_target_pairs={{0,2},{1,3},{2,0},{3,1},{4,6},{5,7},{6,4},{7,5},{8,10},{9,11},{10,... | collective-permute-start | bytes 6291464 | tf_op jit(solution)/shard_map/ppermute | solution.py:933
  318.8 9.9 %collective-permute-start.11 = (bf16[512,1024]{1,0:T(8,128)(2,1)}, bf16[512,1024]{1,0:T(8,128)(2,1)S(1)}, u32[]{:S(2)}, u32[]{:S(2)}) collective-permute-start(bf16[512,1024]{1,0:T(8,128)(2,1)} %get-tuple-element.281), channel_id=1, source_target_pairs={{0,1},{1,0},{2,3},{3,2},{4,5},{5,4},{6,7},{7,6},{8,9},{9,8},{10,11... | collective-permute-start | bytes 3145736 | tf_op jit(solution)/shard_map/ppermute | solution.py:933
  319.0 9.7 %collective-permute-start.12 = (bf16[512,1024]{1,0:T(8,128)(2,1)}, bf16[512,1024]{1,0:T(8,128)(2,1)}, u32[]{:S(2)}, u32[]{:S(2)}) collective-permute-start(bf16[512,1024]{1,0:T(8,128)(2,1)} %get-tuple-element.282), channel_id=1, source_target_pairs={{0,1},{1,0},{2,3},{3,2},{4,5},{5,4},{6,7},{7,6},{8,9},{9,8},{10,11... | collective-permute-start | bytes 3145736 | tf_op jit(solution)/shard_map/ppermute | solution.py:933
  319.3 9.4 %collective-permute-start.13 = (bf16[512,1024]{1,0:T(8,128)(2,1)}, bf16[512,1024]{1,0:T(8,128)(2,1)}, u32[]{:S(2)}, u32[]{:S(2)}) collective-permute-start(bf16[512,1024]{1,0:T(8,128)(2,1)} %get-tuple-element.283), channel_id=1, source_target_pairs={{0,1},{1,0},{2,3},{3,2},{4,5},{5,4},{6,7},{7,6},{8,9},{9,8},{10,11... | collective-permute-start | bytes 3145736 | tf_op jit(solution)/shard_map/ppermute | solution.py:933
  319.5 9.2 %collective-permute-start.10 = (bf16[512,1024]{1,0:T(8,128)(2,1)}, bf16[512,1024]{1,0:T(8,128)(2,1)}, u32[]{:S(2)}, u32[]{:S(2)}) collective-permute-start(bf16[512,1024]{1,0:T(8,128)(2,1)} %get-tuple-element.280), channel_id=1, source_target_pairs={{0,1},{1,0},{2,3},{3,2},{4,5},{5,4},{6,7},{7,6},{8,9},{9,8},{10,11... | collective-permute-start | bytes 3145736 | tf_op jit(solution)/shard_map/ppermute | solution.py:933
  333.1 65.4 %collective-permute-start.18 = (bf16[2,2,64,4096]{3,2,1,0:T(8,128)(2,1)}, bf16[2,2,64,4096]{3,2,1,0:T(8,128)(2,1)}, u32[]{:S(2)}, u32[]{:S(2)}) collective-permute-start(bf16[2,2,64,4096]{3,2,1,0:T(8,128)(2,1)} %sum_terms.24), channel_id=1, source_target_pairs={{0,2},{1,3},{2,0},{3,1},{4,6},{5,7},{6,4},{7,5},{8,10},{9,11},{10,... | collective-permute-start | bytes 6291464 | tf_op jit(solution)/shard_map/ppermute | solution.py:933
  337.4 35.3 %collective-permute-start.14 = (bf16[2,256,1024]{2,1,0:T(8,128)(2,1)}, bf16[2,256,1024]{2,1,0:T(8,128)(2,1)S(1)}, u32[]{:S(2)}, u32[]{:S(2)}) collective-permute-start(bf16[2,256,1024]{2,1,0:T(8,128)(2,1)} %sum_terms.25), channel_id=1, source_target_pairs={{0,4},{1,5},{2,6},{3,7},{4,0},{5,1},{6,2},{7,3},{8,12},{9,13},{10,... | collective-permute-start | bytes 3145736 | tf_op jit(solution)/shard_map/ppermute | solution.py:933
  384.2 9.0 %collective-permute-start.15 = (bf16[512,1024]{1,0:T(8,128)(2,1)}, bf16[512,1024]{1,0:T(8,128)(2,1)}, u32[]{:S(2)}, u32[]{:S(2)}) collective-permute-start(bf16[512,1024]{1,0:T(8,128)(2,1)} %get-tuple-element.310), channel_id=1, source_target_pairs={{0,1},{1,0},{2,3},{3,2},{4,5},{5,4},{6,7},{7,6},{8,9},{9,8},{10,11... | collective-permute-start | bytes 3145736 | tf_op jit(solution)/shard_map/ppermute | solution.py:933
  384.2 9.0 %collective-permute-start.16 = (bf16[512,1024]{1,0:T(8,128)(2,1)}, bf16[512,1024]{1,0:T(8,128)(2,1)}, u32[]{:S(2)}, u32[]{:S(2)}) collective-permute-start(bf16[512,1024]{1,0:T(8,128)(2,1)} %get-tuple-element.311), channel_id=1, source_target_pairs={{0,1},{1,0},{2,3},{3,2},{4,5},{5,4},{6,7},{7,6},{8,9},{9,8},{10,11... | collective-permute-start | bytes 3145736 | tf_op jit(solution)/shard_map/ppermute | solution.py:933
  385.1 21.2 %collective-permute-start.22 = (bf16[512,1024]{1,0:T(8,128)(2,1)}, bf16[512,1024]{1,0:T(8,128)(2,1)}, u32[]{:S(2)}, u32[]{:S(2)}) collective-permute-start(bf16[512,1024]{1,0:T(8,128)(2,1)} %get-tuple-element.312), channel_id=1, source_target_pairs={{0,1},{1,0},{2,3},{3,2},{4,5},{5,4},{6,7},{7,6},{8,9},{9,8},{10,11... | collective-permute-start | bytes 3145736 | tf_op jit(solution)/shard_map/ppermute | solution.py:933
  385.2 23.9 %collective-permute-start.21 = (bf16[512,1024]{1,0:T(8,128)(2,1)}, bf16[512,1024]{1,0:T(8,128)(2,1)S(1)}, u32[]{:S(2)}, u32[]{:S(2)}) collective-permute-start(bf16[512,1024]{1,0:T(8,128)(2,1)} %weight_product.12), channel_id=1, source_target_pairs={{0,1},{1,0},{2,3},{3,2},{4,5},{5,4},{6,7},{7,6},{8,9},{9,8},{10,11... | collective-permute-start | bytes 3145736 | tf_op jit(solution)/shard_map/ppermute | solution.py:933
  395.8 36.1 %collective-permute-start.17 = (bf16[2,2,64,2048]{3,2,1,0:T(8,128)(2,1)}, bf16[2,2,64,2048]{3,2,1,0:T(8,128)(2,1)}, u32[]{:S(2)}, u32[]{:S(2)}) collective-permute-start(bf16[2,2,64,2048]{3,2,1,0:T(8,128)(2,1)} %sum_terms.27), channel_id=1, source_target_pairs={{0,2},{1,3},{2,0},{3,1},{4,6},{5,7},{6,4},{7,5},{8,10},{9,11},{10,... | collective-permute-start | bytes 3145736 | tf_op jit(solution)/shard_map/ppermute | solution.py:933
  398.5 26.8 %collective-permute-start.20 = (bf16[256,1024]{1,0:T(8,128)(2,1)}, bf16[256,1024]{1,0:T(8,128)(2,1)}, u32[]{:S(2)}, u32[]{:S(2)}) collective-permute-start(bf16[256,1024]{1,0:T(8,128)(2,1)} %sum_terms.26), channel_id=1, source_target_pairs={{0,8},{1,9},{2,10},{3,11},{4,12},{5,13},{6,14},{7,15},{8,0},{9,1},... | collective-permute-start | bytes 1572872 | tf_op jit(solution)/shard_map/ppermute | solution.py:933
  403.4 26.3 %collective-permute-start.19 = (bf16[2,64,2048]{2,1,0:T(8,128)(2,1)}, bf16[2,64,2048]{2,1,0:T(8,128)(2,1)}, u32[]{:S(2)}, u32[]{:S(2)}) collective-permute-start(bf16[2,64,2048]{2,1,0:T(8,128)(2,1)} %sum_terms.28), channel_id=1, source_target_pairs={{0,4},{1,5},{2,6},{3,7},{4,0},{5,1},{6,2},{7,3},{8,12},{9,13},{10,... | collective-permute-start | bytes 1572872 | tf_op jit(solution)/shard_map/ppermute | solution.py:933
  408.5 40.2 %collective-permute-start.26 = (bf16[2,2,64,1152]{3,2,1,0:T(8,128)(2,1)}, bf16[2,2,64,1152]{3,2,1,0:T(8,128)(2,1)S(1)}, u32[]{:S(2)}, u32[]{:S(2)}) collective-permute-start(bf16[2,2,64,1152]{3,2,1,0:T(8,128)(2,1)} %sum_terms.30), channel_id=1, source_target_pairs={{0,2},{1,3},{2,0},{3,1},{4,6},{5,7},{6,4},{7,5},{8,10},{9,11},{10,... | collective-permute-start | bytes 1769480 | tf_op jit(solution)/shard_map/ppermute | solution.py:933
  409.1 37.4 %collective-permute-start.27 = (bf16[2,64,2048]{2,1,0:T(8,128)(2,1)}, bf16[2,64,2048]{2,1,0:T(8,128)(2,1)}, u32[]{:S(2)}, u32[]{:S(2)}) collective-permute-start(bf16[2,64,2048]{2,1,0:T(8,128)(2,1)} %sum_terms.29), channel_id=1, source_target_pairs={{0,4},{1,5},{2,6},{3,7},{4,0},{5,1},{6,2},{7,3},{8,12},{9,13},{10,... | collective-permute-start | bytes 1572872 | tf_op jit(solution)/shard_map/ppermute | solution.py:933
  434.1 29.1 %collective-permute-start.24 = (bf16[2,64,2048]{2,1,0:T(8,128)(2,1)}, bf16[2,64,2048]{2,1,0:T(8,128)(2,1)S(1)}, u32[]{:S(2)}, u32[]{:S(2)}) collective-permute-start(bf16[2,64,2048]{2,1,0:T(8,128)(2,1)} %sum_terms.34), channel_id=1, source_target_pairs={{0,4},{1,5},{2,6},{3,7},{4,0},{5,1},{6,2},{7,3},{8,12},{9,13},{10,... | collective-permute-start | bytes 1572872 | tf_op jit(solution)/shard_map/ppermute | solution.py:933
  434.2 32.1 %collective-permute-start.31 = (bf16[2,2,64,1024]{3,2,1,0:T(8,128)(2,1)}, bf16[2,2,64,1024]{3,2,1,0:T(8,128)(2,1)S(1)}, u32[]{:S(2)}, u32[]{:S(2)}) collective-permute-start(bf16[2,2,64,1024]{3,2,1,0:T(8,128)(2,1)} %sum_terms.31), channel_id=1, source_target_pairs={{0,2},{1,3},{2,0},{3,1},{4,6},{5,7},{6,4},{7,5},{8,10},{9,11},{10,... | collective-permute-start | bytes 1572872 | tf_op jit(solution)/shard_map/ppermute | solution.py:933
  434.9 18.2 %collective-permute-start.25 = (bf16[64,2048]{1,0:T(8,128)(2,1)}, bf16[64,2048]{1,0:T(8,128)(2,1)}, u32[]{:S(2)}, u32[]{:S(2)}) collective-permute-start(bf16[64,2048]{1,0:T(8,128)(2,1)} %sum_terms.33), channel_id=1, source_target_pairs={{0,8},{1,9},{2,10},{3,11},{4,12},{5,13},{6,14},{7,15},{8,0},{9,1},... | collective-permute-start | bytes 786440 | tf_op jit(solution)/shard_map/ppermute | solution.py:933
  451.6 21.8 %collective-permute-start.29 = (bf16[2,64,1152]{2,1,0:T(8,128)(2,1)}, bf16[2,64,1152]{2,1,0:T(8,128)(2,1)S(1)}, u32[]{:S(2)}, u32[]{:S(2)}) collective-permute-start(bf16[2,64,1152]{2,1,0:T(8,128)(2,1)} %sum_terms.36), channel_id=1, source_target_pairs={{0,4},{1,5},{2,6},{3,7},{4,0},{5,1},{6,2},{7,3},{8,12},{9,13},{10,... | collective-permute-start | bytes 884744 | tf_op jit(solution)/shard_map/ppermute | solution.py:933
  451.7 18.7 %collective-permute-start.30 = (bf16[64,2048]{1,0:T(8,128)(2,1)S(1)}, bf16[64,2048]{1,0:T(8,128)(2,1)S(1)}, u32[]{:S(2)}, u32[]{:S(2)}) collective-permute-start(bf16[64,2048]{1,0:T(8,128)(2,1)S(1)} %copy-done.12), channel_id=1, source_target_pairs={{0,8},{1,9},{2,10},{3,11},{4,12},{5,13},{6,14},{7,15},{8,0},{9,1},... | collective-permute-start | bytes 786440 | tf_op jit(solution)/shard_map/ppermute | solution.py:933
  466.2 13.4 %collective-permute-start.28 = (bf16[64,2048]{1,0:T(8,128)(2,1)}, bf16[64,2048]{1,0:T(8,128)(2,1)S(1)}, u32[]{:S(2)}, u32[]{:S(2)}) collective-permute-start(bf16[64,2048]{1,0:T(8,128)(2,1)} %sum_terms.38), channel_id=1, source_target_pairs={{0,8},{1,9},{2,10},{3,11},{4,12},{5,13},{6,14},{7,15},{8,0},{9,1},... | collective-permute-start | bytes 786440 | tf_op jit(solution)/shard_map/ppermute | solution.py:933
  469.1 14.5 %collective-permute-start.33 = (bf16[2,64,1024]{2,1,0:T(8,128)(2,1)}, bf16[2,64,1024]{2,1,0:T(8,128)(2,1)S(1)}, u32[]{:S(2)}, u32[]{:S(2)}) collective-permute-start(bf16[2,64,1024]{2,1,0:T(8,128)(2,1)} %sum_terms.39), channel_id=1, source_target_pairs={{0,4},{1,5},{2,6},{3,7},{4,0},{5,1},{6,2},{7,3},{8,12},{9,13},{10,... | collective-permute-start | bytes 786440 | tf_op jit(solution)/shard_map/ppermute | solution.py:933
  476.1 10.1 %collective-permute-start.32 = (bf16[64,1152]{1,0:T(8,128)(2,1)}, bf16[64,1152]{1,0:T(8,128)(2,1)S(1)}, u32[]{:S(2)}, u32[]{:S(2)}) collective-permute-start(bf16[64,1152]{1,0:T(8,128)(2,1)} %sum_terms.41), channel_id=1, source_target_pairs={{0,8},{1,9},{2,10},{3,11},{4,12},{5,13},{6,14},{7,15},{8,0},{9,1},... | collective-permute-start | bytes 442376 | tf_op jit(solution)/shard_map/ppermute | solution.py:933
  486.2 10.7 %collective-permute-start.34 = (bf16[64,1024]{1,0:T(8,128)(2,1)}, bf16[64,1024]{1,0:T(8,128)(2,1)S(1)}, u32[]{:S(2)}, u32[]{:S(2)}) collective-permute-start(bf16[64,1024]{1,0:T(8,128)(2,1)} %sum_terms.43), channel_id=1, source_target_pairs={{0,8},{1,9},{2,10},{3,11},{4,12},{5,13},{6,14},{7,15},{8,0},{9,1},... | collective-permute-start | bytes 393224 | tf_op jit(solution)/shard_map/ppermute | solution.py:933
  489.9 5.5 %collective-permute-start.35 = (f32[7,128]{1,0:T(8,128)S(1)}, f32[7,128]{1,0:T(8,128)S(1)}, u32[]{:S(2)}, u32[]{:S(2)}) collective-permute-start(f32[7,128]{1,0:T(8,128)S(1)} %slice.73), channel_id=1, source_target_pairs={{16,0},{17,1},{18,2},{19,3},{20,4},{21,5},{22,6},{23,7},{24,8},{25... | collective-permute-start | bytes 10760 | tf_op jit(solution)/shard_map/ppermute | solution.py:987
  (34 other events, 324.6 us)

commit v4 on v3

--- a/solution.py
+++ b/solution.py
@@ -19,6 +19,7 @@
 GROUP = 4 * HEAD
 TILE = 512
 WIDE = 1024
+BROAD = 2048
 VMEM = 62 * 2**20
 SMALL = 10**6
 LARGE = 10**11
@@ -100,26 +101,24 @@
         def _():
             pltpu.make_async_copy(recv, v_x, sem_x.at[0]).start()
 
-        def column(source, target, index):
+        def column(source, target, index, size):
             def at(i):
                 return pltpu.make_async_copy(
-                    source.at[:, part(i, WIDE)], target.at[:, part(i, WIDE)], sem_w.at[index + i]
+                    source.at[:, part(i, size)], target.at[:, part(i, size)], sem_w.at[index + i]
                 )
 
             return at
 
         def down_copy(i):
             return pltpu.make_async_copy(
-                w_down.at[part(i, WIDE)], v_down.at[part(i, WIDE)], sem_w.at[3 + 1 + hidden // WIDE + i]
+                w_down.at[part(i, BROAD)], v_down.at[part(i, BROAD)], sem_w.at[3 + 1 + hidden // BROAD + i]
             )
 
-        in_copy, out_copy, up_copy = column(w_in, v_in, 0), column(w_out, v_out, 3), column(w_up, v_up, 4)
+        in_copy = column(w_in, v_in, 0, WIDE)
+        out_copy = column(w_out, v_out, 3, WIDE)
+        up_copy = column(w_up, v_up, 4, BROAD)
         for i in range(3):
             in_copy(i).start()
-        out_copy(0).start()
-        for i in range(hidden // WIDE):
-            up_copy(i).start()
-            down_copy(i).start()
 
         def bias_rows(i):
             at = part(i, 128)
@@ -136,7 +135,7 @@
             normed, _ = row_stats(v_x[at, :].astype(f32))
             v_a[at, :] = (normed * norm(0) + norm(1)).astype(bf16)
 
-        loop(rows // 64, first_norm)
+        loop(rows // 64, first_norm, 2)
         outs = []
 
         def send(source, target, index):
@@ -154,6 +153,10 @@
             v_qkv[:, at] = tile.astype(bf16)
 
         loop(3 * width // WIDE, project)
+        out_copy(0).start()
+        for i in range(hidden // BROAD):
+            up_copy(i).start()
+            down_copy(i).start()
         send(v_qkv, s_qkv.at[here], 2)
         lane = lax.broadcasted_iota(jnp.int32, (1, GROUP), 1) // HEAD
         groups = width // GROUP
@@ -174,18 +177,21 @@
                 p_copy(i - 2).wait()
 
             half = rows // 2
-            for r in range(2):
+
+            def rows_part(r, keys):
                 picked_rows = slice(r * half, (r + 1) * half)
                 scaled = query[picked_rows] * score_scale
                 total = jnp.zeros((half, GROUP), f32)
                 sums = jnp.ones((half, GROUP), f32)
                 for h in range(4):
                     masked = jnp.where(lane == h, scaled, 0).astype(bf16)
-                    scores = nt(masked, key) + v_bias[picked_rows, :]
+                    scores = nt(masked, key[:keys]) + v_bias[picked_rows, :keys]
                     top = jnp.max(scores, axis=-1, keepdims=True)
                     raised = jnp.exp(scores - top).astype(bf16)
-                    v_p[i % 2, h, picked_rows, :] = raised
-                    product = nn(raised, jnp.where(lane == h, value, 1).astype(bf16))
+                    v_p[i % 2, h, picked_rows, :keys] = raised
+                    if keys < rows:
+                        v_p[i % 2, h, picked_rows, keys:] = jnp.zeros((half, rows - keys), bf16)
+                    product = nn(raised, jnp.where(lane == h, value[:keys], 1).astype(bf16))
                     total = jnp.where(lane == h, product, total)
                     sums = jnp.where(lane == (h ^ 1), product, sums)
                 inverse = 1.0 / jnp.concatenate(
@@ -193,6 +199,17 @@
                 )
                 v_l[picked_rows, at] = inverse
                 v_c[picked_rows, at] = (total * inverse).astype(bf16)
+
+            @pl.when(causal)
+            def _():
+                rows_part(0, half)
+                rows_part(1, rows)
+
+            @pl.when(jnp.logical_not(causal))
+            def _():
+                rows_part(0, rows)
+                rows_part(1, rows)
+
             p_copy(i).start()
 
         loop(groups, attend)
@@ -223,36 +240,32 @@
 
         nothing = jnp.zeros((8, width), f32)
         sums_one = (nothing, nothing)
-        sums_one = lax.fori_loop(0, rows // 64, second_norm, sums_one)
+        sums_one = lax.fori_loop(0, rows // 64, second_norm, sums_one, unroll=2)
         send(v_h, s_h.at[here], 3)
         send(v_b, s_b.at[here], 4)
 
         def feed(i):
             up_copy(i).wait()
             down_copy(i).wait()
-            at = part(i, WIDE)
-            half = rows // 2
-            for r in range(2):
-                rr = slice(r * half, (r + 1) * half)
-                shift = vectors[:, pl.ds(pl.multiple_of(8 * width + i * WIDE, WIDE), WIDE)]
-                pre = nn(v_b[rr, :], v_up[:, at]) + shift
-                act, slope = gate(pre)
-                act = act.astype(bf16)
-                v_g[rr, at] = act
-                v_d[rr, at] = slope.astype(bf16)
-                v_acc[rr, :] += nn(act, v_down[at, :])
+            at = part(i, BROAD)
+            shift = vectors[:, pl.ds(pl.multiple_of(8 * width + i * BROAD, BROAD), BROAD)]
+            act, slope = gate(nn(v_b[...], v_up[:, at]) + shift)
+            act = act.astype(bf16)
+            v_g[:, at] = act
+            v_d[:, at] = slope.astype(bf16)
+            v_acc[...] += nn(act, v_down[at, :])
             g_copy(i).start()
             d_copy(i).start()
 
         def g_copy(i):
-            at = part(i, WIDE)
+            at = part(i, BROAD)
             return pltpu.make_async_copy(v_g.at[:, at], s_g.at[here, at], sem_g.at[i])
 
         def d_copy(i):
-            at = part(i, WIDE)
+            at = part(i, BROAD)
             return pltpu.make_async_copy(v_d.at[:, at], s_d.at[here, at], sem_d.at[i])
 
-        loop(hidden // WIDE, feed)
+        loop(hidden // BROAD, feed)
 
         def finish(i, carry):
             at = part(i, 64)
@@ -263,14 +276,14 @@
             return (carry[0] + square(output, mask), carry[1] + square(branch, mask))
 
         sums_two = (nothing, nothing)
-        sums_two = lax.fori_loop(0, rows // 64, finish, sums_two)
+        sums_two = lax.fori_loop(0, rows // 64, finish, sums_two, unroll=2)
         send(v_z, z_out, 7)
         send(v_z, layers.at[0, picked, 0], 5)
         for k, value in enumerate((sums_one[0], sums_two[0], sums_one[1], sums_two[1])):
             squares_out[k] = value
         for copy in outs:
             copy.wait()
-        for i in range(hidden // WIDE):
+        for i in range(hidden // BROAD):
             g_copy(i).wait()
             d_copy(i).wait()
         p_copy(groups - 2).wait()
@@ -439,13 +452,19 @@
             ]
             for copy in entries:
                 copy.start()
-        if attends:
+        def enter_attention():
             for k in (5, 1, 2, 3):
                 loads[k].start()
             p_copy(0).start()
             p_copy(1).start()
+
+        def enter_last():
             loads[6].start()
             loads[0].start()
+
+        if stage == SECOND:
+            enter_attention()
+            enter_last()
         nothing = jnp.zeros((8, width), f32)
 
         def fold(values):
@@ -461,7 +480,7 @@
 
         if feeds:
             pltpu.make_async_copy(recv, v_dy, sem_x.at[0]).wait()
-            total = lax.fori_loop(0, rows // 64, enter, nothing)
+            total = lax.fori_loop(0, rows // 64, enter, nothing, unroll=2)
             smalls[7:8, :] = jnp.sum(total, axis=0, keepdims=True)
         if stage == BOTH:
             feed_copy = pltpu.make_async_copy(v_dy, g_feed.at[here], sem_o.at[4])
@@ -471,14 +490,13 @@
             down_copy(i).wait()
             up_copy(i).wait()
             d_copy(i).wait()
+            if stage == BOTH:
+                pl.when(i == tiles - 2)(enter_attention)
+                pl.when(i == tiles - 1)(enter_last)
             at = part(i, WIDE)
-            half = rows // 2
-            for r in range(2):
-                rr = slice(r * half, (r + 1) * half)
-                pre = nt(v_dy[rr, :], v_down[at, :]) * v_d[i % 2, rr, :].astype(f32)
-                pre = pre.astype(bf16)
-                v_du[rr, at] = pre
-                v_acc[rr, :] += nt(pre, v_up[:, at])
+            pre = (nt(v_dy[...], v_down[at, :]) * v_d[i % 2].astype(f32)).astype(bf16)
+            v_du[:, at] = pre
+            v_acc[...] += nt(pre, v_up[:, at])
             smalls[pl.ds(8 + i, 1), :] = jnp.sum(v_du[:, at].astype(f32), axis=0, keepdims=True)
             pltpu.make_async_copy(v_du.at[:, at], g_up.at[here, at], sem_o.at[3]).start()
 
@@ -507,7 +525,7 @@
             return carry[0] + one, carry[1] + two, carry[2] + fold(low.astype(f32))
 
         if feeds:
-            sums = lax.fori_loop(0, rows // 64, second_norm, (nothing,) * 3)
+            sums = lax.fori_loop(0, rows // 64, second_norm, (nothing,) * 3, unroll=2)
             for k, value in zip((2, 3, 6), sums):
                 smalls[k : k + 1, :] = jnp.sum(value, axis=0, keepdims=True)
             outs = [pltpu.make_async_copy(v_do, g_mid.at[here], sem_o.at[0])]
@@ -570,11 +588,7 @@
             loads[6].wait()
             loads[0].wait()
 
-            def enter_grad(i):
-                at = part(i, TILE)
-                v_h[:, at] = nt(v_dqkv[...], v_in[at, :])
-
-            loop(width // TILE, enter_grad)
+            v_h[...] = nt(v_dqkv[...], v_in[...])
 
         def first_norm(i, carry):
             at = part(i, 64)
@@ -583,7 +597,7 @@
             return carry[0] + one, carry[1] + two
 
         if attends:
-            sums = lax.fori_loop(0, rows // 64, first_norm, (nothing,) * 2)
+            sums = lax.fori_loop(0, rows // 64, first_norm, (nothing,) * 2, unroll=2)
             for k, value in enumerate(sums):
                 smalls[k : k + 1, :] = jnp.sum(value, axis=0, keepdims=True)
             dx_copy = pltpu.make_async_copy(v_dx, dx_out, sem_o.at[2])

time: 507 us -> 472 us (0.931)
  Pallas kernels: 307 us -> 283 us
  waiting for transfers between devices: 126 us -> 111 us
    pallas_call x3, Pallas kernels: 88.3 us -> 71.6 us  [forward_call(): pl.pallas_call(functools.partial(forward_kernel, slot, plan, len(stash)),...]
    ppermute x5, waiting for transfers between devices: 86.1 us -> 70.9 us  [send(): return lax.ppermute(value, 'section', [(1 - to, to)])]
    pallas_call x4, Pallas kernels: 90.4 us -> 83.7 us  [backward_call(): pl.pallas_call(functools.partial(backward_kernel, slot, plan, stage, len(...]
  transfers between devices with their start and end apart: 36 -> 36, of which waited for: 15 -> 15; matrix products, arithmetic and copies ran while one was open for 3% -> 3% of each run, Pallas kernels for 34% -> 37%
where the time goes in v4:
time: 472 us; the launch traced here: 463 us
  Pallas kernels  283 us (60%)
  waiting for transfers between devices  111 us (24%)
  starting transfers between devices  37 us (8%)
  local copies, waits for them, and re-layouts  20.8 us (4%)
  matrix products  5.28 us (1%)
    pallas_call x4, Pallas kernels, backward_call(): pl.pallas_call(functools.partial(backward_kernel, slot, plan, stage, len(...  83.7 us
    pallas_call x3, Pallas kernels, forward_call(): pl.pallas_call(functools.partial(forward_kernel, slot, plan, len(stash)),...  71.6 us
    ppermute x5, waiting for transfers between devices, send(): return lax.ppermute(value, 'section', [(1 - to, to)])  70.9 us
    pallas_call x8, Pallas kernels, weight_call(): pl.pallas_call(functools.partial(weight_kernel, widths, half), grid=(heig...  59.6 us
    pallas_call x23, Pallas kernels, sum_call(): pl.pallas_call(kernel, in_specs=[any_] * len(operands), out_specs=any_, o...  54 us
    ppermute x31, waiting for transfers between devices, crossed(): lax.ppermute(value, 'dp', [(i, i ^ 1 << bit) for i in range(lax.axis_size...  40.1 us
    ppermute x31, starting transfers between devices, crossed(): lax.ppermute(value, 'dp', [(i, i ^ 1 << bit) for i in range(lax.axis_size...  25.4 us
    pallas_call x1, Pallas kernels, turn_call(): pl.pallas_call(functools.partial(turn_kernel, [s.shape[1] // size for s i...  14.7 us
  transfers between devices with their start and end apart: 36, of which 15 were waited for; matrix products, arithmetic and copies ran while one was open for 3% of the time, Pallas kernels for 37%

profile of v4, /device:TPU:0, one launch (start us, length us, event | category | flops | bytes accessed | tf_op | source)
XLA Modules:
  0.0 462.7 jit_solution(13962578217526372733)
XLA Ops:
  3.1 31.1 %layer_forward.3 = (bf16[512,1024]{1,0:T(8,128)(2,1)}, f32[4,8,1024]{2,1,0:T(8,128)}, bf16[1024,1024]{1,0:T(8,128)(2,1)}, bf16[1024,1024]{1,0:T(8,128)(2,1)}, bf...) custom-call(s32[2,1]{1,0:T(2,128)} %copy.64.refs_0_, ...), custom_call_target="tpu_custom_call" | custom-call | flops 99999997952 | bytes 1 | tf_op jit(solution)/shard_map/layer_forward/pallas_call | solution.py:320
  36.1 4.6 fusion.6
  41.5 17.5 %collective-permute-done.refs_4_ = bf16[512,1024]{1,0:T(8,128)(2,1)S(1)} collective-permute-done((bf16[512,1024]{1,0:T(8,128)(2,1)}, bf16[512,1024]{1,0:T(8,128)(2,1)S(1)}, u32[]{:S(2)}, u32[]{:S(2)}) %collective-permute-start) | collective-permute-done | bytes 1048608 | tf_op jit(solution)/shard_map/ppermute | solution.py:1001
  60.1 31.7 %layer_forward.4 = (bf16[512,1024]{1,0:T(8,128)(2,1)}, f32[4,8,1024]{2,1,0:T(8,128)}, bf16[1024,1024]{1,0:T(8,128)(2,1)}, bf16[1024,1024]{1,0:T(8,128)(2,1)}, bf...) custom-call(s32[2,1]{1,0:T(2,128)} %copy.64.refs_0_, ...), custom_call_target="tpu_custom_call", output_to_operand_aliasing={{2}: (9, {}), {3}: (10, {}), {4}: (11, {}), {5}: (12, {}), ... | custom-call | flops 99999997952 | bytes 1 | tf_op jit(solution)/shard_map/layer_forward/pallas_call | solution.py:320
  91.7 5.7 %collective-permute-start.1 = (bf16[512,1024]{1,0:T(8,128)(2,1)}, bf16[512,1024]{1,0:T(8,128)(2,1)}, u32[]{:S(2)}, u32[]{:S(2)}) collective-permute-start(bf16[512,1024]{1,0:T(8,128)(2,1)} %get-tuple-element.220), channel_id=1, source_target_pairs={{0,16},{1,17},{2,18},{3,19},{4,20},{5,21},{6,22},{7,23},{8,24},{9,... | collective-permute-start | bytes 3145736 | tf_op jit(solution)/shard_map/ppermute | solution.py:1001
  100.5 18.7 %collective-permute-done.1.refs_4_ = bf16[512,1024]{1,0:T(8,128)(2,1)} collective-permute-done((bf16[512,1024]{1,0:T(8,128)(2,1)}, bf16[512,1024]{1,0:T(8,128)(2,1)}, u32[]{:S(2)}, u32[]{:S(2)}) %collective-permute-start.1) | collective-permute-done | bytes 1048608 | tf_op jit(solution)/shard_map/ppermute | solution.py:1001
  119.2 8.8 %layer_forward.5 = (bf16[512,1024]{1,0:T(8,128)(2,1)}, f32[4,8,1024]{2,1,0:T(8,128)}, bf16[1024,1024]{1,0:T(8,128)(2,1)}, bf16[1024,1024]{1,0:T(8,128)(2,1)}, bf...) custom-call(s32[2,1]{1,0:T(2,128)} %copy.64.refs_0_, ...), custom_call_target="tpu_custom_call", output_to_operand_aliasing={{2}: (9, {}), {3}: (10, {}), {4}: (11, {}), {5}: (12, {}), ... | custom-call | flops 99999997952 | bytes 1 | tf_op jit(solution)/shard_map/layer_forward/pallas_call | solution.py:320
  128.0 28.6 %collective-permute-done.2.refs_3_ = bf16[512,1024]{1,0:T(8,128)(2,1)S(1)} collective-permute-done((bf16[512,1024]{1,0:T(8,128)(2,1)}, bf16[512,1024]{1,0:T(8,128)(2,1)S(1)}, u32[]{:S(2)}, u32[]{:S(2)}) %collective-permute-start.2) | collective-permute-done | bytes 1048608 | tf_op jit(solution)/shard_map/ppermute | solution.py:1001
  157.6 37.2 %layer_backward.5 = (f32[12,1024]{1,0:T(8,128)}, bf16[1024,4096]{1,0:T(8,128)(2,1)}, bf16[1024,1024]{1,0:T(8,128)(2,1)}, bf16[512,1024]{1,0:T(8,128)(2,1)}, bf16...) custom-call(s32[2,1]{1,0:T(2,128)} %copy.64.refs_0_, ...), custom_call_target="tpu_custom_call", output_to_operand_aliasing={{1}: (15, {}), {2}: (16, {}), {4}: (17, {}), {5}: (18, {}),... | custom-call | flops 99999997952 | bytes 1 | tf_op jit(solution)/shard_map/layer_backward/pallas_call | solution.py:642
  206.0 2.8 collective-permute-start.7
  208.9 14.7 %turn.1 = (bf16[2,512,1024]{2,1,0:T(8,128)(2,1)}, bf16[2,512,1024]{2,1,0:T(8,128)(2,1)}, bf16[2,512,1024]{2,1,0:T(8,128)(2,1)}, bf16[2,2048,1024]{2,1,0:T(8,128)(2,1)}) custom-call(bf16[1024,1024]{1,0:T(8,128)(2,1)} %get-tuple-element.251.refs_0_, bf16[1024,1024]{1,0:T(8,128)(2,1)} %get-tuple-element.252.refs_1_, ...), custom_call_target="tpu_custom_call" | custom-call | flops 1 | bytes 1 | tf_op jit(solution)/shard_map/turn/pallas_call | solution.py:715
  224.1 4.2 collective-permute-done.3.rest_0_.refs_3_
  229.3 8.7 %weight_product.8 = bf16[2048,1024]{1,0:T(8,128)(2,1)} custom-call(bf16[2,2048,1024]{2,1,0:T(8,128)(2,1)} %get-tuple-element.265.left, bf16[1024,1024]{1,0:T(8,128)(2,1)} %get-tuple-element.266.right, bf16[512,1024]{1,0:T(8,128)(2,1)} %copy-done.6), custom_call_target="tpu_custom_call" | custom-call | flops 1 | bytes 1 | tf_op jit(solution)/shard_map/weight_product/pallas_call | solution.py:769
  238.0 8.7 %weight_product.9 = bf16[2048,1024]{1,0:T(8,128)(2,1)} custom-call(bf16[2,2048,1024]{2,1,0:T(8,128)(2,1)} %get-tuple-element.265.left, bf16[1024,1024]{1,0:T(8,128)(2,1)} %get-tuple-element.266.right, bf16[512,1024]{1,0:T(8,128)(2,1)} %copy-done.6), custom_call_target="tpu_custom_call" | custom-call | flops 1 | bytes 1 | tf_op jit(solution)/shard_map/weight_product/pallas_call | solution.py:769
  246.8 3.2 sum_terms.23
  251.8 20.6 %layer_backward.6 = (f32[12,1024]{1,0:T(8,128)}, bf16[1024,4096]{1,0:T(8,128)(2,1)}, bf16[1024,1024]{1,0:T(8,128)(2,1)}, f32[512,1024]{1,0:T(8,128)}) custom-call(s32[2,1]{1,0:T(2,128)} %copy.64.refs_0_, f32[1,12288]{1,0:T(1,128)} %refs_1_.5, bf16[2,1,512,1024]{3,2,1,0:T(8,128)(2,1)} %refs_2_.13, ...), custom_call_target="tpu_custom_call", output_to_operand_aliasing={{1}: (15, {}), {2}: (16, {})} | custom-call | flops 99999997952 | bytes 1 | tf_op jit(solution)/shard_map/layer_backward/pallas_call | solution.py:642
  272.4 9.7 %weight_product.10 = (bf16[512,1024]{1,0:T(8,128)(2,1)}, bf16[512,1024]{1,0:T(8,128)(2,1)}, bf16[512,1024]{1,0:T(8,128)(2,1)}, bf16[512,1024]{1,0:T(8,128)(2,1)}) custom-call(bf16[2,512,1024]{2,1,0:T(8,128)(2,1)} %get-tuple-element.284.left, bf16[1024,4096]{1,0:T(8,128)(2,1)} %get-tuple-element.285.right), custom_call_target="tpu_custom_call" | custom-call | flops 1 | bytes 1 | tf_op jit(solution)/shard_map/weight_product/pallas_call | solution.py:769
  283.1 8.8 %weight_product.11 = bf16[512,4096]{1,0:T(8,128)(2,1)} custom-call(bf16[2,512,1024]{2,1,0:T(8,128)(2,1)} %get-tuple-element.284.left, bf16[1024,4096]{1,0:T(8,128)(2,1)} %get-tuple-element.285.right), custom_call_target="tpu_custom_call" | custom-call | flops 1 | bytes 1 | tf_op jit(solution)/shard_map/weight_product/pallas_call | solution.py:769
  292.9 3.4 sum_terms.24
  298.4 2.9 sum_terms.25
  303.1 4.2 weight_product.12
  307.3 4.2 weight_product.13
  311.4 24.1 %layer_backward.7 = (f32[12,1024]{1,0:T(8,128)}, bf16[512,1024]{1,0:T(8,128)(2,1)}, bf16[1024,3072]{1,0:T(8,128)(2,1)}, bf16[1,2,1,512,1024]{4,3,2,1,0:T(8,128)(2,1)}) custom-call(s32[2,1]{1,0:T(2,128)} %copy.64.refs_0_, f32[1,12288]{1,0:T(1,128)} %refs_1_.5, bf16[2,1,512,1024]{3,2,1,0:T(8,128)(2,1)} %refs_2_.13, ...), custom_call_target="tpu_custom_call", output_to_operand_aliasing={{2}: (17, {}), {3}: (18, {})} | custom-call | flops 99999997952 | bytes 1 | tf_op jit(solution)/shard_map/layer_backward/pallas_call | solution.py:642
  336.5 2.6 sum_terms.26
  339.2 7.9 %weight_product.14 = (bf16[512,1024]{1,0:T(8,128)(2,1)}, bf16[512,1024]{1,0:T(8,128)(2,1)}, bf16[512,1024]{1,0:T(8,128)(2,1)}) custom-call(bf16[2,512,1024]{2,1,0:T(8,128)(2,1)} %get-tuple-element.313.left, bf16[1024,3072]{1,0:T(8,128)(2,1)} %get-tuple-element.314.right), custom_call_target="tpu_custom_call" | custom-call | flops 1 | bytes 1 | tf_op jit(solution)/shard_map/weight_product/pallas_call | solution.py:769
  348.7 7.4 %weight_product.15 = bf16[512,3072]{1,0:T(8,128)(2,1)} custom-call(bf16[2,512,1024]{2,1,0:T(8,128)(2,1)} %get-tuple-element.313.left, bf16[1024,3072]{1,0:T(8,128)(2,1)} %get-tuple-element.314.right), custom_call_target="tpu_custom_call" | custom-call | flops 1 | bytes 1 | tf_op jit(solution)/shard_map/weight_product/pallas_call | solution.py:769
  361.4 2.6 collective-permute-start.20
  375.7 12.6 %collective-permute-done.20.refs_4_ = bf16[256,1024]{1,0:T(8,128)(2,1)} collective-permute-done((bf16[256,1024]{1,0:T(8,128)(2,1)}, bf16[256,1024]{1,0:T(8,128)(2,1)}, u32[]{:S(2)}, u32[]{:S(2)}) %collective-permute-start.20) | collective-permute-done | bytes 524320 | tf_op jit(solution)/shard_map/ppermute | solution.py:947
  388.3 3.0 sum_terms.32
  399.4 9.9 %collective-permute-done.27.refs_4_ = bf16[2,64,2048]{2,1,0:T(8,128)(2,1)} collective-permute-done((bf16[2,64,2048]{2,1,0:T(8,128)(2,1)}, bf16[2,64,2048]{2,1,0:T(8,128)(2,1)}, u32[]{:S(2)}, u32[]{:S(2)}) %collective-permute-start.27) | collective-permute-done | bytes 524320 | tf_op jit(solution)/shard_map/ppermute | solution.py:947
  418.3 7.8 %collective-permute-done.24.refs_4_ = bf16[2,64,2048]{2,1,0:T(8,128)(2,1)S(1)} collective-permute-done((bf16[2,64,2048]{2,1,0:T(8,128)(2,1)}, bf16[2,64,2048]{2,1,0:T(8,128)(2,1)S(1)}, u32[]{:S(2)}, u32[]{:S(2)}) %collective-permute-start.24) | collective-permute-done | bytes 524320 | tf_op jit(solution)/shard_map/ppermute | solution.py:947
  439.0 2.8 collective-permute-start.32
  (186 shorter events, 98.8 us)
Async XLA Ops:
  34.2 24.9 %collective-permute-start = (bf16[512,1024]{1,0:T(8,128)(2,1)}, bf16[512,1024]{1,0:T(8,128)(2,1)S(1)}, u32[]{:S(2)}, u32[]{:S(2)}) collective-permute-start(bf16[512,1024]{1,0:T(8,128)(2,1)} %get-tuple-element.207), channel_id=1, source_target_pairs={{0,16},{1,17},{2,18},{3,19},{4,20},{5,21},{6,22},{7,23},{8,24},{9,... | collective-permute-start | bytes 3145736 | tf_op jit(solution)/shard_map/ppermute | solution.py:1001
  91.7 27.5 %collective-permute-start.1 = (bf16[512,1024]{1,0:T(8,128)(2,1)}, bf16[512,1024]{1,0:T(8,128)(2,1)}, u32[]{:S(2)}, u32[]{:S(2)}) collective-permute-start(bf16[512,1024]{1,0:T(8,128)(2,1)} %get-tuple-element.220), channel_id=1, source_target_pairs={{0,16},{1,17},{2,18},{3,19},{4,20},{5,21},{6,22},{7,23},{8,24},{9,... | collective-permute-start | bytes 3145736 | tf_op jit(solution)/shard_map/ppermute | solution.py:1001
  99.2 57.4 %collective-permute-start.2 = (bf16[512,1024]{1,0:T(8,128)(2,1)}, bf16[512,1024]{1,0:T(8,128)(2,1)S(1)}, u32[]{:S(2)}, u32[]{:S(2)}) collective-permute-start(bf16[512,1024]{1,0:T(8,128)(2,1)} %get-tuple-element.233), channel_id=1, source_target_pairs={{16,0},{17,1},{18,2},{19,3},{20,4},{21,5},{22,6},{23,7},{24,8},{25... | collective-permute-start | bytes 3145736 | tf_op jit(solution)/shard_map/ppermute | solution.py:1001
  194.8 33.5 %collective-permute-start.3 = (bf16[512,1024]{1,0:T(8,128)(2,1)}, bf16[512,1024]{1,0:T(8,128)(2,1)S(1)}, u32[]{:S(2)}, u32[]{:S(2)}) collective-permute-start(bf16[512,1024]{1,0:T(8,128)(2,1)} %get-tuple-element.246), channel_id=1, source_target_pairs={{16,0},{17,1},{18,2},{19,3},{20,4},{21,5},{22,6},{23,7},{24,8},{25... | collective-permute-start | bytes 3145736 | tf_op jit(solution)/shard_map/ppermute | solution.py:1001
  206.0 17.6 %collective-permute-start.7 = (f32[128]{0:T(128)S(1)}, f32[128]{0:T(128)S(1)}, u32[]{:S(2)}, u32[]{:S(2)}) collective-permute-start(f32[128]{0:T(128)S(1)} %add.60), channel_id=1, source_target_pairs={{0,8},{1,9},{2,10},{3,11},{4,12},{5,13},{6,14},{7,15},{8,0},{9,1},... | collective-permute-start | bytes 1544 | tf_op jit(solution)/shard_map/ppermute | solution.py:947
  238.0 8.7 %collective-permute-start.8 = (bf16[2048,1024]{1,0:T(8,128)(2,1)}, bf16[2048,1024]{1,0:T(8,128)(2,1)}, u32[]{:S(2)}, u32[]{:S(2)}) collective-permute-start(bf16[2048,1024]{1,0:T(8,128)(2,1)} %weight_product.8), channel_id=1, source_target_pairs={{0,1},{1,0},{2,3},{3,2},{4,5},{5,4},{6,7},{7,6},{8,9},{9,8},{10,11... | collective-permute-start | bytes 12582920 | tf_op jit(solution)/shard_map/ppermute | solution.py:947
  249.9 48.4 %collective-permute-start.9 = (bf16[2,2,256,1024]{3,2,1,0:T(8,128)(2,1)}, bf16[2,2,256,1024]{3,2,1,0:T(8,128)(2,1)}, u32[]{:S(2)}, u32[]{:S(2)}) collective-permute-start(bf16[2,2,256,1024]{3,2,1,0:T(8,128)(2,1)} %sum_terms.23), channel_id=1, source_target_pairs={{0,2},{1,3},{2,0},{3,1},{4,6},{5,7},{6,4},{7,5},{8,10},{9,11},{10,... | collective-permute-start | bytes 6291464 | tf_op jit(solution)/shard_map/ppermute | solution.py:947
  282.0 9.9 %collective-permute-start.11 = (bf16[512,1024]{1,0:T(8,128)(2,1)}, bf16[512,1024]{1,0:T(8,128)(2,1)S(1)}, u32[]{:S(2)}, u32[]{:S(2)}) collective-permute-start(bf16[512,1024]{1,0:T(8,128)(2,1)} %get-tuple-element.281), channel_id=1, source_target_pairs={{0,1},{1,0},{2,3},{3,2},{4,5},{5,4},{6,7},{7,6},{8,9},{9,8},{10,11... | collective-permute-start | bytes 3145736 | tf_op jit(solution)/shard_map/ppermute | solution.py:947
  282.2 9.7 %collective-permute-start.12 = (bf16[512,1024]{1,0:T(8,128)(2,1)}, bf16[512,1024]{1,0:T(8,128)(2,1)}, u32[]{:S(2)}, u32[]{:S(2)}) collective-permute-start(bf16[512,1024]{1,0:T(8,128)(2,1)} %get-tuple-element.282), channel_id=1, source_target_pairs={{0,1},{1,0},{2,3},{3,2},{4,5},{5,4},{6,7},{7,6},{8,9},{9,8},{10,11... | collective-permute-start | bytes 3145736 | tf_op jit(solution)/shard_map/ppermute | solution.py:947
  282.5 9.4 %collective-permute-start.13 = (bf16[512,1024]{1,0:T(8,128)(2,1)}, bf16[512,1024]{1,0:T(8,128)(2,1)}, u32[]{:S(2)}, u32[]{:S(2)}) collective-permute-start(bf16[512,1024]{1,0:T(8,128)(2,1)} %get-tuple-element.283), channel_id=1, source_target_pairs={{0,1},{1,0},{2,3},{3,2},{4,5},{5,4},{6,7},{7,6},{8,9},{9,8},{10,11... | collective-permute-start | bytes 3145736 | tf_op jit(solution)/shard_map/ppermute | solution.py:947
  282.7 9.2 %collective-permute-start.10 = (bf16[512,1024]{1,0:T(8,128)(2,1)}, bf16[512,1024]{1,0:T(8,128)(2,1)}, u32[]{:S(2)}, u32[]{:S(2)}) collective-permute-start(bf16[512,1024]{1,0:T(8,128)(2,1)} %get-tuple-element.280), channel_id=1, source_target_pairs={{0,1},{1,0},{2,3},{3,2},{4,5},{5,4},{6,7},{7,6},{8,9},{9,8},{10,11... | collective-permute-start | bytes 3145736 | tf_op jit(solution)/shard_map/ppermute | solution.py:947
  296.3 65.1 %collective-permute-start.18 = (bf16[2,2,64,4096]{3,2,1,0:T(8,128)(2,1)}, bf16[2,2,64,4096]{3,2,1,0:T(8,128)(2,1)}, u32[]{:S(2)}, u32[]{:S(2)}) collective-permute-start(bf16[2,2,64,4096]{3,2,1,0:T(8,128)(2,1)} %sum_terms.24), channel_id=1, source_target_pairs={{0,2},{1,3},{2,0},{3,1},{4,6},{5,7},{6,4},{7,5},{8,10},{9,11},{10,... | collective-permute-start | bytes 6291464 | tf_op jit(solution)/shard_map/ppermute | solution.py:947
  301.3 34.3 %collective-permute-start.14 = (bf16[2,256,1024]{2,1,0:T(8,128)(2,1)}, bf16[2,256,1024]{2,1,0:T(8,128)(2,1)S(1)}, u32[]{:S(2)}, u32[]{:S(2)}) collective-permute-start(bf16[2,256,1024]{2,1,0:T(8,128)(2,1)} %sum_terms.25), channel_id=1, source_target_pairs={{0,4},{1,5},{2,6},{3,7},{4,0},{5,1},{6,2},{7,3},{8,12},{9,13},{10,... | collective-permute-start | bytes 3145736 | tf_op jit(solution)/shard_map/ppermute | solution.py:947
  347.1 9.0 %collective-permute-start.15 = (bf16[512,1024]{1,0:T(8,128)(2,1)}, bf16[512,1024]{1,0:T(8,128)(2,1)}, u32[]{:S(2)}, u32[]{:S(2)}) collective-permute-start(bf16[512,1024]{1,0:T(8,128)(2,1)} %get-tuple-element.310), channel_id=1, source_target_pairs={{0,1},{1,0},{2,3},{3,2},{4,5},{5,4},{6,7},{7,6},{8,9},{9,8},{10,11... | collective-permute-start | bytes 3145736 | tf_op jit(solution)/shard_map/ppermute | solution.py:947
  347.1 9.0 %collective-permute-start.16 = (bf16[512,1024]{1,0:T(8,128)(2,1)}, bf16[512,1024]{1,0:T(8,128)(2,1)}, u32[]{:S(2)}, u32[]{:S(2)}) collective-permute-start(bf16[512,1024]{1,0:T(8,128)(2,1)} %get-tuple-element.311), channel_id=1, source_target_pairs={{0,1},{1,0},{2,3},{3,2},{4,5},{5,4},{6,7},{7,6},{8,9},{9,8},{10,11... | collective-permute-start | bytes 3145736 | tf_op jit(solution)/shard_map/ppermute | solution.py:947
  348.0 21.2 %collective-permute-start.22 = (bf16[512,1024]{1,0:T(8,128)(2,1)}, bf16[512,1024]{1,0:T(8,128)(2,1)}, u32[]{:S(2)}, u32[]{:S(2)}) collective-permute-start(bf16[512,1024]{1,0:T(8,128)(2,1)} %get-tuple-element.312), channel_id=1, source_target_pairs={{0,1},{1,0},{2,3},{3,2},{4,5},{5,4},{6,7},{7,6},{8,9},{9,8},{10,11... | collective-permute-start | bytes 3145736 | tf_op jit(solution)/shard_map/ppermute | solution.py:947
  348.1 23.9 %collective-permute-start.21 = (bf16[512,1024]{1,0:T(8,128)(2,1)}, bf16[512,1024]{1,0:T(8,128)(2,1)S(1)}, u32[]{:S(2)}, u32[]{:S(2)}) collective-permute-start(bf16[512,1024]{1,0:T(8,128)(2,1)} %weight_product.12), channel_id=1, source_target_pairs={{0,1},{1,0},{2,3},{3,2},{4,5},{5,4},{6,7},{7,6},{8,9},{9,8},{10,11... | collective-permute-start | bytes 3145736 | tf_op jit(solution)/shard_map/ppermute | solution.py:947
  358.6 35.9 %collective-permute-start.17 = (bf16[2,2,64,2048]{3,2,1,0:T(8,128)(2,1)}, bf16[2,2,64,2048]{3,2,1,0:T(8,128)(2,1)}, u32[]{:S(2)}, u32[]{:S(2)}) collective-permute-start(bf16[2,2,64,2048]{3,2,1,0:T(8,128)(2,1)} %sum_terms.27), channel_id=1, source_target_pairs={{0,2},{1,3},{2,0},{3,1},{4,6},{5,7},{6,4},{7,5},{8,10},{9,11},{10,... | collective-permute-start | bytes 3145736 | tf_op jit(solution)/shard_map/ppermute | solution.py:947
  361.4 26.9 %collective-permute-start.20 = (bf16[256,1024]{1,0:T(8,128)(2,1)}, bf16[256,1024]{1,0:T(8,128)(2,1)}, u32[]{:S(2)}, u32[]{:S(2)}) collective-permute-start(bf16[256,1024]{1,0:T(8,128)(2,1)} %sum_terms.26), channel_id=1, source_target_pairs={{0,8},{1,9},{2,10},{3,11},{4,12},{5,13},{6,14},{7,15},{8,0},{9,1},... | collective-permute-start | bytes 1572872 | tf_op jit(solution)/shard_map/ppermute | solution.py:947
  366.3 26.1 %collective-permute-start.19 = (bf16[2,64,2048]{2,1,0:T(8,128)(2,1)}, bf16[2,64,2048]{2,1,0:T(8,128)(2,1)}, u32[]{:S(2)}, u32[]{:S(2)}) collective-permute-start(bf16[2,64,2048]{2,1,0:T(8,128)(2,1)} %sum_terms.28), channel_id=1, source_target_pairs={{0,4},{1,5},{2,6},{3,7},{4,0},{5,1},{6,2},{7,3},{8,12},{9,13},{10,... | collective-permute-start | bytes 1572872 | tf_op jit(solution)/shard_map/ppermute | solution.py:947
  371.4 40.0 %collective-permute-start.26 = (bf16[2,2,64,1152]{3,2,1,0:T(8,128)(2,1)}, bf16[2,2,64,1152]{3,2,1,0:T(8,128)(2,1)S(1)}, u32[]{:S(2)}, u32[]{:S(2)}) collective-permute-start(bf16[2,2,64,1152]{3,2,1,0:T(8,128)(2,1)} %sum_terms.30), channel_id=1, source_target_pairs={{0,2},{1,3},{2,0},{3,1},{4,6},{5,7},{6,4},{7,5},{8,10},{9,11},{10,... | collective-permute-start | bytes 1769480 | tf_op jit(solution)/shard_map/ppermute | solution.py:947
  372.0 37.3 %collective-permute-start.27 = (bf16[2,64,2048]{2,1,0:T(8,128)(2,1)}, bf16[2,64,2048]{2,1,0:T(8,128)(2,1)}, u32[]{:S(2)}, u32[]{:S(2)}) collective-permute-start(bf16[2,64,2048]{2,1,0:T(8,128)(2,1)} %sum_terms.29), channel_id=1, source_target_pairs={{0,4},{1,5},{2,6},{3,7},{4,0},{5,1},{6,2},{7,3},{8,12},{9,13},{10,... | collective-permute-start | bytes 1572872 | tf_op jit(solution)/shard_map/ppermute | solution.py:947
  396.9 29.2 %collective-permute-start.24 = (bf16[2,64,2048]{2,1,0:T(8,128)(2,1)}, bf16[2,64,2048]{2,1,0:T(8,128)(2,1)S(1)}, u32[]{:S(2)}, u32[]{:S(2)}) collective-permute-start(bf16[2,64,2048]{2,1,0:T(8,128)(2,1)} %sum_terms.34), channel_id=1, source_target_pairs={{0,4},{1,5},{2,6},{3,7},{4,0},{5,1},{6,2},{7,3},{8,12},{9,13},{10,... | collective-permute-start | bytes 1572872 | tf_op jit(solution)/shard_map/ppermute | solution.py:947
  397.0 32.1 %collective-permute-start.31 = (bf16[2,2,64,1024]{3,2,1,0:T(8,128)(2,1)}, bf16[2,2,64,1024]{3,2,1,0:T(8,128)(2,1)S(1)}, u32[]{:S(2)}, u32[]{:S(2)}) collective-permute-start(bf16[2,2,64,1024]{3,2,1,0:T(8,128)(2,1)} %sum_terms.31), channel_id=1, source_target_pairs={{0,2},{1,3},{2,0},{3,1},{4,6},{5,7},{6,4},{7,5},{8,10},{9,11},{10,... | collective-permute-start | bytes 1572872 | tf_op jit(solution)/shard_map/ppermute | solution.py:947
  397.7 18.2 %collective-permute-start.25 = (bf16[64,2048]{1,0:T(8,128)(2,1)}, bf16[64,2048]{1,0:T(8,128)(2,1)}, u32[]{:S(2)}, u32[]{:S(2)}) collective-permute-start(bf16[64,2048]{1,0:T(8,128)(2,1)} %sum_terms.33), channel_id=1, source_target_pairs={{0,8},{1,9},{2,10},{3,11},{4,12},{5,13},{6,14},{7,15},{8,0},{9,1},... | collective-permute-start | bytes 786440 | tf_op jit(solution)/shard_map/ppermute | solution.py:947
  414.4 22.0 %collective-permute-start.29 = (bf16[2,64,1152]{2,1,0:T(8,128)(2,1)}, bf16[2,64,1152]{2,1,0:T(8,128)(2,1)S(1)}, u32[]{:S(2)}, u32[]{:S(2)}) collective-permute-start(bf16[2,64,1152]{2,1,0:T(8,128)(2,1)} %sum_terms.36), channel_id=1, source_target_pairs={{0,4},{1,5},{2,6},{3,7},{4,0},{5,1},{6,2},{7,3},{8,12},{9,13},{10,... | collective-permute-start | bytes 884744 | tf_op jit(solution)/shard_map/ppermute | solution.py:947
  414.5 18.9 %collective-permute-start.30 = (bf16[64,2048]{1,0:T(8,128)(2,1)S(1)}, bf16[64,2048]{1,0:T(8,128)(2,1)S(1)}, u32[]{:S(2)}, u32[]{:S(2)}) collective-permute-start(bf16[64,2048]{1,0:T(8,128)(2,1)S(1)} %copy-done.12), channel_id=1, source_target_pairs={{0,8},{1,9},{2,10},{3,11},{4,12},{5,13},{6,14},{7,15},{8,0},{9,1},... | collective-permute-start | bytes 786440 | tf_op jit(solution)/shard_map/ppermute | solution.py:947
  429.0 13.4 %collective-permute-start.28 = (bf16[64,2048]{1,0:T(8,128)(2,1)}, bf16[64,2048]{1,0:T(8,128)(2,1)S(1)}, u32[]{:S(2)}, u32[]{:S(2)}) collective-permute-start(bf16[64,2048]{1,0:T(8,128)(2,1)} %sum_terms.38), channel_id=1, source_target_pairs={{0,8},{1,9},{2,10},{3,11},{4,12},{5,13},{6,14},{7,15},{8,0},{9,1},... | collective-permute-start | bytes 786440 | tf_op jit(solution)/shard_map/ppermute | solution.py:947
  431.9 14.5 %collective-permute-start.33 = (bf16[2,64,1024]{2,1,0:T(8,128)(2,1)}, bf16[2,64,1024]{2,1,0:T(8,128)(2,1)S(1)}, u32[]{:S(2)}, u32[]{:S(2)}) collective-permute-start(bf16[2,64,1024]{2,1,0:T(8,128)(2,1)} %sum_terms.39), channel_id=1, source_target_pairs={{0,4},{1,5},{2,6},{3,7},{4,0},{5,1},{6,2},{7,3},{8,12},{9,13},{10,... | collective-permute-start | bytes 786440 | tf_op jit(solution)/shard_map/ppermute | solution.py:947
  439.0 10.0 %collective-permute-start.32 = (bf16[64,1152]{1,0:T(8,128)(2,1)}, bf16[64,1152]{1,0:T(8,128)(2,1)S(1)}, u32[]{:S(2)}, u32[]{:S(2)}) collective-permute-start(bf16[64,1152]{1,0:T(8,128)(2,1)} %sum_terms.41), channel_id=1, source_target_pairs={{0,8},{1,9},{2,10},{3,11},{4,12},{5,13},{6,14},{7,15},{8,0},{9,1},... | collective-permute-start | bytes 442376 | tf_op jit(solution)/shard_map/ppermute | solution.py:947
  448.9 10.7 %collective-permute-start.34 = (bf16[64,1024]{1,0:T(8,128)(2,1)}, bf16[64,1024]{1,0:T(8,128)(2,1)S(1)}, u32[]{:S(2)}, u32[]{:S(2)}) collective-permute-start(bf16[64,1024]{1,0:T(8,128)(2,1)} %sum_terms.43), channel_id=1, source_target_pairs={{0,8},{1,9},{2,10},{3,11},{4,12},{5,13},{6,14},{7,15},{8,0},{9,1},... | collective-permute-start | bytes 393224 | tf_op jit(solution)/shard_map/ppermute | solution.py:947
  452.7 5.5 %collective-permute-start.35 = (f32[7,128]{1,0:T(8,128)S(1)}, f32[7,128]{1,0:T(8,128)S(1)}, u32[]{:S(2)}, u32[]{:S(2)}) collective-permute-start(f32[7,128]{1,0:T(8,128)S(1)} %slice.73), channel_id=1, source_target_pairs={{16,0},{17,1},{18,2},{19,3},{20,4},{21,5},{22,6},{23,7},{24,8},{25... | collective-permute-start | bytes 10760 | tf_op jit(solution)/shard_map/ppermute | solution.py:1001
  (34 other events, 296.1 us)

commit v5 on v4

--- a/solution.py
+++ b/solution.py
@@ -23,7 +23,8 @@
 VMEM = 62 * 2**20
 SMALL = 10**6
 LARGE = 10**11
-LESS = 40 * 2**20
+BOTH, FIRST, SECOND = range(3)
+LESS = 16 * 2**20
 
 
 def nn(a, b):
@@ -69,9 +70,17 @@
     return active, picked
 
 
-def forward_kernel(slot, plan, aliased, *refs):
-    spans, norms, vectors, feat, recv, w_in, w_out, w_up, w_down = refs[:9]
-    refs = refs[9 + aliased :]
+def early_rows(rows):
+    return 3 * rows // 4
+
+
+def forward_kernel(slot, plan, stage, aliased, pieces, *refs):
+    starts, ends = stage != SECOND, stage != FIRST
+    spans, norms, vectors, feat, w_in, w_out, w_up, w_down = refs[:8]
+    recv = refs[8 : 8 + pieces]
+    refs = refs[8 + pieces :]
+    kept = refs[:aliased]
+    refs = refs[aliased:]
     z_out, squares_out = refs[:2]
     s_x, s_a, s_qkv, s_c, s_l, s_h, s_b, s_g, s_d, s_p, layers = refs[2:13]
     (v_in, v_out, v_up, v_down, v_x, v_a, v_qkv, v_c, v_l, v_h, v_b, v_g, v_d, v_p, v_bias, v_acc, v_z,
@@ -90,16 +99,21 @@
 
     @pl.when(active)
     def _():
-        length = spans[picked, 0]
+        length = spans[picked]
         causal = first
 
-        @pl.when(first)
-        def _():
-            pltpu.make_async_copy(feat.at[picked, 0], v_x, sem_x.at[0]).start()
-
-        @pl.when(jnp.logical_not(first))
-        def _():
-            pltpu.make_async_copy(recv, v_x, sem_x.at[0]).start()
+        loaded = pltpu.make_async_copy(feat.at[picked, 0], v_x, sem_x.at[0])
+        if starts:
+            pl.when(first)(loaded.start)
+
+            @pl.when(jnp.logical_not(first))
+            def _():
+                at = 0
+                for piece in recv:
+                    pltpu.make_async_copy(
+                        piece, v_x.at[pl.ds(at, piece.shape[0])], sem_x.at[0]
+                    ).start()
+                    at += piece.shape[0]
 
         def column(source, target, index, size):
             def at(i):
@@ -117,25 +131,10 @@
         in_copy = column(w_in, v_in, 0, WIDE)
         out_copy = column(w_out, v_out, 3, WIDE)
         up_copy = column(w_up, v_up, 4, BROAD)
-        for i in range(3):
-            in_copy(i).start()
-
-        def bias_rows(i):
-            at = part(i, 128)
-            query = lax.broadcasted_iota(jnp.int32, (128, rows), 0) + i * 128
-            key = lax.broadcasted_iota(jnp.int32, (128, rows), 1)
-            open_ = (key < length) & ((key <= query) | jnp.logical_not(causal))
-            v_bias[at, :] = jnp.where(open_, 0.0, big_negative)
-
-        loop(rows // 128, bias_rows)
-        pltpu.make_async_copy(recv, v_x, sem_x.at[0]).wait()
-
-        def first_norm(i):
-            at = part(i, 64)
-            normed, _ = row_stats(v_x[at, :].astype(f32))
-            v_a[at, :] = (normed * norm(0) + norm(1)).astype(bf16)
-
-        loop(rows // 64, first_norm, 2)
+        if starts:
+            for i in range(3):
+                in_copy(i).start()
+
         outs = []
 
         def send(source, target, index):
@@ -143,22 +142,13 @@
             copy.start()
             outs.append(copy)
 
-        send(v_x, s_x.at[here], 0)
-        send(v_a, s_a.at[here], 1)
-        def project(i):
-            in_copy(i).wait()
-            at = part(i, WIDE)
-            shift = vectors[:, pl.ds(pl.multiple_of((4 + i // 2) * width, width), width)]
-            tile = nn(v_a[...], v_in[:, at]) + jnp.where(i == 1, 0.0, shift)
-            v_qkv[:, at] = tile.astype(bf16)
-
-        loop(3 * width // WIDE, project)
-        out_copy(0).start()
-        for i in range(hidden // BROAD):
-            up_copy(i).start()
-            down_copy(i).start()
-        send(v_qkv, s_qkv.at[here], 2)
-        lane = lax.broadcasted_iota(jnp.int32, (1, GROUP), 1) // HEAD
+        valid = lambda i, n: (lax.broadcasted_iota(jnp.int32, (n, 1), 0) + i * n < length).astype(f32)
+
+        def square(values, mask):
+            return jnp.sum((values * values * mask).reshape(-1, 8, width), axis=0)
+
+        nothing = jnp.zeros((8, width), f32)
+        sums_one = (nothing, nothing)
         groups = width // GROUP
 
         def p_copy(i):
@@ -166,104 +156,151 @@
                 v_p.at[i % 2], s_p.at[slot, pl.ds(i * 4, 4)], sem_p.at[i % 2]
             )
 
-        def attend(i):
-            at = part(i, GROUP)
-            query = v_qkv[:, at]
-            key = v_qkv[:, pl.ds(pl.multiple_of(width + i * GROUP, GROUP), GROUP)]
-            value = v_qkv[:, pl.ds(pl.multiple_of(2 * width + i * GROUP, GROUP), GROUP)]
-
-            @pl.when(i >= 2)
-            def _():
-                p_copy(i - 2).wait()
-
-            half = rows // 2
-
-            def rows_part(r, keys):
-                picked_rows = slice(r * half, (r + 1) * half)
-                scaled = query[picked_rows] * score_scale
-                total = jnp.zeros((half, GROUP), f32)
-                sums = jnp.ones((half, GROUP), f32)
-                for h in range(4):
-                    masked = jnp.where(lane == h, scaled, 0).astype(bf16)
-                    scores = nt(masked, key[:keys]) + v_bias[picked_rows, :keys]
-                    top = jnp.max(scores, axis=-1, keepdims=True)
-                    raised = jnp.exp(scores - top).astype(bf16)
-                    v_p[i % 2, h, picked_rows, :keys] = raised
-                    if keys < rows:
-                        v_p[i % 2, h, picked_rows, keys:] = jnp.zeros((half, rows - keys), bf16)
-                    product = nn(raised, jnp.where(lane == h, value[:keys], 1).astype(bf16))
-                    total = jnp.where(lane == h, product, total)
-                    sums = jnp.where(lane == (h ^ 1), product, sums)
-                inverse = 1.0 / jnp.concatenate(
-                    [pltpu.roll(sums[:, k : k + 128], HEAD, 1) for k in (0, 128)], axis=1
-                )
-                v_l[picked_rows, at] = inverse
-                v_c[picked_rows, at] = (total * inverse).astype(bf16)
-
-            @pl.when(causal)
-            def _():
-                rows_part(0, half)
-                rows_part(1, rows)
-
-            @pl.when(jnp.logical_not(causal))
-            def _():
-                rows_part(0, rows)
-                rows_part(1, rows)
-
-            p_copy(i).start()
-
-        loop(groups, attend)
-        send(v_c, s_c.at[here], 8)
-        send(v_l, s_l.at[here], 9)
-        out_copy(0).wait()
-        def mix(i):
-            at = part(i, WIDE)
-            v_acc[:, at] = nn(v_c[...], v_out[:, at]) + bias(6)
-
-        loop(width // WIDE, mix)
-
-        valid = lambda i, n: (lax.broadcasted_iota(jnp.int32, (n, 1), 0) + i * n < length).astype(f32)
-
-        def square(values, mask):
-            return jnp.sum((values * values * mask).reshape(-1, 8, width), axis=0)
-
-        def second_norm(i, carry):
-            at = part(i, 64)
-            branch = v_acc[at, :]
-            middle = v_x[at, :].astype(f32) + branch
-            v_h[at, :] = middle
-            normed, _ = row_stats(middle)
-            v_b[at, :] = (normed * norm(2) + norm(3)).astype(bf16)
-            v_acc[at, :] = jnp.broadcast_to(bias(7), (64, width))
-            mask = valid(i, 64)
-            return (carry[0] + square(middle, mask), carry[1] + square(branch, mask))
-
-        nothing = jnp.zeros((8, width), f32)
-        sums_one = (nothing, nothing)
-        sums_one = lax.fori_loop(0, rows // 64, second_norm, sums_one, unroll=2)
-        send(v_h, s_h.at[here], 3)
-        send(v_b, s_b.at[here], 4)
+        def start_feed():
+            for i in range(hidden // BROAD):
+                up_copy(i).start()
+                down_copy(i).start()
+
+        half = rows // 2
+        low = early_rows(rows) if stage == SECOND else 0
+        high = early_rows(rows) if stage == FIRST else rows
+        these = slice(low, high)
+        count = high - low
+        there = pl.ds(slot * rows + low, count)
+        if stage == SECOND:
+            start_feed()
+            entries = [
+                pltpu.make_async_copy(kept[5].at[there], v_h.at[pl.ds(low, count)], sem_o.at[0]),
+                pltpu.make_async_copy(kept[6].at[there], v_b.at[pl.ds(low, count)], sem_o.at[1]),
+            ]
+            for copy in entries:
+                copy.start()
+            for copy in entries:
+                copy.wait()
+            v_acc[these, :] = jnp.broadcast_to(bias(7), (count, width))
+        if starts:
+            def bias_rows(i):
+                at = part(i, 128)
+                query = lax.broadcasted_iota(jnp.int32, (128, rows), 0) + i * 128
+                key = lax.broadcasted_iota(jnp.int32, (128, rows), 1)
+                open_ = (key < length) & ((key <= query) | jnp.logical_not(causal))
+                v_bias[at, :] = jnp.where(open_, 0.0, big_negative)
+
+            loop(rows // 128, bias_rows)
+            loaded.wait()
+
+            def first_norm(i):
+                at = part(i, 64)
+                normed, _ = row_stats(v_x[at, :].astype(f32))
+                v_a[at, :] = (normed * norm(0) + norm(1)).astype(bf16)
+
+            loop(rows // 64, first_norm, 2)
+            send(v_x, s_x.at[here], 0)
+            send(v_a, s_a.at[here], 1)
+            def project(i):
+                in_copy(i).wait()
+                at = part(i, WIDE)
+                shift = vectors[:, pl.ds(pl.multiple_of((4 + i // 2) * width, width), width)]
+                tile = nn(v_a[...], v_in[:, at]) + jnp.where(i == 1, 0.0, shift)
+                v_qkv[:, at] = tile.astype(bf16)
+
+            loop(3 * width // WIDE, project)
+            out_copy(0).start()
+            start_feed()
+            send(v_qkv, s_qkv.at[here], 2)
+            lane = lax.broadcasted_iota(jnp.int32, (1, GROUP), 1) // HEAD
+
+            def attend(i):
+                at = part(i, GROUP)
+                query = v_qkv[:, at]
+                key = v_qkv[:, pl.ds(pl.multiple_of(width + i * GROUP, GROUP), GROUP)]
+                value = v_qkv[:, pl.ds(pl.multiple_of(2 * width + i * GROUP, GROUP), GROUP)]
+
+                @pl.when(i >= 2)
+                def _():
+                    p_copy(i - 2).wait()
+
+                half = rows // 2
+
+                def rows_part(r, keys):
+                    picked_rows = slice(r * half, (r + 1) * half)
+                    scaled = query[picked_rows] * score_scale
+                    total = jnp.zeros((half, GROUP), f32)
+                    sums = jnp.ones((half, GROUP), f32)
+                    for h in range(4):
+                        masked = jnp.where(lane == h, scaled, 0).astype(bf16)
+                        scores = nt(masked, key[:keys]) + v_bias[picked_rows, :keys]
+                        top = jnp.max(scores, axis=-1, keepdims=True)
+                        raised = jnp.exp(scores - top).astype(bf16)
+                        v_p[i % 2, h, picked_rows, :keys] = raised
+                        if keys < rows:
+                            v_p[i % 2, h, picked_rows, keys:] = jnp.zeros((half, rows - keys), bf16)
+                        product = nn(raised, jnp.where(lane == h, value[:keys], 1).astype(bf16))
+                        total = jnp.where(lane == h, product, total)
+                        sums = jnp.where(lane == (h ^ 1), product, sums)
+                    inverse = 1.0 / jnp.concatenate(
+                        [pltpu.roll(sums[:, k : k + 128], HEAD, 1) for k in (0, 128)], axis=1
+                    )
+                    v_l[picked_rows, at] = inverse
+                    v_c[picked_rows, at] = (total * inverse).astype(bf16)
+
+                @pl.when(causal)
+                def _():
+                    rows_part(0, half)
+                    rows_part(1, rows)
+
+                @pl.when(jnp.logical_not(causal))
+                def _():
+                    rows_part(0, rows)
+                    rows_part(1, rows)
+
+                p_copy(i).start()
+
+            loop(groups, attend)
+            send(v_c, s_c.at[here], 8)
+            send(v_l, s_l.at[here], 9)
+            out_copy(0).wait()
+            def mix(i):
+                at = part(i, WIDE)
+                v_acc[:, at] = nn(v_c[...], v_out[:, at]) + bias(6)
+
+            loop(width // WIDE, mix)
+
+            def second_norm(i, carry):
+                at = part(i, 64)
+                branch = v_acc[at, :]
+                middle = v_x[at, :].astype(f32) + branch
+                v_h[at, :] = middle
+                normed, _ = row_stats(middle)
+                v_b[at, :] = (normed * norm(2) + norm(3)).astype(bf16)
+                v_acc[at, :] = jnp.broadcast_to(bias(7), (64, width))
+                mask = valid(i, 64)
+                return (carry[0] + square(middle, mask), carry[1] + square(branch, mask))
+
+            sums_one = lax.fori_loop(0, rows // 64, second_norm, sums_one, unroll=2)
+            send(v_h, s_h.at[here], 3)
+            send(v_b, s_b.at[here], 4)
 
         def feed(i):
             up_copy(i).wait()
             down_copy(i).wait()
             at = part(i, BROAD)
             shift = vectors[:, pl.ds(pl.multiple_of(8 * width + i * BROAD, BROAD), BROAD)]
-            act, slope = gate(nn(v_b[...], v_up[:, at]) + shift)
+            act, slope = gate(nn(v_b[these, :], v_up[:, at]) + shift)
             act = act.astype(bf16)
-            v_g[:, at] = act
-            v_d[:, at] = slope.astype(bf16)
-            v_acc[...] += nn(act, v_down[at, :])
+            v_g[these, at] = act
+            v_d[these, at] = slope.astype(bf16)
+            v_acc[these, :] += nn(act, v_down[at, :])
             g_copy(i).start()
             d_copy(i).start()
 
         def g_copy(i):
             at = part(i, BROAD)
-            return pltpu.make_async_copy(v_g.at[:, at], s_g.at[here, at], sem_g.at[i])
+            return pltpu.make_async_copy(v_g.at[pl.ds(low, count), at], s_g.at[there, at], sem_g.at[i])
 
         def d_copy(i):
             at = part(i, BROAD)
-            return pltpu.make_async_copy(v_d.at[:, at], s_d.at[here, at], sem_d.at[i])
+            return pltpu.make_async_copy(v_d.at[pl.ds(low, count), at], s_d.at[there, at], sem_d.at[i])
 
         loop(hidden // BROAD, feed)
 
@@ -275,10 +312,9 @@
             mask = valid(i, 64)
             return (carry[0] + square(output, mask), carry[1] + square(branch, mask))
 
-        sums_two = (nothing, nothing)
-        sums_two = lax.fori_loop(0, rows // 64, finish, sums_two, unroll=2)
-        send(v_z, z_out, 7)
-        send(v_z, layers.at[0, picked, 0], 5)
+        sums_two = lax.fori_loop(low // 64, high // 64, finish, (nothing, nothing), unroll=2)
+        send(v_z.at[pl.ds(low, count)], z_out, 7)
+        send(v_z.at[pl.ds(low, count)], layers.at[0, picked, 0, pl.ds(low, count)], 5)
         for k, value in enumerate((sums_one[0], sums_two[0], sums_one[1], sums_two[1])):
             squares_out[k] = value
         for copy in outs:
@@ -286,8 +322,9 @@
         for i in range(hidden // BROAD):
             g_copy(i).wait()
             d_copy(i).wait()
-        p_copy(groups - 2).wait()
-        p_copy(groups - 1).wait()
+        if starts:
+            p_copy(groups - 2).wait()
+            p_copy(groups - 1).wait()
 
     @pl.when(jnp.logical_not(active))
     def _():
@@ -311,18 +348,19 @@
     ]
 
 
-def forward_call(slot, plan, spans, norms, vectors, feat, recv, weights, stash=()):
-    rows, width = recv.shape
+def forward_call(slot, plan, stage, spans, norms, vectors, feat, recv, weights, stash=()):
+    rows, width = feat.shape[2:]
+    count = {BOTH: rows, FIRST: early_rows(rows), SECOND: rows - early_rows(rows)}[stage]
     hidden = weights[2].shape[1]
     any_ = pl.BlockSpec(memory_space=pl.ANY)
     vm = pl.BlockSpec(memory_space=pltpu.VMEM)
     shapes = stash_shapes(rows, width, hidden)
     results = pl.pallas_call(
-        functools.partial(forward_kernel, slot, plan, len(stash)),
-        in_specs=[pl.BlockSpec(memory_space=pltpu.SMEM), vm, vm] + [any_] * (6 + len(stash)),
+        functools.partial(forward_kernel, slot, plan, stage, len(stash), len(recv)),
+        in_specs=[pl.BlockSpec(memory_space=pltpu.SMEM), vm, vm] + [any_] * (5 + len(recv) + len(stash)),
         out_specs=[any_, vm] + [any_] * len(shapes),
-        out_shape=[jax.ShapeDtypeStruct((rows, width), bf16), jax.ShapeDtypeStruct((4, 8, width), f32)] + shapes,
-        input_output_aliases={9 + k: 2 + k for k in range(len(stash))},
+        out_shape=[jax.ShapeDtypeStruct((count, width), bf16), jax.ShapeDtypeStruct((4, 8, width), f32)] + shapes,
+        input_output_aliases={8 + len(recv) + k: 2 + k for k in range(len(stash))},
         scratch_shapes=[
             pltpu.VMEM(w.shape, bf16) for w in weights
         ] + [
@@ -349,11 +387,8 @@
         compiler_params=pltpu.CompilerParams(vmem_limit_bytes=VMEM),
         cost_estimate=pl.CostEstimate(flops=LARGE, bytes_accessed=1, transcendentals=0),
         name="layer_forward",
-    )(spans, norms, vectors, feat, recv, *weights, *stash)
+    )(spans, norms, vectors, feat, *weights, *recv, *stash)
     return results[0], results[1], results[2:]
-
-
-BOTH, FIRST, SECOND = range(3)
 
 
 def backward_kernel(slot, plan, stage, aliased, given, *refs):
@@ -392,7 +427,7 @@
 
     @pl.when(active)
     def _():
-        length = spans[picked, 0]
+        length = spans[picked]
         if stage != BOTH:
             smalls[...] = jnp.zeros_like(smalls)
 
@@ -862,7 +897,9 @@
             pltpu.SemaphoreType.DMA((max(sum(len(arrays) for arrays, _ in terms), 1), cells)),
             pltpu.SemaphoreType.DMA((cells,)),
         ],
-        compiler_params=pltpu.CompilerParams(vmem_limit_bytes=VMEM),
+        compiler_params=pltpu.CompilerParams(
+            vmem_limit_bytes=VMEM if len(free) > 1 or rows > columns // 8 else LESS
+        ),
         cost_estimate=pl.CostEstimate(flops=SMALL, bytes_accessed=1, transcendentals=0),
         name="sum_terms",
     )(*operands)
@@ -1000,18 +1037,20 @@
     def send(value, to):
         return lax.ppermute(value, "section", [(1 - to, to)])
 
-    nowhere = jnp.zeros((rows, width), bf16)
-
-    def forward(slot, plan, norms, recv, stash=()):
-        return forward_call(slot, plan, lengths, norms, vectors, features, recv, weights, stash)
+    spans = lengths[:, 0]
+
+    def forward(slot, plan, norms, recv, stash=(), stage=BOTH):
+        return forward_call(
+            slot, plan, stage, spans, norms, vectors, features, recv, weights, stash
+        )
 
     def backward(slot, plan, stage, norms, recv, stash, grads, given=()):
         return backward_call(
-            slot, plan, stage, lengths, norms, cotangent, recv, weights, stash, given, grads
+            slot, plan, stage, spans, norms, cotangent, recv, weights, stash, given, grads
         )
 
-    z_one, squares_one, stash = forward(0, (0, None), vectors, nowhere)
-    received_one = send(z_one, 1)
+    z_one, squares_one, stash = forward(0, (0, None), vectors, ())
+    received_one = (send(z_one, 1),)
     table, z_one = lax.optimization_barrier((codebook_table, z_one))
     condition_table = jnp.dot(table, adaptive_weight, preferred_element_type=f32)
     one_hot = (
@@ -1024,10 +1063,10 @@
     norms_one, norms_two = norms[:1], norms[1:]
     z_two, squares_two, stash = forward(1, (1, 0), norms_one, received_one, stash)
     received_two = send(z_two, 1)
-    grads = backward(1, (None, 0), BOTH, norms_one, nowhere, stash, {})
+    grads = backward(1, (None, 0), BOTH, norms_one, z_two, stash, {})
     smalls_one = grads["smalls"]
     back_one = send(grads["dx"], 0)
-    z_three, squares_three, stash = forward(0, (None, 1), norms_two, received_two, stash)
+    z_three, squares_three, stash = forward(0, (None, 1), norms_two, (received_two,), stash)
     grads = backward(0, (0, 1), BOTH, norms_two, back_one, stash, grads)
     smalls_two = grads["smalls"]
     back_two = send(grads["dx"], 0)

time: 472 us -> 466 us (0.987)
  waiting for transfers between devices: 111 us -> 119 us
  Pallas kernels: 283 us -> 276 us
  local copies, waits for them, and re-layouts: 20.8 us -> 15.9 us
    pallas_call x23, Pallas kernels: 54 us -> 46.1 us  [sum_call(): pl.pallas_call(kernel, in_specs=[any_] * len(operands), out_specs=any_, o...]
    ppermute x31, waiting for transfers between devices: 40.1 us -> 47.4 us  [crossed(): lax.ppermute(value, 'dp', [(i, i ^ 1 << bit) for i in range(lax.axis_size...]
    unnamed x60 -> x61, local copies, waits for them, and re-layouts: 13.8 us -> 11.7 us
  transfers between devices with their start and end apart: 36 -> 36, of which waited for: 15 -> 16; matrix products, arithmetic and copies ran while one was open for 3% -> 3% of each run, Pallas kernels for 37% -> 35%
where the time goes in v5:
time: 466 us; the launch traced here: 457 us
  Pallas kernels  276 us (59%)
  waiting for transfers between devices  119 us (26%)
  starting transfers between devices  34.9 us (7%)
  local copies, waits for them, and re-layouts  15.9 us (3%)
  matrix products  5.28 us (1%)
    pallas_call x4, Pallas kernels, backward_call(): pl.pallas_call(functools.partial(backward_kernel, slot, plan, stage, len(...  83.6 us
    pallas_call x3, Pallas kernels, forward_call(): pl.pallas_call(functools.partial(forward_kernel, slot, plan, stage, len(s...  72.2 us
    ppermute x5, waiting for transfers between devices, send(): return lax.ppermute(value, 'section', [(1 - to, to)])  71.9 us
    pallas_call x8, Pallas kernels, weight_call(): pl.pallas_call(functools.partial(weight_kernel, widths, half), grid=(heig...  59.6 us
    ppermute x31, waiting for transfers between devices, crossed(): lax.ppermute(value, 'dp', [(i, i ^ 1 << bit) for i in range(lax.axis_size...  47.4 us
    pallas_call x23, Pallas kernels, sum_call(): pl.pallas_call(kernel, in_specs=[any_] * len(operands), out_specs=any_, o...  46.1 us
    ppermute x31, starting transfers between devices, crossed(): lax.ppermute(value, 'dp', [(i, i ^ 1 << bit) for i in range(lax.axis_size...  23.3 us
    pallas_call x1, Pallas kernels, turn_call(): pl.pallas_call(functools.partial(turn_kernel, [s.shape[1] // size for s i...  14.7 us
  transfers between devices with their start and end apart: 36, of which 16 were waited for; matrix products, arithmetic and copies ran while one was open for 3% of the time, Pallas kernels for 35%

profile of v5, /device:TPU:0, one launch (start us, length us, event | category | flops | bytes accessed | tf_op | source)
XLA Modules:
  0.0 456.9 jit_solution(485869532178301371)
XLA Ops:
  0.7 31.7 %layer_forward.3 = (bf16[512,1024]{1,0:T(8,128)(2,1)}, f32[4,8,1024]{2,1,0:T(8,128)}, bf16[1024,1024]{1,0:T(8,128)(2,1)}, bf16[1024,1024]{1,0:T(8,128)(2,1)}, bf...) custom-call(s32[2]{0:T(128)} %bitcast.106, ...), custom_call_target="tpu_custom_call" | custom-call | flops 99999997952 | bytes 1 | tf_op jit(solution)/shard_map/layer_forward/pallas_call | solution.py:358
  34.3 4.6 %fusion.6 = f32[7,4096]{1,0:T(8,128)S(1)} fusion(bf16[7,1024]{1,0:T(8,128)(2,1)S(1)} %copy-done, bf16[1024,4096]{1,0:T(8,128)(2,1)} %param.20), kind=kOutput, calls=%fused_computation.22 | convolution fusion | flops 58720256 | bytes 8517632 | tf_op jit(solution)/shard_map/dot_general | solution.py:1055
  39.8 17.6 %collective-permute-done.refs_8_ = bf16[512,1024]{1,0:T(8,128)(2,1)S(1)} collective-permute-done((bf16[512,1024]{1,0:T(8,128)(2,1)}, bf16[512,1024]{1,0:T(8,128)(2,1)S(1)}, u32[]{:S(2)}, u32[]{:S(2)}) %collective-permute-start) | collective-permute-done | bytes 1048608 | tf_op jit(solution)/shard_map/ppermute | solution.py:1038
  58.3 31.7 %layer_forward.4 = (bf16[512,1024]{1,0:T(8,128)(2,1)}, f32[4,8,1024]{2,1,0:T(8,128)}, bf16[1024,1024]{1,0:T(8,128)(2,1)}, bf16[1024,1024]{1,0:T(8,128)(2,1)}, bf...) custom-call(s32[2]{0:T(128)} %bitcast.107, ...), custom_call_target="tpu_custom_call", output_to_operand_aliasing={{2}: (9, {}), {3}: (10, {}), {4}: (11, {}), {5}: (12, {}), ... | custom-call | flops 99999997952 | bytes 1 | tf_op jit(solution)/shard_map/layer_forward/pallas_call | solution.py:358
  90.0 5.7 %collective-permute-start.1 = (bf16[512,1024]{1,0:T(8,128)(2,1)}, bf16[512,1024]{1,0:T(8,128)(2,1)}, u32[]{:S(2)}, u32[]{:S(2)}) collective-permute-start(bf16[512,1024]{1,0:T(8,128)(2,1)} %get-tuple-element.220.refs_3_), channel_id=1, source_target_pairs={{0,16},{1,17},{2,18},{3,19},{4,20},{5,21},{6,22},{7,23},{8,24},{9,... | collective-permute-start | bytes 3145736 | tf_op jit(solution)/shard_map/ppermute | solution.py:1038
  98.8 18.7 %collective-permute-done.1.refs_8_ = bf16[512,1024]{1,0:T(8,128)(2,1)} collective-permute-done((bf16[512,1024]{1,0:T(8,128)(2,1)}, bf16[512,1024]{1,0:T(8,128)(2,1)}, u32[]{:S(2)}, u32[]{:S(2)}) %collective-permute-start.1) | collective-permute-done | bytes 1048608 | tf_op jit(solution)/shard_map/ppermute | solution.py:1038
  117.5 8.8 %layer_forward.5 = (bf16[512,1024]{1,0:T(8,128)(2,1)}, f32[4,8,1024]{2,1,0:T(8,128)}, bf16[1024,1024]{1,0:T(8,128)(2,1)}, bf16[1024,1024]{1,0:T(8,128)(2,1)}, bf...) custom-call(s32[2]{0:T(128)} %bitcast.109, ...), custom_call_target="tpu_custom_call", output_to_operand_aliasing={{2}: (9, {}), {3}: (10, {}), {4}: (11, {}), {5}: (12, {}), ... | custom-call | flops 99999997952 | bytes 1 | tf_op jit(solution)/shard_map/layer_forward/pallas_call | solution.py:358
  126.3 28.6 %collective-permute-done.2.refs_3_ = bf16[512,1024]{1,0:T(8,128)(2,1)S(1)} collective-permute-done((bf16[512,1024]{1,0:T(8,128)(2,1)}, bf16[512,1024]{1,0:T(8,128)(2,1)S(1)}, u32[]{:S(2)}, u32[]{:S(2)}) %collective-permute-start.2) | collective-permute-done | bytes 1048608 | tf_op jit(solution)/shard_map/ppermute | solution.py:1038
  155.8 37.2 %layer_backward.5 = (f32[12,1024]{1,0:T(8,128)}, bf16[1024,4096]{1,0:T(8,128)(2,1)}, bf16[1024,1024]{1,0:T(8,128)(2,1)}, bf16[512,1024]{1,0:T(8,128)(2,1)}, bf16...) custom-call(s32[2]{0:T(128)} %bitcast.110, ...), custom_call_target="tpu_custom_call", output_to_operand_aliasing={{1}: (15, {}), {2}: (16, {}), {4}: (17, {}), {5}: (18, {}),... | custom-call | flops 99999997952 | bytes 1 | tf_op jit(solution)/shard_map/layer_backward/pallas_call | solution.py:677
  207.1 14.7 %turn.1 = (bf16[2,512,1024]{2,1,0:T(8,128)(2,1)}, bf16[2,512,1024]{2,1,0:T(8,128)(2,1)}, bf16[2,512,1024]{2,1,0:T(8,128)(2,1)}, bf16[2,2048,1024]{2,1,0:T(8,128)(2,1)}) custom-call(bf16[1024,1024]{1,0:T(8,128)(2,1)} %get-tuple-element.251.refs_0_, bf16[1024,1024]{1,0:T(8,128)(2,1)} %get-tuple-element.252.refs_1_, ...), custom_call_target="tpu_custom_call" | custom-call | flops 1 | bytes 1 | tf_op jit(solution)/shard_map/turn/pallas_call | solution.py:750
  222.3 4.2 collective-permute-done.3.rest_0_.refs_3_
  227.5 8.7 %weight_product.8 = bf16[2048,1024]{1,0:T(8,128)(2,1)} custom-call(bf16[2,2048,1024]{2,1,0:T(8,128)(2,1)} %get-tuple-element.265.left, bf16[1024,1024]{1,0:T(8,128)(2,1)} %get-tuple-element.266.right, bf16[512,1024]{1,0:T(8,128)(2,1)} %copy-done.15), custom_call_target="tpu_custom_call" | custom-call | flops 1 | bytes 1 | tf_op jit(solution)/shard_map/weight_product/pallas_call | solution.py:804
  236.2 8.8 %weight_product.9 = bf16[2048,1024]{1,0:T(8,128)(2,1)} custom-call(bf16[2,2048,1024]{2,1,0:T(8,128)(2,1)} %get-tuple-element.265.left, bf16[1024,1024]{1,0:T(8,128)(2,1)} %get-tuple-element.266.right, bf16[512,1024]{1,0:T(8,128)(2,1)} %copy-done.15), custom_call_target="tpu_custom_call" | custom-call | flops 1 | bytes 1 | tf_op jit(solution)/shard_map/weight_product/pallas_call | solution.py:804
  245.0 3.2 sum_terms.23
  250.0 20.6 %layer_backward.6 = (f32[12,1024]{1,0:T(8,128)}, bf16[1024,4096]{1,0:T(8,128)(2,1)}, bf16[1024,1024]{1,0:T(8,128)(2,1)}, f32[512,1024]{1,0:T(8,128)}) custom-call(s32[2]{0:T(128)} %bitcast.111, f32[1,12288]{1,0:T(1,128)} %refs_1_.5, bf16[2,1,512,1024]{3,2,1,0:T(8,128)(2,1)} %refs_2_.13, ...), custom_call_target="tpu_custom_call", output_to_operand_aliasing={{1}: (15, {}), {2}: (16, {})} | custom-call | flops 99999997952 | bytes 1 | tf_op jit(solution)/shard_map/layer_backward/pallas_call | solution.py:677
  270.5 9.7 %weight_product.10 = (bf16[512,1024]{1,0:T(8,128)(2,1)}, bf16[512,1024]{1,0:T(8,128)(2,1)}, bf16[512,1024]{1,0:T(8,128)(2,1)}, bf16[512,1024]{1,0:T(8,128)(2,1)}) custom-call(bf16[2,512,1024]{2,1,0:T(8,128)(2,1)} %get-tuple-element.284.left, bf16[1024,4096]{1,0:T(8,128)(2,1)} %get-tuple-element.285.right), custom_call_target="tpu_custom_call" | custom-call | flops 1 | bytes 1 | tf_op jit(solution)/shard_map/weight_product/pallas_call | solution.py:804
  281.4 8.8 %weight_product.11 = bf16[512,4096]{1,0:T(8,128)(2,1)} custom-call(bf16[2,512,1024]{2,1,0:T(8,128)(2,1)} %get-tuple-element.284.left, bf16[1024,4096]{1,0:T(8,128)(2,1)} %get-tuple-element.285.right), custom_call_target="tpu_custom_call" | custom-call | flops 1 | bytes 1 | tf_op jit(solution)/shard_map/weight_product/pallas_call | solution.py:804
  291.2 3.4 sum_terms.24
  296.6 2.9 sum_terms.25
  301.3 4.2 weight_product.12
  305.5 4.2 weight_product.13
  309.7 24.1 %layer_backward.7 = (f32[12,1024]{1,0:T(8,128)}, bf16[512,1024]{1,0:T(8,128)(2,1)}, bf16[1024,3072]{1,0:T(8,128)(2,1)}, bf16[1,2,1,512,1024]{4,3,2,1,0:T(8,128)(2,1)}) custom-call(s32[2]{0:T(128)} %bitcast.112, f32[1,12288]{1,0:T(1,128)} %refs_1_.5, bf16[2,1,512,1024]{3,2,1,0:T(8,128)(2,1)} %refs_2_.13, ...), custom_call_target="tpu_custom_call", output_to_operand_aliasing={{2}: (17, {}), {3}: (18, {})} | custom-call | flops 99999997952 | bytes 1 | tf_op jit(solution)/shard_map/layer_backward/pallas_call | solution.py:677
  337.4 7.9 %weight_product.14 = (bf16[512,1024]{1,0:T(8,128)(2,1)}, bf16[512,1024]{1,0:T(8,128)(2,1)}, bf16[512,1024]{1,0:T(8,128)(2,1)}) custom-call(bf16[2,512,1024]{2,1,0:T(8,128)(2,1)} %get-tuple-element.313.left, bf16[1024,3072]{1,0:T(8,128)(2,1)} %get-tuple-element.314.right), custom_call_target="tpu_custom_call" | custom-call | flops 1 | bytes 1 | tf_op jit(solution)/shard_map/weight_product/pallas_call | solution.py:804
  347.0 7.4 %weight_product.15 = bf16[512,3072]{1,0:T(8,128)(2,1)} custom-call(bf16[2,512,1024]{2,1,0:T(8,128)(2,1)} %get-tuple-element.313.left, bf16[1024,3072]{1,0:T(8,128)(2,1)} %get-tuple-element.314.right), custom_call_target="tpu_custom_call" | custom-call | flops 1 | bytes 1 | tf_op jit(solution)/shard_map/weight_product/pallas_call | solution.py:804
  375.8 10.7 %collective-permute-done.20.refs_4_ = bf16[256,1024]{1,0:T(8,128)(2,1)} collective-permute-done((bf16[256,1024]{1,0:T(8,128)(2,1)}, bf16[256,1024]{1,0:T(8,128)(2,1)}, u32[]{:S(2)}, u32[]{:S(2)}) %collective-permute-start.20) | collective-permute-done | bytes 524320 | tf_op jit(solution)/shard_map/ppermute | solution.py:984
  386.6 3.0 sum_terms.32
  389.6 3.2 collective-permute-done.19.refs_4_
  399.5 10.1 %collective-permute-done.27.refs_4_ = bf16[2,64,2048]{2,1,0:T(8,128)(2,1)} collective-permute-done((bf16[2,64,2048]{2,1,0:T(8,128)(2,1)}, bf16[2,64,2048]{2,1,0:T(8,128)(2,1)}, u32[]{:S(2)}, u32[]{:S(2)}) %collective-permute-start.27) | collective-permute-done | bytes 524320 | tf_op jit(solution)/shard_map/ppermute | solution.py:984
  412.7 4.1 collective-permute-done.25.refs_5_
  419.1 7.3 %collective-permute-done.24.refs_4_ = bf16[2,64,2048]{2,1,0:T(8,128)(2,1)S(1)} collective-permute-done((bf16[2,64,2048]{2,1,0:T(8,128)(2,1)S(1)}, bf16[2,64,2048]{2,1,0:T(8,128)(2,1)S(1)}, u32[]{:S(2)}, u32[]{:S(2)}) %collective-permute-start.24) | collective-permute-done | bytes 524320 | tf_op jit(solution)/shard_map/ppermute | solution.py:984
  434.2 2.9 collective-permute-start.32
  437.7 4.3 collective-permute-done.28.refs_5_
  (186 shorter events, 90.8 us)
Async XLA Ops:
  32.4 24.9 %collective-permute-start = (bf16[512,1024]{1,0:T(8,128)(2,1)}, bf16[512,1024]{1,0:T(8,128)(2,1)S(1)}, u32[]{:S(2)}, u32[]{:S(2)}) collective-permute-start(bf16[512,1024]{1,0:T(8,128)(2,1)} %get-tuple-element.207), channel_id=1, source_target_pairs={{0,16},{1,17},{2,18},{3,19},{4,20},{5,21},{6,22},{7,23},{8,24},{9,... | collective-permute-start | bytes 3145736 | tf_op jit(solution)/shard_map/ppermute | solution.py:1038
  90.0 27.5 %collective-permute-start.1 = (bf16[512,1024]{1,0:T(8,128)(2,1)}, bf16[512,1024]{1,0:T(8,128)(2,1)}, u32[]{:S(2)}, u32[]{:S(2)}) collective-permute-start(bf16[512,1024]{1,0:T(8,128)(2,1)} %get-tuple-element.220.refs_3_), channel_id=1, source_target_pairs={{0,16},{1,17},{2,18},{3,19},{4,20},{5,21},{6,22},{7,23},{8,24},{9,... | collective-permute-start | bytes 3145736 | tf_op jit(solution)/shard_map/ppermute | solution.py:1038
  97.5 57.4 %collective-permute-start.2 = (bf16[512,1024]{1,0:T(8,128)(2,1)}, bf16[512,1024]{1,0:T(8,128)(2,1)S(1)}, u32[]{:S(2)}, u32[]{:S(2)}) collective-permute-start(bf16[512,1024]{1,0:T(8,128)(2,1)} %get-tuple-element.233), channel_id=1, source_target_pairs={{16,0},{17,1},{18,2},{19,3},{20,4},{21,5},{22,6},{23,7},{24,8},{25... | collective-permute-start | bytes 3145736 | tf_op jit(solution)/shard_map/ppermute | solution.py:1038
  193.0 33.5 %collective-permute-start.3 = (bf16[512,1024]{1,0:T(8,128)(2,1)}, bf16[512,1024]{1,0:T(8,128)(2,1)S(1)}, u32[]{:S(2)}, u32[]{:S(2)}) collective-permute-start(bf16[512,1024]{1,0:T(8,128)(2,1)} %get-tuple-element.246), channel_id=1, source_target_pairs={{16,0},{17,1},{18,2},{19,3},{20,4},{21,5},{22,6},{23,7},{24,8},{25... | collective-permute-start | bytes 3145736 | tf_op jit(solution)/shard_map/ppermute | solution.py:1038
  204.2 17.6 %collective-permute-start.7 = (f32[128]{0:T(128)S(1)}, f32[128]{0:T(128)S(1)}, u32[]{:S(2)}, u32[]{:S(2)}) collective-permute-start(f32[128]{0:T(128)S(1)} %add.60), channel_id=1, source_target_pairs={{0,8},{1,9},{2,10},{3,11},{4,12},{5,13},{6,14},{7,15},{8,0},{9,1},... | collective-permute-start | bytes 1544 | tf_op jit(solution)/shard_map/ppermute | solution.py:984
  236.2 8.8 %collective-permute-start.8 = (bf16[2048,1024]{1,0:T(8,128)(2,1)}, bf16[2048,1024]{1,0:T(8,128)(2,1)}, u32[]{:S(2)}, u32[]{:S(2)}) collective-permute-start(bf16[2048,1024]{1,0:T(8,128)(2,1)} %weight_product.8), channel_id=1, source_target_pairs={{0,1},{1,0},{2,3},{3,2},{4,5},{5,4},{6,7},{7,6},{8,9},{9,8},{10,11... | collective-permute-start | bytes 12582920 | tf_op jit(solution)/shard_map/ppermute | solution.py:984
  248.2 48.4 %collective-permute-start.9 = (bf16[2,2,256,1024]{3,2,1,0:T(8,128)(2,1)}, bf16[2,2,256,1024]{3,2,1,0:T(8,128)(2,1)}, u32[]{:S(2)}, u32[]{:S(2)}) collective-permute-start(bf16[2,2,256,1024]{3,2,1,0:T(8,128)(2,1)} %sum_terms.23), channel_id=1, source_target_pairs={{0,2},{1,3},{2,0},{3,1},{4,6},{5,7},{6,4},{7,5},{8,10},{9,11},{10,... | collective-permute-start | bytes 6291464 | tf_op jit(solution)/shard_map/ppermute | solution.py:984
  280.3 9.9 %collective-permute-start.10 = (bf16[512,1024]{1,0:T(8,128)(2,1)}, bf16[512,1024]{1,0:T(8,128)(2,1)S(1)}, u32[]{:S(2)}, u32[]{:S(2)}) collective-permute-start(bf16[512,1024]{1,0:T(8,128)(2,1)} %get-tuple-element.280), channel_id=1, source_target_pairs={{0,1},{1,0},{2,3},{3,2},{4,5},{5,4},{6,7},{7,6},{8,9},{9,8},{10,11... | collective-permute-start | bytes 3145736 | tf_op jit(solution)/shard_map/ppermute | solution.py:984
  280.5 9.7 %collective-permute-start.11 = (bf16[512,1024]{1,0:T(8,128)(2,1)}, bf16[512,1024]{1,0:T(8,128)(2,1)}, u32[]{:S(2)}, u32[]{:S(2)}) collective-permute-start(bf16[512,1024]{1,0:T(8,128)(2,1)} %get-tuple-element.281), channel_id=1, source_target_pairs={{0,1},{1,0},{2,3},{3,2},{4,5},{5,4},{6,7},{7,6},{8,9},{9,8},{10,11... | collective-permute-start | bytes 3145736 | tf_op jit(solution)/shard_map/ppermute | solution.py:984
  280.8 9.4 %collective-permute-start.12 = (bf16[512,1024]{1,0:T(8,128)(2,1)}, bf16[512,1024]{1,0:T(8,128)(2,1)}, u32[]{:S(2)}, u32[]{:S(2)}) collective-permute-start(bf16[512,1024]{1,0:T(8,128)(2,1)} %get-tuple-element.282), channel_id=1, source_target_pairs={{0,1},{1,0},{2,3},{3,2},{4,5},{5,4},{6,7},{7,6},{8,9},{9,8},{10,11... | collective-permute-start | bytes 3145736 | tf_op jit(solution)/shard_map/ppermute | solution.py:984
  281.0 9.2 %collective-permute-start.13 = (bf16[512,1024]{1,0:T(8,128)(2,1)}, bf16[512,1024]{1,0:T(8,128)(2,1)}, u32[]{:S(2)}, u32[]{:S(2)}) collective-permute-start(bf16[512,1024]{1,0:T(8,128)(2,1)} %get-tuple-element.283), channel_id=1, source_target_pairs={{0,1},{1,0},{2,3},{3,2},{4,5},{5,4},{6,7},{7,6},{8,9},{9,8},{10,11... | collective-permute-start | bytes 3145736 | tf_op jit(solution)/shard_map/ppermute | solution.py:984
  294.6 65.1 %collective-permute-start.18 = (bf16[2,2,64,4096]{3,2,1,0:T(8,128)(2,1)}, bf16[2,2,64,4096]{3,2,1,0:T(8,128)(2,1)}, u32[]{:S(2)}, u32[]{:S(2)}) collective-permute-start(bf16[2,2,64,4096]{3,2,1,0:T(8,128)(2,1)} %sum_terms.24), channel_id=1, source_target_pairs={{0,2},{1,3},{2,0},{3,1},{4,6},{5,7},{6,4},{7,5},{8,10},{9,11},{10,... | collective-permute-start | bytes 6291464 | tf_op jit(solution)/shard_map/ppermute | solution.py:984
  299.5 34.3 %collective-permute-start.14 = (bf16[2,256,1024]{2,1,0:T(8,128)(2,1)}, bf16[2,256,1024]{2,1,0:T(8,128)(2,1)S(1)}, u32[]{:S(2)}, u32[]{:S(2)}) collective-permute-start(bf16[2,256,1024]{2,1,0:T(8,128)(2,1)} %sum_terms.25), channel_id=1, source_target_pairs={{0,4},{1,5},{2,6},{3,7},{4,0},{5,1},{6,2},{7,3},{8,12},{9,13},{10,... | collective-permute-start | bytes 3145736 | tf_op jit(solution)/shard_map/ppermute | solution.py:984
  345.4 9.0 %collective-permute-start.15 = (bf16[512,1024]{1,0:T(8,128)(2,1)}, bf16[512,1024]{1,0:T(8,128)(2,1)}, u32[]{:S(2)}, u32[]{:S(2)}) collective-permute-start(bf16[512,1024]{1,0:T(8,128)(2,1)} %get-tuple-element.310), channel_id=1, source_target_pairs={{0,1},{1,0},{2,3},{3,2},{4,5},{5,4},{6,7},{7,6},{8,9},{9,8},{10,11... | collective-permute-start | bytes 3145736 | tf_op jit(solution)/shard_map/ppermute | solution.py:984
  345.4 9.0 %collective-permute-start.16 = (bf16[512,1024]{1,0:T(8,128)(2,1)}, bf16[512,1024]{1,0:T(8,128)(2,1)}, u32[]{:S(2)}, u32[]{:S(2)}) collective-permute-start(bf16[512,1024]{1,0:T(8,128)(2,1)} %get-tuple-element.311), channel_id=1, source_target_pairs={{0,1},{1,0},{2,3},{3,2},{4,5},{5,4},{6,7},{7,6},{8,9},{9,8},{10,11... | collective-permute-start | bytes 3145736 | tf_op jit(solution)/shard_map/ppermute | solution.py:984
  346.2 23.1 %collective-permute-start.22 = (bf16[512,1024]{1,0:T(8,128)(2,1)}, bf16[512,1024]{1,0:T(8,128)(2,1)}, u32[]{:S(2)}, u32[]{:S(2)}) collective-permute-start(bf16[512,1024]{1,0:T(8,128)(2,1)} %get-tuple-element.312), channel_id=1, source_target_pairs={{0,1},{1,0},{2,3},{3,2},{4,5},{5,4},{6,7},{7,6},{8,9},{9,8},{10,11... | collective-permute-start | bytes 3145736 | tf_op jit(solution)/shard_map/ppermute | solution.py:984
  346.3 25.9 %collective-permute-start.21 = (bf16[512,1024]{1,0:T(8,128)(2,1)}, bf16[512,1024]{1,0:T(8,128)(2,1)}, u32[]{:S(2)}, u32[]{:S(2)}) collective-permute-start(bf16[512,1024]{1,0:T(8,128)(2,1)} %weight_product.12), channel_id=1, source_target_pairs={{0,1},{1,0},{2,3},{3,2},{4,5},{5,4},{6,7},{7,6},{8,9},{9,8},{10,11... | collective-permute-start | bytes 3145736 | tf_op jit(solution)/shard_map/ppermute | solution.py:984
  356.9 39.6 %collective-permute-start.17 = (bf16[2,2,64,2048]{3,2,1,0:T(8,128)(2,1)}, bf16[2,2,64,2048]{3,2,1,0:T(8,128)(2,1)}, u32[]{:S(2)}, u32[]{:S(2)}) collective-permute-start(bf16[2,2,64,2048]{3,2,1,0:T(8,128)(2,1)} %sum_terms.27), channel_id=1, source_target_pairs={{0,2},{1,3},{2,0},{3,1},{4,6},{5,7},{6,4},{7,5},{8,10},{9,11},{10,... | collective-permute-start | bytes 3145736 | tf_op jit(solution)/shard_map/ppermute | solution.py:984
  359.7 6.9 %collective-permute-start.23 = (bf16[2,2,2,64,128]{4,3,2,1,0:T(8,128)(2,1)S(1)}, bf16[2,2,2,64,128]{4,3,2,1,0:T(8,128)(2,1)S(1)}, u32[]{:S(2)}, u32[]{:S(2)}) collective-permute-start(bf16[2,2,2,64,128]{4,3,2,1,0:T(8,128)(2,1)S(1)} %get-tuple-element.424), channel_id=1, source_target_pairs={{0,1},{1,0},{2,3},{3,2},{4,5},{5,4},{6,7},{7,6},{8,9},{9,8},{10,11... | collective-permute-start | bytes 393224 | tf_op jit(solution)/shard_map/ppermute | solution.py:984
  359.7 26.9 %collective-permute-start.20 = (bf16[256,1024]{1,0:T(8,128)(2,1)}, bf16[256,1024]{1,0:T(8,128)(2,1)}, u32[]{:S(2)}, u32[]{:S(2)}) collective-permute-start(bf16[256,1024]{1,0:T(8,128)(2,1)} %sum_terms.26), channel_id=1, source_target_pairs={{0,8},{1,9},{2,10},{3,11},{4,12},{5,13},{6,14},{7,15},{8,0},{9,1},... | collective-permute-start | bytes 1572872 | tf_op jit(solution)/shard_map/ppermute | solution.py:984
  366.6 26.2 %collective-permute-start.19 = (bf16[2,64,2048]{2,1,0:T(8,128)(2,1)}, bf16[2,64,2048]{2,1,0:T(8,128)(2,1)}, u32[]{:S(2)}, u32[]{:S(2)}) collective-permute-start(bf16[2,64,2048]{2,1,0:T(8,128)(2,1)} %sum_terms.28), channel_id=1, source_target_pairs={{0,4},{1,5},{2,6},{3,7},{4,0},{5,1},{6,2},{7,3},{8,12},{9,13},{10,... | collective-permute-start | bytes 1572872 | tf_op jit(solution)/shard_map/ppermute | solution.py:984
  371.6 39.5 %collective-permute-start.26 = (bf16[2,2,64,1152]{3,2,1,0:T(8,128)(2,1)}, bf16[2,2,64,1152]{3,2,1,0:T(8,128)(2,1)S(1)}, u32[]{:S(2)}, u32[]{:S(2)}) collective-permute-start(bf16[2,2,64,1152]{3,2,1,0:T(8,128)(2,1)} %sum_terms.30), channel_id=1, source_target_pairs={{0,2},{1,3},{2,0},{3,1},{4,6},{5,7},{6,4},{7,5},{8,10},{9,11},{10,... | collective-permute-start | bytes 1769480 | tf_op jit(solution)/shard_map/ppermute | solution.py:984
  372.2 37.4 %collective-permute-start.27 = (bf16[2,64,2048]{2,1,0:T(8,128)(2,1)}, bf16[2,64,2048]{2,1,0:T(8,128)(2,1)}, u32[]{:S(2)}, u32[]{:S(2)}) collective-permute-start(bf16[2,64,2048]{2,1,0:T(8,128)(2,1)} %copy-done.13), channel_id=1, source_target_pairs={{0,4},{1,5},{2,6},{3,7},{4,0},{5,1},{6,2},{7,3},{8,12},{9,13},{10,... | collective-permute-start | bytes 1572872 | tf_op jit(solution)/shard_map/ppermute | solution.py:984
  398.8 27.6 %collective-permute-start.24 = (bf16[2,64,2048]{2,1,0:T(8,128)(2,1)S(1)}, bf16[2,64,2048]{2,1,0:T(8,128)(2,1)S(1)}, u32[]{:S(2)}, u32[]{:S(2)}) collective-permute-start(bf16[2,64,2048]{2,1,0:T(8,128)(2,1)S(1)} %sum_terms.34), channel_id=1, source_target_pairs={{0,4},{1,5},{2,6},{3,7},{4,0},{5,1},{6,2},{7,3},{8,12},{9,13},{10,... | collective-permute-start | bytes 1572872 | tf_op jit(solution)/shard_map/ppermute | solution.py:984
  398.9 28.9 %collective-permute-start.31 = (bf16[2,2,64,1024]{3,2,1,0:T(8,128)(2,1)S(1)}, bf16[2,2,64,1024]{3,2,1,0:T(8,128)(2,1)S(1)}, u32[]{:S(2)}, u32[]{:S(2)}) collective-permute-start(bf16[2,2,64,1024]{3,2,1,0:T(8,128)(2,1)S(1)} %copy-done.16), channel_id=1, source_target_pairs={{0,2},{1,3},{2,0},{3,1},{4,6},{5,7},{6,4},{7,5},{8,10},{9,11},{10,... | collective-permute-start | bytes 1572872 | tf_op jit(solution)/shard_map/ppermute | solution.py:984
  399.5 17.4 %collective-permute-start.25 = (bf16[64,2048]{1,0:T(8,128)(2,1)S(1)}, bf16[64,2048]{1,0:T(8,128)(2,1)S(1)}, u32[]{:S(2)}, u32[]{:S(2)}) collective-permute-start(bf16[64,2048]{1,0:T(8,128)(2,1)S(1)} %sum_terms.33), channel_id=1, source_target_pairs={{0,8},{1,9},{2,10},{3,11},{4,12},{5,13},{6,14},{7,15},{8,0},{9,1},... | collective-permute-start | bytes 786440 | tf_op jit(solution)/shard_map/ppermute | solution.py:984
  412.6 20.4 %collective-permute-start.29 = (bf16[2,64,1152]{2,1,0:T(8,128)(2,1)S(1)}, bf16[2,64,1152]{2,1,0:T(8,128)(2,1)S(1)}, u32[]{:S(2)}, u32[]{:S(2)}) collective-permute-start(bf16[2,64,1152]{2,1,0:T(8,128)(2,1)S(1)} %sum_terms.36), channel_id=1, source_target_pairs={{0,4},{1,5},{2,6},{3,7},{4,0},{5,1},{6,2},{7,3},{8,12},{9,13},{10,... | collective-permute-start | bytes 884744 | tf_op jit(solution)/shard_map/ppermute | solution.py:984
  412.7 18.1 %collective-permute-start.30 = (bf16[64,2048]{1,0:T(8,128)(2,1)S(1)}, bf16[64,2048]{1,0:T(8,128)(2,1)S(1)}, u32[]{:S(2)}, u32[]{:S(2)}) collective-permute-start(bf16[64,2048]{1,0:T(8,128)(2,1)S(1)} %sum_terms.35), channel_id=1, source_target_pairs={{0,8},{1,9},{2,10},{3,11},{4,12},{5,13},{6,14},{7,15},{8,0},{9,1},... | collective-permute-start | bytes 786440 | tf_op jit(solution)/shard_map/ppermute | solution.py:984
  427.7 14.2 %collective-permute-start.28 = (bf16[64,2048]{1,0:T(8,128)(2,1)S(1)}, bf16[64,2048]{1,0:T(8,128)(2,1)S(1)}, u32[]{:S(2)}, u32[]{:S(2)}) collective-permute-start(bf16[64,2048]{1,0:T(8,128)(2,1)S(1)} %sum_terms.38), channel_id=1, source_target_pairs={{0,8},{1,9},{2,10},{3,11},{4,12},{5,13},{6,14},{7,15},{8,0},{9,1},... | collective-permute-start | bytes 786440 | tf_op jit(solution)/shard_map/ppermute | solution.py:984
  429.4 14.6 %collective-permute-start.33 = (bf16[2,64,1024]{2,1,0:T(8,128)(2,1)S(1)}, bf16[2,64,1024]{2,1,0:T(8,128)(2,1)S(1)}, u32[]{:S(2)}, u32[]{:S(2)}) collective-permute-start(bf16[2,64,1024]{2,1,0:T(8,128)(2,1)S(1)} %sum_terms.39), channel_id=1, source_target_pairs={{0,4},{1,5},{2,6},{3,7},{4,0},{5,1},{6,2},{7,3},{8,12},{9,13},{10,... | collective-permute-start | bytes 786440 | tf_op jit(solution)/shard_map/ppermute | solution.py:984
  434.2 12.3 %collective-permute-start.32 = (bf16[64,1152]{1,0:T(8,128)(2,1)S(1)}, bf16[64,1152]{1,0:T(8,128)(2,1)S(1)}, u32[]{:S(2)}, u32[]{:S(2)}) collective-permute-start(bf16[64,1152]{1,0:T(8,128)(2,1)S(1)} %sum_terms.41), channel_id=1, source_target_pairs={{0,8},{1,9},{2,10},{3,11},{4,12},{5,13},{6,14},{7,15},{8,0},{9,1},... | collective-permute-start | bytes 442376 | tf_op jit(solution)/shard_map/ppermute | solution.py:984
  445.3 9.5 %collective-permute-start.34 = (bf16[64,1024]{1,0:T(8,128)(2,1)S(1)}, bf16[64,1024]{1,0:T(8,128)(2,1)S(1)}, u32[]{:S(2)}, u32[]{:S(2)}) collective-permute-start(bf16[64,1024]{1,0:T(8,128)(2,1)S(1)} %sum_terms.43), channel_id=1, source_target_pairs={{0,8},{1,9},{2,10},{3,11},{4,12},{5,13},{6,14},{7,15},{8,0},{9,1},... | collective-permute-start | bytes 393224 | tf_op jit(solution)/shard_map/ppermute | solution.py:984
  (35 other events, 369.3 us)

commit v6 on v5

--- a/solution.py
+++ b/solution.py
@@ -595,7 +595,7 @@
                 masked = jnp.where(lane == h, low, 0).astype(bf16)
                 delta = jnp.sum(jnp.where(lane == h, dots, 0.0), axis=-1, keepdims=True)
                 inner = nt(masked, value) - delta
-                v_s[:, hs] = (v_p[i % 2, h].astype(f32) * inner).astype(bf16)
+                v_s[:, hs] = v_p[i % 2, h] * inner.astype(bf16)
             grad_query = (nn(v_s[...], v_k[...]) * score_scale).astype(bf16)
             query_t = query.T
             low_t = low.T
@@ -760,14 +760,21 @@
 
 
 def weight_kernel(widths, half, left, right, *rest):
-    late, outs = rest[: -len(widths)], rest[-len(widths) :]
-    if late:
-        rows = late[0].shape[0]
-        second = jnp.where(lax.axis_index("section") == 0, late[0][...], right[rows:, :])
-        total = nn(left[0, :, :rows], right[:rows, :]) + nn(left[0, :, rows:], second)
+    if len(rest) > len(widths):
+        late, *outs, joined = rest
+        rows = late.shape[0]
+
+        @pl.when(pl.program_id(0) == 0)
+        def _():
+            joined[:rows, :] = right[:rows, :]
+            joined[rows:, :] = jnp.where(
+                lax.axis_index("section") == 0, late[...], right[rows:, :]
+            )
+
+        right = joined
     else:
-        total = nn(left[0], right[...])
-    total = total.astype(bf16)
+        outs = rest
+    total = nn(left[0], right[...]).astype(bf16)
     at = 0
     for width, out in zip(widths, outs):
         step, offset = divmod(at, right.shape[1])
@@ -785,7 +792,7 @@
 def weight_call(left, right, start, widths, half, late=None):
     _, height, rows = left.shape
     columns = sum(widths)
-    tall = min(height, 512)
+    tall = min(height, WIDE)
     wide = min(columns, WIDE)
     specs = [
         pl.BlockSpec((1, tall, rows), lambda i, j: (half, i, 0)),
@@ -807,6 +814,7 @@
         in_specs=specs,
         out_specs=[out(width) for width in widths],
         out_shape=[jax.ShapeDtypeStruct((height, width), bf16) for width in widths],
+        scratch_shapes=[] if late is None else [pltpu.VMEM((rows, columns), bf16)],
         compiler_params=pltpu.CompilerParams(vmem_limit_bytes=VMEM),
         cost_estimate=pl.CostEstimate(flops=1, bytes_accessed=1, transcendentals=0),
         name="weight_product",

time: 466 us -> 465 us (level)
  no operation moved by 1% of the time
where the time goes in v6:
time: 465 us; the launch traced here: 456 us
  Pallas kernels  276 us (59%)
  waiting for transfers between devices  119 us (26%)
  starting transfers between devices  34.9 us (8%)
  local copies, waits for them, and re-layouts  15.9 us (3%)
  matrix products  5.28 us (1%)
    pallas_call x4, Pallas kernels, backward_call(): pl.pallas_call(functools.partial(backward_kernel, slot, plan, stage, len(...  83 us
    pallas_call x3, Pallas kernels, forward_call(): pl.pallas_call(functools.partial(forward_kernel, slot, plan, stage, len(s...  72.2 us
    ppermute x5, waiting for transfers between devices, send(): return lax.ppermute(value, 'section', [(1 - to, to)])  71.7 us
    pallas_call x8, Pallas kernels, weight_call(): pl.pallas_call(functools.partial(weight_kernel, widths, half), grid=(heig...  59.7 us
    ppermute x31, waiting for transfers between devices, crossed(): lax.ppermute(value, 'dp', [(i, i ^ 1 << bit) for i in range(lax.axis_size...  47.4 us
    pallas_call x23, Pallas kernels, sum_call(): pl.pallas_call(kernel, in_specs=[any_] * len(operands), out_specs=any_, o...  46.1 us
    ppermute x31, starting transfers between devices, crossed(): lax.ppermute(value, 'dp', [(i, i ^ 1 << bit) for i in range(lax.axis_size...  23.3 us
    pallas_call x1, Pallas kernels, turn_call(): pl.pallas_call(functools.partial(turn_kernel, [s.shape[1] // size for s i...  14.7 us
  transfers between devices with their start and end apart: 36, of which 16 were waited for; matrix products, arithmetic and copies ran while one was open for 3% of the time, Pallas kernels for 35%

profile of v6, /device:TPU:0, one launch (start us, length us, event | category | flops | bytes accessed | tf_op | source)
XLA Modules:
  0.0 456.1 jit_solution(17782153132272570792)
XLA Ops:
  0.7 31.7 %layer_forward.3 = (bf16[512,1024]{1,0:T(8,128)(2,1)}, f32[4,8,1024]{2,1,0:T(8,128)}, bf16[1024,1024]{1,0:T(8,128)(2,1)}, bf16[1024,1024]{1,0:T(8,128)(2,1)}, bf...) custom-call(s32[2]{0:T(128)} %bitcast.106, ...), custom_call_target="tpu_custom_call" | custom-call | flops 99999997952 | bytes 1 | tf_op jit(solution)/shard_map/layer_forward/pallas_call | solution.py:358
  34.3 4.6 %fusion.6 = f32[7,4096]{1,0:T(8,128)S(1)} fusion(bf16[7,1024]{1,0:T(8,128)(2,1)S(1)} %copy-done, bf16[1024,4096]{1,0:T(8,128)(2,1)} %param.20), kind=kOutput, calls=%fused_computation.22 | convolution fusion | flops 58720256 | bytes 8517632 | tf_op jit(solution)/shard_map/dot_general | solution.py:1063
  39.8 17.6 %collective-permute-done.refs_8_ = bf16[512,1024]{1,0:T(8,128)(2,1)S(1)} collective-permute-done((bf16[512,1024]{1,0:T(8,128)(2,1)}, bf16[512,1024]{1,0:T(8,128)(2,1)S(1)}, u32[]{:S(2)}, u32[]{:S(2)}) %collective-permute-start) | collective-permute-done | bytes 1048608 | tf_op jit(solution)/shard_map/ppermute | solution.py:1046
  58.3 31.7 %layer_forward.4 = (bf16[512,1024]{1,0:T(8,128)(2,1)}, f32[4,8,1024]{2,1,0:T(8,128)}, bf16[1024,1024]{1,0:T(8,128)(2,1)}, bf16[1024,1024]{1,0:T(8,128)(2,1)}, bf...) custom-call(s32[2]{0:T(128)} %bitcast.107, ...), custom_call_target="tpu_custom_call", output_to_operand_aliasing={{2}: (9, {}), {3}: (10, {}), {4}: (11, {}), {5}: (12, {}), ... | custom-call | flops 99999997952 | bytes 1 | tf_op jit(solution)/shard_map/layer_forward/pallas_call | solution.py:358
  90.0 5.7 %collective-permute-start.1 = (bf16[512,1024]{1,0:T(8,128)(2,1)}, bf16[512,1024]{1,0:T(8,128)(2,1)}, u32[]{:S(2)}, u32[]{:S(2)}) collective-permute-start(bf16[512,1024]{1,0:T(8,128)(2,1)} %get-tuple-element.220.refs_3_), channel_id=1, source_target_pairs={{0,16},{1,17},{2,18},{3,19},{4,20},{5,21},{6,22},{7,23},{8,24},{9,... | collective-permute-start | bytes 3145736 | tf_op jit(solution)/shard_map/ppermute | solution.py:1046
  98.8 18.7 %collective-permute-done.1.refs_8_ = bf16[512,1024]{1,0:T(8,128)(2,1)} collective-permute-done((bf16[512,1024]{1,0:T(8,128)(2,1)}, bf16[512,1024]{1,0:T(8,128)(2,1)}, u32[]{:S(2)}, u32[]{:S(2)}) %collective-permute-start.1) | collective-permute-done | bytes 1048608 | tf_op jit(solution)/shard_map/ppermute | solution.py:1046
  117.5 8.7 %layer_forward.5 = (bf16[512,1024]{1,0:T(8,128)(2,1)}, f32[4,8,1024]{2,1,0:T(8,128)}, bf16[1024,1024]{1,0:T(8,128)(2,1)}, bf16[1024,1024]{1,0:T(8,128)(2,1)}, bf...) custom-call(s32[2]{0:T(128)} %bitcast.109, ...), custom_call_target="tpu_custom_call", output_to_operand_aliasing={{2}: (9, {}), {3}: (10, {}), {4}: (11, {}), {5}: (12, {}), ... | custom-call | flops 99999997952 | bytes 1 | tf_op jit(solution)/shard_map/layer_forward/pallas_call | solution.py:358
  126.2 28.4 %collective-permute-done.2.refs_3_ = bf16[512,1024]{1,0:T(8,128)(2,1)S(1)} collective-permute-done((bf16[512,1024]{1,0:T(8,128)(2,1)}, bf16[512,1024]{1,0:T(8,128)(2,1)S(1)}, u32[]{:S(2)}, u32[]{:S(2)}) %collective-permute-start.2) | collective-permute-done | bytes 1048608 | tf_op jit(solution)/shard_map/ppermute | solution.py:1046
  155.6 36.9 %layer_backward.5 = (f32[12,1024]{1,0:T(8,128)}, bf16[1024,4096]{1,0:T(8,128)(2,1)}, bf16[1024,1024]{1,0:T(8,128)(2,1)}, bf16[512,1024]{1,0:T(8,128)(2,1)}, bf16...) custom-call(s32[2]{0:T(128)} %bitcast.110, ...), custom_call_target="tpu_custom_call", output_to_operand_aliasing={{1}: (15, {}), {2}: (16, {}), {4}: (17, {}), {5}: (18, {}),... | custom-call | flops 99999997952 | bytes 1 | tf_op jit(solution)/shard_map/layer_backward/pallas_call | solution.py:677
  206.5 14.7 %turn.1 = (bf16[2,512,1024]{2,1,0:T(8,128)(2,1)}, bf16[2,512,1024]{2,1,0:T(8,128)(2,1)}, bf16[2,512,1024]{2,1,0:T(8,128)(2,1)}, bf16[2,2048,1024]{2,1,0:T(8,128)(2,1)}) custom-call(bf16[1024,1024]{1,0:T(8,128)(2,1)} %get-tuple-element.251.refs_0_, bf16[1024,1024]{1,0:T(8,128)(2,1)} %get-tuple-element.252.refs_1_, ...), custom_call_target="tpu_custom_call" | custom-call | flops 1 | bytes 1 | tf_op jit(solution)/shard_map/turn/pallas_call | solution.py:750
  221.8 4.2 collective-permute-done.3.rest_0_.refs_3_
  227.0 8.8 %weight_product.8 = bf16[2048,1024]{1,0:T(8,128)(2,1)} custom-call(bf16[2,2048,1024]{2,1,0:T(8,128)(2,1)} %get-tuple-element.265.left, bf16[1024,1024]{1,0:T(8,128)(2,1)} %get-tuple-element.266.right, bf16[512,1024]{1,0:T(8,128)(2,1)} %copy-done.15), custom_call_target="tpu_custom_call" | custom-call | flops 1 | bytes 1 | tf_op jit(solution)/shard_map/weight_product/pallas_call | solution.py:811
  235.8 8.7 %weight_product.9 = bf16[2048,1024]{1,0:T(8,128)(2,1)} custom-call(bf16[2,2048,1024]{2,1,0:T(8,128)(2,1)} %get-tuple-element.265.left, bf16[1024,1024]{1,0:T(8,128)(2,1)} %get-tuple-element.266.right, bf16[512,1024]{1,0:T(8,128)(2,1)} %copy-done.15), custom_call_target="tpu_custom_call" | custom-call | flops 1 | bytes 1 | tf_op jit(solution)/shard_map/weight_product/pallas_call | solution.py:811
  244.5 3.2 sum_terms.23
  249.4 20.6 %layer_backward.6 = (f32[12,1024]{1,0:T(8,128)}, bf16[1024,4096]{1,0:T(8,128)(2,1)}, bf16[1024,1024]{1,0:T(8,128)(2,1)}, f32[512,1024]{1,0:T(8,128)}) custom-call(s32[2]{0:T(128)} %bitcast.111, f32[1,12288]{1,0:T(1,128)} %refs_1_.5, bf16[2,1,512,1024]{3,2,1,0:T(8,128)(2,1)} %refs_2_.13, ...), custom_call_target="tpu_custom_call", output_to_operand_aliasing={{1}: (15, {}), {2}: (16, {})} | custom-call | flops 99999997952 | bytes 1 | tf_op jit(solution)/shard_map/layer_backward/pallas_call | solution.py:677
  270.0 9.7 %weight_product.10 = (bf16[512,1024]{1,0:T(8,128)(2,1)}, bf16[512,1024]{1,0:T(8,128)(2,1)}, bf16[512,1024]{1,0:T(8,128)(2,1)}, bf16[512,1024]{1,0:T(8,128)(2,1)}) custom-call(bf16[2,512,1024]{2,1,0:T(8,128)(2,1)} %get-tuple-element.284.left, bf16[1024,4096]{1,0:T(8,128)(2,1)} %get-tuple-element.285.right), custom_call_target="tpu_custom_call" | custom-call | flops 1 | bytes 1 | tf_op jit(solution)/shard_map/weight_product/pallas_call | solution.py:811
  280.8 8.8 %weight_product.11 = bf16[512,4096]{1,0:T(8,128)(2,1)} custom-call(bf16[2,512,1024]{2,1,0:T(8,128)(2,1)} %get-tuple-element.284.left, bf16[1024,4096]{1,0:T(8,128)(2,1)} %get-tuple-element.285.right), custom_call_target="tpu_custom_call" | custom-call | flops 1 | bytes 1 | tf_op jit(solution)/shard_map/weight_product/pallas_call | solution.py:811
  290.6 3.4 sum_terms.24
  296.1 2.9 sum_terms.25
  300.8 4.2 weight_product.12
  305.0 4.2 weight_product.13
  309.1 23.8 %layer_backward.7 = (f32[12,1024]{1,0:T(8,128)}, bf16[512,1024]{1,0:T(8,128)(2,1)}, bf16[1024,3072]{1,0:T(8,128)(2,1)}, bf16[1,2,1,512,1024]{4,3,2,1,0:T(8,128)(2,1)}) custom-call(s32[2]{0:T(128)} %bitcast.112, f32[1,12288]{1,0:T(1,128)} %refs_1_.5, bf16[2,1,512,1024]{3,2,1,0:T(8,128)(2,1)} %refs_2_.13, ...), custom_call_target="tpu_custom_call", output_to_operand_aliasing={{2}: (17, {}), {3}: (18, {})} | custom-call | flops 99999997952 | bytes 1 | tf_op jit(solution)/shard_map/layer_backward/pallas_call | solution.py:677
  336.6 7.9 %weight_product.14 = (bf16[512,1024]{1,0:T(8,128)(2,1)}, bf16[512,1024]{1,0:T(8,128)(2,1)}, bf16[512,1024]{1,0:T(8,128)(2,1)}) custom-call(bf16[2,512,1024]{2,1,0:T(8,128)(2,1)} %get-tuple-element.313.left, bf16[1024,3072]{1,0:T(8,128)(2,1)} %get-tuple-element.314.right), custom_call_target="tpu_custom_call" | custom-call | flops 1 | bytes 1 | tf_op jit(solution)/shard_map/weight_product/pallas_call | solution.py:811
  346.2 7.4 %weight_product.15 = bf16[512,3072]{1,0:T(8,128)(2,1)} custom-call(bf16[2,512,1024]{2,1,0:T(8,128)(2,1)} %get-tuple-element.313.left, bf16[1024,3072]{1,0:T(8,128)(2,1)} %get-tuple-element.314.right), custom_call_target="tpu_custom_call" | custom-call | flops 1 | bytes 1 | tf_op jit(solution)/shard_map/weight_product/pallas_call | solution.py:811
  375.0 10.7 %collective-permute-done.20.refs_4_ = bf16[256,1024]{1,0:T(8,128)(2,1)} collective-permute-done((bf16[256,1024]{1,0:T(8,128)(2,1)}, bf16[256,1024]{1,0:T(8,128)(2,1)}, u32[]{:S(2)}, u32[]{:S(2)}) %collective-permute-start.20) | collective-permute-done | bytes 524320 | tf_op jit(solution)/shard_map/ppermute | solution.py:992
  385.8 3.0 sum_terms.32
  388.8 3.2 collective-permute-done.19.refs_4_
  398.8 10.1 %collective-permute-done.27.refs_4_ = bf16[2,64,2048]{2,1,0:T(8,128)(2,1)} collective-permute-done((bf16[2,64,2048]{2,1,0:T(8,128)(2,1)}, bf16[2,64,2048]{2,1,0:T(8,128)(2,1)}, u32[]{:S(2)}, u32[]{:S(2)}) %collective-permute-start.27) | collective-permute-done | bytes 524320 | tf_op jit(solution)/shard_map/ppermute | solution.py:992
  411.9 4.1 collective-permute-done.25.refs_5_
  418.3 7.3 %collective-permute-done.24.refs_4_ = bf16[2,64,2048]{2,1,0:T(8,128)(2,1)S(1)} collective-permute-done((bf16[2,64,2048]{2,1,0:T(8,128)(2,1)S(1)}, bf16[2,64,2048]{2,1,0:T(8,128)(2,1)S(1)}, u32[]{:S(2)}, u32[]{:S(2)}) %collective-permute-start.24) | collective-permute-done | bytes 524320 | tf_op jit(solution)/shard_map/ppermute | solution.py:992
  433.4 2.9 collective-permute-start.32
  436.9 4.3 collective-permute-done.28.refs_5_
  (186 shorter events, 90.8 us)
Async XLA Ops:
  32.4 24.9 %collective-permute-start = (bf16[512,1024]{1,0:T(8,128)(2,1)}, bf16[512,1024]{1,0:T(8,128)(2,1)S(1)}, u32[]{:S(2)}, u32[]{:S(2)}) collective-permute-start(bf16[512,1024]{1,0:T(8,128)(2,1)} %get-tuple-element.207), channel_id=1, source_target_pairs={{0,16},{1,17},{2,18},{3,19},{4,20},{5,21},{6,22},{7,23},{8,24},{9,... | collective-permute-start | bytes 3145736 | tf_op jit(solution)/shard_map/ppermute | solution.py:1046
  90.0 27.5 %collective-permute-start.1 = (bf16[512,1024]{1,0:T(8,128)(2,1)}, bf16[512,1024]{1,0:T(8,128)(2,1)}, u32[]{:S(2)}, u32[]{:S(2)}) collective-permute-start(bf16[512,1024]{1,0:T(8,128)(2,1)} %get-tuple-element.220.refs_3_), channel_id=1, source_target_pairs={{0,16},{1,17},{2,18},{3,19},{4,20},{5,21},{6,22},{7,23},{8,24},{9,... | collective-permute-start | bytes 3145736 | tf_op jit(solution)/shard_map/ppermute | solution.py:1046
  97.5 57.1 %collective-permute-start.2 = (bf16[512,1024]{1,0:T(8,128)(2,1)}, bf16[512,1024]{1,0:T(8,128)(2,1)S(1)}, u32[]{:S(2)}, u32[]{:S(2)}) collective-permute-start(bf16[512,1024]{1,0:T(8,128)(2,1)} %get-tuple-element.233), channel_id=1, source_target_pairs={{16,0},{17,1},{18,2},{19,3},{20,4},{21,5},{22,6},{23,7},{24,8},{25... | collective-permute-start | bytes 3145736 | tf_op jit(solution)/shard_map/ppermute | solution.py:1046
  192.5 33.5 %collective-permute-start.3 = (bf16[512,1024]{1,0:T(8,128)(2,1)}, bf16[512,1024]{1,0:T(8,128)(2,1)S(1)}, u32[]{:S(2)}, u32[]{:S(2)}) collective-permute-start(bf16[512,1024]{1,0:T(8,128)(2,1)} %get-tuple-element.246), channel_id=1, source_target_pairs={{16,0},{17,1},{18,2},{19,3},{20,4},{21,5},{22,6},{23,7},{24,8},{25... | collective-permute-start | bytes 3145736 | tf_op jit(solution)/shard_map/ppermute | solution.py:1046
  203.7 17.6 %collective-permute-start.7 = (f32[128]{0:T(128)S(1)}, f32[128]{0:T(128)S(1)}, u32[]{:S(2)}, u32[]{:S(2)}) collective-permute-start(f32[128]{0:T(128)S(1)} %add.60), channel_id=1, source_target_pairs={{0,8},{1,9},{2,10},{3,11},{4,12},{5,13},{6,14},{7,15},{8,0},{9,1},... | collective-permute-start | bytes 1544 | tf_op jit(solution)/shard_map/ppermute | solution.py:992
  235.7 8.7 %collective-permute-start.8 = (bf16[2048,1024]{1,0:T(8,128)(2,1)}, bf16[2048,1024]{1,0:T(8,128)(2,1)}, u32[]{:S(2)}, u32[]{:S(2)}) collective-permute-start(bf16[2048,1024]{1,0:T(8,128)(2,1)} %weight_product.8), channel_id=1, source_target_pairs={{0,1},{1,0},{2,3},{3,2},{4,5},{5,4},{6,7},{7,6},{8,9},{9,8},{10,11... | collective-permute-start | bytes 12582920 | tf_op jit(solution)/shard_map/ppermute | solution.py:992
  247.7 48.4 %collective-permute-start.9 = (bf16[2,2,256,1024]{3,2,1,0:T(8,128)(2,1)}, bf16[2,2,256,1024]{3,2,1,0:T(8,128)(2,1)}, u32[]{:S(2)}, u32[]{:S(2)}) collective-permute-start(bf16[2,2,256,1024]{3,2,1,0:T(8,128)(2,1)} %sum_terms.23), channel_id=1, source_target_pairs={{0,2},{1,3},{2,0},{3,1},{4,6},{5,7},{6,4},{7,5},{8,10},{9,11},{10,... | collective-permute-start | bytes 6291464 | tf_op jit(solution)/shard_map/ppermute | solution.py:992
  279.7 9.9 %collective-permute-start.10 = (bf16[512,1024]{1,0:T(8,128)(2,1)}, bf16[512,1024]{1,0:T(8,128)(2,1)S(1)}, u32[]{:S(2)}, u32[]{:S(2)}) collective-permute-start(bf16[512,1024]{1,0:T(8,128)(2,1)} %get-tuple-element.280), channel_id=1, source_target_pairs={{0,1},{1,0},{2,3},{3,2},{4,5},{5,4},{6,7},{7,6},{8,9},{9,8},{10,11... | collective-permute-start | bytes 3145736 | tf_op jit(solution)/shard_map/ppermute | solution.py:992
  279.9 9.7 %collective-permute-start.11 = (bf16[512,1024]{1,0:T(8,128)(2,1)}, bf16[512,1024]{1,0:T(8,128)(2,1)}, u32[]{:S(2)}, u32[]{:S(2)}) collective-permute-start(bf16[512,1024]{1,0:T(8,128)(2,1)} %get-tuple-element.281), channel_id=1, source_target_pairs={{0,1},{1,0},{2,3},{3,2},{4,5},{5,4},{6,7},{7,6},{8,9},{9,8},{10,11... | collective-permute-start | bytes 3145736 | tf_op jit(solution)/shard_map/ppermute | solution.py:992
  280.3 9.4 %collective-permute-start.12 = (bf16[512,1024]{1,0:T(8,128)(2,1)}, bf16[512,1024]{1,0:T(8,128)(2,1)}, u32[]{:S(2)}, u32[]{:S(2)}) collective-permute-start(bf16[512,1024]{1,0:T(8,128)(2,1)} %get-tuple-element.282), channel_id=1, source_target_pairs={{0,1},{1,0},{2,3},{3,2},{4,5},{5,4},{6,7},{7,6},{8,9},{9,8},{10,11... | collective-permute-start | bytes 3145736 | tf_op jit(solution)/shard_map/ppermute | solution.py:992
  280.5 9.2 %collective-permute-start.13 = (bf16[512,1024]{1,0:T(8,128)(2,1)}, bf16[512,1024]{1,0:T(8,128)(2,1)}, u32[]{:S(2)}, u32[]{:S(2)}) collective-permute-start(bf16[512,1024]{1,0:T(8,128)(2,1)} %get-tuple-element.283), channel_id=1, source_target_pairs={{0,1},{1,0},{2,3},{3,2},{4,5},{5,4},{6,7},{7,6},{8,9},{9,8},{10,11... | collective-permute-start | bytes 3145736 | tf_op jit(solution)/shard_map/ppermute | solution.py:992
  294.0 64.8 %collective-permute-start.18 = (bf16[2,2,64,4096]{3,2,1,0:T(8,128)(2,1)}, bf16[2,2,64,4096]{3,2,1,0:T(8,128)(2,1)}, u32[]{:S(2)}, u32[]{:S(2)}) collective-permute-start(bf16[2,2,64,4096]{3,2,1,0:T(8,128)(2,1)} %sum_terms.24), channel_id=1, source_target_pairs={{0,2},{1,3},{2,0},{3,1},{4,6},{5,7},{6,4},{7,5},{8,10},{9,11},{10,... | collective-permute-start | bytes 6291464 | tf_op jit(solution)/shard_map/ppermute | solution.py:992
  299.0 34.0 %collective-permute-start.14 = (bf16[2,256,1024]{2,1,0:T(8,128)(2,1)}, bf16[2,256,1024]{2,1,0:T(8,128)(2,1)S(1)}, u32[]{:S(2)}, u32[]{:S(2)}) collective-permute-start(bf16[2,256,1024]{2,1,0:T(8,128)(2,1)} %sum_terms.25), channel_id=1, source_target_pairs={{0,4},{1,5},{2,6},{3,7},{4,0},{5,1},{6,2},{7,3},{8,12},{9,13},{10,... | collective-permute-start | bytes 3145736 | tf_op jit(solution)/shard_map/ppermute | solution.py:992
  344.6 9.0 %collective-permute-start.15 = (bf16[512,1024]{1,0:T(8,128)(2,1)}, bf16[512,1024]{1,0:T(8,128)(2,1)}, u32[]{:S(2)}, u32[]{:S(2)}) collective-permute-start(bf16[512,1024]{1,0:T(8,128)(2,1)} %get-tuple-element.310), channel_id=1, source_target_pairs={{0,1},{1,0},{2,3},{3,2},{4,5},{5,4},{6,7},{7,6},{8,9},{9,8},{10,11... | collective-permute-start | bytes 3145736 | tf_op jit(solution)/shard_map/ppermute | solution.py:992
  344.6 9.0 %collective-permute-start.16 = (bf16[512,1024]{1,0:T(8,128)(2,1)}, bf16[512,1024]{1,0:T(8,128)(2,1)}, u32[]{:S(2)}, u32[]{:S(2)}) collective-permute-start(bf16[512,1024]{1,0:T(8,128)(2,1)} %get-tuple-element.311), channel_id=1, source_target_pairs={{0,1},{1,0},{2,3},{3,2},{4,5},{5,4},{6,7},{7,6},{8,9},{9,8},{10,11... | collective-permute-start | bytes 3145736 | tf_op jit(solution)/shard_map/ppermute | solution.py:992
  345.4 23.1 %collective-permute-start.22 = (bf16[512,1024]{1,0:T(8,128)(2,1)}, bf16[512,1024]{1,0:T(8,128)(2,1)}, u32[]{:S(2)}, u32[]{:S(2)}) collective-permute-start(bf16[512,1024]{1,0:T(8,128)(2,1)} %get-tuple-element.312), channel_id=1, source_target_pairs={{0,1},{1,0},{2,3},{3,2},{4,5},{5,4},{6,7},{7,6},{8,9},{9,8},{10,11... | collective-permute-start | bytes 3145736 | tf_op jit(solution)/shard_map/ppermute | solution.py:992
  345.5 25.9 %collective-permute-start.21 = (bf16[512,1024]{1,0:T(8,128)(2,1)}, bf16[512,1024]{1,0:T(8,128)(2,1)}, u32[]{:S(2)}, u32[]{:S(2)}) collective-permute-start(bf16[512,1024]{1,0:T(8,128)(2,1)} %weight_product.12), channel_id=1, source_target_pairs={{0,1},{1,0},{2,3},{3,2},{4,5},{5,4},{6,7},{7,6},{8,9},{9,8},{10,11... | collective-permute-start | bytes 3145736 | tf_op jit(solution)/shard_map/ppermute | solution.py:992
  356.1 39.6 %collective-permute-start.17 = (bf16[2,2,64,2048]{3,2,1,0:T(8,128)(2,1)}, bf16[2,2,64,2048]{3,2,1,0:T(8,128)(2,1)}, u32[]{:S(2)}, u32[]{:S(2)}) collective-permute-start(bf16[2,2,64,2048]{3,2,1,0:T(8,128)(2,1)} %sum_terms.27), channel_id=1, source_target_pairs={{0,2},{1,3},{2,0},{3,1},{4,6},{5,7},{6,4},{7,5},{8,10},{9,11},{10,... | collective-permute-start | bytes 3145736 | tf_op jit(solution)/shard_map/ppermute | solution.py:992
  358.9 6.9 %collective-permute-start.23 = (bf16[2,2,2,64,128]{4,3,2,1,0:T(8,128)(2,1)S(1)}, bf16[2,2,2,64,128]{4,3,2,1,0:T(8,128)(2,1)S(1)}, u32[]{:S(2)}, u32[]{:S(2)}) collective-permute-start(bf16[2,2,2,64,128]{4,3,2,1,0:T(8,128)(2,1)S(1)} %get-tuple-element.424), channel_id=1, source_target_pairs={{0,1},{1,0},{2,3},{3,2},{4,5},{5,4},{6,7},{7,6},{8,9},{9,8},{10,11... | collective-permute-start | bytes 393224 | tf_op jit(solution)/shard_map/ppermute | solution.py:992
  358.9 26.9 %collective-permute-start.20 = (bf16[256,1024]{1,0:T(8,128)(2,1)}, bf16[256,1024]{1,0:T(8,128)(2,1)}, u32[]{:S(2)}, u32[]{:S(2)}) collective-permute-start(bf16[256,1024]{1,0:T(8,128)(2,1)} %sum_terms.26), channel_id=1, source_target_pairs={{0,8},{1,9},{2,10},{3,11},{4,12},{5,13},{6,14},{7,15},{8,0},{9,1},... | collective-permute-start | bytes 1572872 | tf_op jit(solution)/shard_map/ppermute | solution.py:992
  365.8 26.2 %collective-permute-start.19 = (bf16[2,64,2048]{2,1,0:T(8,128)(2,1)}, bf16[2,64,2048]{2,1,0:T(8,128)(2,1)}, u32[]{:S(2)}, u32[]{:S(2)}) collective-permute-start(bf16[2,64,2048]{2,1,0:T(8,128)(2,1)} %sum_terms.28), channel_id=1, source_target_pairs={{0,4},{1,5},{2,6},{3,7},{4,0},{5,1},{6,2},{7,3},{8,12},{9,13},{10,... | collective-permute-start | bytes 1572872 | tf_op jit(solution)/shard_map/ppermute | solution.py:992
  370.8 39.4 %collective-permute-start.26 = (bf16[2,2,64,1152]{3,2,1,0:T(8,128)(2,1)}, bf16[2,2,64,1152]{3,2,1,0:T(8,128)(2,1)S(1)}, u32[]{:S(2)}, u32[]{:S(2)}) collective-permute-start(bf16[2,2,64,1152]{3,2,1,0:T(8,128)(2,1)} %sum_terms.30), channel_id=1, source_target_pairs={{0,2},{1,3},{2,0},{3,1},{4,6},{5,7},{6,4},{7,5},{8,10},{9,11},{10,... | collective-permute-start | bytes 1769480 | tf_op jit(solution)/shard_map/ppermute | solution.py:992
  371.4 37.4 %collective-permute-start.27 = (bf16[2,64,2048]{2,1,0:T(8,128)(2,1)}, bf16[2,64,2048]{2,1,0:T(8,128)(2,1)}, u32[]{:S(2)}, u32[]{:S(2)}) collective-permute-start(bf16[2,64,2048]{2,1,0:T(8,128)(2,1)} %copy-done.13), channel_id=1, source_target_pairs={{0,4},{1,5},{2,6},{3,7},{4,0},{5,1},{6,2},{7,3},{8,12},{9,13},{10,... | collective-permute-start | bytes 1572872 | tf_op jit(solution)/shard_map/ppermute | solution.py:992
  398.0 27.6 %collective-permute-start.24 = (bf16[2,64,2048]{2,1,0:T(8,128)(2,1)S(1)}, bf16[2,64,2048]{2,1,0:T(8,128)(2,1)S(1)}, u32[]{:S(2)}, u32[]{:S(2)}) collective-permute-start(bf16[2,64,2048]{2,1,0:T(8,128)(2,1)S(1)} %sum_terms.34), channel_id=1, source_target_pairs={{0,4},{1,5},{2,6},{3,7},{4,0},{5,1},{6,2},{7,3},{8,12},{9,13},{10,... | collective-permute-start | bytes 1572872 | tf_op jit(solution)/shard_map/ppermute | solution.py:992
  398.1 28.9 %collective-permute-start.31 = (bf16[2,2,64,1024]{3,2,1,0:T(8,128)(2,1)S(1)}, bf16[2,2,64,1024]{3,2,1,0:T(8,128)(2,1)S(1)}, u32[]{:S(2)}, u32[]{:S(2)}) collective-permute-start(bf16[2,2,64,1024]{3,2,1,0:T(8,128)(2,1)S(1)} %copy-done.16), channel_id=1, source_target_pairs={{0,2},{1,3},{2,0},{3,1},{4,6},{5,7},{6,4},{7,5},{8,10},{9,11},{10,... | collective-permute-start | bytes 1572872 | tf_op jit(solution)/shard_map/ppermute | solution.py:992
  398.7 17.3 %collective-permute-start.25 = (bf16[64,2048]{1,0:T(8,128)(2,1)S(1)}, bf16[64,2048]{1,0:T(8,128)(2,1)S(1)}, u32[]{:S(2)}, u32[]{:S(2)}) collective-permute-start(bf16[64,2048]{1,0:T(8,128)(2,1)S(1)} %sum_terms.33), channel_id=1, source_target_pairs={{0,8},{1,9},{2,10},{3,11},{4,12},{5,13},{6,14},{7,15},{8,0},{9,1},... | collective-permute-start | bytes 786440 | tf_op jit(solution)/shard_map/ppermute | solution.py:992
  411.8 20.4 %collective-permute-start.29 = (bf16[2,64,1152]{2,1,0:T(8,128)(2,1)S(1)}, bf16[2,64,1152]{2,1,0:T(8,128)(2,1)S(1)}, u32[]{:S(2)}, u32[]{:S(2)}) collective-permute-start(bf16[2,64,1152]{2,1,0:T(8,128)(2,1)S(1)} %sum_terms.36), channel_id=1, source_target_pairs={{0,4},{1,5},{2,6},{3,7},{4,0},{5,1},{6,2},{7,3},{8,12},{9,13},{10,... | collective-permute-start | bytes 884744 | tf_op jit(solution)/shard_map/ppermute | solution.py:992
  411.9 18.1 %collective-permute-start.30 = (bf16[64,2048]{1,0:T(8,128)(2,1)S(1)}, bf16[64,2048]{1,0:T(8,128)(2,1)S(1)}, u32[]{:S(2)}, u32[]{:S(2)}) collective-permute-start(bf16[64,2048]{1,0:T(8,128)(2,1)S(1)} %sum_terms.35), channel_id=1, source_target_pairs={{0,8},{1,9},{2,10},{3,11},{4,12},{5,13},{6,14},{7,15},{8,0},{9,1},... | collective-permute-start | bytes 786440 | tf_op jit(solution)/shard_map/ppermute | solution.py:992
  426.9 14.2 %collective-permute-start.28 = (bf16[64,2048]{1,0:T(8,128)(2,1)S(1)}, bf16[64,2048]{1,0:T(8,128)(2,1)S(1)}, u32[]{:S(2)}, u32[]{:S(2)}) collective-permute-start(bf16[64,2048]{1,0:T(8,128)(2,1)S(1)} %sum_terms.38), channel_id=1, source_target_pairs={{0,8},{1,9},{2,10},{3,11},{4,12},{5,13},{6,14},{7,15},{8,0},{9,1},... | collective-permute-start | bytes 786440 | tf_op jit(solution)/shard_map/ppermute | solution.py:992
  428.6 14.6 %collective-permute-start.33 = (bf16[2,64,1024]{2,1,0:T(8,128)(2,1)S(1)}, bf16[2,64,1024]{2,1,0:T(8,128)(2,1)S(1)}, u32[]{:S(2)}, u32[]{:S(2)}) collective-permute-start(bf16[2,64,1024]{2,1,0:T(8,128)(2,1)S(1)} %sum_terms.39), channel_id=1, source_target_pairs={{0,4},{1,5},{2,6},{3,7},{4,0},{5,1},{6,2},{7,3},{8,12},{9,13},{10,... | collective-permute-start | bytes 786440 | tf_op jit(solution)/shard_map/ppermute | solution.py:992
  433.4 12.3 %collective-permute-start.32 = (bf16[64,1152]{1,0:T(8,128)(2,1)S(1)}, bf16[64,1152]{1,0:T(8,128)(2,1)S(1)}, u32[]{:S(2)}, u32[]{:S(2)}) collective-permute-start(bf16[64,1152]{1,0:T(8,128)(2,1)S(1)} %sum_terms.41), channel_id=1, source_target_pairs={{0,8},{1,9},{2,10},{3,11},{4,12},{5,13},{6,14},{7,15},{8,0},{9,1},... | collective-permute-start | bytes 442376 | tf_op jit(solution)/shard_map/ppermute | solution.py:992
  444.5 9.5 %collective-permute-start.34 = (bf16[64,1024]{1,0:T(8,128)(2,1)S(1)}, bf16[64,1024]{1,0:T(8,128)(2,1)S(1)}, u32[]{:S(2)}, u32[]{:S(2)}) collective-permute-start(bf16[64,1024]{1,0:T(8,128)(2,1)S(1)} %sum_terms.43), channel_id=1, source_target_pairs={{0,8},{1,9},{2,10},{3,11},{4,12},{5,13},{6,14},{7,15},{8,0},{9,1},... | collective-permute-start | bytes 393224 | tf_op jit(solution)/shard_map/ppermute | solution.py:992
  (35 other events, 368.1 us)

commit v7 on v6

--- a/solution.py
+++ b/solution.py
@@ -526,7 +526,7 @@
             up_copy(i).wait()
             d_copy(i).wait()
             if stage == BOTH:
-                pl.when(i == tiles - 2)(enter_attention)
+                pl.when(i == tiles - 3)(enter_attention)
                 pl.when(i == tiles - 1)(enter_last)
             at = part(i, WIDE)
             pre = (nt(v_dy[...], v_down[at, :]) * v_d[i % 2].astype(f32)).astype(bf16)

time: 465 us -> 469 us (level)
  no operation moved by 1% of the time
where the time goes in v7:
time: 469 us; the launch traced here: 461 us
  Pallas kernels  278 us (59%)
  waiting for transfers between devices  121 us (26%)
  starting transfers between devices  34.9 us (7%)
  local copies, waits for them, and re-layouts  15.9 us (3%)
  matrix products  5.28 us (1%)
    pallas_call x4, Pallas kernels, backward_call(): pl.pallas_call(functools.partial(backward_kernel, slot, plan, stage, len(...  85.1 us
    ppermute x5, waiting for transfers between devices, send(): return lax.ppermute(value, 'section', [(1 - to, to)])  74.1 us
    pallas_call x3, Pallas kernels, forward_call(): pl.pallas_call(functools.partial(forward_kernel, slot, plan, stage, len(s...  72.2 us
    pallas_call x8, Pallas kernels, weight_call(): pl.pallas_call(functools.partial(weight_kernel, widths, half), grid=(heig...  59.7 us
    ppermute x31, waiting for transfers between devices, crossed(): lax.ppermute(value, 'dp', [(i, i ^ 1 << bit) for i in range(lax.axis_size...  47.4 us
    pallas_call x23, Pallas kernels, sum_call(): pl.pallas_call(kernel, in_specs=[any_] * len(operands), out_specs=any_, o...  46.1 us
    ppermute x31, starting transfers between devices, crossed(): lax.ppermute(value, 'dp', [(i, i ^ 1 << bit) for i in range(lax.axis_size...  23.3 us
    pallas_call x1, Pallas kernels, turn_call(): pl.pallas_call(functools.partial(turn_kernel, [s.shape[1] // size for s i...  14.7 us
  transfers between devices with their start and end apart: 36, of which 16 were waited for; matrix products, arithmetic and copies ran while one was open for 3% of the time, Pallas kernels for 35%

profile of v7, /device:TPU:0, one launch (start us, length us, event | category | flops | bytes accessed | tf_op | source)
XLA Modules:
  0.0 460.6 jit_solution(10544614116287865973)
XLA Ops:
  0.7 31.7 %layer_forward.3 = (bf16[512,1024]{1,0:T(8,128)(2,1)}, f32[4,8,1024]{2,1,0:T(8,128)}, bf16[1024,1024]{1,0:T(8,128)(2,1)}, bf16[1024,1024]{1,0:T(8,128)(2,1)}, bf...) custom-call(s32[2]{0:T(128)} %bitcast.106, ...), custom_call_target="tpu_custom_call" | custom-call | flops 99999997952 | bytes 1 | tf_op jit(solution)/shard_map/layer_forward/pallas_call | solution.py:358
  34.3 4.6 fusion.6
  39.8 17.6 %collective-permute-done.refs_8_ = bf16[512,1024]{1,0:T(8,128)(2,1)S(1)} collective-permute-done((bf16[512,1024]{1,0:T(8,128)(2,1)}, bf16[512,1024]{1,0:T(8,128)(2,1)S(1)}, u32[]{:S(2)}, u32[]{:S(2)}) %collective-permute-start) | collective-permute-done | bytes 1048608 | tf_op jit(solution)/shard_map/ppermute | solution.py:1046
  58.3 31.7 %layer_forward.4 = (bf16[512,1024]{1,0:T(8,128)(2,1)}, f32[4,8,1024]{2,1,0:T(8,128)}, bf16[1024,1024]{1,0:T(8,128)(2,1)}, bf16[1024,1024]{1,0:T(8,128)(2,1)}, bf...) custom-call(s32[2]{0:T(128)} %bitcast.107, ...), custom_call_target="tpu_custom_call", output_to_operand_aliasing={{2}: (9, {}), {3}: (10, {}), {4}: (11, {}), {5}: (12, {}), ... | custom-call | flops 99999997952 | bytes 1 | tf_op jit(solution)/shard_map/layer_forward/pallas_call | solution.py:358
  90.0 5.7 %collective-permute-start.1 = (bf16[512,1024]{1,0:T(8,128)(2,1)}, bf16[512,1024]{1,0:T(8,128)(2,1)}, u32[]{:S(2)}, u32[]{:S(2)}) collective-permute-start(bf16[512,1024]{1,0:T(8,128)(2,1)} %get-tuple-element.220.refs_3_), channel_id=1, source_target_pairs={{0,16},{1,17},{2,18},{3,19},{4,20},{5,21},{6,22},{7,23},{8,24},{9,... | collective-permute-start | bytes 3145736 | tf_op jit(solution)/shard_map/ppermute | solution.py:1046
  98.8 18.7 %collective-permute-done.1.refs_8_ = bf16[512,1024]{1,0:T(8,128)(2,1)} collective-permute-done((bf16[512,1024]{1,0:T(8,128)(2,1)}, bf16[512,1024]{1,0:T(8,128)(2,1)}, u32[]{:S(2)}, u32[]{:S(2)}) %collective-permute-start.1) | collective-permute-done | bytes 1048608 | tf_op jit(solution)/shard_map/ppermute | solution.py:1046
  117.5 8.7 %layer_forward.5 = (bf16[512,1024]{1,0:T(8,128)(2,1)}, f32[4,8,1024]{2,1,0:T(8,128)}, bf16[1024,1024]{1,0:T(8,128)(2,1)}, bf16[1024,1024]{1,0:T(8,128)(2,1)}, bf...) custom-call(s32[2]{0:T(128)} %bitcast.109, ...), custom_call_target="tpu_custom_call", output_to_operand_aliasing={{2}: (9, {}), {3}: (10, {}), {4}: (11, {}), {5}: (12, {}), ... | custom-call | flops 99999997952 | bytes 1 | tf_op jit(solution)/shard_map/layer_forward/pallas_call | solution.py:358
  126.2 30.8 %collective-permute-done.2.refs_3_ = bf16[512,1024]{1,0:T(8,128)(2,1)S(1)} collective-permute-done((bf16[512,1024]{1,0:T(8,128)(2,1)}, bf16[512,1024]{1,0:T(8,128)(2,1)S(1)}, u32[]{:S(2)}, u32[]{:S(2)}) %collective-permute-start.2) | collective-permute-done | bytes 1048608 | tf_op jit(solution)/shard_map/ppermute | solution.py:1046
  158.0 38.9 %layer_backward.5 = (f32[12,1024]{1,0:T(8,128)}, bf16[1024,4096]{1,0:T(8,128)(2,1)}, bf16[1024,1024]{1,0:T(8,128)(2,1)}, bf16[512,1024]{1,0:T(8,128)(2,1)}, bf16...) custom-call(s32[2]{0:T(128)} %bitcast.110, ...), custom_call_target="tpu_custom_call", output_to_operand_aliasing={{1}: (15, {}), {2}: (16, {}), {4}: (17, {}), {5}: (18, {}),... | custom-call | flops 99999997952 | bytes 1 | tf_op jit(solution)/shard_map/layer_backward/pallas_call | solution.py:677
  211.0 14.7 %turn.1 = (bf16[2,512,1024]{2,1,0:T(8,128)(2,1)}, bf16[2,512,1024]{2,1,0:T(8,128)(2,1)}, bf16[2,512,1024]{2,1,0:T(8,128)(2,1)}, bf16[2,2048,1024]{2,1,0:T(8,128)(2,1)}) custom-call(bf16[1024,1024]{1,0:T(8,128)(2,1)} %get-tuple-element.251.refs_0_, bf16[1024,1024]{1,0:T(8,128)(2,1)} %get-tuple-element.252.refs_1_, ...), custom_call_target="tpu_custom_call" | custom-call | flops 1 | bytes 1 | tf_op jit(solution)/shard_map/turn/pallas_call | solution.py:750
  226.2 4.2 collective-permute-done.3.rest_0_.refs_3_
  231.4 8.8 %weight_product.8 = bf16[2048,1024]{1,0:T(8,128)(2,1)} custom-call(bf16[2,2048,1024]{2,1,0:T(8,128)(2,1)} %get-tuple-element.265.left, bf16[1024,1024]{1,0:T(8,128)(2,1)} %get-tuple-element.266.right, bf16[512,1024]{1,0:T(8,128)(2,1)} %copy-done.15), custom_call_target="tpu_custom_call" | custom-call | flops 1 | bytes 1 | tf_op jit(solution)/shard_map/weight_product/pallas_call | solution.py:811
  240.2 8.7 %weight_product.9 = bf16[2048,1024]{1,0:T(8,128)(2,1)} custom-call(bf16[2,2048,1024]{2,1,0:T(8,128)(2,1)} %get-tuple-element.265.left, bf16[1024,1024]{1,0:T(8,128)(2,1)} %get-tuple-element.266.right, bf16[512,1024]{1,0:T(8,128)(2,1)} %copy-done.15), custom_call_target="tpu_custom_call" | custom-call | flops 1 | bytes 1 | tf_op jit(solution)/shard_map/weight_product/pallas_call | solution.py:811
  248.9 3.2 sum_terms.23
  253.9 20.6 %layer_backward.6 = (f32[12,1024]{1,0:T(8,128)}, bf16[1024,4096]{1,0:T(8,128)(2,1)}, bf16[1024,1024]{1,0:T(8,128)(2,1)}, f32[512,1024]{1,0:T(8,128)}) custom-call(s32[2]{0:T(128)} %bitcast.111, f32[1,12288]{1,0:T(1,128)} %refs_1_.5, bf16[2,1,512,1024]{3,2,1,0:T(8,128)(2,1)} %refs_2_.13, ...), custom_call_target="tpu_custom_call", output_to_operand_aliasing={{1}: (15, {}), {2}: (16, {})} | custom-call | flops 99999997952 | bytes 1 | tf_op jit(solution)/shard_map/layer_backward/pallas_call | solution.py:677
  274.5 9.7 %weight_product.10 = (bf16[512,1024]{1,0:T(8,128)(2,1)}, bf16[512,1024]{1,0:T(8,128)(2,1)}, bf16[512,1024]{1,0:T(8,128)(2,1)}, bf16[512,1024]{1,0:T(8,128)(2,1)}) custom-call(bf16[2,512,1024]{2,1,0:T(8,128)(2,1)} %get-tuple-element.284.left, bf16[1024,4096]{1,0:T(8,128)(2,1)} %get-tuple-element.285.right), custom_call_target="tpu_custom_call" | custom-call | flops 1 | bytes 1 | tf_op jit(solution)/shard_map/weight_product/pallas_call | solution.py:811
  285.3 8.8 %weight_product.11 = bf16[512,4096]{1,0:T(8,128)(2,1)} custom-call(bf16[2,512,1024]{2,1,0:T(8,128)(2,1)} %get-tuple-element.284.left, bf16[1024,4096]{1,0:T(8,128)(2,1)} %get-tuple-element.285.right), custom_call_target="tpu_custom_call" | custom-call | flops 1 | bytes 1 | tf_op jit(solution)/shard_map/weight_product/pallas_call | solution.py:811
  295.1 3.4 sum_terms.24
  300.5 2.9 sum_terms.25
  305.3 4.2 weight_product.12
  309.4 4.2 weight_product.13
  313.6 23.8 %layer_backward.7 = (f32[12,1024]{1,0:T(8,128)}, bf16[512,1024]{1,0:T(8,128)(2,1)}, bf16[1024,3072]{1,0:T(8,128)(2,1)}, bf16[1,2,1,512,1024]{4,3,2,1,0:T(8,128)(2,1)}) custom-call(s32[2]{0:T(128)} %bitcast.112, f32[1,12288]{1,0:T(1,128)} %refs_1_.5, bf16[2,1,512,1024]{3,2,1,0:T(8,128)(2,1)} %refs_2_.13, ...), custom_call_target="tpu_custom_call", output_to_operand_aliasing={{2}: (17, {}), {3}: (18, {})} | custom-call | flops 99999997952 | bytes 1 | tf_op jit(solution)/shard_map/layer_backward/pallas_call | solution.py:677
  341.1 7.9 %weight_product.14 = (bf16[512,1024]{1,0:T(8,128)(2,1)}, bf16[512,1024]{1,0:T(8,128)(2,1)}, bf16[512,1024]{1,0:T(8,128)(2,1)}) custom-call(bf16[2,512,1024]{2,1,0:T(8,128)(2,1)} %get-tuple-element.313.left, bf16[1024,3072]{1,0:T(8,128)(2,1)} %get-tuple-element.314.right), custom_call_target="tpu_custom_call" | custom-call | flops 1 | bytes 1 | tf_op jit(solution)/shard_map/weight_product/pallas_call | solution.py:811
  350.6 7.4 %weight_product.15 = bf16[512,3072]{1,0:T(8,128)(2,1)} custom-call(bf16[2,512,1024]{2,1,0:T(8,128)(2,1)} %get-tuple-element.313.left, bf16[1024,3072]{1,0:T(8,128)(2,1)} %get-tuple-element.314.right), custom_call_target="tpu_custom_call" | custom-call | flops 1 | bytes 1 | tf_op jit(solution)/shard_map/weight_product/pallas_call | solution.py:811
  379.5 10.7 %collective-permute-done.20.refs_4_ = bf16[256,1024]{1,0:T(8,128)(2,1)} collective-permute-done((bf16[256,1024]{1,0:T(8,128)(2,1)}, bf16[256,1024]{1,0:T(8,128)(2,1)}, u32[]{:S(2)}, u32[]{:S(2)}) %collective-permute-start.20) | collective-permute-done | bytes 524320 | tf_op jit(solution)/shard_map/ppermute | solution.py:992
  390.2 3.0 sum_terms.32
  393.2 3.2 collective-permute-done.19.refs_4_
  403.2 10.1 %collective-permute-done.27.refs_4_ = bf16[2,64,2048]{2,1,0:T(8,128)(2,1)} collective-permute-done((bf16[2,64,2048]{2,1,0:T(8,128)(2,1)}, bf16[2,64,2048]{2,1,0:T(8,128)(2,1)}, u32[]{:S(2)}, u32[]{:S(2)}) %collective-permute-start.27) | collective-permute-done | bytes 524320 | tf_op jit(solution)/shard_map/ppermute | solution.py:992
  416.4 4.1 collective-permute-done.25.refs_5_
  422.7 7.3 %collective-permute-done.24.refs_4_ = bf16[2,64,2048]{2,1,0:T(8,128)(2,1)S(1)} collective-permute-done((bf16[2,64,2048]{2,1,0:T(8,128)(2,1)S(1)}, bf16[2,64,2048]{2,1,0:T(8,128)(2,1)S(1)}, u32[]{:S(2)}, u32[]{:S(2)}) %collective-permute-start.24) | collective-permute-done | bytes 524320 | tf_op jit(solution)/shard_map/ppermute | solution.py:992
  437.8 2.9 collective-permute-start.32
  441.3 4.3 collective-permute-done.28.refs_5_
  (186 shorter events, 90.8 us)
Async XLA Ops:
  32.4 24.9 %collective-permute-start = (bf16[512,1024]{1,0:T(8,128)(2,1)}, bf16[512,1024]{1,0:T(8,128)(2,1)S(1)}, u32[]{:S(2)}, u32[]{:S(2)}) collective-permute-start(bf16[512,1024]{1,0:T(8,128)(2,1)} %get-tuple-element.207), channel_id=1, source_target_pairs={{0,16},{1,17},{2,18},{3,19},{4,20},{5,21},{6,22},{7,23},{8,24},{9,... | collective-permute-start | bytes 3145736 | tf_op jit(solution)/shard_map/ppermute | solution.py:1046
  90.0 27.5 %collective-permute-start.1 = (bf16[512,1024]{1,0:T(8,128)(2,1)}, bf16[512,1024]{1,0:T(8,128)(2,1)}, u32[]{:S(2)}, u32[]{:S(2)}) collective-permute-start(bf16[512,1024]{1,0:T(8,128)(2,1)} %get-tuple-element.220.refs_3_), channel_id=1, source_target_pairs={{0,16},{1,17},{2,18},{3,19},{4,20},{5,21},{6,22},{7,23},{8,24},{9,... | collective-permute-start | bytes 3145736 | tf_op jit(solution)/shard_map/ppermute | solution.py:1046
  97.5 59.5 %collective-permute-start.2 = (bf16[512,1024]{1,0:T(8,128)(2,1)}, bf16[512,1024]{1,0:T(8,128)(2,1)S(1)}, u32[]{:S(2)}, u32[]{:S(2)}) collective-permute-start(bf16[512,1024]{1,0:T(8,128)(2,1)} %get-tuple-element.233), channel_id=1, source_target_pairs={{16,0},{17,1},{18,2},{19,3},{20,4},{21,5},{22,6},{23,7},{24,8},{25... | collective-permute-start | bytes 3145736 | tf_op jit(solution)/shard_map/ppermute | solution.py:1046
  196.9 33.5 %collective-permute-start.3 = (bf16[512,1024]{1,0:T(8,128)(2,1)}, bf16[512,1024]{1,0:T(8,128)(2,1)S(1)}, u32[]{:S(2)}, u32[]{:S(2)}) collective-permute-start(bf16[512,1024]{1,0:T(8,128)(2,1)} %get-tuple-element.246), channel_id=1, source_target_pairs={{16,0},{17,1},{18,2},{19,3},{20,4},{21,5},{22,6},{23,7},{24,8},{25... | collective-permute-start | bytes 3145736 | tf_op jit(solution)/shard_map/ppermute | solution.py:1046
  208.1 17.6 %collective-permute-start.7 = (f32[128]{0:T(128)S(1)}, f32[128]{0:T(128)S(1)}, u32[]{:S(2)}, u32[]{:S(2)}) collective-permute-start(f32[128]{0:T(128)S(1)} %add.60), channel_id=1, source_target_pairs={{0,8},{1,9},{2,10},{3,11},{4,12},{5,13},{6,14},{7,15},{8,0},{9,1},... | collective-permute-start | bytes 1544 | tf_op jit(solution)/shard_map/ppermute | solution.py:992
  240.2 8.7 %collective-permute-start.8 = (bf16[2048,1024]{1,0:T(8,128)(2,1)}, bf16[2048,1024]{1,0:T(8,128)(2,1)}, u32[]{:S(2)}, u32[]{:S(2)}) collective-permute-start(bf16[2048,1024]{1,0:T(8,128)(2,1)} %weight_product.8), channel_id=1, source_target_pairs={{0,1},{1,0},{2,3},{3,2},{4,5},{5,4},{6,7},{7,6},{8,9},{9,8},{10,11... | collective-permute-start | bytes 12582920 | tf_op jit(solution)/shard_map/ppermute | solution.py:992
  252.1 48.4 %collective-permute-start.9 = (bf16[2,2,256,1024]{3,2,1,0:T(8,128)(2,1)}, bf16[2,2,256,1024]{3,2,1,0:T(8,128)(2,1)}, u32[]{:S(2)}, u32[]{:S(2)}) collective-permute-start(bf16[2,2,256,1024]{3,2,1,0:T(8,128)(2,1)} %sum_terms.23), channel_id=1, source_target_pairs={{0,2},{1,3},{2,0},{3,1},{4,6},{5,7},{6,4},{7,5},{8,10},{9,11},{10,... | collective-permute-start | bytes 6291464 | tf_op jit(solution)/shard_map/ppermute | solution.py:992
  284.2 9.9 %collective-permute-start.10 = (bf16[512,1024]{1,0:T(8,128)(2,1)}, bf16[512,1024]{1,0:T(8,128)(2,1)S(1)}, u32[]{:S(2)}, u32[]{:S(2)}) collective-permute-start(bf16[512,1024]{1,0:T(8,128)(2,1)} %get-tuple-element.280), channel_id=1, source_target_pairs={{0,1},{1,0},{2,3},{3,2},{4,5},{5,4},{6,7},{7,6},{8,9},{9,8},{10,11... | collective-permute-start | bytes 3145736 | tf_op jit(solution)/shard_map/ppermute | solution.py:992
  284.4 9.7 %collective-permute-start.11 = (bf16[512,1024]{1,0:T(8,128)(2,1)}, bf16[512,1024]{1,0:T(8,128)(2,1)}, u32[]{:S(2)}, u32[]{:S(2)}) collective-permute-start(bf16[512,1024]{1,0:T(8,128)(2,1)} %get-tuple-element.281), channel_id=1, source_target_pairs={{0,1},{1,0},{2,3},{3,2},{4,5},{5,4},{6,7},{7,6},{8,9},{9,8},{10,11... | collective-permute-start | bytes 3145736 | tf_op jit(solution)/shard_map/ppermute | solution.py:992
  284.7 9.4 %collective-permute-start.12 = (bf16[512,1024]{1,0:T(8,128)(2,1)}, bf16[512,1024]{1,0:T(8,128)(2,1)}, u32[]{:S(2)}, u32[]{:S(2)}) collective-permute-start(bf16[512,1024]{1,0:T(8,128)(2,1)} %get-tuple-element.282), channel_id=1, source_target_pairs={{0,1},{1,0},{2,3},{3,2},{4,5},{5,4},{6,7},{7,6},{8,9},{9,8},{10,11... | collective-permute-start | bytes 3145736 | tf_op jit(solution)/shard_map/ppermute | solution.py:992
  284.9 9.2 %collective-permute-start.13 = (bf16[512,1024]{1,0:T(8,128)(2,1)}, bf16[512,1024]{1,0:T(8,128)(2,1)}, u32[]{:S(2)}, u32[]{:S(2)}) collective-permute-start(bf16[512,1024]{1,0:T(8,128)(2,1)} %get-tuple-element.283), channel_id=1, source_target_pairs={{0,1},{1,0},{2,3},{3,2},{4,5},{5,4},{6,7},{7,6},{8,9},{9,8},{10,11... | collective-permute-start | bytes 3145736 | tf_op jit(solution)/shard_map/ppermute | solution.py:992
  298.5 64.8 %collective-permute-start.18 = (bf16[2,2,64,4096]{3,2,1,0:T(8,128)(2,1)}, bf16[2,2,64,4096]{3,2,1,0:T(8,128)(2,1)}, u32[]{:S(2)}, u32[]{:S(2)}) collective-permute-start(bf16[2,2,64,4096]{3,2,1,0:T(8,128)(2,1)} %sum_terms.24), channel_id=1, source_target_pairs={{0,2},{1,3},{2,0},{3,1},{4,6},{5,7},{6,4},{7,5},{8,10},{9,11},{10,... | collective-permute-start | bytes 6291464 | tf_op jit(solution)/shard_map/ppermute | solution.py:992
  303.4 34.0 %collective-permute-start.14 = (bf16[2,256,1024]{2,1,0:T(8,128)(2,1)}, bf16[2,256,1024]{2,1,0:T(8,128)(2,1)S(1)}, u32[]{:S(2)}, u32[]{:S(2)}) collective-permute-start(bf16[2,256,1024]{2,1,0:T(8,128)(2,1)} %sum_terms.25), channel_id=1, source_target_pairs={{0,4},{1,5},{2,6},{3,7},{4,0},{5,1},{6,2},{7,3},{8,12},{9,13},{10,... | collective-permute-start | bytes 3145736 | tf_op jit(solution)/shard_map/ppermute | solution.py:992
  349.0 9.0 %collective-permute-start.15 = (bf16[512,1024]{1,0:T(8,128)(2,1)}, bf16[512,1024]{1,0:T(8,128)(2,1)}, u32[]{:S(2)}, u32[]{:S(2)}) collective-permute-start(bf16[512,1024]{1,0:T(8,128)(2,1)} %get-tuple-element.310), channel_id=1, source_target_pairs={{0,1},{1,0},{2,3},{3,2},{4,5},{5,4},{6,7},{7,6},{8,9},{9,8},{10,11... | collective-permute-start | bytes 3145736 | tf_op jit(solution)/shard_map/ppermute | solution.py:992
  349.0 9.0 %collective-permute-start.16 = (bf16[512,1024]{1,0:T(8,128)(2,1)}, bf16[512,1024]{1,0:T(8,128)(2,1)}, u32[]{:S(2)}, u32[]{:S(2)}) collective-permute-start(bf16[512,1024]{1,0:T(8,128)(2,1)} %get-tuple-element.311), channel_id=1, source_target_pairs={{0,1},{1,0},{2,3},{3,2},{4,5},{5,4},{6,7},{7,6},{8,9},{9,8},{10,11... | collective-permute-start | bytes 3145736 | tf_op jit(solution)/shard_map/ppermute | solution.py:992
  349.9 23.1 %collective-permute-start.22 = (bf16[512,1024]{1,0:T(8,128)(2,1)}, bf16[512,1024]{1,0:T(8,128)(2,1)}, u32[]{:S(2)}, u32[]{:S(2)}) collective-permute-start(bf16[512,1024]{1,0:T(8,128)(2,1)} %get-tuple-element.312), channel_id=1, source_target_pairs={{0,1},{1,0},{2,3},{3,2},{4,5},{5,4},{6,7},{7,6},{8,9},{9,8},{10,11... | collective-permute-start | bytes 3145736 | tf_op jit(solution)/shard_map/ppermute | solution.py:992
  350.0 25.9 %collective-permute-start.21 = (bf16[512,1024]{1,0:T(8,128)(2,1)}, bf16[512,1024]{1,0:T(8,128)(2,1)}, u32[]{:S(2)}, u32[]{:S(2)}) collective-permute-start(bf16[512,1024]{1,0:T(8,128)(2,1)} %weight_product.12), channel_id=1, source_target_pairs={{0,1},{1,0},{2,3},{3,2},{4,5},{5,4},{6,7},{7,6},{8,9},{9,8},{10,11... | collective-permute-start | bytes 3145736 | tf_op jit(solution)/shard_map/ppermute | solution.py:992
  360.5 39.6 %collective-permute-start.17 = (bf16[2,2,64,2048]{3,2,1,0:T(8,128)(2,1)}, bf16[2,2,64,2048]{3,2,1,0:T(8,128)(2,1)}, u32[]{:S(2)}, u32[]{:S(2)}) collective-permute-start(bf16[2,2,64,2048]{3,2,1,0:T(8,128)(2,1)} %sum_terms.27), channel_id=1, source_target_pairs={{0,2},{1,3},{2,0},{3,1},{4,6},{5,7},{6,4},{7,5},{8,10},{9,11},{10,... | collective-permute-start | bytes 3145736 | tf_op jit(solution)/shard_map/ppermute | solution.py:992
  363.3 6.9 %collective-permute-start.23 = (bf16[2,2,2,64,128]{4,3,2,1,0:T(8,128)(2,1)S(1)}, bf16[2,2,2,64,128]{4,3,2,1,0:T(8,128)(2,1)S(1)}, u32[]{:S(2)}, u32[]{:S(2)}) collective-permute-start(bf16[2,2,2,64,128]{4,3,2,1,0:T(8,128)(2,1)S(1)} %get-tuple-element.424), channel_id=1, source_target_pairs={{0,1},{1,0},{2,3},{3,2},{4,5},{5,4},{6,7},{7,6},{8,9},{9,8},{10,11... | collective-permute-start | bytes 393224 | tf_op jit(solution)/shard_map/ppermute | solution.py:992
  363.3 26.9 %collective-permute-start.20 = (bf16[256,1024]{1,0:T(8,128)(2,1)}, bf16[256,1024]{1,0:T(8,128)(2,1)}, u32[]{:S(2)}, u32[]{:S(2)}) collective-permute-start(bf16[256,1024]{1,0:T(8,128)(2,1)} %sum_terms.26), channel_id=1, source_target_pairs={{0,8},{1,9},{2,10},{3,11},{4,12},{5,13},{6,14},{7,15},{8,0},{9,1},... | collective-permute-start | bytes 1572872 | tf_op jit(solution)/shard_map/ppermute | solution.py:992
  370.2 26.2 %collective-permute-start.19 = (bf16[2,64,2048]{2,1,0:T(8,128)(2,1)}, bf16[2,64,2048]{2,1,0:T(8,128)(2,1)}, u32[]{:S(2)}, u32[]{:S(2)}) collective-permute-start(bf16[2,64,2048]{2,1,0:T(8,128)(2,1)} %sum_terms.28), channel_id=1, source_target_pairs={{0,4},{1,5},{2,6},{3,7},{4,0},{5,1},{6,2},{7,3},{8,12},{9,13},{10,... | collective-permute-start | bytes 1572872 | tf_op jit(solution)/shard_map/ppermute | solution.py:992
  375.2 39.4 %collective-permute-start.26 = (bf16[2,2,64,1152]{3,2,1,0:T(8,128)(2,1)}, bf16[2,2,64,1152]{3,2,1,0:T(8,128)(2,1)S(1)}, u32[]{:S(2)}, u32[]{:S(2)}) collective-permute-start(bf16[2,2,64,1152]{3,2,1,0:T(8,128)(2,1)} %sum_terms.30), channel_id=1, source_target_pairs={{0,2},{1,3},{2,0},{3,1},{4,6},{5,7},{6,4},{7,5},{8,10},{9,11},{10,... | collective-permute-start | bytes 1769480 | tf_op jit(solution)/shard_map/ppermute | solution.py:992
  375.9 37.4 %collective-permute-start.27 = (bf16[2,64,2048]{2,1,0:T(8,128)(2,1)}, bf16[2,64,2048]{2,1,0:T(8,128)(2,1)}, u32[]{:S(2)}, u32[]{:S(2)}) collective-permute-start(bf16[2,64,2048]{2,1,0:T(8,128)(2,1)} %copy-done.13), channel_id=1, source_target_pairs={{0,4},{1,5},{2,6},{3,7},{4,0},{5,1},{6,2},{7,3},{8,12},{9,13},{10,... | collective-permute-start | bytes 1572872 | tf_op jit(solution)/shard_map/ppermute | solution.py:992
  402.5 27.6 %collective-permute-start.24 = (bf16[2,64,2048]{2,1,0:T(8,128)(2,1)S(1)}, bf16[2,64,2048]{2,1,0:T(8,128)(2,1)S(1)}, u32[]{:S(2)}, u32[]{:S(2)}) collective-permute-start(bf16[2,64,2048]{2,1,0:T(8,128)(2,1)S(1)} %sum_terms.34), channel_id=1, source_target_pairs={{0,4},{1,5},{2,6},{3,7},{4,0},{5,1},{6,2},{7,3},{8,12},{9,13},{10,... | collective-permute-start | bytes 1572872 | tf_op jit(solution)/shard_map/ppermute | solution.py:992
  402.6 28.9 %collective-permute-start.31 = (bf16[2,2,64,1024]{3,2,1,0:T(8,128)(2,1)S(1)}, bf16[2,2,64,1024]{3,2,1,0:T(8,128)(2,1)S(1)}, u32[]{:S(2)}, u32[]{:S(2)}) collective-permute-start(bf16[2,2,64,1024]{3,2,1,0:T(8,128)(2,1)S(1)} %copy-done.16), channel_id=1, source_target_pairs={{0,2},{1,3},{2,0},{3,1},{4,6},{5,7},{6,4},{7,5},{8,10},{9,11},{10,... | collective-permute-start | bytes 1572872 | tf_op jit(solution)/shard_map/ppermute | solution.py:992
  403.2 17.3 %collective-permute-start.25 = (bf16[64,2048]{1,0:T(8,128)(2,1)S(1)}, bf16[64,2048]{1,0:T(8,128)(2,1)S(1)}, u32[]{:S(2)}, u32[]{:S(2)}) collective-permute-start(bf16[64,2048]{1,0:T(8,128)(2,1)S(1)} %sum_terms.33), channel_id=1, source_target_pairs={{0,8},{1,9},{2,10},{3,11},{4,12},{5,13},{6,14},{7,15},{8,0},{9,1},... | collective-permute-start | bytes 786440 | tf_op jit(solution)/shard_map/ppermute | solution.py:992
  416.2 20.4 %collective-permute-start.29 = (bf16[2,64,1152]{2,1,0:T(8,128)(2,1)S(1)}, bf16[2,64,1152]{2,1,0:T(8,128)(2,1)S(1)}, u32[]{:S(2)}, u32[]{:S(2)}) collective-permute-start(bf16[2,64,1152]{2,1,0:T(8,128)(2,1)S(1)} %sum_terms.36), channel_id=1, source_target_pairs={{0,4},{1,5},{2,6},{3,7},{4,0},{5,1},{6,2},{7,3},{8,12},{9,13},{10,... | collective-permute-start | bytes 884744 | tf_op jit(solution)/shard_map/ppermute | solution.py:992
  416.3 18.1 %collective-permute-start.30 = (bf16[64,2048]{1,0:T(8,128)(2,1)S(1)}, bf16[64,2048]{1,0:T(8,128)(2,1)S(1)}, u32[]{:S(2)}, u32[]{:S(2)}) collective-permute-start(bf16[64,2048]{1,0:T(8,128)(2,1)S(1)} %sum_terms.35), channel_id=1, source_target_pairs={{0,8},{1,9},{2,10},{3,11},{4,12},{5,13},{6,14},{7,15},{8,0},{9,1},... | collective-permute-start | bytes 786440 | tf_op jit(solution)/shard_map/ppermute | solution.py:992
  431.3 14.2 %collective-permute-start.28 = (bf16[64,2048]{1,0:T(8,128)(2,1)S(1)}, bf16[64,2048]{1,0:T(8,128)(2,1)S(1)}, u32[]{:S(2)}, u32[]{:S(2)}) collective-permute-start(bf16[64,2048]{1,0:T(8,128)(2,1)S(1)} %sum_terms.38), channel_id=1, source_target_pairs={{0,8},{1,9},{2,10},{3,11},{4,12},{5,13},{6,14},{7,15},{8,0},{9,1},... | collective-permute-start | bytes 786440 | tf_op jit(solution)/shard_map/ppermute | solution.py:992
  433.0 14.6 %collective-permute-start.33 = (bf16[2,64,1024]{2,1,0:T(8,128)(2,1)S(1)}, bf16[2,64,1024]{2,1,0:T(8,128)(2,1)S(1)}, u32[]{:S(2)}, u32[]{:S(2)}) collective-permute-start(bf16[2,64,1024]{2,1,0:T(8,128)(2,1)S(1)} %sum_terms.39), channel_id=1, source_target_pairs={{0,4},{1,5},{2,6},{3,7},{4,0},{5,1},{6,2},{7,3},{8,12},{9,13},{10,... | collective-permute-start | bytes 786440 | tf_op jit(solution)/shard_map/ppermute | solution.py:992
  437.8 12.3 %collective-permute-start.32 = (bf16[64,1152]{1,0:T(8,128)(2,1)S(1)}, bf16[64,1152]{1,0:T(8,128)(2,1)S(1)}, u32[]{:S(2)}, u32[]{:S(2)}) collective-permute-start(bf16[64,1152]{1,0:T(8,128)(2,1)S(1)} %sum_terms.41), channel_id=1, source_target_pairs={{0,8},{1,9},{2,10},{3,11},{4,12},{5,13},{6,14},{7,15},{8,0},{9,1},... | collective-permute-start | bytes 442376 | tf_op jit(solution)/shard_map/ppermute | solution.py:992
  448.9 9.5 %collective-permute-start.34 = (bf16[64,1024]{1,0:T(8,128)(2,1)S(1)}, bf16[64,1024]{1,0:T(8,128)(2,1)S(1)}, u32[]{:S(2)}, u32[]{:S(2)}) collective-permute-start(bf16[64,1024]{1,0:T(8,128)(2,1)S(1)} %sum_terms.43), channel_id=1, source_target_pairs={{0,8},{1,9},{2,10},{3,11},{4,12},{5,13},{6,14},{7,15},{8,0},{9,1},... | collective-permute-start | bytes 393224 | tf_op jit(solution)/shard_map/ppermute | solution.py:992
  (35 other events, 376.3 us)
